TPU v7x, 256 devices: a whole 4x4x8 slice. The times are simulated.
256 devices in a mesh: gx: 16 (over y, x), gy: 16 (over z, core).
Axes of the slice: x: 4, y: 4, z: 8, core: 2. Of those that a mesh axis runs over, the one named last changes fastest.
Arguments:
- vectors: float32 [8, 128, 256, 256], P(None, 'gx', 'gy'), may hold values from -10 to 10
- weight_x: float32 [128, 256, 256], P('gx', 'gy'), may hold values from 0.05 to 1
- weight_y: float32 [128, 256, 256], P('gx', 'gy'), may hold values from 0.05 to 1
- weight_z: float32 [128, 256, 256], P('gx', 'gy'), may hold values from 0.05 to 1
Outputs:
- refined: float32 [8, 128, 256, 256], P(None, 'gx', 'gy')
- eigenvalues: float32 [8], replicated
All inputs are finite; a program needn't handle non-finite values.
Results may differ from a plain program's by a relative error of at most 0.000075.
Values sent between devices are 32-bit elements; how exact they have to be, the bound alone decides.
No kernel may reach another device: no remote copies, remote signals or barrier semaphores. Data moves between devices by JAX's collectives and lax.ppermute only.
A program may use at most 128 MiB of HBM per device.

v0:
```python
import jax
import jax.numpy as jnp
from jax import lax
from jax.sharding import PartitionSpec as P

COARSE_SWEEPS = 4


OMEGA = 0.8
SHIFT = 0.1


def shifted(shard, axis, by):
    count = lax.axis_size(axis)
    pairs = [(i, i + by) for i in range(count) if 0 <= i + by < count]
    return lax.ppermute(shard, axis, pairs)


def with_halo(cells, sides, width):
    for axis, dim in sides:
        count = lax.axis_size(axis)
        ends = count - 1
        head = lax.slice_in_dim(cells, 0, width, axis=dim)
        tail = lax.slice_in_dim(cells, cells.shape[dim] - width, cells.shape[dim], axis=dim)
        cells = jnp.concatenate(
            [
                lax.ppermute(tail, axis, [(i, (i + 1) % count) for i in range(ends)]),
                cells,
                lax.ppermute(head, axis, [((i + 1) % count, i) for i in range(ends)]),
            ],
            axis=dim,
        )
    return cells


def lower_x(weights):
    rim = shifted(weights[-1:], "gx", 1)
    return jnp.concatenate([rim, weights[:-1]], 0)


def lower_y(weights):
    rim = shifted(weights[:, -1:], "gy", 1)
    return jnp.concatenate([rim, weights[:, :-1]], 1)


def lower_z(weights):
    return jnp.concatenate([jnp.zeros_like(weights[:, :, :1]), weights[:, :, :-1]], 2)


def trimmed(array):
    return array[..., 1:-1, 1:-1, :]


def inner_sum(field, parts):
    wx, lx, wy, ly, wz, lz = parts
    centre = trimmed(field)
    zpadded = jnp.pad(centre, ((0, 0), (0, 0), (0, 0), (1, 1)))
    total = wx[None] * field[:, 2:, 1:-1] + lx[None] * field[:, :-2, 1:-1]
    total = total + wy[None] * field[:, 1:-1, 2:] + ly[None] * field[:, 1:-1, :-2]
    total = total + wz[None] * zpadded[..., 2:] + lz[None] * zpadded[..., :-2]
    return total


def neighbours(field, parts, level):
    if level == "fine":
        padded = with_halo(field, (("gx", 1), ("gy", 2)), 1)
    else:
        padded = with_halo(field, (("gx", 1), ("gy", 2)), 1)
    return inner_sum(padded, parts)


def jacobi(guess, source, diag, parts, level):
    return (
        guess
        + OMEGA * (source - (diag[None] * guess - neighbours(guess, parts, level))) / diag[None]
    )


def rayleigh_sums(vectors, applied, degree):
    return lax.psum(
        (
            jnp.sum(vectors * applied, axis=(1, 2, 3)),
            jnp.sum(vectors * (degree[None] * vectors), axis=(1, 2, 3)),
        ),
        ("gx", "gy"),
    )


def coarse_weights(wx, wy, wz, degree):
    sx, sy, sz = wx.shape
    shape = (sx // 2, 2, sy // 2, 2, sz // 2, 2)
    cx = wx.reshape(shape)[:, 1].sum(axis=(2, 4))
    cy = wy.reshape(shape)[:, :, :, 1].sum(axis=(1, 4))
    cz = wz.reshape(shape)[..., 1].sum(axis=(1, 3))
    dsum = degree.reshape(shape).sum(axis=(1, 3, 5))
    return (cx, cy, cz, dsum)


def restrict(field):
    kk, sx, sy, sz = field.shape
    return field.reshape(kk, sx // 2, 2, sy // 2, 2, sz // 2, 2).sum(axis=(2, 4, 6))


def prolong(field):
    kk, sx, sy, sz = field.shape
    return jnp.broadcast_to(field[:, :, None, :, None, :, None], (kk, sx, 2, sy, 2, sz, 2)).reshape(
        kk, 2 * sx, 2 * sy, 2 * sz
    )


def per_device(vectors, weight_x, weight_y, weight_z):
    local_x, local_y, depth = weight_x.shape
    span_x = local_x * lax.axis_size("gx")
    span_y = local_y * lax.axis_size("gy")
    pos_x = lax.axis_index("gx") * local_x + lax.broadcasted_iota(jnp.int32, (local_x, 1, 1), 0)
    pos_y = lax.axis_index("gy") * local_y + lax.broadcasted_iota(jnp.int32, (1, local_y, 1), 1)
    pos_z = lax.broadcasted_iota(jnp.int32, (1, 1, depth), 2)
    wx = jnp.where(pos_x < span_x - 1, weight_x, jnp.zeros_like(weight_x))
    wy = jnp.where(pos_y < span_y - 1, weight_y, jnp.zeros_like(weight_y))
    wz = jnp.where(pos_z < depth - 1, weight_z, jnp.zeros_like(weight_z))
    parts = (wx, lower_x(wx), wy, lower_y(wy), wz, lower_z(wz))
    degree = parts[0] + parts[1] + parts[2] + parts[3] + parts[4] + parts[5]
    applied = degree[None] * vectors - neighbours(vectors, parts, "fine")
    numer, denom = rayleigh_sums(vectors, applied, degree)
    eigenvalues = numer / denom
    resid = applied - eigenvalues[:, None, None, None] * (degree[None] * vectors)
    dfine = (1.0 + SHIFT) * degree
    guess = OMEGA * resid / dfine[None]
    guess = jacobi(guess, resid, dfine, parts, "fine")
    fine_rest = resid - (dfine[None] * guess - neighbours(guess, parts, "fine"))
    cx, cy, cz, dsum = coarse_weights(wx, wy, wz, degree)
    cparts = (cx, lower_x(cx), cy, lower_y(cy), cz, lower_z(cz))
    dcoarse = cparts[0] + cparts[1] + cparts[2] + cparts[3] + cparts[4] + cparts[5] + SHIFT * dsum
    rcoarse = restrict(fine_rest)
    correction = OMEGA * rcoarse / dcoarse[None]
    for sweep in range(COARSE_SWEEPS - 1):
        correction = jacobi(correction, rcoarse, dcoarse, cparts, "coarse")
    guess = guess + prolong(correction)
    guess = jacobi(guess, resid, dfine, parts, "fine")
    updated = vectors - guess
    local_gram = jnp.einsum(
        "aijk,bijk->ab", updated, degree[None] * updated, precision=lax.Precision.HIGHEST
    )
    gram = lax.psum(local_gram, ("gx", "gy"))
    gram = gram / (span_x * span_y * depth)
    chol = jnp.linalg.cholesky(gram)
    flat = updated.reshape(updated.shape[0], -1)
    refined = jax.scipy.linalg.solve_triangular(chol, flat, lower=True).reshape(updated.shape)
    return (refined, eigenvalues)


def solution(mesh):
    return jax.shard_map(
        per_device,
        mesh=mesh,
        in_specs=(
            P(None, "gx", "gy", None),
            P("gx", "gy", None),
            P("gx", "gy", None),
            P("gx", "gy", None),
        ),
        out_specs=(P(None, "gx", "gy", None), P()),
        check_vma=False,
    )
```

profile of v0, /device:TPU:1, one launch (start us, length us, event | category | flops | bytes accessed | tf_op | source)
XLA Modules:
  0.0 427.5 jit_solution(8508537190117706973)
XLA Ops:
  1.7 3.9 collective-permute-start
  6.6 4.4 %collective-permute-start.1 = (f32[8,1,256]{2,1,0:T(1,128)S(1)}, f32[8,1,256]{2,1,0:T(1,128)S(1)}, u32[]{:S(2)}, u32[]{:S(2)}) collective-permute-start(f32[8,1,256]{2,1,0:T(1,128)S(1)} %slice.374), channel_id=1, source_target_pairs={{0,1},{1,2},{2,3},{3,4},{4,5},{5,6},{6,7},{7,8},{8,9},{9,10},{10,1... | collective-permute-start | bytes 24584 | tf_op jit(solution)/shard_map/ppermute | solution.py:16
  12.0 3.1 collective-permute-start.3
  16.5 9.8 %reshape.74 = f32[4,2,8,2,128,2]{5,4,3,2,1,0:T(8,128)} reshape(f32[8,16,256]{2,1,0:T(8,128)S(1)} %broadcast_select_fusion.2) | data formatting | bytes 262144 | tf_op jit(solution)/shard_map/reshape | solution.py:92
  26.6 1.9 collective-permute-start.4
  28.6 3.6 collective-permute-start.5
  33.8 2.1 fusion
  35.9 82.2 %all-reduce.9 = (f32[8]{0:T(128)S(1)}, f32[8]{0:T(128)S(1)}) all-reduce(f32[8]{0:T(128)S(1)} %get-tuple-element.19, f32[8]{0:T(128)S(1)} %get-tuple-element.18), channel_id=1, replica_groups=mesh['gx'=16,'gy'=16] {'gx','gy'}, use_global_device_ids=true, to_apply=%region_1.2 | all-reduce | flops 16 | bytes 128 | tf_op jit(solution)/shard_map/psum | solution.py:80
  118.1 1.7 multiply_divide_fusion
  121.8 4.7 %collective-permute-start.7 = (f32[8,1,16,256]{3,2,1,0:T(8,128)}, f32[8,1,16,256]{3,2,1,0:T(8,128)}, u32[]{:S(2)}, u32[]{:S(2)}) collective-permute-start(f32[8,1,16,256]{3,2,1,0:T(8,128)} %get-tuple-element.44), channel_id=1, source_target_pairs={{0,16},{16,32},{32,48},{48,64},{64,80},{80,96},{96,112},{112,128},... | collective-permute-start | bytes 393224 | tf_op jit(solution)/shard_map/ppermute | solution.py:27
  126.5 2.8 slice_reduce_fusion.2
  130.5 2.5 collective-permute-start.14
  133.0 9.7 %reshape.75 = f32[4,2,8,2,128,2]{5,4,3,2,1,0:T(8,128)} reshape(f32[8,16,256]{2,1,0:T(8,128)S(1)} %broadcast_select_fusion.1) | data formatting | bytes 262144 | tf_op jit(solution)/shard_map/reshape | solution.py:93
  143.8 3.4 collective-permute-start.8
  147.2 2.9 collective-permute-start.9
  150.1 2.8 slice_reduce_fusion.1
  153.5 2.5 collective-permute-start.15
  156.1 9.8 %reshape.76 = f32[4,2,8,2,128,2]{5,4,3,2,1,0:T(8,128)} reshape(f32[8,16,256]{2,1,0:T(8,128)S(1)} %broadcast_select_fusion) | data formatting | bytes 262144 | tf_op jit(solution)/shard_map/reshape | solution.py:94
  166.1 5.3 %fusion.13 = f32[8,8,16,256]{3,2,1,0:T(8,128)S(1)} fusion(f32[8,8,16,256]{3,2,1,0:T(8,128)} %copy-done.1, f32[8,8,16,256]{3,2,1,0:T(8,128)S(1)} %get-tuple-element.27, f32[8,10,1,256]{3,2,1,0:T(1,128)S(1)} %copy.441, f32[8,1,16,256]{3,2,1,0:T(8,128)} %copy-done.25, f32[8,1,16,256]{3,2,1,0:T(8,128)} %collective-permute-done.7, ...), kind=kLoop, calls=%fused_computation.28 | loop fusion | flops 6553600 | bytes 4489216 | tf_op jit(solution)/shard_map/add | solution.py:74
  173.4 4.7 %collective-permute-start.11 = (f32[8,1,16,256]{3,2,1,0:T(8,128)}, f32[8,1,16,256]{3,2,1,0:T(8,128)}, u32[]{:S(2)}, u32[]{:S(2)}) collective-permute-start(f32[8,1,16,256]{3,2,1,0:T(8,128)} %get-tuple-element.42), channel_id=1, source_target_pairs={{0,16},{16,32},{32,48},{48,64},{64,80},{80,96},{96,112},{112,128},... | collective-permute-start | bytes 393224 | tf_op jit(solution)/shard_map/ppermute | solution.py:27
  178.1 6.8 %slice_reduce_fusion = f32[4,8,128]{2,1,0:T(8,128)} fusion(f32[4,2,8,2,128,2]{5,4,3,2,1,0:T(8,128)} %reshape.76), kind=kLoop, calls=%fused_computation | loop fusion | flops 12288 | bytes 81920 | tf_op jit(solution)/shard_map/reduce_sum | solution.py:94
  184.8 10.5 %reshape.77 = f32[4,2,8,2,128,2]{5,4,3,2,1,0:T(8,128)} reshape(f32[8,16,256]{2,1,0:T(8,128)} %copy-done.8) | data formatting | bytes 262144 | tf_op jit(solution)/shard_map/reshape | solution.py:95
  195.3 4.6 %reduce_sum.69 = f32[4,8,128]{2,1,0:T(8,128)} reduce(f32[4,2,8,2,128,2]{5,4,3,2,1,0:T(8,128)} %reshape.77, f32[]{:T(128)} %constant.65.clone.1), dimensions={1,3,5}, to_apply=%region_8.9 | reduce | flops 28672 | bytes 147460 | tf_op jit(solution)/shard_map/reduce_sum | solution.py:95
  201.2 3.0 collective-permute-start.12
  204.3 2.5 collective-permute-start.13
  208.5 2.8 fusion.19
  211.3 9.8 %copy.446 = f32[8,8,16,256]{0,3,2,1:T(8,128)} copy(f32[8,8,16,256]{3,2,1,0:T(8,128)} %fusion.19) | data formatting | bytes 2097152 | tf_op jit(solution)/shard_map/sub | solution.py:130
  221.1 13.1 %reduce_sum.65 = f32[8,4,8,128]{0,3,2,1:T(8,128)} reduce(f32[8,4,2,8,2,128,2]{0,6,5,4,3,2,1:T(2,128)} %bitcast.30, f32[]{:T(128)} %constant.65.clone.1), dimensions={2,4,6}, to_apply=%region_4.5 | reduce | flops 229376 | bytes 1179652 | tf_op jit(solution)/shard_map/reduce_sum | solution.py:101
  234.2 2.8 copy.447
  239.4 4.0 collective-permute-start.17
  244.4 2.9 collective-permute-start.18
  247.4 4.3 %collective-permute-start.19 = (f32[8,6,1,128]{3,2,1,0:T(1,128)S(1)}, f32[8,6,1,128]{3,2,1,0:T(1,128)S(1)}, u32[]{:S(2)}, u32[]{:S(2)}) collective-permute-start(f32[8,6,1,128]{3,2,1,0:T(1,128)S(1)} %get-tuple-element.53), channel_id=1, source_target_pairs={{0,1},{1,2},{2,3},{3,4},{4,5},{5,6},{6,7},{7,8},{8,9},{9,10},{10,1... | collective-permute-start | bytes 73736 | tf_op jit(solution)/shard_map/ppermute | solution.py:27
  255.1 4.6 %collective-permute-start.21 = (f32[8,1,8,128]{3,2,1,0:T(8,128)S(1)}, f32[8,1,8,128]{3,2,1,0:T(8,128)S(1)}, u32[]{:S(2)}, u32[]{:S(2)}) collective-permute-start(f32[8,1,8,128]{3,2,1,0:T(8,128)S(1)} %get-tuple-element.56), channel_id=1, source_target_pairs={{0,16},{16,32},{32,48},{48,64},{64,80},{80,96},{96,112},{112,128},... | collective-permute-start | bytes 98312 | tf_op jit(solution)/shard_map/ppermute | solution.py:27
  260.7 1.9 collective-permute-start.22
  262.6 5.1 %collective-permute-start.23 = (f32[8,6,1,128]{3,2,1,0:T(1,128)S(1)}, f32[8,6,1,128]{3,2,1,0:T(1,128)S(1)}, u32[]{:S(2)}, u32[]{:S(2)}) collective-permute-start(f32[8,6,1,128]{3,2,1,0:T(1,128)S(1)} %get-tuple-element.51), channel_id=1, source_target_pairs={{0,1},{1,2},{2,3},{3,4},{4,5},{5,6},{6,7},{7,8},{8,9},{9,10},{10,1... | collective-permute-start | bytes 73736 | tf_op jit(solution)/shard_map/ppermute | solution.py:27
  270.1 4.6 %collective-permute-start.25 = (f32[8,1,8,128]{3,2,1,0:T(8,128)S(1)}, f32[8,1,8,128]{3,2,1,0:T(8,128)S(1)}, u32[]{:S(2)}, u32[]{:S(2)}) collective-permute-start(f32[8,1,8,128]{3,2,1,0:T(8,128)S(1)} %get-tuple-element.54), channel_id=1, source_target_pairs={{0,16},{16,32},{32,48},{48,64},{64,80},{80,96},{96,112},{112,128},... | collective-permute-start | bytes 98312 | tf_op jit(solution)/shard_map/ppermute | solution.py:27
  275.8 1.9 collective-permute-start.26
  277.7 5.1 %collective-permute-start.27 = (f32[8,6,1,128]{3,2,1,0:T(1,128)S(1)}, f32[8,6,1,128]{3,2,1,0:T(1,128)S(1)}, u32[]{:S(2)}, u32[]{:S(2)}) collective-permute-start(f32[8,6,1,128]{3,2,1,0:T(1,128)S(1)} %get-tuple-element.49), channel_id=1, source_target_pairs={{0,1},{1,2},{2,3},{3,4},{4,5},{5,6},{6,7},{7,8},{8,9},{9,10},{10,1... | collective-permute-start | bytes 73736 | tf_op jit(solution)/shard_map/ppermute | solution.py:27
  284.5 2.9 copy.451
  287.4 7.1 %broadcast_in_dim.30 = f32[8,4,2,8,2,128,2]{0,6,5,4,3,2,1:T(2,128)} broadcast(f32[8,4,8,128]{0,3,2,1:T(8,128)} %copy.451), dimensions={0,1,3,5} | broadcast | bytes 1179648 | tf_op jit(solution)/shard_map/broadcast_in_dim | solution.py:106
  294.5 10.6 %copy.452 = f32[8,8,16,256]{3,2,1,0:T(8,128)} copy(f32[8,8,16,256]{0,3,2,1:T(8,128)} %bitcast.31) | data formatting | bytes 2097152 | tf_op jit(solution)/shard_map/reshape | solution.py:106
  308.1 4.6 %collective-permute-start.29 = (f32[8,1,16,256]{3,2,1,0:T(8,128)S(1)}, f32[8,1,16,256]{3,2,1,0:T(8,128)S(1)}, u32[]{:S(2)}, u32[]{:S(2)}) collective-permute-start(f32[8,1,16,256]{3,2,1,0:T(8,128)S(1)} %get-tuple-element.40), channel_id=1, source_target_pairs={{0,16},{16,32},{32,48},{48,64},{64,80},{80,96},{96,112},{112,128},... | collective-permute-start | bytes 393224 | tf_op jit(solution)/shard_map/ppermute | solution.py:27
  313.1 1.5 collective-permute-done.29
  314.7 1.9 collective-permute-start.30
  316.7 5.3 %collective-permute-start.31 = (f32[8,10,1,256]{3,0,2,1:T(8,128)S(1)}, f32[8,10,1,256]{3,0,2,1:T(8,128)S(1)}, u32[]{:S(2)}, u32[]{:S(2)}) collective-permute-start(f32[8,10,1,256]{3,0,2,1:T(8,128)S(1)} %copy.455), channel_id=1, source_target_pairs={{0,1},{1,2},{2,3},{3,4},{4,5},{5,6},{6,7},{7,8},{8,9},{9,10},{10,1... | collective-permute-start | bytes 245768 | tf_op jit(solution)/shard_map/ppermute | solution.py:27
  323.3 1.6 broadcast_multiply_fusion
  324.9 3.0 convolution_bitcast_fusion
  327.9 93.9 %psum.23 = f32[8,8]{0,1:T(8,128)S(1)} all-reduce(f32[8,8]{0,1:T(8,128)S(1)} %convolution_bitcast_fusion), channel_id=1, replica_groups=mesh['gx'=16,'gy'=16] {'gx','gy'}, use_global_device_ids=true, to_apply=%region_9.10 | all-reduce | flops 64 | bytes 512 | tf_op jit(solution)/shard_map/psum | solution.py:144
  (174 shorter events, 39.2 us)
Async XLA Ops:
  1.6 24.6 %copy-start.2 = (f32[8,16,256]{2,1,0:T(8,128)}, f32[8,16,256]{2,1,0:T(8,128)S(1)}, u32[]{:S(2)}) copy-start(f32[8,16,256]{2,1,0:T(8,128)S(1)} %broadcast_select_fusion.2) | copy-start | bytes 393220
  1.7 30.6 %collective-permute-start = (f32[1,16,256]{2,1,0:T(8,128)S(1)}, f32[1,16,256]{2,1,0:T(8,128)S(1)}, u32[]{:S(2)}, u32[]{:S(2)}) collective-permute-start(f32[1,16,256]{2,1,0:T(8,128)S(1)} %slice.372), channel_id=1, source_target_pairs={{0,16},{16,32},{32,48},{48,64},{64,80},{80,96},{96,112},{112,128},... | collective-permute-start | bytes 49160 | tf_op jit(solution)/shard_map/ppermute | solution.py:16
  6.6 25.6 %collective-permute-start.1 = (f32[8,1,256]{2,1,0:T(1,128)S(1)}, f32[8,1,256]{2,1,0:T(1,128)S(1)}, u32[]{:S(2)}, u32[]{:S(2)}) collective-permute-start(f32[8,1,256]{2,1,0:T(1,128)S(1)} %slice.374), channel_id=1, source_target_pairs={{0,1},{1,2},{2,3},{3,4},{4,5},{5,6},{6,7},{7,8},{8,9},{9,10},{10,1... | collective-permute-start | bytes 24584 | tf_op jit(solution)/shard_map/ppermute | solution.py:16
  12.0 14.3 %collective-permute-start.3 = (f32[8,1,16,256]{3,2,1,0:T(8,128)S(1)}, f32[8,1,16,256]{3,2,1,0:T(8,128)S(1)}, u32[]{:S(2)}, u32[]{:S(2)}) collective-permute-start(f32[8,1,16,256]{3,2,1,0:T(8,128)S(1)} %get-tuple-element.47), channel_id=1, source_target_pairs={{0,16},{16,32},{32,48},{48,64},{64,80},{80,96},{96,112},{112,128},... | collective-permute-start | bytes 393224 | tf_op jit(solution)/shard_map/ppermute | solution.py:27
  15.2 11.3 %collective-permute-start.2 = (f32[8,1,16,256]{3,2,1,0:T(8,128)S(1)}, f32[8,1,16,256]{3,2,1,0:T(8,128)S(1)}, u32[]{:S(2)}, u32[]{:S(2)}) collective-permute-start(f32[8,1,16,256]{3,2,1,0:T(8,128)S(1)} %get-tuple-element.46), channel_id=1, source_target_pairs={{16,0},{32,16},{48,32},{64,48},{80,64},{96,80},{112,96},{128,112},... | collective-permute-start | bytes 393224 | tf_op jit(solution)/shard_map/ppermute | solution.py:29
  26.6 6.4 %collective-permute-start.4 = (f32[8,10,1,256]{3,0,2,1:T(8,128)S(1)}, f32[8,10,1,256]{3,0,2,1:T(8,128)S(1)}, u32[]{:S(2)}, u32[]{:S(2)}) collective-permute-start(f32[8,10,1,256]{3,0,2,1:T(8,128)S(1)} %copy.466), channel_id=1, source_target_pairs={{1,0},{2,1},{3,2},{4,3},{5,4},{6,5},{7,6},{8,7},{9,8},{10,9},{11,1... | collective-permute-start | bytes 245768 | tf_op jit(solution)/shard_map/ppermute | solution.py:29
  28.6 5.1 %collective-permute-start.5 = (f32[8,10,1,256]{3,0,2,1:T(8,128)S(1)}, f32[8,10,1,256]{3,0,2,1:T(8,128)S(1)}, u32[]{:S(2)}, u32[]{:S(2)}) collective-permute-start(f32[8,10,1,256]{3,0,2,1:T(8,128)S(1)} %copy.467), channel_id=1, source_target_pairs={{0,1},{1,2},{2,3},{3,4},{4,5},{5,6},{6,7},{7,8},{8,9},{9,10},{10,1... | collective-permute-start | bytes 245768 | tf_op jit(solution)/shard_map/ppermute | solution.py:27
  33.8 84.3 %copy-start.5 = (f32[8,16,256]{2,1,0:T(8,128)S(1)}, f32[8,16,256]{2,1,0:T(8,128)}, u32[]{:S(2)}) copy-start(f32[8,16,256]{2,1,0:T(8,128)} %get-tuple-element.28) | copy-start | bytes 393220
  119.8 22.9 %copy-start.1 = (f32[8,8,16,256]{3,2,1,0:T(8,128)}, f32[8,8,16,256]{3,2,1,0:T(8,128)S(1)}, u32[]{:S(2)}) copy-start(f32[8,8,16,256]{3,2,1,0:T(8,128)S(1)} %get-tuple-element.26) | copy-start | bytes 3145732
  120.6 22.2 %collective-permute-start.6 = (f32[8,1,16,256]{3,2,1,0:T(8,128)}, f32[8,1,16,256]{3,2,1,0:T(8,128)S(1)}, u32[]{:S(2)}, u32[]{:S(2)}) collective-permute-start(f32[8,1,16,256]{3,2,1,0:T(8,128)} %get-tuple-element.45), channel_id=1, source_target_pairs={{16,0},{32,16},{48,32},{64,48},{80,64},{96,80},{112,96},{128,112},... | collective-permute-start | bytes 393224 | tf_op jit(solution)/shard_map/ppermute | solution.py:29
  121.8 20.9 %collective-permute-start.7 = (f32[8,1,16,256]{3,2,1,0:T(8,128)}, f32[8,1,16,256]{3,2,1,0:T(8,128)}, u32[]{:S(2)}, u32[]{:S(2)}) collective-permute-start(f32[8,1,16,256]{3,2,1,0:T(8,128)} %get-tuple-element.44), channel_id=1, source_target_pairs={{0,16},{16,32},{32,48},{48,64},{64,80},{80,96},{96,112},{112,128},... | collective-permute-start | bytes 393224 | tf_op jit(solution)/shard_map/ppermute | solution.py:27
  130.5 76.3 %collective-permute-start.14 = (f32[1,8,128]{2,1,0:T(8,128)}, f32[1,8,128]{2,1,0:T(8,128)}, u32[]{:S(2)}, u32[]{:S(2)}) collective-permute-start(f32[1,8,128]{2,1,0:T(8,128)} %slice.384), channel_id=1, source_target_pairs={{0,16},{16,32},{32,48},{48,64},{64,80},{80,96},{96,112},{112,128},... | collective-permute-start | bytes 12296 | tf_op jit(solution)/shard_map/ppermute | solution.py:16
  143.8 22.1 %collective-permute-start.8 = (f32[8,10,1,256]{3,0,2,1:T(8,128)S(1)}, f32[8,10,1,256]{3,0,2,1:T(8,128)S(1)}, u32[]{:S(2)}, u32[]{:S(2)}) collective-permute-start(f32[8,10,1,256]{3,0,2,1:T(8,128)S(1)} %copy.438), channel_id=1, source_target_pairs={{1,0},{2,1},{3,2},{4,3},{5,4},{6,5},{7,6},{8,7},{9,8},{10,9},{11,1... | collective-permute-start | bytes 245768 | tf_op jit(solution)/shard_map/ppermute | solution.py:29
  147.2 18.7 %collective-permute-start.9 = (f32[8,10,1,256]{3,0,2,1:T(8,128)S(1)}, f32[8,10,1,256]{3,0,2,1:T(8,128)S(1)}, u32[]{:S(2)}, u32[]{:S(2)}) collective-permute-start(f32[8,10,1,256]{3,0,2,1:T(8,128)S(1)} %copy.440), channel_id=1, source_target_pairs={{0,1},{1,2},{2,3},{3,4},{4,5},{5,6},{6,7},{7,8},{8,9},{9,10},{10,1... | collective-permute-start | bytes 245768 | tf_op jit(solution)/shard_map/ppermute | solution.py:27
  153.5 12.5 %copy-start.4 = (f32[8,16,256]{2,1,0:T(8,128)S(1)}, f32[8,16,256]{2,1,0:T(8,128)}, u32[]{:S(2)}) copy-start(f32[8,16,256]{2,1,0:T(8,128)} %copy-done.2) | copy-start | bytes 393220
  153.5 53.3 %collective-permute-start.15 = (f32[4,1,128]{2,1,0:T(1,128)}, f32[4,1,128]{2,1,0:T(1,128)}, u32[]{:S(2)}, u32[]{:S(2)}) collective-permute-start(f32[4,1,128]{2,1,0:T(1,128)} %slice.387), channel_id=1, source_target_pairs={{0,1},{1,2},{2,3},{3,4},{4,5},{5,6},{6,7},{7,8},{8,9},{9,10},{10,1... | collective-permute-start | bytes 6152 | tf_op jit(solution)/shard_map/ppermute | solution.py:16
  172.1 27.9 %collective-permute-start.10 = (f32[8,1,16,256]{3,2,1,0:T(8,128)}, f32[8,1,16,256]{3,2,1,0:T(8,128)}, u32[]{:S(2)}, u32[]{:S(2)}) collective-permute-start(f32[8,1,16,256]{3,2,1,0:T(8,128)} %get-tuple-element.43), channel_id=1, source_target_pairs={{16,0},{32,16},{48,32},{64,48},{80,64},{96,80},{112,96},{128,112},... | collective-permute-start | bytes 393224 | tf_op jit(solution)/shard_map/ppermute | solution.py:29
  173.4 26.6 %collective-permute-start.11 = (f32[8,1,16,256]{3,2,1,0:T(8,128)}, f32[8,1,16,256]{3,2,1,0:T(8,128)}, u32[]{:S(2)}, u32[]{:S(2)}) collective-permute-start(f32[8,1,16,256]{3,2,1,0:T(8,128)} %get-tuple-element.42), channel_id=1, source_target_pairs={{0,16},{16,32},{32,48},{48,64},{64,80},{80,96},{96,112},{112,128},... | collective-permute-start | bytes 393224 | tf_op jit(solution)/shard_map/ppermute | solution.py:27
  201.2 7.0 %collective-permute-start.12 = (f32[8,10,1,256]{3,0,2,1:T(8,128)S(1)}, f32[8,10,1,256]{3,0,2,1:T(8,128)S(1)}, u32[]{:S(2)}, u32[]{:S(2)}) collective-permute-start(f32[8,10,1,256]{3,0,2,1:T(8,128)S(1)} %copy.442), channel_id=1, source_target_pairs={{1,0},{2,1},{3,2},{4,3},{5,4},{6,5},{7,6},{8,7},{9,8},{10,9},{11,1... | collective-permute-start | bytes 245768 | tf_op jit(solution)/shard_map/ppermute | solution.py:29
  204.3 4.1 collective-permute-start.13
  237.0 31.6 %copy-start.10 = (f32[8,4,8,128]{3,2,1,0:T(8,128)S(1)}, f32[8,4,8,128]{3,2,1,0:T(8,128)}, u32[]{:S(2)}) copy-start(f32[8,4,8,128]{3,2,1,0:T(8,128)} %copy.447) | copy-start | bytes 393220
  237.0 31.6 %copy-start.22 = (f32[4,8,128]{2,1,0:T(8,128)S(1)}, f32[4,8,128]{2,1,0:T(8,128)}, u32[]{:S(2)}) copy-start(f32[4,8,128]{2,1,0:T(8,128)} %copy-done.20) | copy-start | bytes 49156
  237.0 31.6 %copy-start.24 = (f32[4,8,128]{2,1,0:T(8,128)S(1)}, f32[4,8,128]{2,1,0:T(8,128)}, u32[]{:S(2)}) copy-start(f32[4,8,128]{2,1,0:T(8,128)} %slice_reduce_fusion) | copy-start | bytes 49156
  237.0 31.6 %copy-start.29 = (f32[4,8,128]{2,1,0:T(8,128)S(1)}, f32[4,8,128]{2,1,0:T(8,128)}, u32[]{:S(2)}) copy-start(f32[4,8,128]{2,1,0:T(8,128)} %get-tuple-element.24) | copy-start | bytes 49156
  237.0 31.6 %copy-start.30 = (f32[4,8,128]{2,1,0:T(8,128)S(1)}, f32[4,8,128]{2,1,0:T(8,128)}, u32[]{:S(2)}) copy-start(f32[4,8,128]{2,1,0:T(8,128)} %get-tuple-element.25) | copy-start | bytes 49156
  237.0 31.6 %copy-start.31 = (f32[4,8,128]{2,1,0:T(8,128)S(1)}, f32[4,8,128]{2,1,0:T(8,128)}, u32[]{:S(2)}) copy-start(f32[4,8,128]{2,1,0:T(8,128)} %get-tuple-element.62) | copy-start | bytes 49156
  237.1 31.6 %copy-start.32 = (f32[4,8,128]{2,1,0:T(8,128)S(1)}, f32[4,8,128]{2,1,0:T(8,128)}, u32[]{:S(2)}) copy-start(f32[4,8,128]{2,1,0:T(8,128)} %get-tuple-element.63) | copy-start | bytes 49156
  238.1 5.3 %collective-permute-start.16 = (f32[8,1,8,128]{3,2,1,0:T(8,128)S(1)}, f32[8,1,8,128]{3,2,1,0:T(8,128)S(1)}, u32[]{:S(2)}, u32[]{:S(2)}) collective-permute-start(f32[8,1,8,128]{3,2,1,0:T(8,128)S(1)} %get-tuple-element.59), channel_id=1, source_target_pairs={{16,0},{32,16},{48,32},{64,48},{80,64},{96,80},{112,96},{128,112},... | collective-permute-start | bytes 98312 | tf_op jit(solution)/shard_map/ppermute | solution.py:29
  239.4 5.0 %collective-permute-start.17 = (f32[8,1,8,128]{3,2,1,0:T(8,128)S(1)}, f32[8,1,8,128]{3,2,1,0:T(8,128)S(1)}, u32[]{:S(2)}, u32[]{:S(2)}) collective-permute-start(f32[8,1,8,128]{3,2,1,0:T(8,128)S(1)} %get-tuple-element.58), channel_id=1, source_target_pairs={{0,16},{16,32},{32,48},{48,64},{64,80},{80,96},{96,112},{112,128},... | collective-permute-start | bytes 98312 | tf_op jit(solution)/shard_map/ppermute | solution.py:27
  244.4 7.3 %collective-permute-start.18 = (f32[8,6,1,128]{3,2,1,0:T(1,128)S(1)}, f32[8,6,1,128]{3,2,1,0:T(1,128)S(1)}, u32[]{:S(2)}, u32[]{:S(2)}) collective-permute-start(f32[8,6,1,128]{3,2,1,0:T(1,128)S(1)} %get-tuple-element.52), channel_id=1, source_target_pairs={{1,0},{2,1},{3,2},{4,3},{5,4},{6,5},{7,6},{8,7},{9,8},{10,9},{11,1... | collective-permute-start | bytes 73736 | tf_op jit(solution)/shard_map/ppermute | solution.py:29
  247.4 5.3 %collective-permute-start.19 = (f32[8,6,1,128]{3,2,1,0:T(1,128)S(1)}, f32[8,6,1,128]{3,2,1,0:T(1,128)S(1)}, u32[]{:S(2)}, u32[]{:S(2)}) collective-permute-start(f32[8,6,1,128]{3,2,1,0:T(1,128)S(1)} %get-tuple-element.53), channel_id=1, source_target_pairs={{0,1},{1,2},{2,3},{3,4},{4,5},{5,6},{6,7},{7,8},{8,9},{9,10},{10,1... | collective-permute-start | bytes 73736 | tf_op jit(solution)/shard_map/ppermute | solution.py:27
  253.8 5.9 %collective-permute-start.20 = (f32[8,1,8,128]{3,2,1,0:T(8,128)S(1)}, f32[8,1,8,128]{3,2,1,0:T(8,128)S(1)}, u32[]{:S(2)}, u32[]{:S(2)}) collective-permute-start(f32[8,1,8,128]{3,2,1,0:T(8,128)S(1)} %get-tuple-element.57), channel_id=1, source_target_pairs={{16,0},{32,16},{48,32},{64,48},{80,64},{96,80},{112,96},{128,112},... | collective-permute-start | bytes 98312 | tf_op jit(solution)/shard_map/ppermute | solution.py:29
  255.1 5.6 %collective-permute-start.21 = (f32[8,1,8,128]{3,2,1,0:T(8,128)S(1)}, f32[8,1,8,128]{3,2,1,0:T(8,128)S(1)}, u32[]{:S(2)}, u32[]{:S(2)}) collective-permute-start(f32[8,1,8,128]{3,2,1,0:T(8,128)S(1)} %get-tuple-element.56), channel_id=1, source_target_pairs={{0,16},{16,32},{32,48},{48,64},{64,80},{80,96},{96,112},{112,128},... | collective-permute-start | bytes 98312 | tf_op jit(solution)/shard_map/ppermute | solution.py:27
  260.7 7.0 %collective-permute-start.22 = (f32[8,6,1,128]{3,2,1,0:T(1,128)S(1)}, f32[8,6,1,128]{3,2,1,0:T(1,128)S(1)}, u32[]{:S(2)}, u32[]{:S(2)}) collective-permute-start(f32[8,6,1,128]{3,2,1,0:T(1,128)S(1)} %get-tuple-element.50), channel_id=1, source_target_pairs={{1,0},{2,1},{3,2},{4,3},{5,4},{6,5},{7,6},{8,7},{9,8},{10,9},{11,1... | collective-permute-start | bytes 73736 | tf_op jit(solution)/shard_map/ppermute | solution.py:29
  262.6 6.0 %collective-permute-start.23 = (f32[8,6,1,128]{3,2,1,0:T(1,128)S(1)}, f32[8,6,1,128]{3,2,1,0:T(1,128)S(1)}, u32[]{:S(2)}, u32[]{:S(2)}) collective-permute-start(f32[8,6,1,128]{3,2,1,0:T(1,128)S(1)} %get-tuple-element.51), channel_id=1, source_target_pairs={{0,1},{1,2},{2,3},{3,4},{4,5},{5,6},{6,7},{7,8},{8,9},{9,10},{10,1... | collective-permute-start | bytes 73736 | tf_op jit(solution)/shard_map/ppermute | solution.py:27
  268.8 5.9 %collective-permute-start.24 = (f32[8,1,8,128]{3,2,1,0:T(8,128)S(1)}, f32[8,1,8,128]{3,2,1,0:T(8,128)S(1)}, u32[]{:S(2)}, u32[]{:S(2)}) collective-permute-start(f32[8,1,8,128]{3,2,1,0:T(8,128)S(1)} %get-tuple-element.55), channel_id=1, source_target_pairs={{16,0},{32,16},{48,32},{64,48},{80,64},{96,80},{112,96},{128,112},... | collective-permute-start | bytes 98312 | tf_op jit(solution)/shard_map/ppermute | solution.py:29
  270.1 5.6 %collective-permute-start.25 = (f32[8,1,8,128]{3,2,1,0:T(8,128)S(1)}, f32[8,1,8,128]{3,2,1,0:T(8,128)S(1)}, u32[]{:S(2)}, u32[]{:S(2)}) collective-permute-start(f32[8,1,8,128]{3,2,1,0:T(8,128)S(1)} %get-tuple-element.54), channel_id=1, source_target_pairs={{0,16},{16,32},{32,48},{48,64},{64,80},{80,96},{96,112},{112,128},... | collective-permute-start | bytes 98312 | tf_op jit(solution)/shard_map/ppermute | solution.py:27
  275.8 7.0 %collective-permute-start.26 = (f32[8,6,1,128]{3,2,1,0:T(1,128)S(1)}, f32[8,6,1,128]{3,2,1,0:T(1,128)S(1)}, u32[]{:S(2)}, u32[]{:S(2)}) collective-permute-start(f32[8,6,1,128]{3,2,1,0:T(1,128)S(1)} %get-tuple-element.48), channel_id=1, source_target_pairs={{1,0},{2,1},{3,2},{4,3},{5,4},{6,5},{7,6},{8,7},{9,8},{10,9},{11,1... | collective-permute-start | bytes 73736 | tf_op jit(solution)/shard_map/ppermute | solution.py:29
  277.7 6.0 %collective-permute-start.27 = (f32[8,6,1,128]{3,2,1,0:T(1,128)S(1)}, f32[8,6,1,128]{3,2,1,0:T(1,128)S(1)}, u32[]{:S(2)}, u32[]{:S(2)}) collective-permute-start(f32[8,6,1,128]{3,2,1,0:T(1,128)S(1)} %get-tuple-element.49), channel_id=1, source_target_pairs={{0,1},{1,2},{2,3},{3,4},{4,5},{5,6},{6,7},{7,8},{8,9},{9,10},{10,1... | collective-permute-start | bytes 73736 | tf_op jit(solution)/shard_map/ppermute | solution.py:27
  306.5 16.7 %copy-start.7 = (f32[8,16,256]{2,1,0:T(8,128)S(1)}, f32[8,16,256]{2,1,0:T(8,128)}, u32[]{:S(2)}) copy-start(f32[8,16,256]{2,1,0:T(8,128)} %get-tuple-element.28) | copy-start | bytes 393220
  306.6 16.7 %copy-start.9 = (f32[8,16,256]{2,1,0:T(8,128)S(1)}, f32[8,16,256]{2,1,0:T(8,128)}, u32[]{:S(2)}) copy-start(f32[8,16,256]{2,1,0:T(8,128)} %copy-done.8) | copy-start | bytes 393220
  306.6 16.7 %copy-start.13 = (f32[8,16,256]{2,1,0:T(8,128)S(1)}, f32[8,16,256]{2,1,0:T(8,128)}, u32[]{:S(2)}) copy-start(f32[8,16,256]{2,1,0:T(8,128)} %copy-done.11) | copy-start | bytes 393220
  306.6 16.7 %copy-start.16 = (f32[8,16,256]{2,1,0:T(8,128)S(1)}, f32[8,16,256]{2,1,0:T(8,128)}, u32[]{:S(2)}) copy-start(f32[8,16,256]{2,1,0:T(8,128)} %copy-done.14) | copy-start | bytes 393220
  306.6 16.7 %copy-start.19 = (f32[8,16,256]{2,1,0:T(8,128)S(1)}, f32[8,16,256]{2,1,0:T(8,128)}, u32[]{:S(2)}) copy-start(f32[8,16,256]{2,1,0:T(8,128)} %copy-done.17) | copy-start | bytes 393220
  306.6 6.5 %collective-permute-start.28 = (f32[8,1,16,256]{3,2,1,0:T(8,128)S(1)}, f32[8,1,16,256]{3,2,1,0:T(8,128)S(1)}, u32[]{:S(2)}, u32[]{:S(2)}) collective-permute-start(f32[8,1,16,256]{3,2,1,0:T(8,128)S(1)} %get-tuple-element.41), channel_id=1, source_target_pairs={{16,0},{32,16},{48,32},{64,48},{80,64},{96,80},{112,96},{128,112},... | collective-permute-start | bytes 393224 | tf_op jit(solution)/shard_map/ppermute | solution.py:29
  308.1 6.5 %collective-permute-start.29 = (f32[8,1,16,256]{3,2,1,0:T(8,128)S(1)}, f32[8,1,16,256]{3,2,1,0:T(8,128)S(1)}, u32[]{:S(2)}, u32[]{:S(2)}) collective-permute-start(f32[8,1,16,256]{3,2,1,0:T(8,128)S(1)} %get-tuple-element.40), channel_id=1, source_target_pairs={{0,16},{16,32},{32,48},{48,64},{64,80},{80,96},{96,112},{112,128},... | collective-permute-start | bytes 393224 | tf_op jit(solution)/shard_map/ppermute | solution.py:27
  314.7 7.2 %collective-permute-start.30 = (f32[8,10,1,256]{3,0,2,1:T(8,128)S(1)}, f32[8,10,1,256]{3,0,2,1:T(8,128)S(1)}, u32[]{:S(2)}, u32[]{:S(2)}) collective-permute-start(f32[8,10,1,256]{3,0,2,1:T(8,128)S(1)} %copy.453), channel_id=1, source_target_pairs={{1,0},{2,1},{3,2},{4,3},{5,4},{6,5},{7,6},{8,7},{9,8},{10,9},{11,1... | collective-permute-start | bytes 245768 | tf_op jit(solution)/shard_map/ppermute | solution.py:29
  316.7 6.5 %collective-permute-start.31 = (f32[8,10,1,256]{3,0,2,1:T(8,128)S(1)}, f32[8,10,1,256]{3,0,2,1:T(8,128)S(1)}, u32[]{:S(2)}, u32[]{:S(2)}) collective-permute-start(f32[8,10,1,256]{3,0,2,1:T(8,128)S(1)} %copy.455), channel_id=1, source_target_pairs={{0,1},{1,2},{2,3},{3,4},{4,5},{5,6},{6,7},{7,8},{8,9},{9,10},{10,1... | collective-permute-start | bytes 245768 | tf_op jit(solution)/shard_map/ppermute | solution.py:27
  (21 other events, 130.1 us)
where the time goes:
time: 429 us; the launch traced here: 427 us
  blocking collectives  176 us (41%)
  starting transfers between devices  98.6 us (23%)
  local copies, waits for them, and re-layouts  80.4 us (19%)
  other arithmetic  57.3 us (13%)
  waiting for transfers between devices  9.35 us (2%)
    psum x1, blocking collectives, per_device(): gram = lax.psum(local_gram, ('gx', 'gy'))  93.9 us
    psum x1, blocking collectives, rayleigh_sums(): lax.psum((jnp.sum(vectors * applied, axis=(1, 2, 3)), jnp.sum(vectors * (...  82.2 us
    ppermute x14, starting transfers between devices, with_halo(): lax.ppermute(tail, axis, [(i, (i + 1) % count) for i in range(ends)])  59 us
    ppermute x14, starting transfers between devices, with_halo(): lax.ppermute(head, axis, [((i + 1) % count, i) for i in range(ends)])  26.2 us
    ppermute x4, starting transfers between devices, shifted(): return lax.ppermute(shard, axis, pairs)  13.3 us
    reduce_sum x1, other arithmetic, restrict(): field.reshape(kk, sx // 2, 2, sy // 2, 2, sz // 2, 2).sum(axis=(2, 4, 6))  13.1 us
    reshape x1, local copies, waits for them, and re-layouts, prolong(): jnp.broadcast_to(field[:, :, None, :, None, :, None], (kk, sx, 2, sy, 2,...  10.6 us
    reshape x1, local copies, waits for them, and re-layouts, coarse_weights(): dsum = degree.reshape(shape).sum(axis=(1, 3, 5))  10.5 us
  transfers between devices with their start and end apart: 32, of which 10 were waited for; matrix products, arithmetic and copies ran while one was open for 17% of the time, Pallas kernels for 0%

commit v1 on v0

v1 whole, which is shorter than its diff:
```python
import jax
import jax.numpy as jnp
from jax import lax
from jax.experimental import pallas as pl
from jax.experimental.pallas import tpu as pltpu
from jax.sharding import PartitionSpec as P

OMEGA = 0.8
SHIFT = 0.1
DIAG = 1.0 + SHIFT
C = OMEGA / DIAG
Z0 = 2.0 * C - DIAG * C * C
Z1 = C * C
G0, G1, G2 = 1.0 - DIAG * Z0, Z0 - DIAG * Z1, Z1
KEEP = 1.0 - DIAG * C
B0, B1, B2 = KEEP * Z0 + C, KEEP * Z1 + C * Z0, C * Z1

K = 8
LX, LY, NZ = 8, 16, 256
CX, CY, CZ = LX // 2, LY // 2, NZ // 2
H = 3
CH = 4
JW = 8
MIB = 1024 * 1024
VMEM = pl.BlockSpec(memory_space=pltpu.VMEM)


def call(body, outs, ins, scratch=(), flops=1_000_000):
    nbytes = sum(4 * a.size for a in ins)
    return pl.pallas_call(
        body,
        out_shape=[jax.ShapeDtypeStruct(s, jnp.float32) for s in outs],
        in_specs=[VMEM] * len(ins),
        out_specs=[VMEM] * len(outs),
        scratch_shapes=[pltpu.VMEM(s, jnp.float32) for s in scratch],
        compiler_params=pltpu.CompilerParams(vmem_limit_bytes=56 * MIB),
        cost_estimate=pl.CostEstimate(flops=flops, bytes_accessed=nbytes, transcendentals=0),
    )(*ins)


def row(ref, *at):
    *lead, r = at
    r_ = ref[(*lead, pl.ds(r, 1), slice(None))]
    return jnp.broadcast_to(r_, (8, r_.shape[-1]))


def up_z(a):
    return pltpu.roll(a, a.shape[-1] - 1, a.ndim - 1)


def down_z(a):
    return pltpu.roll(a, 1, a.ndim - 1)


def prepare(v, wx, wy, wz, vt, wm, xu, xd, ylo, yhi):
    last_x = lax.axis_index("gx") == lax.axis_size("gx") - 1
    last_y = lax.axis_index("gy") == lax.axis_size("gy") - 1
    keep_x = jnp.where(last_x, 0.0, 1.0)
    keep_y = jnp.where(last_y, 0.0, 1.0)
    for x in range(LX):
        for t in range(0, LY, 8):
            vt[x, t : t + 8] = jnp.swapaxes(v[:, x, t : t + 8, :], 0, 1)
    wm[0] = wx[...]
    wm[0, LX - 1] = wx[LX - 1] * keep_x
    sub = lax.broadcasted_iota(jnp.int32, (LX, LY, NZ), 1)
    wm[1] = jnp.where(sub == LY - 1, wy[...] * keep_y, wy[...])
    lane = lax.broadcasted_iota(jnp.int32, (LX, LY, NZ), 2)
    wm[2] = jnp.where(lane == NZ - 1, 0.0, wz[...])
    for d in range(H):
        xu[d * LY : (d + 1) * LY] = vt[LX - H + d]
        xd[d * LY : (d + 1) * LY] = vt[d]
    at = H * LY
    for w, x in UP_W:
        xu[at] = wm[w, x, 0:8]
        xu[at + 1] = wm[w, x, 8:16]
        at += 2
    at = H * LY
    for w, x in DN_W:
        xd[at] = wm[w, x, 0:8]
        xd[at + 1] = wm[w, x, 8:16]
        at += 2
    ylo[...] = vt[:, 0:H]
    yhi[...] = vt[:, LY - H : LY]


UP_W = [(0, 5), (0, 6), (0, 7), (1, 6), (1, 7), (2, 6), (2, 7)]
DN_W = [(0, 0), (0, 1), (1, 0), (1, 1), (2, 0), (2, 1)]
NXB = H * LY + 2 * len(UP_W)
YV = [(d, p) for d in (1, 2, 3) for p in range(d - H, LX + H - d)]
YP = list(range(-2, LX + 2))
NYB = len(YV) + len(YP)


def weight_plane(wm, xl, xr, w, p):
    if 0 <= p < LX:
        return wm[w, p, 0:8], wm[w, p, 8:16]
    if p < 0:
        at = H * LY + 2 * UP_W.index((w, p + LX))
        return xl[at], xl[at + 1]
    at = H * LY + 2 * DN_W.index((w, p - LX))
    return xr[at], xr[at + 1]


def fine_y_send(wm, ylo, yhi, xl, xr, yu, yd):
    def cell(p, y):
        if p < 0:
            return xl[(p + H) * LY + y]
        if p >= LX:
            return xr[(p - LX) * LY + y]
        return ylo[p, y] if y < H else yhi[p, y - (LY - H)]

    for n, (d, p) in enumerate(YV):
        yu[n] = cell(p, LY - d)
        yd[n] = cell(p, d - 1)
    for n, p in enumerate(YP, len(YV)):
        wxl, wxh = weight_plane(wm, xl, xr, 0, p)
        wyl, wyh = weight_plane(wm, xl, xr, 1, p)
        wzl, wzh = weight_plane(wm, xl, xr, 2, p)
        yu[n, 0:2] = wxh[6:8]
        yu[n, 2:5] = wyh[5:8]
        yu[n, 5:7] = wzh[6:8]
        yu[n, 7:8] = wzh[7:8]
        yd[n, 0:2] = wxl[0:2]
        yd[n, 2:4] = wyl[0:2]
        yd[n, 4:6] = wzl[0:2]
        yd[n, 6:8] = wzl[0:2]


def planes(radius, body, own, halo):
    def step(n, _):
        body(n + halo, radius)
        return 0

    lax.fori_loop(0, own, step, 0)
    for d in range(1, radius + 1):
        body(halo - d, radius - d)
        body(halo + own - 1 + d, radius - d)


def compress(a, odd=False):
    lane = lax.broadcasted_iota(jnp.int32, (8, 128), 1)
    t = a if odd else a + up_z(a)
    at = (2 * lane + (1 if odd else 0)) & 127
    lo = jnp.take_along_axis(t[:, :128], at, 1)
    hi = jnp.take_along_axis(t[:, 128:], at, 1)
    return jnp.where(lane < 64, lo, hi)


def expand(a):
    lane = lax.broadcasted_iota(jnp.int32, (8, 128), 1)
    half = lane >> 1
    return jnp.concatenate(
        [jnp.take_along_axis(a, half, 1), jnp.take_along_axis(a, half + 64, 1)], 1
    )


def fine_level(vt, wm, xl, xr, yl, yr, pb, nwo, xs, nd, V, W, NW, Y1, Y2, Y3, CW, Q):
    V[H : H + LX, H : H + LY] = vt[...]
    for d in range(H):
        V[d, H : H + LY] = xl[d * LY : (d + 1) * LY]
        V[H + LX + d, H : H + LY] = xr[d * LY : (d + 1) * LY]
    for n, (d, p) in enumerate(YV):
        V[p + H, H - d] = yl[n]
        V[p + H, H + LY - 1 + d] = yr[n]
    for p in range(-H, LX + 2):
        for w in range(3):
            if p == -H and w:
                continue
            lo, hi = weight_plane(wm, xl, xr, w, p)
            W[w, p + H, JW : JW + 8] = lo
            W[w, p + H, JW + 8 : JW + 16] = hi
    for n, p in enumerate(YP, len(YV)):
        i = p + H
        W[0, i, JW - 2 : JW] = yl[n, 0:2]
        W[1, i, JW - 3 : JW] = yl[n, 2:5]
        W[2, i, JW - 2 : JW] = yl[n, 5:7]
        W[0, i, JW + LY : JW + LY + 2] = yr[n, 0:2]
        W[1, i, JW + LY : JW + LY + 2] = yr[n, 2:4]
        W[2, i, JW + LY : JW + LY + 2] = yr[n, 4:6]

    def norm(i, _):
        wx, lx = W[0, i], W[0, i - 1]
        wy = W[1, i]
        ly = pltpu.roll(wy, 1, 0)
        wz = W[2, i]
        lz = down_z(wz)
        deg = wx + lx + wy + ly + wz + lz
        inv = 1.0 / deg
        for a, w in enumerate((wx, lx, wy, ly, wz, lz)):
            NW[a, i] = w * inv
        NW[6, i] = deg
        return 0

    lax.fori_loop(1, LX + 5, norm, 0)

    def apply(src, dst):
        def body(i, reach):
            for j in range(H - reach, H + LY + reach):
                r = j - H + JW
                c = src[i, j]
                dst[i, j] = (
                    row(NW, 0, i, r) * src[i + 1, j]
                    + row(NW, 1, i, r) * src[i - 1, j]
                    + row(NW, 2, i, r) * src[i, j + 1]
                    + row(NW, 3, i, r) * src[i, j - 1]
                    + row(NW, 4, i, r) * up_z(c)
                    + row(NW, 5, i, r) * down_z(c)
                )

        return body

    planes(2, apply(V, Y1), LX, H)
    planes(1, apply(Y1, Y2), LX, H)
    planes(0, apply(Y2, Y3), LX, H)

    for x in range(CX):
        i = 2 * x + H
        own = slice(JW, JW + LY)
        wx, lx = W[0, i + 1, own], W[0, i - 1, own]
        wy = W[1, i] + W[1, i + 1]
        ly = pltpu.roll(wy, 1, 0)
        wz = W[2, i, own] + W[2, i + 1, own]
        dg = NW[6, i, own] + NW[6, i + 1, own]
        for q, (a, odd) in enumerate(
            ((wx, False), (lx, False), (wy[own], False), (ly[own], False), (wz, True), (dg, False))
        ):
            Q[q, x * LY : x * LY + 8] = compress(a[0:8], odd)
            Q[q, x * LY + 8 : x * LY + 16] = compress(a[8:16], odd)
    ri = lax.broadcasted_iota(jnp.int32, (CX * CY, CX * LY), 0)
    ci = lax.broadcasted_iota(jnp.int32, (CX * CY, CX * LY), 1)
    both = jnp.where((ci >> 1) == ri, 1.0, 0.0)
    first = jnp.where(ci == 2 * ri, 1.0, 0.0)
    second = jnp.where(ci == 2 * ri + 1, 1.0, 0.0)

    def rows(m, q):
        return jnp.dot(m, Q[q], precision=lax.Precision.HIGHEST, preferred_element_type=jnp.float32)

    cx, lcx = rows(both, 0), rows(both, 1)
    cy, lcy = rows(second, 2), rows(first, 3)
    cz, dsum = rows(both, 4), rows(both, 5)
    lcz = down_z(cz)
    dc = cx + lcx + cy + lcy + cz + lcz + SHIFT * dsum
    inv = 1.0 / dc
    for a, w in enumerate((cx, lcx, cy, lcy, cz, lcz)):
        w = w * inv
        for x in range(CX):
            xs[2 * CX * CY + 6 * x + a] = w[x * CY : (x + 1) * CY]
    for x in range(CX):
        CW[x] = inv[x * CY : (x + 1) * CY]
    for a in range(7):
        nwo[a] = NW[a, H : H + LX, JW : JW + LY]

    def block(x, sums):
        num, den = sums
        for y in range(CY):
            ra = rb = None
            for dx in range(2):
                for dy in range(2):
                    i = H + 2 * x + dx
                    j = H + 2 * y + dy
                    v, y1, y2, y3 = V[i, j], Y1[i, j], Y2[i, j], Y3[i, j]
                    deg = row(NW, 6, i, j - H + JW)
                    gb = G0 * v + G1 * y1 + G2 * y2
                    ga = gb - (G0 * y1 + G1 * y2 + G2 * y3)
                    b = B0 * v + B1 * y1 + B2 * y2
                    pb[i - H, j - H, 0:8] = v - (b - (B0 * y1 + B1 * y2 + B2 * y3))
                    pb[i - H, j - H, 8:16] = b
                    dv = deg * v
                    num = num + dv * (v - y1)
                    den = den + dv * v
                    ra = deg * ga if ra is None else ra + deg * ga
                    rb = deg * gb if rb is None else rb + deg * gb
            over = row(CW, x, y)
            at = 2 * (x * CY + y)
            xs[at] = compress(ra) * over
            xs[at + 1] = compress(rb) * over
        return num, den

    zero = jnp.zeros((8, NZ), jnp.float32)
    num, den = lax.fori_loop(0, CX, block, (zero, zero))
    nd[0] = num
    nd[1] = den


NCS = 2 * CX * CY + 6 * CX
CF = [(d, i) for d in (1, 2, 3, 4) for i in range(d, CX + 2 * CH - d)]
CP = list(range(2, CX + 2 * CH - 2))
NCY = 2 * len(CF) + 3 * len(CP)


def coarse_plane(own, left, right, i):
    if i < CH:
        return left, i
    if i < CH + CX:
        return own, i - CH
    return right, i - CH - CX


def coarse_y_send(own, left, right, yu, yd):
    for n, (d, i) in enumerate(CF):
        src, x = coarse_plane(own, left, right, i)
        for half in range(2):
            yu[2 * n + half] = src[2 * (x * CY + CY - d) + half]
            yd[2 * n + half] = src[2 * (x * CY + d - 1) + half]
    at = 2 * len(CF)
    for i in CP:
        src, x = coarse_plane(own, left, right, i)
        for t in range(3):
            for u in range(2):
                w = 2 * CX * CY + 6 * x + 2 * t + u
                yu[at, 4 * u : 4 * u + 4] = src[w, 4:8]
                yd[at, 4 * u : 4 * u + 4] = src[w, 0:4]
            at += 1


def coarse_level(own, left, right, yl, yr, pb, nwo, nd, po, bo, sums, F, CW, EA, EB, EX):
    JC = 8
    for i in range(CX + 2 * CH):
        src, x = coarse_plane(own, left, right, i)
        for y in range(CY):
            at = 2 * (x * CY + y)
            for half in range(2):
                f = OMEGA * src[at + half]
                F[i, y + CH, half] = f
                EA[i, y + CH, half] = f
        for a in range(6):
            CW[a, i, JC : JC + CY] = OMEGA * src[2 * CX * CY + 6 * x + a]
    for n, (d, i) in enumerate(CF):
        for half in range(2):
            lo = OMEGA * yl[2 * n + half]
            hi = OMEGA * yr[2 * n + half]
            F[i, CH - d, half] = lo
            EA[i, CH - d, half] = lo
            F[i, CH + CY - 1 + d, half] = hi
            EA[i, CH + CY - 1 + d, half] = hi
    at = 2 * len(CF)
    for i in CP:
        for t in range(3):
            for u in range(2):
                CW[2 * t + u, i, JC - 4 : JC] = OMEGA * yl[at, 4 * u : 4 * u + 4]
                CW[2 * t + u, i, JC + CY : JC + CY + 4] = OMEGA * yr[at, 4 * u : 4 * u + 4]
            at += 1

    def sweep(src, dst):
        def body(i, reach):
            for j in range(CH - reach, CH + CY + reach):
                r = j - CH + JC
                ws = [row(CW, a, i, r) for a in range(6)]
                for half in range(2):
                    c = src[i, j, half]
                    dst[i, j, half] = (
                        (1.0 - OMEGA) * c
                        + F[i, j, half]
                        + ws[0] * src[i + 1, j, half]
                        + ws[1] * src[i - 1, j, half]
                        + ws[2] * src[i, j + 1, half]
                        + ws[3] * src[i, j - 1, half]
                        + ws[4] * up_z(c)
                        + ws[5] * down_z(c)
                    )

        return body

    planes(3, sweep(EA, EB), CX, CH)
    planes(2, sweep(EB, EA), CX, CH)
    planes(1, sweep(EA, EB), CX, CH)

    def spread(i, reach):
        for j in range(CH - reach, CH + CY + reach):
            for half in range(2):
                EX[i, j, half] = expand(EB[i, j, half])

    planes(1, spread, CX, CH)

    def block(x, _):
        for y in range(CY):
            for half in range(2):
                e = EX[x + CH, y + CH, half]
                ez = (up_z(e), down_z(e))
                ke = KEEP * e
                ce = C * e
                for dx in range(2):
                    ex = C * EX[x + CH + 2 * dx - 1, y + CH, half]
                    for dy in range(2):
                        ey = C * EX[x + CH, y + CH + 2 * dy - 1, half]
                        xx, yy = 2 * x + dx, 2 * y + dy
                        nw = [row(nwo, a, xx, yy) for a in range(6)]
                        s = (
                            ke
                            + (nw[dx] + nw[2 + dy]) * ce
                            + nw[1 - dx] * ex
                            + nw[3 - dy] * ey
                            + C * (nw[4] * ez[0] + nw[5] * ez[1])
                        )
                        if half == 0:
                            po[xx, yy] = pb[xx, yy, 0:8] - s
                        else:
                            bo[xx, yy] = pb[xx, yy, 8:16] + s
        return 0

    lax.fori_loop(0, CX, block, 0)

    def gram(n, acc):
        x = n >> 2
        acc = list(acc)
        for q in range(4):
            yy = (n & 3) * 4 + q
            deg = row(nwo, 6, x, yy)
            for h in range(0, NZ, 128):
                z = slice(h, h + 128)
                p = po[x, yy, :, z]
                b = bo[x, yy, :, z]
                dp = deg[:, z] * p
                db = deg[:, z] * b
                for s in range(8):
                    rb = pltpu.roll(db, s, 0) if s else db
                    if s < 5:
                        rp = pltpu.roll(dp, s, 0) if s else dp
                        acc[s] = acc[s] + p * rp
                        acc[5 + s] = acc[5 + s] + b * rb
                    acc[10 + s] = acc[10 + s] + p * rb
        return tuple(acc)

    zero = jnp.zeros((8, 128), jnp.float32)
    acc = list(lax.fori_loop(0, 4 * LX, gram, (zero,) * 18))
    for q in range(2):
        acc.append(nd[q, :, :128] + nd[q, :, 128:])
    ones = jnp.ones((8, 128), jnp.float32)

    def over_lanes(m):
        return lax.dot_general(
            ones,
            m,
            (((1,), (1,)), ((), ())),
            precision=lax.Precision.HIGHEST,
            preferred_element_type=jnp.float32,
        )

    t0 = over_lanes(jnp.concatenate(acc[:16], 0))
    t1 = over_lanes(jnp.concatenate(acc[16:] + [zero] * 12, 0))
    sums[0:1] = t0[0:1]
    sums[1:2] = t1[0:1]


def finish(parts, po, bo, out, eig, SP):
    t = parts[...]
    n = t.shape[0]
    while n > 1:
        n //= 2
        t = t[:n] + t[n:]
    t = t[0]
    eye = lax.broadcasted_iota(jnp.int32, (128, 128), 0) == lax.broadcasted_iota(
        jnp.int32, (128, 128), 1
    )
    ones = jnp.ones((128, 128), jnp.float32)
    for q in range(2):
        m = jnp.where(eye, jnp.broadcast_to(t[q : q + 1], (128, 128)), 0.0)
        SP[128 * q : 128 * (q + 1)] = jnp.dot(
            m, ones, precision=lax.Precision.HIGHEST, preferred_element_type=jnp.float32
        )
    eig[...] = jnp.broadcast_to(t[1:2] / pltpu.roll(t[1:2], 120, 1), (8, 128))

    def entry(block, k):
        return row(SP, 8 * block + k)

    def sym(base, a, b):
        s = (a - b) % 8
        return entry(base + s, a) if s < 5 else entry(base + 8 - s, b)

    def cross(a, b):
        return entry(10 + (a - b) % 8, a)

    lam = [entry(18, k) / entry(19, k) for k in range(K)]
    voxels = LX * LY * NZ * lax.axis_size("gx") * lax.axis_size("gy")
    g = {}
    for a in range(K):
        for b in range(a + 1):
            g[a, b] = (
                sym(0, a, b) + lam[b] * cross(a, b) + lam[a] * (cross(b, a) + lam[b] * sym(5, a, b))
            ) * (1.0 / voxels)
    low, inv = {}, []
    for j in range(K):
        d = g[j, j]
        r = lax.rsqrt(d)
        r = r * (1.5 - 0.5 * d * r * r)
        inv.append(r)
        for a in range(j + 1, K):
            low[a, j] = g[a, j] * r
        for a in range(j + 1, K):
            for b in range(j + 1, a + 1):
                g[a, b] = g[a, b] - low[a, j] * low[b, j]

    for k in range(K):
        SP[8 * k : 8 * k + 8] = lam[k]
        SP[64 + 8 * k : 72 + 8 * k] = inv[k]
    at = {}
    for n, (a, b) in enumerate(sorted(low)):
        at[a, b] = 128 + 8 * n
        SP[128 + 8 * n : 136 + 8 * n] = low[a, b]

    def body(x, _):
        for t in range(0, LY, 8):
            for h in range(0, NZ, 128):
                z = slice(h, h + 128)
                p = jnp.swapaxes(po[x, t : t + 8, :, z], 0, 1)
                b = jnp.swapaxes(bo[x, t : t + 8, :, z], 0, 1)
                done = []
                for k in range(K):
                    u = p[k] + SP[8 * k : 8 * k + 8] * b[k]
                    for j in range(k):
                        u = u - SP[at[k, j] : at[k, j] + 8] * done[j]
                    u = u * SP[64 + 8 * k : 72 + 8 * k]
                    done.append(u)
                    out[k, x, t : t + 8, z] = u
        return 0

    lax.fori_loop(0, LX, body, 0)


def both_ways(up, down, axis):
    n = lax.axis_size(axis)
    fwd = [(i, (i + 1) % n) for i in range(n)]
    back = [((i + 1) % n, i) for i in range(n)]
    return lax.ppermute(up, axis, fwd), lax.ppermute(down, axis, back)


def per_device(vectors, weight_x, weight_y, weight_z):
    vt, wm, xu, xd, ylo, yhi = call(
        prepare,
        [
            (LX, LY, K, NZ),
            (3, LX, LY, NZ),
            (NXB, 8, NZ),
            (NXB, 8, NZ),
            (LX, H, K, NZ),
            (LX, H, K, NZ),
        ],
        (vectors, weight_x, weight_y, weight_z),
    )
    xl, xr = both_ways(xu, xd, "gx")
    yu, yd = call(fine_y_send, [(NYB, 8, NZ)] * 2, (wm, ylo, yhi, xl, xr))
    yl, yr = both_ways(yu, yd, "gy")
    ext = (LX + 2 * H, LY + 2 * H, K, NZ)
    pb, nwo, xs, nd = call(
        fine_level,
        [(LX, LY, 16, NZ), (7, LX, LY, NZ), (NCS, 8, CZ), (2, 8, NZ)],
        (vt, wm, xl, xr, yl, yr),
        [
            ext,
            (3, LX + 2 * H, 32, NZ),
            (7, LX + 2 * H, 32, NZ),
            ext,
            ext,
            ext,
            (CX, CY, CZ),
            (6, CX * LY, CZ),
        ],
    )
    cl, cr = both_ways(xs, xs, "gx")
    yu, yd = call(coarse_y_send, [(NCY, 8, CZ)] * 2, (xs, cl, cr))
    yl, yr = both_ways(yu, yd, "gy")
    cext = (CX + 2 * CH, CY + 2 * CH, 2, 8, CZ)
    po, bo, sums = call(
        coarse_level,
        [(LX, LY, K, NZ), (LX, LY, K, NZ), (2, 128)],
        (xs, cl, cr, yl, yr, pb, nwo, nd),
        [
            cext,
            (6, CX + 2 * CH, 24, CZ),
            cext,
            cext,
            (CX + 2 * CH, CY + 2 * CH, 2, 8, NZ),
        ],
    )
    n = lax.axis_size("gx") * lax.axis_size("gy")
    parts = lax.all_to_all(jnp.broadcast_to(sums[None], (n, 2, 128)), ("gx", "gy"), 0, 0)
    refined, eig = call(
        finish,
        [(K, LX, LY, NZ), (8, 128)],
        (parts, po, bo),
        [(384, 128)],
    )
    return refined, eig[0, 16:24]


def solution(mesh):
    return jax.shard_map(
        per_device,
        mesh=mesh,
        in_specs=(
            P(None, "gx", "gy", None),
            P("gx", "gy", None),
            P("gx", "gy", None),
            P("gx", "gy", None),
        ),
        out_specs=(P(None, "gx", "gy", None), P()),
        check_vma=False,
    )
```

time: 429 us -> 116 us (0.27)
  blocking collectives: 176 us -> 25.6 us
  starting transfers between devices: 98.6 us -> 17.3 us
  local copies, waits for them, and re-layouts: 80.4 us -> 5.12 us
  other arithmetic: 57.3 us -> 0 us
  Pallas kernels: 0 us -> 31.7 us
  waiting for transfers between devices: 9.35 us -> 35.9 us
    psum x2 -> x0, blocking collectives: 176 us -> none  [the longest x1 93.9 us: per_device(): gram = lax.psum(local_gram, ('gx', 'gy'))]
    ppermute x32 -> x8, starting transfers between devices: 98.6 us -> 17.3 us  [both_ways(): return (lax.ppermute(up, axis, fwd), lax.ppermute(down, axis, back))]
    reshape x5 -> x0, local copies, waits for them, and re-layouts: 50.4 us -> none  [the longest x1 10.6 us: prolong(): jnp.broadcast_to(field[:, :, None, :, None, :, None], (kk, sx, 2, sy, 2,...]
    reduce_sum x6 -> x0, other arithmetic: 32.2 us -> none  [the longest x1 13.1 us: restrict(): field.reshape(kk, sx // 2, 2, sy // 2, 2, sz // 2, 2).sum(axis=(2, 4, 6))]
    pallas_call x0 -> x6, Pallas kernels: none -> 31.7 us  [call(): pl.pallas_call(body, out_shape=[jax.ShapeDtypeStruct(s, jnp.float32) for...]
    ppermute x32 -> x8, waiting for transfers between devices: 9.35 us -> 35.9 us  [both_ways(): return (lax.ppermute(up, axis, fwd), lax.ppermute(down, axis, back))]
    all_to_all x0 -> x1, blocking collectives: none -> 25.6 us  [per_device(): lax.all_to_all(jnp.broadcast_to(sums[None], (n, 2, 128)), ('gx', 'gy'), 0...]
    add x6 -> x0, other arithmetic: 10.2 us -> none  [the longest x4 7.41 us: jacobi(): guess + OMEGA * (source - (diag[None] * guess - neighbours(guess, parts,...]
  transfers between devices with their start and end apart: 32 -> 8, of which waited for: 10 -> 7; matrix products, arithmetic and copies ran while one was open for 17% -> 0% of each run, Pallas kernels for 0% -> 0%
where the time goes in v1:
time: 116 us
  waiting for transfers between devices  35.9 us (31%)
  Pallas kernels  31.7 us (27%)
  blocking collectives  25.6 us (22%)
  starting transfers between devices  17.3 us (15%)
  local copies, waits for them, and re-layouts  5.12 us (4%)
    ppermute x8, waiting for transfers between devices, both_ways(): return (lax.ppermute(up, axis, fwd), lax.ppermute(down, axis, back))  35.9 us
    pallas_call x6, Pallas kernels, call(): pl.pallas_call(body, out_shape=[jax.ShapeDtypeStruct(s, jnp.float32) for...  31.7 us
    all_to_all x1, blocking collectives, per_device(): lax.all_to_all(jnp.broadcast_to(sums[None], (n, 2, 128)), ('gx', 'gy'), 0...  25.6 us
    ppermute x8, starting transfers between devices, both_ways(): return (lax.ppermute(up, axis, fwd), lax.ppermute(down, axis, back))  17.3 us
    unnamed x16, local copies, waits for them, and re-layouts  3.14 us
  transfers between devices with their start and end apart: 8, of which 7 were waited for; matrix products, arithmetic and copies ran while one was open for 0% of the time, Pallas kernels for 0%

profile of v1, /device:TPU:1, one launch (start us, length us, event | category | flops | bytes accessed | tf_op | source)
XLA Modules:
  0.0 116.2 jit_solution(6698439267427474851)
XLA Ops:
  0.6 2.9 %shard_map.59 = (f32[8,16,8,256]{3,2,1,0:T(8,128)}, f32[3,8,16,256]{3,2,1,0:T(8,128)}, f32[62,8,256]{2,1,0:T(8,128)}, f32[62,8,256]{2,1,0:T(8,128)}, f32[8,3,8,256]{3,2,1,0:T(8,128)}, /*index=5*/f32[8,3,8,256]{3,2,1,0:T(8,128)}) custom-call(f32[8,8,16,256]{3,2,1,0:T(8,128)} %v.1, f32[8,16,256]{2,1,0:T(8,128)} %wx.1, f32[8,16,256]{2,1,0:T(8,128)} %wy.1, ...), custom_call_target="tpu_custom_call" | custom-call | flops 1000000 | bytes 1441792 | tf_op jit(solution)/shard_map/pallas_call | solution.py:30
  3.5 2.0 %collective-permute-start = (f32[62,8,256]{2,1,0:T(8,128)}, f32[62,8,256]{2,1,0:T(8,128)S(1)}, u32[]{:S(2)}, u32[]{:S(2)}) collective-permute-start(f32[62,8,256]{2,1,0:T(8,128)} %get-tuple-element.23), channel_id=1, source_target_pairs={{0,16},{16,32},{32,48},{48,64},{64,80},{80,96},{96,112},{112,128},... | collective-permute-start | bytes 1523720 | tf_op jit(solution)/shard_map/ppermute | solution.py:524
  5.6 3.8 %collective-permute-start.1 = (f32[62,8,256]{2,1,0:T(8,128)}, f32[62,8,256]{2,1,0:T(8,128)S(1)}, u32[]{:S(2)}, u32[]{:S(2)}) collective-permute-start(f32[62,8,256]{2,1,0:T(8,128)} %get-tuple-element.24), channel_id=1, source_target_pairs={{16,0},{32,16},{48,32},{64,48},{80,64},{96,80},{112,96},{128,112},... | collective-permute-start | bytes 1523720 | tf_op jit(solution)/shard_map/ppermute | solution.py:524
  9.3 9.5 %collective-permute-done.xl = f32[62,8,256]{2,1,0:T(8,128)S(1)} collective-permute-done((f32[62,8,256]{2,1,0:T(8,128)}, f32[62,8,256]{2,1,0:T(8,128)S(1)}, u32[]{:S(2)}, u32[]{:S(2)}) %collective-permute-start) | collective-permute-done | bytes 507936 | tf_op jit(solution)/shard_map/ppermute | solution.py:524
  18.8 0.0 copy-start
  18.8 0.0 collective-permute-done.1.xr
  18.8 0.0 copy-start.1
  18.8 0.8 copy-done
  19.6 0.2 copy-done.1
  19.8 2.4 %shard_map.60 = (f32[42,8,256]{2,1,0:T(8,128)}, f32[42,8,256]{2,1,0:T(8,128)}) custom-call(f32[3,8,16,256]{3,2,1,0:T(8,128)} %get-tuple-element.22.wm, f32[8,3,8,256]{3,2,1,0:T(8,128)} %get-tuple-element.25.ylo, f32[8,3,8,256]{3,2,1,0:T(8,128)} %get-tuple-element.26.yhi, f32[62,8,256]{2,1,0:T(8,128)} %copy-done, f32[62,8,256]{2,1,0:T(8,128)} %copy-done.1), custom_call_target="tpu_custom_call" | custom-call | flops 1000000 | bytes 1802240 | tf_op jit(solution)/shard_map/pallas_call | solution.py:30
  22.2 4.7 %collective-permute-start.2 = (f32[42,8,256]{2,1,0:T(8,128)}, f32[42,8,256]{2,1,0:T(8,128)S(1)}, u32[]{:S(2)}, u32[]{:S(2)}) collective-permute-start(f32[42,8,256]{2,1,0:T(8,128)} %get-tuple-element.27), channel_id=1, source_target_pairs={{0,1},{1,2},{2,3},{3,4},{4,5},{5,6},{6,7},{7,8},{8,9},{9,10},{10,1... | collective-permute-start | bytes 1032200 | tf_op jit(solution)/shard_map/ppermute | solution.py:524
  27.0 0.0 collective-permute-start.3
  27.0 4.5 %collective-permute-done.2.yl = f32[42,8,256]{2,1,0:T(8,128)S(1)} collective-permute-done((f32[42,8,256]{2,1,0:T(8,128)}, f32[42,8,256]{2,1,0:T(8,128)S(1)}, u32[]{:S(2)}, u32[]{:S(2)}) %collective-permute-start.2) | collective-permute-done | bytes 344096 | tf_op jit(solution)/shard_map/ppermute | solution.py:524
  31.5 0.0 copy-start.4
  31.5 2.7 %collective-permute-done.3.yr = f32[42,8,256]{2,1,0:T(8,128)S(1)} collective-permute-done((f32[42,8,256]{2,1,0:T(8,128)}, f32[42,8,256]{2,1,0:T(8,128)S(1)}, u32[]{:S(2)}, u32[]{:S(2)}) %collective-permute-start.3) | collective-permute-done | bytes 344096 | tf_op jit(solution)/shard_map/ppermute | solution.py:524
  34.1 0.0 copy-start.5
  34.1 0.0 copy-done.4
  34.1 0.7 copy-done.5
  34.9 10.8 %shard_map.61 = (f32[8,16,16,256]{3,2,1,0:T(8,128)}, f32[7,8,16,256]{3,2,1,0:T(8,128)}, f32[88,8,128]{2,1,0:T(8,128)}, f32[2,8,256]{2,1,0:T(8,128)}) custom-call(f32[8,16,8,256]{3,2,1,0:T(8,128)} %get-tuple-element.21.vt, f32[3,8,16,256]{3,2,1,0:T(8,128)} %get-tuple-element.22.wm, f32[62,8,256]{2,1,0:T(8,128)} %copy-done, f32[62,8,256]{2,1,0:T(8,128)} %copy-done.1, ...), custom_call_target="tpu_custom_call" | custom-call | flops 1000000 | bytes 3145728 | tf_op jit(solution)/shard_map/pallas_call | solution.py:30
  45.7 4.7 %collective-permute-start.5 = (f32[88,8,128]{2,1,0:T(8,128)}, f32[88,8,128]{2,1,0:T(8,128)S(1)}, u32[]{:S(2)}, u32[]{:S(2)}) collective-permute-start(f32[88,8,128]{2,1,0:T(8,128)} %get-tuple-element.29.own), channel_id=1, source_target_pairs={{16,0},{32,16},{48,32},{64,48},{80,64},{96,80},{112,96},{128,112},... | collective-permute-start | bytes 1081352 | tf_op jit(solution)/shard_map/ppermute | solution.py:524
  50.3 0.0 collective-permute-start.4
  50.3 7.2 %collective-permute-done.5.right = f32[88,8,128]{2,1,0:T(8,128)S(1)} collective-permute-done((f32[88,8,128]{2,1,0:T(8,128)}, f32[88,8,128]{2,1,0:T(8,128)S(1)}, u32[]{:S(2)}, u32[]{:S(2)}) %collective-permute-start.5) | collective-permute-done | bytes 360480 | tf_op jit(solution)/shard_map/ppermute | solution.py:524
  57.5 0.0 copy-start.2
  57.5 5.1 %collective-permute-done.4.left = f32[88,8,128]{2,1,0:T(8,128)S(1)} collective-permute-done((f32[88,8,128]{2,1,0:T(8,128)}, f32[88,8,128]{2,1,0:T(8,128)S(1)}, u32[]{:S(2)}, u32[]{:S(2)}) %collective-permute-start.4) | collective-permute-done | bytes 360480 | tf_op jit(solution)/shard_map/ppermute | solution.py:524
  62.6 0.0 copy-done.2
  62.6 0.0 copy-start.3
  62.6 0.7 copy-done.3
  63.3 2.1 %shard_map.62 = (f32[80,8,128]{2,1,0:T(8,128)}, f32[80,8,128]{2,1,0:T(8,128)}) custom-call(f32[88,8,128]{2,1,0:T(8,128)} %get-tuple-element.29.own, f32[88,8,128]{2,1,0:T(8,128)} %copy-done.3, f32[88,8,128]{2,1,0:T(8,128)} %copy-done.2), custom_call_target="tpu_custom_call" | custom-call | flops 1000000 | bytes 1081344 | tf_op jit(solution)/shard_map/pallas_call | solution.py:30
  65.5 2.0 %collective-permute-start.6 = (f32[80,8,128]{2,1,0:T(8,128)}, f32[80,8,128]{2,1,0:T(8,128)S(1)}, u32[]{:S(2)}, u32[]{:S(2)}) collective-permute-start(f32[80,8,128]{2,1,0:T(8,128)} %get-tuple-element.30), channel_id=1, source_target_pairs={{0,1},{1,2},{2,3},{3,4},{4,5},{5,6},{6,7},{7,8},{8,9},{9,10},{10,1... | collective-permute-start | bytes 983048 | tf_op jit(solution)/shard_map/ppermute | solution.py:524
  67.5 0.0 collective-permute-start.7
  67.5 4.3 %collective-permute-done.6.yl = f32[80,8,128]{2,1,0:T(8,128)S(1)} collective-permute-done((f32[80,8,128]{2,1,0:T(8,128)}, f32[80,8,128]{2,1,0:T(8,128)S(1)}, u32[]{:S(2)}, u32[]{:S(2)}) %collective-permute-start.6) | collective-permute-done | bytes 327712 | tf_op jit(solution)/shard_map/ppermute | solution.py:524
  71.8 0.0 copy-start.6
  71.8 2.7 %collective-permute-done.7.yr = f32[80,8,128]{2,1,0:T(8,128)S(1)} collective-permute-done((f32[80,8,128]{2,1,0:T(8,128)}, f32[80,8,128]{2,1,0:T(8,128)S(1)}, u32[]{:S(2)}, u32[]{:S(2)}) %collective-permute-start.7) | collective-permute-done | bytes 327712 | tf_op jit(solution)/shard_map/ppermute | solution.py:524
  74.5 0.0 copy-start.7
  74.5 0.0 copy-done.6
  74.5 0.7 copy-done.7
  75.2 9.6 %shard_map.63 = (f32[8,16,8,256]{3,2,1,0:T(8,128)}, f32[8,16,8,256]{3,2,1,0:T(8,128)}, f32[2,128]{1,0:T(2,128)}) custom-call(f32[88,8,128]{2,1,0:T(8,128)} %get-tuple-element.29.own, f32[88,8,128]{2,1,0:T(8,128)} %copy-done.3, f32[88,8,128]{2,1,0:T(8,128)} %copy-done.2, f32[80,8,128]{2,1,0:T(8,128)} %copy-done.6, f32[80,8,128]{2,1,0:T(8,128)} %copy-done.7, ...), custom_call_target="tpu_custom_call" | custom-call | flops 1000000 | bytes 4767744 | tf_op jit(solution)/shard_map/pallas_call | solution.py:30
  84.8 0.7 broadcast_in_dim.2
  85.5 25.6 %all_to_all.5.parts = f32[256,2,128]{2,1,0:T(2,128)} all-to-all(f32[256,2,128]{2,1,0:T(2,128)S(1)} %broadcast_in_dim.2), channel_id=1, replica_groups=mesh['gx'=16,'gy'=16] {'gx','gy'}, dimensions={0} | all-to-all | bytes 524288 | tf_op jit(solution)/shard_map/all_to_all | solution.py:576
  111.1 3.8 %shard_map.64 = (f32[8,8,16,256]{3,2,1,0:T(8,128)}, f32[8,128]{1,0:T(8,128)}) custom-call(f32[256,2,128]{2,1,0:T(2,128)} %all_to_all.5.parts, f32[8,16,8,256]{3,2,1,0:T(8,128)} %get-tuple-element.36.po, f32[8,16,8,256]{3,2,1,0:T(8,128)} %get-tuple-element.37.bo), custom_call_target="tpu_custom_call" | custom-call | flops 1000000 | bytes 2359296 | tf_op jit(solution)/shard_map/pallas_call | solution.py:30
  114.9 1.2 %slice_bitcast_fusion = f32[8]{0:T(128)} fusion(f32[8,128]{1,0:T(8,128)} %get-tuple-element.39), kind=kLoop, calls=%fused_computation | loop fusion | bytes 64 | tf_op jit(solution)/shard_map/squeeze | solution.py:583
Async XLA Ops:
  3.5 15.3 %collective-permute-start = (f32[62,8,256]{2,1,0:T(8,128)}, f32[62,8,256]{2,1,0:T(8,128)S(1)}, u32[]{:S(2)}, u32[]{:S(2)}) collective-permute-start(f32[62,8,256]{2,1,0:T(8,128)} %get-tuple-element.23), channel_id=1, source_target_pairs={{0,16},{16,32},{32,48},{48,64},{64,80},{80,96},{96,112},{112,128},... | collective-permute-start | bytes 1523720 | tf_op jit(solution)/shard_map/ppermute | solution.py:524
  5.6 13.3 %collective-permute-start.1 = (f32[62,8,256]{2,1,0:T(8,128)}, f32[62,8,256]{2,1,0:T(8,128)S(1)}, u32[]{:S(2)}, u32[]{:S(2)}) collective-permute-start(f32[62,8,256]{2,1,0:T(8,128)} %get-tuple-element.24), channel_id=1, source_target_pairs={{16,0},{32,16},{48,32},{64,48},{80,64},{96,80},{112,96},{128,112},... | collective-permute-start | bytes 1523720 | tf_op jit(solution)/shard_map/ppermute | solution.py:524
  18.8 0.8 copy-start
  18.8 1.0 copy-start.1
  22.2 9.2 %collective-permute-start.2 = (f32[42,8,256]{2,1,0:T(8,128)}, f32[42,8,256]{2,1,0:T(8,128)S(1)}, u32[]{:S(2)}, u32[]{:S(2)}) collective-permute-start(f32[42,8,256]{2,1,0:T(8,128)} %get-tuple-element.27), channel_id=1, source_target_pairs={{0,1},{1,2},{2,3},{3,4},{4,5},{5,6},{6,7},{7,8},{8,9},{9,10},{10,1... | collective-permute-start | bytes 1032200 | tf_op jit(solution)/shard_map/ppermute | solution.py:524
  27.0 7.2 %collective-permute-start.3 = (f32[42,8,256]{2,1,0:T(8,128)}, f32[42,8,256]{2,1,0:T(8,128)S(1)}, u32[]{:S(2)}, u32[]{:S(2)}) collective-permute-start(f32[42,8,256]{2,1,0:T(8,128)} %get-tuple-element.28), channel_id=1, source_target_pairs={{1,0},{2,1},{3,2},{4,3},{5,4},{6,5},{7,6},{8,7},{9,8},{10,9},{11,1... | collective-permute-start | bytes 1032200 | tf_op jit(solution)/shard_map/ppermute | solution.py:524
  31.5 2.7 %copy-start.4 = (f32[42,8,256]{2,1,0:T(8,128)}, f32[42,8,256]{2,1,0:T(8,128)S(1)}, u32[]{:S(2)}) copy-start(f32[42,8,256]{2,1,0:T(8,128)S(1)} %collective-permute-done.2.yl) | copy-start | bytes 1032196
  34.1 0.7 copy-start.5
  45.7 11.8 %collective-permute-start.5 = (f32[88,8,128]{2,1,0:T(8,128)}, f32[88,8,128]{2,1,0:T(8,128)S(1)}, u32[]{:S(2)}, u32[]{:S(2)}) collective-permute-start(f32[88,8,128]{2,1,0:T(8,128)} %get-tuple-element.29.own), channel_id=1, source_target_pairs={{16,0},{32,16},{48,32},{64,48},{80,64},{96,80},{112,96},{128,112},... | collective-permute-start | bytes 1081352 | tf_op jit(solution)/shard_map/ppermute | solution.py:524
  50.3 12.3 %collective-permute-start.4 = (f32[88,8,128]{2,1,0:T(8,128)}, f32[88,8,128]{2,1,0:T(8,128)S(1)}, u32[]{:S(2)}, u32[]{:S(2)}) collective-permute-start(f32[88,8,128]{2,1,0:T(8,128)} %get-tuple-element.29.own), channel_id=1, source_target_pairs={{0,16},{16,32},{32,48},{48,64},{64,80},{80,96},{96,112},{112,128},... | collective-permute-start | bytes 1081352 | tf_op jit(solution)/shard_map/ppermute | solution.py:524
  57.5 5.1 %copy-start.2 = (f32[88,8,128]{2,1,0:T(8,128)}, f32[88,8,128]{2,1,0:T(8,128)S(1)}, u32[]{:S(2)}) copy-start(f32[88,8,128]{2,1,0:T(8,128)S(1)} %collective-permute-done.5.right) | copy-start | bytes 1081348
  62.6 0.7 copy-start.3
  65.5 6.4 %collective-permute-start.6 = (f32[80,8,128]{2,1,0:T(8,128)}, f32[80,8,128]{2,1,0:T(8,128)S(1)}, u32[]{:S(2)}, u32[]{:S(2)}) collective-permute-start(f32[80,8,128]{2,1,0:T(8,128)} %get-tuple-element.30), channel_id=1, source_target_pairs={{0,1},{1,2},{2,3},{3,4},{4,5},{5,6},{6,7},{7,8},{8,9},{9,10},{10,1... | collective-permute-start | bytes 983048 | tf_op jit(solution)/shard_map/ppermute | solution.py:524
  67.5 7.0 %collective-permute-start.7 = (f32[80,8,128]{2,1,0:T(8,128)}, f32[80,8,128]{2,1,0:T(8,128)S(1)}, u32[]{:S(2)}, u32[]{:S(2)}) collective-permute-start(f32[80,8,128]{2,1,0:T(8,128)} %get-tuple-element.31), channel_id=1, source_target_pairs={{1,0},{2,1},{3,2},{4,3},{5,4},{6,5},{7,6},{8,7},{9,8},{10,9},{11,1... | collective-permute-start | bytes 983048 | tf_op jit(solution)/shard_map/ppermute | solution.py:524
  71.8 2.7 %copy-start.6 = (f32[80,8,128]{2,1,0:T(8,128)}, f32[80,8,128]{2,1,0:T(8,128)S(1)}, u32[]{:S(2)}) copy-start(f32[80,8,128]{2,1,0:T(8,128)S(1)} %collective-permute-done.6.yl) | copy-start | bytes 983044
  74.5 0.7 copy-start.7

commit v2 on v1

--- a/solution.py
+++ b/solution.py
@@ -25,7 +25,7 @@
 VMEM = pl.BlockSpec(memory_space=pltpu.VMEM)
 
 
-def call(body, outs, ins, scratch=(), flops=1_000_000):
+def call(body, outs, ins, scratch=(), limit=10):
     nbytes = sum(4 * a.size for a in ins)
     return pl.pallas_call(
         body,
@@ -33,8 +33,8 @@
         in_specs=[VMEM] * len(ins),
         out_specs=[VMEM] * len(outs),
         scratch_shapes=[pltpu.VMEM(s, jnp.float32) for s in scratch],
-        compiler_params=pltpu.CompilerParams(vmem_limit_bytes=56 * MIB),
-        cost_estimate=pl.CostEstimate(flops=flops, bytes_accessed=nbytes, transcendentals=0),
+        compiler_params=pltpu.CompilerParams(vmem_limit_bytes=limit * MIB),
+        cost_estimate=pl.CostEstimate(flops=1_000_000, bytes_accessed=nbytes, transcendentals=0),
     )(*ins)
 
 
@@ -438,8 +438,8 @@
 
     t0 = over_lanes(jnp.concatenate(acc[:16], 0))
     t1 = over_lanes(jnp.concatenate(acc[16:] + [zero] * 12, 0))
-    sums[0:1] = t0[0:1]
-    sums[1:2] = t1[0:1]
+    both = jnp.concatenate([t0[0:1], t1[0:1]], 0)
+    sums[...] = jnp.broadcast_to(both[None], sums.shape)
 
 
 def finish(parts, po, bo, out, eig, SP):
@@ -458,7 +458,8 @@
         SP[128 * q : 128 * (q + 1)] = jnp.dot(
             m, ones, precision=lax.Precision.HIGHEST, preferred_element_type=jnp.float32
         )
-    eig[...] = jnp.broadcast_to(t[1:2] / pltpu.roll(t[1:2], 120, 1), (8, 128))
+    lams = t[1:2] / pltpu.roll(t[1:2], 120, 1)
+    eig[...] = pltpu.roll(lams, 112, 1)[:, :K]
 
     def entry(block, k):
         return row(SP, 8 * block + k)
@@ -555,14 +556,16 @@
             (CX, CY, CZ),
             (6, CX * LY, CZ),
         ],
+        limit=24,
     )
     cl, cr = both_ways(xs, xs, "gx")
     yu, yd = call(coarse_y_send, [(NCY, 8, CZ)] * 2, (xs, cl, cr))
     yl, yr = both_ways(yu, yd, "gy")
+    n = lax.axis_size("gx") * lax.axis_size("gy")
     cext = (CX + 2 * CH, CY + 2 * CH, 2, 8, CZ)
     po, bo, sums = call(
         coarse_level,
-        [(LX, LY, K, NZ), (LX, LY, K, NZ), (2, 128)],
+        [(LX, LY, K, NZ), (LX, LY, K, NZ), (n, 2, 128)],
         (xs, cl, cr, yl, yr, pb, nwo, nd),
         [
             cext,
@@ -571,16 +574,16 @@
             cext,
             (CX + 2 * CH, CY + 2 * CH, 2, 8, NZ),
         ],
+        limit=16,
     )
-    n = lax.axis_size("gx") * lax.axis_size("gy")
-    parts = lax.all_to_all(jnp.broadcast_to(sums[None], (n, 2, 128)), ("gx", "gy"), 0, 0)
+    parts = lax.all_to_all(sums, ("gx", "gy"), 0, 0)
     refined, eig = call(
         finish,
-        [(K, LX, LY, NZ), (8, 128)],
+        [(K, LX, LY, NZ), (1, K)],
         (parts, po, bo),
         [(384, 128)],
     )
-    return refined, eig[0, 16:24]
+    return refined, eig.reshape(K)
 
 
 def solution(mesh):

time: 116 us -> 99.1 us (0.85)
  Pallas kernels: 31.7 us -> 16.6 us
  local copies, waits for them, and re-layouts: 5.12 us -> 3.93 us
    pallas_call x6, Pallas kernels: 31.7 us -> 16.6 us  [call(): pl.pallas_call(body, out_shape=[jax.ShapeDtypeStruct(s, jnp.float32) for...]
    squeeze x1 -> x0, local copies, waits for them, and re-layouts: 1.25 us -> none  [per_device(): return (refined, eig[0, 16:24])]
    unnamed x16 -> x8, local copies, waits for them, and re-layouts: 3.14 us -> 3.93 us
where the time goes in v2:
time: 99.1 us; the launch traced here: 98.9 us
  waiting for transfers between devices  34.8 us (35%)
  blocking collectives  25.3 us (26%)
  starting transfers between devices  17.7 us (18%)
  Pallas kernels  16.6 us (17%)
  local copies, waits for them, and re-layouts  3.93 us (4%)
    ppermute x8, waiting for transfers between devices, both_ways(): return (lax.ppermute(up, axis, fwd), lax.ppermute(down, axis, back))  34.8 us
    all_to_all x1, blocking collectives, per_device(): parts = lax.all_to_all(sums, ('gx', 'gy'), 0, 0)  25.3 us
    ppermute x8, starting transfers between devices, both_ways(): return (lax.ppermute(up, axis, fwd), lax.ppermute(down, axis, back))  17.7 us
    pallas_call x6, Pallas kernels, call(): pl.pallas_call(body, out_shape=[jax.ShapeDtypeStruct(s, jnp.float32) for...  16.6 us
    unnamed x8, local copies, waits for them, and re-layouts  3.93 us
  transfers between devices with their start and end apart: 8, of which 7 were waited for; matrix products, arithmetic and copies ran while one was open for 0% of the time, Pallas kernels for 0%

profile of v2, /device:TPU:1, one launch (start us, length us, event | category | flops | bytes accessed | tf_op | source)
XLA Modules:
  0.0 98.9 jit_solution(18088177121792464167)
XLA Ops:
  0.6 0.0 copy-start
  0.6 1.2 %copy-done = f32[8,8,16,256]{3,2,1,0:T(8,128)S(1)} copy-done((f32[8,8,16,256]{3,2,1,0:T(8,128)S(1)}, f32[8,8,16,256]{3,2,1,0:T(8,128)}, u32[]{:S(2)}) %copy-start) | copy-done | bytes 1048600
  1.9 0.0 copy-start.1
  1.9 0.9 copy-done.1
  2.8 0.0 copy-start.2
  2.8 0.9 copy-done.2
  3.7 0.0 copy-start.3
  3.7 0.9 copy-done.3
  4.6 0.3 shard_map.59
  4.9 2.1 %collective-permute-start = (f32[62,8,256]{2,1,0:T(8,128)S(1)}, f32[62,8,256]{2,1,0:T(8,128)S(1)}, u32[]{:S(2)}, u32[]{:S(2)}) collective-permute-start(f32[62,8,256]{2,1,0:T(8,128)S(1)} %get-tuple-element.23), channel_id=1, source_target_pairs={{0,16},{16,32},{32,48},{48,64},{64,80},{80,96},{96,112},{112,128},... | collective-permute-start | bytes 1523720 | tf_op jit(solution)/shard_map/ppermute | solution.py:525
  7.0 3.8 %collective-permute-start.1 = (f32[62,8,256]{2,1,0:T(8,128)S(1)}, f32[62,8,256]{2,1,0:T(8,128)S(1)}, u32[]{:S(2)}, u32[]{:S(2)}) collective-permute-start(f32[62,8,256]{2,1,0:T(8,128)S(1)} %get-tuple-element.24), channel_id=1, source_target_pairs={{16,0},{32,16},{48,32},{64,48},{80,64},{96,80},{112,96},{128,112},... | collective-permute-start | bytes 1523720 | tf_op jit(solution)/shard_map/ppermute | solution.py:525
  10.8 9.2 %collective-permute-done.xl = f32[62,8,256]{2,1,0:T(8,128)S(1)} collective-permute-done((f32[62,8,256]{2,1,0:T(8,128)S(1)}, f32[62,8,256]{2,1,0:T(8,128)S(1)}, u32[]{:S(2)}, u32[]{:S(2)}) %collective-permute-start) | collective-permute-done | bytes 507936 | tf_op jit(solution)/shard_map/ppermute | solution.py:525
  20.0 0.0 collective-permute-done.1.xr
  20.0 0.1 shard_map.60
  20.1 4.7 %collective-permute-start.2 = (f32[42,8,256]{2,1,0:T(8,128)S(1)}, f32[42,8,256]{2,1,0:T(8,128)S(1)}, u32[]{:S(2)}, u32[]{:S(2)}) collective-permute-start(f32[42,8,256]{2,1,0:T(8,128)S(1)} %get-tuple-element.27), channel_id=1, source_target_pairs={{0,1},{1,2},{2,3},{3,4},{4,5},{5,6},{6,7},{7,8},{8,9},{9,10},{10,1... | collective-permute-start | bytes 1032200 | tf_op jit(solution)/shard_map/ppermute | solution.py:525
  24.9 0.0 collective-permute-start.3
  24.9 4.2 %collective-permute-done.2.yl = f32[42,8,256]{2,1,0:T(8,128)S(1)} collective-permute-done((f32[42,8,256]{2,1,0:T(8,128)S(1)}, f32[42,8,256]{2,1,0:T(8,128)S(1)}, u32[]{:S(2)}, u32[]{:S(2)}) %collective-permute-start.2) | collective-permute-done | bytes 344096 | tf_op jit(solution)/shard_map/ppermute | solution.py:525
  29.1 2.8 %collective-permute-done.3.yr = f32[42,8,256]{2,1,0:T(8,128)S(1)} collective-permute-done((f32[42,8,256]{2,1,0:T(8,128)S(1)}, f32[42,8,256]{2,1,0:T(8,128)S(1)}, u32[]{:S(2)}, u32[]{:S(2)}) %collective-permute-start.3) | collective-permute-done | bytes 344096 | tf_op jit(solution)/shard_map/ppermute | solution.py:525
  31.8 7.7 %shard_map.61 = (f32[8,16,16,256]{3,2,1,0:T(8,128)S(1)}, f32[7,8,16,256]{3,2,1,0:T(8,128)S(1)}, f32[88,8,128]{2,1,0:T(8,128)S(1)}, f32[2,8,256]{2,1,0:T(8,128)S(1)}) custom-call(f32[8,16,8,256]{3,2,1,0:T(8,128)S(1)} %get-tuple-element.21.vt, f32[3,8,16,256]{3,2,1,0:T(8,128)S(1)} %get-tuple-element.22.wm, f32[62,8,256]{2,1,0:T(8,128)S(1)} %collective-permute-done.xl, ...), custom_call_target="tpu_custom_call" | custom-call | flops 1000000 | bytes 3145728 | tf_op jit(solution)/shard_map/pallas_call | solution.py:30
  39.5 4.9 %collective-permute-start.5 = (f32[88,8,128]{2,1,0:T(8,128)S(1)}, f32[88,8,128]{2,1,0:T(8,128)S(1)}, u32[]{:S(2)}, u32[]{:S(2)}) collective-permute-start(f32[88,8,128]{2,1,0:T(8,128)S(1)} %get-tuple-element.29.own), channel_id=1, source_target_pairs={{16,0},{32,16},{48,32},{64,48},{80,64},{96,80},{112,96},{128,112},... | collective-permute-start | bytes 1081352 | tf_op jit(solution)/shard_map/ppermute | solution.py:525
  44.4 0.0 collective-permute-start.4
  44.4 6.9 %collective-permute-done.5.right = f32[88,8,128]{2,1,0:T(8,128)S(1)} collective-permute-done((f32[88,8,128]{2,1,0:T(8,128)S(1)}, f32[88,8,128]{2,1,0:T(8,128)S(1)}, u32[]{:S(2)}, u32[]{:S(2)}) %collective-permute-start.5) | collective-permute-done | bytes 360480 | tf_op jit(solution)/shard_map/ppermute | solution.py:525
  51.3 5.2 %collective-permute-done.4.left = f32[88,8,128]{2,1,0:T(8,128)S(1)} collective-permute-done((f32[88,8,128]{2,1,0:T(8,128)S(1)}, f32[88,8,128]{2,1,0:T(8,128)S(1)}, u32[]{:S(2)}, u32[]{:S(2)}) %collective-permute-start.4) | collective-permute-done | bytes 360480 | tf_op jit(solution)/shard_map/ppermute | solution.py:525
  56.6 0.1 shard_map.62
  56.6 1.7 %collective-permute-start.6 = (f32[80,8,128]{2,1,0:T(8,128)S(1)}, f32[80,8,128]{2,1,0:T(8,128)S(1)}, u32[]{:S(2)}, u32[]{:S(2)}) collective-permute-start(f32[80,8,128]{2,1,0:T(8,128)S(1)} %get-tuple-element.30), channel_id=1, source_target_pairs={{0,1},{1,2},{2,3},{3,4},{4,5},{5,6},{6,7},{7,8},{8,9},{9,10},{10,1... | collective-permute-start | bytes 983048 | tf_op jit(solution)/shard_map/ppermute | solution.py:525
  58.4 0.3 collective-permute-start.7
  58.7 3.7 %collective-permute-done.6.yl = f32[80,8,128]{2,1,0:T(8,128)S(1)} collective-permute-done((f32[80,8,128]{2,1,0:T(8,128)S(1)}, f32[80,8,128]{2,1,0:T(8,128)S(1)}, u32[]{:S(2)}, u32[]{:S(2)}) %collective-permute-start.6) | collective-permute-done | bytes 327712 | tf_op jit(solution)/shard_map/ppermute | solution.py:525
  62.4 2.8 %collective-permute-done.7.yr = f32[80,8,128]{2,1,0:T(8,128)S(1)} collective-permute-done((f32[80,8,128]{2,1,0:T(8,128)S(1)}, f32[80,8,128]{2,1,0:T(8,128)S(1)}, u32[]{:S(2)}, u32[]{:S(2)}) %collective-permute-start.7) | collective-permute-done | bytes 327712 | tf_op jit(solution)/shard_map/ppermute | solution.py:525
  65.2 6.3 %shard_map.63 = (f32[8,16,8,256]{3,2,1,0:T(8,128)S(1)}, f32[8,16,8,256]{3,2,1,0:T(8,128)S(1)}, f32[256,2,128]{2,1,0:T(2,128)S(1)}) custom-call(f32[88,8,128]{2,1,0:T(8,128)S(1)} %get-tuple-element.29.own, f32[88,8,128]{2,1,0:T(8,128)S(1)} %collective-permute-done.4.left, f32[88,8,128]{2,1,0:T(8,128)S(1)} %collective-permute-done.5.right, ...), custom_call_target="tpu_custom_call" | custom-call | flops 1000000 | bytes 4767744 | tf_op jit(solution)/shard_map/pallas_call | solution.py:30
  71.4 25.3 %all_to_all.5.parts = f32[256,2,128]{2,1,0:T(2,128)S(1)} all-to-all(f32[256,2,128]{2,1,0:T(2,128)S(1)} %get-tuple-element.35), channel_id=1, replica_groups=mesh['gx'=16,'gy'=16] {'gx','gy'}, dimensions={0} | all-to-all | bytes 524288 | tf_op jit(solution)/shard_map/all_to_all | solution.py:579
  96.7 2.2 %shard_map.64 = (f32[8,8,16,256]{3,2,1,0:T(8,128)}, f32[1,8]{1,0:T(1,128)}) custom-call(f32[256,2,128]{2,1,0:T(2,128)S(1)} %all_to_all.5.parts, f32[8,16,8,256]{3,2,1,0:T(8,128)S(1)} %get-tuple-element.36.po, f32[8,16,8,256]{3,2,1,0:T(8,128)S(1)} %get-tuple-element.37.bo), custom_call_target="tpu_custom_call" | custom-call | flops 1000000 | bytes 2359296 | tf_op jit(solution)/shard_map/pallas_call | solution.py:30
Async XLA Ops:
  0.6 1.2 %copy-start = (f32[8,8,16,256]{3,2,1,0:T(8,128)S(1)}, f32[8,8,16,256]{3,2,1,0:T(8,128)}, u32[]{:S(2)}) copy-start(f32[8,8,16,256]{3,2,1,0:T(8,128)} %v.1) | copy-start | bytes 3145732
  1.9 0.9 copy-start.1
  2.8 0.9 copy-start.2
  3.7 0.9 copy-start.3
  4.9 15.2 %collective-permute-start = (f32[62,8,256]{2,1,0:T(8,128)S(1)}, f32[62,8,256]{2,1,0:T(8,128)S(1)}, u32[]{:S(2)}, u32[]{:S(2)}) collective-permute-start(f32[62,8,256]{2,1,0:T(8,128)S(1)} %get-tuple-element.23), channel_id=1, source_target_pairs={{0,16},{16,32},{32,48},{48,64},{64,80},{80,96},{96,112},{112,128},... | collective-permute-start | bytes 1523720 | tf_op jit(solution)/shard_map/ppermute | solution.py:525
  7.0 13.1 %collective-permute-start.1 = (f32[62,8,256]{2,1,0:T(8,128)S(1)}, f32[62,8,256]{2,1,0:T(8,128)S(1)}, u32[]{:S(2)}, u32[]{:S(2)}) collective-permute-start(f32[62,8,256]{2,1,0:T(8,128)S(1)} %get-tuple-element.24), channel_id=1, source_target_pairs={{16,0},{32,16},{48,32},{64,48},{80,64},{96,80},{112,96},{128,112},... | collective-permute-start | bytes 1523720 | tf_op jit(solution)/shard_map/ppermute | solution.py:525
  20.1 8.9 %collective-permute-start.2 = (f32[42,8,256]{2,1,0:T(8,128)S(1)}, f32[42,8,256]{2,1,0:T(8,128)S(1)}, u32[]{:S(2)}, u32[]{:S(2)}) collective-permute-start(f32[42,8,256]{2,1,0:T(8,128)S(1)} %get-tuple-element.27), channel_id=1, source_target_pairs={{0,1},{1,2},{2,3},{3,4},{4,5},{5,6},{6,7},{7,8},{8,9},{9,10},{10,1... | collective-permute-start | bytes 1032200 | tf_op jit(solution)/shard_map/ppermute | solution.py:525
  24.9 7.0 %collective-permute-start.3 = (f32[42,8,256]{2,1,0:T(8,128)S(1)}, f32[42,8,256]{2,1,0:T(8,128)S(1)}, u32[]{:S(2)}, u32[]{:S(2)}) collective-permute-start(f32[42,8,256]{2,1,0:T(8,128)S(1)} %get-tuple-element.28), channel_id=1, source_target_pairs={{1,0},{2,1},{3,2},{4,3},{5,4},{6,5},{7,6},{8,7},{9,8},{10,9},{11,1... | collective-permute-start | bytes 1032200 | tf_op jit(solution)/shard_map/ppermute | solution.py:525
  39.5 11.9 %collective-permute-start.5 = (f32[88,8,128]{2,1,0:T(8,128)S(1)}, f32[88,8,128]{2,1,0:T(8,128)S(1)}, u32[]{:S(2)}, u32[]{:S(2)}) collective-permute-start(f32[88,8,128]{2,1,0:T(8,128)S(1)} %get-tuple-element.29.own), channel_id=1, source_target_pairs={{16,0},{32,16},{48,32},{64,48},{80,64},{96,80},{112,96},{128,112},... | collective-permute-start | bytes 1081352 | tf_op jit(solution)/shard_map/ppermute | solution.py:525
  44.4 12.1 %collective-permute-start.4 = (f32[88,8,128]{2,1,0:T(8,128)S(1)}, f32[88,8,128]{2,1,0:T(8,128)S(1)}, u32[]{:S(2)}, u32[]{:S(2)}) collective-permute-start(f32[88,8,128]{2,1,0:T(8,128)S(1)} %get-tuple-element.29.own), channel_id=1, source_target_pairs={{0,16},{16,32},{32,48},{48,64},{64,80},{80,96},{96,112},{112,128},... | collective-permute-start | bytes 1081352 | tf_op jit(solution)/shard_map/ppermute | solution.py:525
  56.6 5.8 %collective-permute-start.6 = (f32[80,8,128]{2,1,0:T(8,128)S(1)}, f32[80,8,128]{2,1,0:T(8,128)S(1)}, u32[]{:S(2)}, u32[]{:S(2)}) collective-permute-start(f32[80,8,128]{2,1,0:T(8,128)S(1)} %get-tuple-element.30), channel_id=1, source_target_pairs={{0,1},{1,2},{2,3},{3,4},{4,5},{5,6},{6,7},{7,8},{8,9},{9,10},{10,1... | collective-permute-start | bytes 983048 | tf_op jit(solution)/shard_map/ppermute | solution.py:525
  58.4 6.8 %collective-permute-start.7 = (f32[80,8,128]{2,1,0:T(8,128)S(1)}, f32[80,8,128]{2,1,0:T(8,128)S(1)}, u32[]{:S(2)}, u32[]{:S(2)}) collective-permute-start(f32[80,8,128]{2,1,0:T(8,128)S(1)} %get-tuple-element.31), channel_id=1, source_target_pairs={{1,0},{2,1},{3,2},{4,3},{5,4},{6,5},{7,6},{8,7},{9,8},{10,9},{11,1... | collective-permute-start | bytes 983048 | tf_op jit(solution)/shard_map/ppermute | solution.py:525

commit v3 on v2

v3 whole, which is shorter than its diff:
```python
import jax
import jax.numpy as jnp
from jax import lax
from jax.experimental import pallas as pl
from jax.experimental.pallas import tpu as pltpu
from jax.sharding import PartitionSpec as P

OMEGA = 0.8
SHIFT = 0.1
DIAG = 1.0 + SHIFT
C = OMEGA / DIAG
Z0 = 2.0 * C - DIAG * C * C
Z1 = C * C
G0, G1, G2 = 1.0 - DIAG * Z0, Z0 - DIAG * Z1, Z1
KEEP = 1.0 - DIAG * C
B0, B1, B2 = KEEP * Z0 + C, KEEP * Z1 + C * Z0, C * Z1

K = 8
LX, LY, NZ = 8, 16, 256
CX, CY, CZ = LX // 2, LY // 2, NZ // 2
H = 3
CH = 4
JW = 8
MIB = 1024 * 1024
VMEM = pl.BlockSpec(memory_space=pltpu.VMEM)


HBM = pl.BlockSpec(memory_space=pltpu.HBM)


def call(body, outs, ins, scratch=(), limit=8, where=VMEM, us=1):
    return pl.pallas_call(
        body,
        out_shape=[jax.ShapeDtypeStruct(s, jnp.float32) for s in outs],
        in_specs=[where] * len(ins),
        out_specs=[VMEM] * len(outs),
        scratch_shapes=[pltpu.VMEM(s, jnp.float32) if isinstance(s, tuple) else s for s in scratch],
        compiler_params=pltpu.CompilerParams(vmem_limit_bytes=limit * MIB),
        cost_estimate=pl.CostEstimate(
            flops=0, bytes_accessed=us * 3_000_000, transcendentals=0
        ),
    )(*ins)


def row(ref, *at):
    *lead, r = at
    r_ = ref[(*lead, pl.ds(r, 1), slice(None))]
    return jnp.broadcast_to(r_, (8, r_.shape[-1]))


def up_z(a):
    return pltpu.roll(a, a.shape[-1] - 1, a.ndim - 1)


def down_z(a):
    return pltpu.roll(a, 1, a.ndim - 1)


UP_W = [(0, 5), (0, 6), (0, 7), (1, 6), (1, 7), (2, 6), (2, 7)]
DN_W = [(0, 0), (0, 1), (1, 0), (1, 1), (2, 0), (2, 1)]
NV = H * LY
NXU = NV + 2 * len(UP_W) + 2 * CX
NXD = NV + 2 * len(DN_W) + 2 * CX
NYB = H * LX + LX + CX
CELLS = [(1, 1), (1, 2), (2, 1)]
WP = [-2, -1, LX, LX + 1]
CWP = [-3, -2, -1, CX, CX + 1, CX + 2]
NCB = 2 * len(CELLS) + len(WP) + len(CWP)


def put_rows(up, down, n, lows, highs):
    up[n, 0:2] = highs[0][6:8]
    up[n, 2:5] = highs[1][5:8]
    up[n, 5:8] = highs[2][5:8]
    down[n, 0:2] = lows[0][0:2]
    down[n, 2:4] = lows[1][0:2]
    down[n, 4:8] = lows[2][0:4]


def put_coarse_rows(up, down, n, arrays):
    for a, w in enumerate(arrays):
        r, z = 4 * (a & 1), 128 * (a >> 1)
        up[n, r : r + 4, z : z + 128] = w[4:8]
        down[n, r : r + 4, z : z + 128] = w[0:4]


def coarse_rows(msg, n, a):
    r, z = 4 * (a & 1), 128 * (a >> 1)
    return msg[n, r : r + 4, z : z + 128]


def prepare(v_, wx_, wy_, wz_, vt, wm, cw, xu, xd, yu, yd, v, wx, wy, wz, Q, sem):
    copies = [
        pltpu.make_async_copy(a, b, sem.at[n])
        for n, (a, b) in enumerate(((v_, v), (wx_, wx), (wy_, wy), (wz_, wz)))
    ]
    for c in copies:
        c.start()
    for c in copies[1:]:
        c.wait()
    last_x = lax.axis_index("gx") == lax.axis_size("gx") - 1
    last_y = lax.axis_index("gy") == lax.axis_size("gy") - 1
    keep_x = jnp.where(last_x, 0.0, 1.0)
    keep_y = jnp.where(last_y, 0.0, 1.0)
    wm[0] = wx[...]
    wm[0, LX - 1] = wx[LX - 1] * keep_x
    sub = lax.broadcasted_iota(jnp.int32, (LX, LY, NZ), 1)
    wm[1] = jnp.where(sub == LY - 1, wy[...] * keep_y, wy[...])
    lane = lax.broadcasted_iota(jnp.int32, (LX, LY, NZ), 2)
    wm[2] = jnp.where(lane == NZ - 1, 0.0, wz[...])

    for x in range(CX):
        i = 2 * x
        wyp = wm[1, i] + wm[1, i + 1]
        wzp = wm[2, i] + wm[2, i + 1]
        parts = (
            (wm[0, i + 1], SUM),
            (wm[0, i], SUM),
            (wyp, SUM),
            (wzp, ODD),
            (wzp, EVEN),
        )
        for q, (a, how) in enumerate(parts):
            Q[q, x * LY : x * LY + 8] = compress(a[0:8], how)
            Q[q, x * LY + 8 : x * LY + 16] = compress(a[8:16], how)
    ri = lax.broadcasted_iota(jnp.int32, (CX * CY, CX * LY), 0)
    ci = lax.broadcasted_iota(jnp.int32, (CX * CY, CX * LY), 1)
    both = jnp.where((ci >> 1) == ri, 1.0, 0.0)
    first = jnp.where(ci == 2 * ri, 1.0, 0.0)
    second = jnp.where(ci == 2 * ri + 1, 1.0, 0.0)

    def rows(m, q):
        return jnp.dot(m, Q[q], precision=lax.Precision.HIGHEST, preferred_element_type=jnp.float32)

    inside = 2.0 * (rows(both, 1) + rows(first, 2) + rows(both, 4))
    for a, w in enumerate((rows(both, 0), rows(second, 2), rows(both, 3), inside)):
        for x in range(CX):
            cw[a, x] = w[x * CY : (x + 1) * CY]

    for msg, planes_ in ((xu, UP_W), (xd, DN_W)):
        at = NV
        for w, x in planes_:
            msg[at] = wm[w, x, 0:8]
            msg[at + 1] = wm[w, x, 8:16]
            at += 2
        for x in range(CX):
            for a in range(4):
                z = 128 * (a & 1)
                msg[at + 2 * x + (a >> 1), :, z : z + 128] = cw[a, x]
    for x in range(LX):
        put_rows(
            yu,
            yd,
            H * LX + x,
            [wm[w, x, 0:8] for w in range(3)],
            [wm[w, x, 8:16] for w in range(3)],
        )
    for x in range(CX):
        put_coarse_rows(yu, yd, H * LX + LX + x, [cw[a, x] for a in range(4)])

    copies[0].wait()
    for x in range(LX):
        for t in range(0, LY, 8):
            vt[x, t : t + 8] = jnp.swapaxes(v[:, x, t : t + 8, :], 0, 1)
    for d in range(H):
        xu[d * LY : (d + 1) * LY] = vt[LX - H + d]
        xd[d * LY : (d + 1) * LY] = vt[d]
    for x in range(LX):
        for d in range(1, H + 1):
            yu[x * H + d - 1] = vt[x, LY - d]
            yd[x * H + d - 1] = vt[x, d - 1]


def x_cell(xl, xr, p, y):
    return xl[(p + H) * LY + y] if p < 0 else xr[(p - LX) * LY + y]


def x_weight(xl, xr, w, p):
    if p < 0:
        at = NV + 2 * UP_W.index((w, p + LX))
        return xl[at], xl[at + 1]
    at = NV + 2 * DN_W.index((w, p - LX))
    return xr[at], xr[at + 1]


def x_coarse(xl, xr, a, p):
    z = 128 * (a & 1)
    if p < 0:
        return xl[NXU - 2 * CX + 2 * (p + CX) + (a >> 1), :, z : z + 128]
    return xr[NXD - 2 * CX + 2 * (p - CX) + (a >> 1), :, z : z + 128]


def corner_send(xl, xr, cu, cd):
    n = 0
    for side in (-1, 1):
        for dx, dy in CELLS:
            p = -dx if side < 0 else LX - 1 + dx
            cu[n] = x_cell(xl, xr, p, LY - dy)
            cd[n] = x_cell(xl, xr, p, dy - 1)
            n += 1
    for p in WP:
        tiles = [x_weight(xl, xr, w, p) for w in range(3)]
        put_rows(cu, cd, n, [t[0] for t in tiles], [t[1] for t in tiles])
        n += 1
    for p in CWP:
        put_coarse_rows(cu, cd, n, [x_coarse(xl, xr, a, p) for a in range(4)])
        n += 1


def planes(radius, body, own, halo):
    def step(n, _):
        body(n + halo, radius)
        return 0

    lax.fori_loop(0, own, step, 0)
    for d in range(1, radius + 1):
        body(halo - d, radius - d)
        body(halo + own - 1 + d, radius - d)


SUM, EVEN, ODD = 0, 1, 2


def compress(a, how=SUM):
    lane = lax.broadcasted_iota(jnp.int32, (8, 128), 1)
    t = a + up_z(a) if how == SUM else a
    at = (2 * lane + (1 if how == ODD else 0)) & 127
    lo = jnp.take_along_axis(t[:, :128], at, 1)
    hi = jnp.take_along_axis(t[:, 128:], at, 1)
    return jnp.where(lane < 64, lo, hi)


def expand(a):
    lane = lax.broadcasted_iota(jnp.int32, (8, 128), 1)
    half = lane >> 1
    return jnp.concatenate(
        [jnp.take_along_axis(a, half, 1), jnp.take_along_axis(a, half + 64, 1)], 1
    )


def stencil(w, at):
    c = at(0, 0)
    return (
        w(0) * at(1, 0)
        + w(1) * at(-1, 0)
        + w(2) * at(0, 1)
        + w(3) * at(0, -1)
        + w(4) * up_z(c)
        + w(5) * down_z(c)
    )


def fine_level(vt, wm, cw, xl, xr, yl, yr, V, W, NW, Y1, Y2, Y3, f, over):
    V[H : H + LX, H : H + LY] = vt[...]
    for d in range(H):
        V[d, H : H + LY] = xl[d * LY : (d + 1) * LY]
        V[H + LX + d, H : H + LY] = xr[d * LY : (d + 1) * LY]
    for x in range(LX):
        for d in range(1, H + 1):
            V[x + H, H - d] = yl[x * H + d - 1]
            V[x + H, H + LY - 1 + d] = yr[x * H + d - 1]
    for w in range(3):
        W[w, H : H + LX, JW : JW + LY] = wm[w]
        for p in list(range(-H if w == 0 else -2, 0)) + [LX, LX + 1]:
            lo, hi = x_weight(xl, xr, w, p)
            W[w, p + H, JW : JW + 8] = lo
            W[w, p + H, JW + 8 : JW + 16] = hi
    for x in range(LX):
        n, i = H * LX + x, x + H
        W[0, i, JW - 2 : JW] = yl[n, 0:2]
        W[1, i, JW - 3 : JW] = yl[n, 2:5]
        W[2, i, JW - 2 : JW] = yl[n, 6:8]
        W[0, i, JW + LY : JW + LY + 2] = yr[n, 0:2]
        W[1, i, JW + LY : JW + LY + 2] = yr[n, 2:4]
        W[2, i, JW + LY : JW + LY + 2] = yr[n, 4:6]

    def norm(i, _):
        wx, lx = W[0, i], W[0, i - 1]
        wy = W[1, i]
        ly = pltpu.roll(wy, 1, 0)
        wz = W[2, i]
        lz = down_z(wz)
        deg = wx + lx + wy + ly + wz + lz
        inv = 1.0 / deg
        for a, w in enumerate((wx, lx, wy, ly, wz, lz)):
            NW[a, i] = w * inv
        NW[6, i] = deg
        return 0

    lax.fori_loop(1, LX + 5, norm, 0)

    def apply(src, dst, *parts):
        for first, step, count, low, high in parts:

            def body(n, _):
                i = H + first + step * n
                for y in range(low, high + 1):
                    r, j = y + JW, y + H
                    dst[i, j] = stencil(
                        lambda a: row(NW, a, i, r), lambda dx, dy: src[i + dx, j + dy]
                    )
                return 0

            lax.fori_loop(0, count, body, 0)

    apply(V, Y1, (1, 1, 6, -2, 17), (0, 7, 2, 0, 15), (-2, 1, 2, 1, 14), (8, 1, 2, 1, 14))
    apply(Y1, Y2, (2, 1, 4, -1, 16), (1, 5, 2, 0, 15), (0, 7, 2, 1, 14), (-1, 9, 2, 2, 13))
    apply(Y2, Y3, (2, 1, 4, 0, 15), (1, 5, 2, 1, 14), (0, 7, 2, 2, 13))

    first_row = lax.broadcasted_iota(jnp.int32, (CY, CZ), 0) == 0
    for x in range(CX):
        cx, cy, cz = cw[0, x], cw[1, x], cw[2, x]
        lcx = cw[0, x - 1] if x else x_coarse(xl, xr, 0, -1)
        edge = coarse_rows(yl, H * LX + LX + x, 1)[3:4]
        lcy = jnp.where(first_row, jnp.broadcast_to(edge, (CY, CZ)), pltpu.roll(cy, 1, 0))
        over[x] = 1.0 / (
            DIAG * (cx + lcx + cy + lcy + cz + down_z(cz)) + SHIFT * cw[3, x]
        )

    def block(x, _):
        for y in range(CY):
            ra, rb = 0.0, 0.0
            for dx in range(2):
                for dy in range(2):
                    i = H + 2 * x + dx
                    j = H + 2 * y + dy
                    ga, gb = rest(V[i, j], Y1[i, j], Y2[i, j], Y3[i, j])
                    deg = row(NW, 6, i, j - H + JW)
                    ra = ra + deg * ga
                    rb = rb + deg * gb
            inv = row(over, x, y)
            f[x, y, 0] = compress(ra) * inv
            f[x, y, 1] = compress(rb) * inv
        return 0

    lax.fori_loop(0, CX, block, 0)


def rest(v, y1, y2, y3):
    gb = G0 * v + G1 * y1 + G2 * y2
    return gb - (G0 * y1 + G1 * y2 + G2 * y3), gb


def smooth(v, y1, y2, y3):
    b = B0 * v + B1 * y1 + B2 * y2
    return v - (b - (B0 * y1 + B1 * y2 + B2 * y3)), b


def fine_corners(V, W, NW, Y1, Y2, Y3, f_, over, cl, cr, f, fix):
    f[...] = f_[...]
    for side in range(2):
        for top in range(2):
            msg = cr if top else cl

            def px(dx):
                return LX - 1 + dx if side else -dx

            def py(dy):
                return LY - 1 + dy if top else -dy

            got = {}
            for n, (dx, dy) in enumerate(CELLS):
                got[px(dx), py(dy)] = msg[len(CELLS) * side + n]

            def raw(w, x, y):
                out_x = x < 0 or x >= LX
                out_y = y < 0 or y >= LY
                if out_x and out_y:
                    n = 2 * len(CELLS) + WP.index(x)
                    if top:
                        r = (0, 2, 4)[w] + y - LY
                    else:
                        r = (2, 5, 8)[w] + y
                    return msg[n, r : r + 1]
                return W[w, x + H, y + JW : y + JW + 1]

            weights = {}

            def weight(x, y):
                if (x, y) not in weights:
                    wx, lx = raw(0, x, y), raw(0, x - 1, y)
                    wy, ly = raw(1, x, y), raw(1, x, y - 1)
                    wz = raw(2, x, y)
                    ws = (wx, lx, wy, ly, wz, down_z(wz))
                    inv = 1.0 / (wx + lx + wy + ly + wz + ws[5])
                    weights[x, y] = [jnp.broadcast_to(w * inv, (8, NZ)) for w in ws]
                return weights[x, y]

            def look(known, ref):
                def at(x, y):
                    return known[x, y] if (x, y) in known else ref[x + H, y + H]

                return at

            def run(at, cells, fresh):
                out = {}
                for dx, dy in cells:
                    x, y = px(dx), py(dy)
                    if fresh(dx, dy):
                        ws = weight(x, y)
                    else:
                        ws = [row(NW, a, x + H, y + JW) for a in range(6)]
                    out[x, y] = stencil(
                        lambda a: ws[a], lambda ex, ey: at(x + ex, y + ey)
                    )
                return out

            def fresh(dx, dy):
                return (dx > 0 and dy >= 0) or (dy > 0 and dx >= 0)

            v = look(got, V)
            y1 = look(run(v, [(1, 0), (2, 0), (1, 1), (0, 1), (0, 2)], fresh), Y1)
            y2 = look(run(y1, [(0, 0), (1, 0), (1, -1), (0, 1), (-1, 1)], fresh), Y2)
            y3 = look(run(y2, [(0, 0), (-1, 0), (0, -1)], fresh), Y3)
            ra, rb = 0.0, 0.0
            for n, (dx, dy) in enumerate(((0, 0), (-1, 0), (0, -1), (-1, -1))):
                x, y = px(dx), py(dy)
                four = (v(x, y), y1(x, y), y2(x, y), y3(x, y))
                ga, gb = rest(*four)
                deg = row(NW, 6, x + H, y + JW)
                ra = ra + deg * ga
                rb = rb + deg * gb
                p, b = smooth(*four)
                fix[2 * side + top, n, 0:8] = p
                fix[2 * side + top, n, 8:16] = b
            x, y = (CX - 1) * side, (CY - 1) * top
            inv = row(over, x, y)
            f[x, y, 0] = compress(ra) * inv
            f[x, y, 1] = compress(rb) * inv


def meanwhile(vt, NW, Y1, Y2, Y3, fix, cw, xl, xr, yl, yr, cl, cr, pb, nd, CW, R):
    def step(x, sums):
        num, den = sums
        for y in range(LY):
            v, y1 = vt[x, y], Y1[x + H, y + H]
            p, b = smooth(v, y1, Y2[x + H, y + H], Y3[x + H, y + H])
            pb[x, y, 0:8] = p
            pb[x, y, 8:16] = b
            dv = row(NW, 6, x + H, y + JW) * v
            num = num + dv * (v - y1)
            den = den + dv * v
        return num, den

    zero = jnp.zeros((8, NZ), jnp.float32)
    num, den = lax.fori_loop(0, LX, step, (zero, zero))
    nd[0] = num
    nd[1] = den
    for side in range(2):
        for top in range(2):
            for n, (dx, dy) in enumerate(((0, 0), (-1, 0), (0, -1), (-1, -1))):
                x = LX - 1 + dx if side else -dx
                y = LY - 1 + dy if top else -dy
                pb[x, y] = fix[2 * side + top, n]

    for a in range(4):
        for i in range(CX + 2 * CH):
            p = i - CH
            mid = cw[a, p] if 0 <= p < CX else x_coarse(xl, xr, a, p)
            R[a, i, JC : JC + CY] = mid
            if 0 <= p < CX:
                lo = coarse_rows(yl, H * LX + LX + p, a)
                hi = coarse_rows(yr, H * LX + LX + p, a)
            elif p in CWP:
                n = 2 * len(CELLS) + len(WP) + CWP.index(p)
                lo, hi = coarse_rows(cl, n, a), coarse_rows(cr, n, a)
            else:
                continue
            R[a, i, JC - 4 : JC] = lo
            R[a, i, JC + CY : JC + CY + 4] = hi
    for i in range(1, CX + 2 * CH - 1):
        cx, lcx, cy, cz = R[0, i], R[0, i - 1], R[1, i], R[2, i]
        ws = (cx, lcx, cy, pltpu.roll(cy, 1, 0), cz, down_z(cz))
        total = ws[0] + ws[1] + ws[2] + ws[3] + ws[4] + ws[5]
        inv = OMEGA / (DIAG * total + SHIFT * R[3, i])
        for a in range(6):
            CW[a, i] = ws[a] * inv


JC = 8
CCELLS = [(dx, dy) for dx in (1, 2, 3) for dy in range(1, CH + 1 - dx)]


def coarse_corner_send(left, right, cu, cd):
    n = 0
    for side in range(2):
        for dx, dy in CCELLS:
            x = dx - 1 if side else CX - dx
            src = right if side else left
            for half in range(2):
                cu[n] = src[x, CY - dy, half]
                cd[n] = src[x, dy - 1, half]
                n += 1


def coarse_level(own, left, right, yl, yr, cl, cr, CW, pb, NW, nd, po, bo, sums, F, EA, EB, EX):
    def put(i, j, half, f):
        f = OMEGA * f
        F[i, j, half] = f
        EA[i, j, half] = f

    for x in range(CX):
        for half in range(2):
            for y in range(CY):
                put(x, y + CH, half, left[x, y, half])
                put(x + CH, y + CH, half, own[x, y, half])
                put(x + CH + CX, y + CH, half, right[x, y, half])
            for y in range(CH):
                put(x + CH, y, half, yl[x, y, half])
                put(x + CH, y + CH + CY, half, yr[x, y, half])
    n = 0
    for side in range(2):
        for dx, dy in CCELLS:
            i = CH + CX - 1 + dx if side else CH - dx
            for half in range(2):
                put(i, CH - dy, half, cl[n])
                put(i, CH + CY - 1 + dy, half, cr[n])
                n += 1

    def sweep(src, dst):
        def body(i, reach):
            for j in range(CH - reach, CH + CY + reach):
                r = j - CH + JC
                ws = [row(CW, a, i, r) for a in range(6)]
                for half in range(2):
                    c = src[i, j, half]
                    dst[i, j, half] = (
                        (1.0 - OMEGA) * c
                        + F[i, j, half]
                        + ws[0] * src[i + 1, j, half]
                        + ws[1] * src[i - 1, j, half]
                        + ws[2] * src[i, j + 1, half]
                        + ws[3] * src[i, j - 1, half]
                        + ws[4] * up_z(c)
                        + ws[5] * down_z(c)
                    )

        return body

    planes(3, sweep(EA, EB), CX, CH)
    planes(2, sweep(EB, EA), CX, CH)
    planes(1, sweep(EA, EB), CX, CH)

    def spread(i, reach):
        for j in range(CH - reach, CH + CY + reach):
            for half in range(2):
                EX[i, j, half] = expand(EB[i, j, half])

    planes(1, spread, CX, CH)

    def block(x, _):
        for y in range(CY):
            for half in range(2):
                e = EX[x + CH, y + CH, half]
                ez = (up_z(e), down_z(e))
                ke = KEEP * e
                ce = C * e
                for dx in range(2):
                    ex = C * EX[x + CH + 2 * dx - 1, y + CH, half]
                    for dy in range(2):
                        ey = C * EX[x + CH, y + CH + 2 * dy - 1, half]
                        xx, yy = 2 * x + dx, 2 * y + dy
                        nw = [row(NW, a, xx + H, yy + JW) for a in range(6)]
                        s = (
                            ke
                            + (nw[dx] + nw[2 + dy]) * ce
                            + nw[1 - dx] * ex
                            + nw[3 - dy] * ey
                            + C * (nw[4] * ez[0] + nw[5] * ez[1])
                        )
                        if half == 0:
                            po[xx, yy] = pb[xx, yy, 0:8] - s
                        else:
                            bo[xx, yy] = pb[xx, yy, 8:16] + s
        return 0

    lax.fori_loop(0, CX, block, 0)

    def gram(n, acc):
        x = n >> 2
        acc = list(acc)
        for q in range(4):
            yy = (n & 3) * 4 + q
            deg = row(NW, 6, x + H, yy + JW)
            for h in range(0, NZ, 128):
                z = slice(h, h + 128)
                p = po[x, yy, :, z]
                b = bo[x, yy, :, z]
                dp = deg[:, z] * p
                db = deg[:, z] * b
                for s in range(8):
                    rb = pltpu.roll(db, s, 0) if s else db
                    if s < 5:
                        rp = pltpu.roll(dp, s, 0) if s else dp
                        acc[s] = acc[s] + p * rp
                        acc[5 + s] = acc[5 + s] + b * rb
                    acc[10 + s] = acc[10 + s] + p * rb
        return tuple(acc)

    zero = jnp.zeros((8, 128), jnp.float32)
    acc = list(lax.fori_loop(0, 4 * LX, gram, (zero,) * 18))
    for q in range(2):
        acc.append(nd[q, :, :128] + nd[q, :, 128:])
    ones = jnp.ones((8, 128), jnp.float32)

    def over_lanes(m):
        return lax.dot_general(
            ones,
            m,
            (((1,), (1,)), ((), ())),
            precision=lax.Precision.HIGHEST,
            preferred_element_type=jnp.float32,
        )

    t0 = over_lanes(jnp.concatenate(acc[:16], 0))
    t1 = over_lanes(jnp.concatenate(acc[16:] + [zero] * 12, 0))
    both = jnp.concatenate([t0[0:1], t1[0:1]], 0)
    sums[...] = jnp.broadcast_to(both[None], sums.shape)


def finish(parts, po, bo, out, eig, SP):
    t = parts[...]
    n = t.shape[0]
    while n > 1:
        n //= 2
        t = t[:n] + t[n:]
    t = t[0]
    eye = lax.broadcasted_iota(jnp.int32, (128, 128), 0) == lax.broadcasted_iota(
        jnp.int32, (128, 128), 1
    )
    ones = jnp.ones((128, 128), jnp.float32)
    for q in range(2):
        m = jnp.where(eye, jnp.broadcast_to(t[q : q + 1], (128, 128)), 0.0)
        SP[128 * q : 128 * (q + 1)] = jnp.dot(
            m, ones, precision=lax.Precision.HIGHEST, preferred_element_type=jnp.float32
        )
    lams = t[1:2] / pltpu.roll(t[1:2], 120, 1)
    eig[...] = pltpu.roll(lams, 112, 1)[:, :K]

    def entry(block, k):
        return row(SP, 8 * block + k)

    def sym(base, a, b):
        s = (a - b) % 8
        return entry(base + s, a) if s < 5 else entry(base + 8 - s, b)

    def cross(a, b):
        return entry(10 + (a - b) % 8, a)

    lam = [entry(18, k) / entry(19, k) for k in range(K)]
    voxels = LX * LY * NZ * lax.axis_size("gx") * lax.axis_size("gy")
    g = {}
    for a in range(K):
        for b in range(a + 1):
            g[a, b] = (
                sym(0, a, b) + lam[b] * cross(a, b) + lam[a] * (cross(b, a) + lam[b] * sym(5, a, b))
            ) * (1.0 / voxels)
    low, inv = {}, []
    for j in range(K):
        d = g[j, j]
        r = lax.rsqrt(d)
        r = r * (1.5 - 0.5 * d * r * r)
        inv.append(r)
        for a in range(j + 1, K):
            low[a, j] = g[a, j] * r
        for a in range(j + 1, K):
            for b in range(j + 1, a + 1):
                g[a, b] = g[a, b] - low[a, j] * low[b, j]

    for k in range(K):
        SP[8 * k : 8 * k + 8] = lam[k]
        SP[64 + 8 * k : 72 + 8 * k] = inv[k]
    at = {}
    for n, (a, b) in enumerate(sorted(low)):
        at[a, b] = 128 + 8 * n
        SP[128 + 8 * n : 136 + 8 * n] = low[a, b]

    def body(x, _):
        for t in range(0, LY, 8):
            for h in range(0, NZ, 128):
                z = slice(h, h + 128)
                p = jnp.swapaxes(po[x, t : t + 8, :, z], 0, 1)
                b = jnp.swapaxes(bo[x, t : t + 8, :, z], 0, 1)
                done = []
                for k in range(K):
                    u = p[k] + SP[8 * k : 8 * k + 8] * b[k]
                    for j in range(k):
                        u = u - SP[at[k, j] : at[k, j] + 8] * done[j]
                    u = u * SP[64 + 8 * k : 72 + 8 * k]
                    done.append(u)
                    out[k, x, t : t + 8, z] = u
        return 0

    lax.fori_loop(0, LX, body, 0)


def both_ways(up, down, axis):
    n = lax.axis_size(axis)
    fwd = [(i, (i + 1) % n) for i in range(n)]
    back = [((i + 1) % n, i) for i in range(n)]
    return lax.ppermute(up, axis, fwd), lax.ppermute(down, axis, back)


def per_device(vectors, weight_x, weight_y, weight_z):
    vt, wm, cw, xu, xd, yu, yd = call(
        prepare,
        [
            (LX, LY, K, NZ),
            (3, LX, LY, NZ),
            (4, CX, CY, CZ),
            (NXU, 8, NZ),
            (NXD, 8, NZ),
            (NYB, 8, NZ),
            (NYB, 8, NZ),
        ],
        (vectors, weight_x, weight_y, weight_z),
        [
            (K, LX, LY, NZ),
            (LX, LY, NZ),
            (LX, LY, NZ),
            (LX, LY, NZ),
            (5, CX * LY, CZ),
            pltpu.SemaphoreType.DMA((4,)),
        ],
        where=HBM,
        limit=56,
    )
    xl, xr = both_ways(xu, xd, "gx")
    yl, yr = both_ways(yu, yd, "gy")
    cu, cd = call(corner_send, [(NCB, 8, NZ)] * 2, (xl, xr))
    cl, cr = both_ways(cu, cd, "gy")
    ext = (LX + 2 * H, LY + 2 * H, K, NZ)
    V, W, NW, Y1, Y2, Y3, f, over = call(
        fine_level,
        [
            ext,
            (3, LX + 2 * H, 32, NZ),
            (7, LX + 2 * H, 32, NZ),
            ext,
            ext,
            ext,
            (CX, CY, 2, 8, CZ),
            (CX, CY, CZ),
        ],
        (vt, wm, cw, xl, xr, yl, yr),
        us=6,
    )
    f, fix = call(
        fine_corners,
        [(CX, CY, 2, 8, CZ), (4, 4, 16, NZ)],
        (V, W, NW, Y1, Y2, Y3, f, over, cl, cr),
    )
    left, right = both_ways(f, f, "gx")
    fl, fr = both_ways(f[:, CY - CH :], f[:, :CH], "gy")
    pb, nd, CW = call(
        meanwhile,
        [(LX, LY, 16, NZ), (2, 8, NZ), (6, CX + 2 * CH, 24, CZ)],
        (vt, NW, Y1, Y2, Y3, fix, cw, xl, xr, yl, yr, cl, cr),
        [(4, CX + 2 * CH, 24, CZ)],
        us=2,
    )
    cu, cd = call(coarse_corner_send, [(4 * len(CCELLS), 8, CZ)] * 2, (left, right))
    cl, cr = both_ways(cu, cd, "gy")
    n = lax.axis_size("gx") * lax.axis_size("gy")
    cext = (CX + 2 * CH, CY + 2 * CH, 2, 8, CZ)
    po, bo, sums = call(
        coarse_level,
        [(LX, LY, K, NZ), (LX, LY, K, NZ), (n, 2, 128)],
        (f, left, right, fl, fr, cl, cr, CW, pb, NW, nd),
        [cext, cext, cext, (CX + 2 * CH, CY + 2 * CH, 2, 8, NZ)],
        limit=12,
    )
    parts = lax.all_to_all(sums, ("gx", "gy"), 0, 0)
    refined, eig = call(
        finish,
        [(K, LX, LY, NZ), (1, K)],
        (parts, po, bo),
        [(384, 128)],
    )
    return refined, eig.reshape(K)


def solution(mesh):
    return jax.shard_map(
        per_device,
        mesh=mesh,
        in_specs=(
            P(None, "gx", "gy", None),
            P("gx", "gy", None),
            P("gx", "gy", None),
            P("gx", "gy", None),
        ),
        out_specs=(P(None, "gx", "gy", None), P()),
        check_vma=False,
    )
```

time: 99.1 us -> 91.2 us (0.920)
  waiting for transfers between devices: 34.8 us -> 16.8 us
  starting transfers between devices: 17.7 us -> 26.2 us
  Pallas kernels: 16.6 us -> 20.1 us
  blocking collectives: 25.3 us -> 24 us
    ppermute x8 -> x12, waiting for transfers between devices: 34.8 us -> 16.8 us  [both_ways(): return (lax.ppermute(up, axis, fwd), lax.ppermute(down, axis, back))]
    ppermute x8 -> x12, starting transfers between devices: 17.7 us -> 26.2 us  [both_ways(): return (lax.ppermute(up, axis, fwd), lax.ppermute(down, axis, back))]
    pallas_call x6 -> x8, Pallas kernels: 16.6 us -> 20.1 us  [call(): pl.pallas_call(body, out_shape=[jax.ShapeDtypeStruct(s, jnp.float32) for...]
    all_to_all x1, blocking collectives: 25.3 us -> 24 us  [per_device(): parts = lax.all_to_all(sums, ('gx', 'gy'), 0, 0)]
  transfers between devices with their start and end apart: 8 -> 12, of which waited for: 7 -> 6; matrix products, arithmetic and copies ran while one was open for 0% -> 0% of each run, Pallas kernels for 0% -> 8%
where the time goes in v3:
time: 91.2 us; the launch traced here: 91 us
  starting transfers between devices  26.2 us (29%)
  blocking collectives  24 us (26%)
  Pallas kernels  20.1 us (22%)
  waiting for transfers between devices  16.8 us (18%)
  local copies, waits for them, and re-layouts  3.08 us (3%)
    ppermute x12, starting transfers between devices, both_ways(): return (lax.ppermute(up, axis, fwd), lax.ppermute(down, axis, back))  26.2 us
    all_to_all x1, blocking collectives, per_device(): parts = lax.all_to_all(sums, ('gx', 'gy'), 0, 0)  24 us
    pallas_call x8, Pallas kernels, call(): pl.pallas_call(body, out_shape=[jax.ShapeDtypeStruct(s, jnp.float32) for...  20.1 us
    ppermute x12, waiting for transfers between devices, both_ways(): return (lax.ppermute(up, axis, fwd), lax.ppermute(down, axis, back))  16.8 us
    unnamed x8, local copies, waits for them, and re-layouts  3.06 us
  transfers between devices with their start and end apart: 12, of which 6 were waited for; matrix products, arithmetic and copies ran while one was open for 0% of the time, Pallas kernels for 8%

profile of v3, /device:TPU:1, one launch (start us, length us, event | category | flops | bytes accessed | tf_op | source)
XLA Modules:
  0.0 91.0 jit_solution(4881653991568335812)
XLA Ops:
  0.6 3.5 %shard_map.59 = (f32[8,16,8,256]{3,2,1,0:T(8,128)}, f32[3,8,16,256]{3,2,1,0:T(8,128)}, f32[4,4,8,128]{3,2,1,0:T(8,128)}, f32[70,8,256]{2,1,0:T(8,128)}, f32[68,8...) custom-call(f32[8,8,16,256]{3,2,1,0:T(8,128)} %v_.1, f32[8,16,256]{2,1,0:T(8,128)} %wx_.1, ...), custom_call_target="tpu_custom_call" | custom-call | bytes 3000000 | tf_op jit(solution)/shard_map/pallas_call | solution.py:32
  4.2 2.1 %collective-permute-start = (f32[70,8,256]{2,1,0:T(8,128)}, f32[70,8,256]{2,1,0:T(8,128)S(1)}, u32[]{:S(2)}, u32[]{:S(2)}) collective-permute-start(f32[70,8,256]{2,1,0:T(8,128)} %get-tuple-element.34), channel_id=1, source_target_pairs={{0,16},{16,32},{32,48},{48,64},{64,80},{80,96},{96,112},{112,128},... | collective-permute-start | bytes 1720328 | tf_op jit(solution)/shard_map/ppermute | solution.py:701
  6.3 3.8 %collective-permute-start.1 = (f32[68,8,256]{2,1,0:T(8,128)}, f32[68,8,256]{2,1,0:T(8,128)S(1)}, u32[]{:S(2)}, u32[]{:S(2)}) collective-permute-start(f32[68,8,256]{2,1,0:T(8,128)} %get-tuple-element.35), channel_id=1, source_target_pairs={{16,0},{32,16},{48,32},{64,48},{80,64},{96,80},{112,96},{128,112},... | collective-permute-start | bytes 1671176 | tf_op jit(solution)/shard_map/ppermute | solution.py:701
  10.1 2.5 %collective-permute-start.2 = (f32[36,8,256]{2,1,0:T(8,128)}, f32[36,8,256]{2,1,0:T(8,128)S(1)}, u32[]{:S(2)}, u32[]{:S(2)}) collective-permute-start(f32[36,8,256]{2,1,0:T(8,128)} %get-tuple-element.36), channel_id=1, source_target_pairs={{0,1},{1,2},{2,3},{3,4},{4,5},{5,6},{6,7},{7,8},{8,9},{9,10},{10,1... | collective-permute-start | bytes 884744 | tf_op jit(solution)/shard_map/ppermute | solution.py:701
  12.6 0.2 collective-permute-start.3
  12.8 7.0 %collective-permute-done.1.xr = f32[68,8,256]{2,1,0:T(8,128)S(1)} collective-permute-done((f32[68,8,256]{2,1,0:T(8,128)}, f32[68,8,256]{2,1,0:T(8,128)S(1)}, u32[]{:S(2)}, u32[]{:S(2)}) %collective-permute-start.1) | collective-permute-done | bytes 557088 | tf_op jit(solution)/shard_map/ppermute | solution.py:701
  19.9 1.1 %collective-permute-done.xl = f32[70,8,256]{2,1,0:T(8,128)S(1)} collective-permute-done((f32[70,8,256]{2,1,0:T(8,128)}, f32[70,8,256]{2,1,0:T(8,128)S(1)}, u32[]{:S(2)}, u32[]{:S(2)}) %collective-permute-start) | collective-permute-done | bytes 573472 | tf_op jit(solution)/shard_map/ppermute | solution.py:701
  21.0 4.7 %collective-permute-start.4 = (f32[16,8,256]{2,1,0:T(8,128)S(1)}, f32[16,8,256]{2,1,0:T(8,128)S(1)}, u32[]{:S(2)}, u32[]{:S(2)}) collective-permute-start(f32[16,8,256]{2,1,0:T(8,128)S(1)} %get-tuple-element.46), channel_id=1, source_target_pairs={{0,1},{1,2},{2,3},{3,4},{4,5},{5,6},{6,7},{7,8},{8,9},{9,10},{10,1... | collective-permute-start | bytes 393224 | tf_op jit(solution)/shard_map/ppermute | solution.py:701
  25.7 0.0 collective-permute-start.5
  25.7 0.0 collective-permute-done.2.yl
  25.7 0.0 collective-permute-done.3.yr
  25.7 0.0 copy-start
  25.7 1.2 %copy-done = f32[8,16,8,256]{3,2,1,0:T(8,128)S(1)} copy-done((f32[8,16,8,256]{3,2,1,0:T(8,128)S(1)}, f32[8,16,8,256]{3,2,1,0:T(8,128)}, u32[]{:S(2)}) %copy-start) | copy-done | bytes 1048600
  27.0 0.0 copy-start.2
  27.0 1.0 %copy-done.2 = f32[3,8,16,256]{3,2,1,0:T(8,128)S(1)} copy-done((f32[3,8,16,256]{3,2,1,0:T(8,128)S(1)}, f32[3,8,16,256]{3,2,1,0:T(8,128)}, u32[]{:S(2)}) %copy-start.2) | copy-done | bytes 393240
  28.0 0.0 copy-start.3
  28.0 0.8 copy-done.3
  28.8 6.6 %shard_map.60 = (f32[14,22,8,256]{3,2,1,0:T(8,128)S(1)}, f32[3,14,32,256]{3,2,1,0:T(8,128)S(1)}, f32[7,14,32,256]{3,2,1,0:T(8,128)S(1)}, f32[14,22,8,256]{3,2,1,...) custom-call(f32[8,16,8,256]{3,2,1,0:T(8,128)S(1)} %copy-done, ...), custom_call_target="tpu_custom_call" | custom-call | bytes 18000000 | tf_op jit(solution)/shard_map/pallas_call | solution.py:32
  35.4 0.0 collective-permute-done.4.cl
  35.5 0.0 collective-permute-done.5.cr
  35.5 0.0 copy-start.1
  35.5 0.6 shard_map.62
  36.1 4.6 %collective-permute-start.7 = (f32[4,8,2,8,128]{4,3,2,1,0:T(8,128)S(1)}, f32[4,8,2,8,128]{4,3,2,1,0:T(8,128)S(1)}, u32[]{:S(2)}, u32[]{:S(2)}) collective-permute-start(f32[4,8,2,8,128]{4,3,2,1,0:T(8,128)S(1)} %get-tuple-element.48.own), channel_id=1, source_target_pairs={{16,0},{32,16},{48,32},{64,48},{80,64},{96,80},{112,96},{128,112},... | collective-permute-start | bytes 786440 | tf_op jit(solution)/shard_map/ppermute | solution.py:701
  40.7 0.0 collective-permute-start.6
  40.8 3.2 %collective-permute-start.9 = (f32[4,4,2,8,128]{4,3,2,1,0:T(8,128)S(1)}, f32[4,4,2,8,128]{4,3,2,1,0:T(8,128)S(1)}, u32[]{:S(2)}, u32[]{:S(2)}) collective-permute-start(f32[4,4,2,8,128]{4,3,2,1,0:T(8,128)S(1)} %get-tuple-element.60), channel_id=1, source_target_pairs={{1,0},{2,1},{3,2},{4,3},{5,4},{6,5},{7,6},{8,7},{9,8},{10,9},{11,1... | collective-permute-start | bytes 393224 | tf_op jit(solution)/shard_map/ppermute | solution.py:701
  43.9 0.0 collective-permute-start.8
  43.9 0.1 collective-permute-done.7.right
  44.0 5.2 %collective-permute-done.6.left = f32[4,8,2,8,128]{4,3,2,1,0:T(8,128)S(1)} collective-permute-done((f32[4,8,2,8,128]{4,3,2,1,0:T(8,128)S(1)}, f32[4,8,2,8,128]{4,3,2,1,0:T(8,128)S(1)}, u32[]{:S(2)}, u32[]{:S(2)}) %collective-permute-start.6) | collective-permute-done | bytes 262176 | tf_op jit(solution)/shard_map/ppermute | solution.py:701
  49.3 5.0 %collective-permute-start.10 = (f32[24,8,128]{2,1,0:T(8,128)S(1)}, f32[24,8,128]{2,1,0:T(8,128)S(1)}, u32[]{:S(2)}, u32[]{:S(2)}) collective-permute-start(f32[24,8,128]{2,1,0:T(8,128)S(1)} %get-tuple-element.49), channel_id=1, source_target_pairs={{0,1},{1,2},{2,3},{3,4},{4,5},{5,6},{6,7},{7,8},{8,9},{9,10},{10,1... | collective-permute-start | bytes 294920 | tf_op jit(solution)/shard_map/ppermute | solution.py:701
  54.3 0.0 collective-permute-start.11
  54.3 0.0 copy-done.1
  54.3 0.8 shard_map.64
  55.1 0.0 collective-permute-done.9.yr
  55.1 0.0 collective-permute-done.8.yl
  55.1 0.8 collective-permute-done.10.cl
  56.0 2.5 %collective-permute-done.11.cr = f32[24,8,128]{2,1,0:T(8,128)S(1)} collective-permute-done((f32[24,8,128]{2,1,0:T(8,128)S(1)}, f32[24,8,128]{2,1,0:T(8,128)S(1)}, u32[]{:S(2)}, u32[]{:S(2)}) %collective-permute-start.11) | collective-permute-done | bytes 98336 | tf_op jit(solution)/shard_map/ppermute | solution.py:701
  58.5 6.3 %shard_map.65 = (f32[8,16,8,256]{3,2,1,0:T(8,128)S(1)}, f32[8,16,8,256]{3,2,1,0:T(8,128)S(1)}, f32[256,2,128]{2,1,0:T(2,128)S(1)}) custom-call(f32[4,8,2,8,128]{4,3,2,1,0:T(8,128)S(1)} %get-tuple-element.48.own, f32[4,8,2,8,128]{4,3,2,1,0:T(8,128)S(1)} %collective-permute-done.6.left, f32[4,8,2,8,128]{4,3,2,1,0:T(8,128)S(1)} %collective-permute-done.7.right, ...), custom_call_target="tpu_custom_call" | custom-call | bytes 3000000 | tf_op jit(solution)/shard_map/pallas_call | solution.py:32
  64.7 24.0 %all_to_all.5.parts = f32[256,2,128]{2,1,0:T(2,128)S(1)} all-to-all(f32[256,2,128]{2,1,0:T(2,128)S(1)} %get-tuple-element.55), channel_id=1, replica_groups=mesh['gx'=16,'gy'=16] {'gx','gy'}, dimensions={0} | all-to-all | bytes 524288 | tf_op jit(solution)/shard_map/all_to_all | solution.py:773
  88.7 2.2 %shard_map.66 = (f32[8,8,16,256]{3,2,1,0:T(8,128)}, f32[1,8]{1,0:T(1,128)}) custom-call(f32[256,2,128]{2,1,0:T(2,128)S(1)} %all_to_all.5.parts, f32[8,16,8,256]{3,2,1,0:T(8,128)S(1)} %get-tuple-element.56.po, f32[8,16,8,256]{3,2,1,0:T(8,128)S(1)} %get-tuple-element.57.bo), custom_call_target="tpu_custom_call" | custom-call | bytes 3000000 | tf_op jit(solution)/shard_map/pallas_call | solution.py:32
  (3 shorter events, 0.1 us)
Async XLA Ops:
  4.2 16.8 %collective-permute-start = (f32[70,8,256]{2,1,0:T(8,128)}, f32[70,8,256]{2,1,0:T(8,128)S(1)}, u32[]{:S(2)}, u32[]{:S(2)}) collective-permute-start(f32[70,8,256]{2,1,0:T(8,128)} %get-tuple-element.34), channel_id=1, source_target_pairs={{0,16},{16,32},{32,48},{48,64},{64,80},{80,96},{96,112},{112,128},... | collective-permute-start | bytes 1720328 | tf_op jit(solution)/shard_map/ppermute | solution.py:701
  6.3 13.6 %collective-permute-start.1 = (f32[68,8,256]{2,1,0:T(8,128)}, f32[68,8,256]{2,1,0:T(8,128)S(1)}, u32[]{:S(2)}, u32[]{:S(2)}) collective-permute-start(f32[68,8,256]{2,1,0:T(8,128)} %get-tuple-element.35), channel_id=1, source_target_pairs={{16,0},{32,16},{48,32},{64,48},{80,64},{96,80},{112,96},{128,112},... | collective-permute-start | bytes 1671176 | tf_op jit(solution)/shard_map/ppermute | solution.py:701
  10.1 15.6 %collective-permute-start.2 = (f32[36,8,256]{2,1,0:T(8,128)}, f32[36,8,256]{2,1,0:T(8,128)S(1)}, u32[]{:S(2)}, u32[]{:S(2)}) collective-permute-start(f32[36,8,256]{2,1,0:T(8,128)} %get-tuple-element.36), channel_id=1, source_target_pairs={{0,1},{1,2},{2,3},{3,4},{4,5},{5,6},{6,7},{7,8},{8,9},{9,10},{10,1... | collective-permute-start | bytes 884744 | tf_op jit(solution)/shard_map/ppermute | solution.py:701
  12.6 13.1 %collective-permute-start.3 = (f32[36,8,256]{2,1,0:T(8,128)}, f32[36,8,256]{2,1,0:T(8,128)S(1)}, u32[]{:S(2)}, u32[]{:S(2)}) collective-permute-start(f32[36,8,256]{2,1,0:T(8,128)} %get-tuple-element.37), channel_id=1, source_target_pairs={{1,0},{2,1},{3,2},{4,3},{5,4},{6,5},{7,6},{8,7},{9,8},{10,9},{11,1... | collective-permute-start | bytes 884744 | tf_op jit(solution)/shard_map/ppermute | solution.py:701
  21.0 14.4 %collective-permute-start.4 = (f32[16,8,256]{2,1,0:T(8,128)S(1)}, f32[16,8,256]{2,1,0:T(8,128)S(1)}, u32[]{:S(2)}, u32[]{:S(2)}) collective-permute-start(f32[16,8,256]{2,1,0:T(8,128)S(1)} %get-tuple-element.46), channel_id=1, source_target_pairs={{0,1},{1,2},{2,3},{3,4},{4,5},{5,6},{6,7},{7,8},{8,9},{9,10},{10,1... | collective-permute-start | bytes 393224 | tf_op jit(solution)/shard_map/ppermute | solution.py:701
  25.7 9.7 %collective-permute-start.5 = (f32[16,8,256]{2,1,0:T(8,128)S(1)}, f32[16,8,256]{2,1,0:T(8,128)S(1)}, u32[]{:S(2)}, u32[]{:S(2)}) collective-permute-start(f32[16,8,256]{2,1,0:T(8,128)S(1)} %get-tuple-element.47), channel_id=1, source_target_pairs={{1,0},{2,1},{3,2},{4,3},{5,4},{6,5},{7,6},{8,7},{9,8},{10,9},{11,1... | collective-permute-start | bytes 393224 | tf_op jit(solution)/shard_map/ppermute | solution.py:701
  25.7 1.2 %copy-start = (f32[8,16,8,256]{3,2,1,0:T(8,128)S(1)}, f32[8,16,8,256]{3,2,1,0:T(8,128)}, u32[]{:S(2)}) copy-start(f32[8,16,8,256]{3,2,1,0:T(8,128)} %get-tuple-element.31.vt) | copy-start | bytes 3145732
  27.0 1.0 %copy-start.2 = (f32[3,8,16,256]{3,2,1,0:T(8,128)S(1)}, f32[3,8,16,256]{3,2,1,0:T(8,128)}, u32[]{:S(2)}) copy-start(f32[3,8,16,256]{3,2,1,0:T(8,128)} %get-tuple-element.32.wm) | copy-start | bytes 1179652
  28.0 0.8 copy-start.3
  35.5 18.9 %copy-start.1 = (f32[8,16,8,256]{3,2,1,0:T(8,128)S(1)}, f32[8,16,8,256]{3,2,1,0:T(8,128)}, u32[]{:S(2)}) copy-start(f32[8,16,8,256]{3,2,1,0:T(8,128)} %get-tuple-element.31.vt) | copy-start | bytes 3145732
  36.1 7.9 %collective-permute-start.7 = (f32[4,8,2,8,128]{4,3,2,1,0:T(8,128)S(1)}, f32[4,8,2,8,128]{4,3,2,1,0:T(8,128)S(1)}, u32[]{:S(2)}, u32[]{:S(2)}) collective-permute-start(f32[4,8,2,8,128]{4,3,2,1,0:T(8,128)S(1)} %get-tuple-element.48.own), channel_id=1, source_target_pairs={{16,0},{32,16},{48,32},{64,48},{80,64},{96,80},{112,96},{128,112},... | collective-permute-start | bytes 786440 | tf_op jit(solution)/shard_map/ppermute | solution.py:701
  40.7 8.5 %collective-permute-start.6 = (f32[4,8,2,8,128]{4,3,2,1,0:T(8,128)S(1)}, f32[4,8,2,8,128]{4,3,2,1,0:T(8,128)S(1)}, u32[]{:S(2)}, u32[]{:S(2)}) collective-permute-start(f32[4,8,2,8,128]{4,3,2,1,0:T(8,128)S(1)} %get-tuple-element.48.own), channel_id=1, source_target_pairs={{0,16},{16,32},{32,48},{48,64},{64,80},{80,96},{96,112},{112,128},... | collective-permute-start | bytes 786440 | tf_op jit(solution)/shard_map/ppermute | solution.py:701
  40.8 14.4 %collective-permute-start.9 = (f32[4,4,2,8,128]{4,3,2,1,0:T(8,128)S(1)}, f32[4,4,2,8,128]{4,3,2,1,0:T(8,128)S(1)}, u32[]{:S(2)}, u32[]{:S(2)}) collective-permute-start(f32[4,4,2,8,128]{4,3,2,1,0:T(8,128)S(1)} %get-tuple-element.60), channel_id=1, source_target_pairs={{1,0},{2,1},{3,2},{4,3},{5,4},{6,5},{7,6},{8,7},{9,8},{10,9},{11,1... | collective-permute-start | bytes 393224 | tf_op jit(solution)/shard_map/ppermute | solution.py:701
  43.9 11.2 %collective-permute-start.8 = (f32[4,4,2,8,128]{4,3,2,1,0:T(8,128)S(1)}, f32[4,4,2,8,128]{4,3,2,1,0:T(8,128)S(1)}, u32[]{:S(2)}, u32[]{:S(2)}) collective-permute-start(f32[4,4,2,8,128]{4,3,2,1,0:T(8,128)S(1)} %get-tuple-element.61), channel_id=1, source_target_pairs={{0,1},{1,2},{2,3},{3,4},{4,5},{5,6},{6,7},{7,8},{8,9},{9,10},{10,1... | collective-permute-start | bytes 393224 | tf_op jit(solution)/shard_map/ppermute | solution.py:701
  49.3 6.7 %collective-permute-start.10 = (f32[24,8,128]{2,1,0:T(8,128)S(1)}, f32[24,8,128]{2,1,0:T(8,128)S(1)}, u32[]{:S(2)}, u32[]{:S(2)}) collective-permute-start(f32[24,8,128]{2,1,0:T(8,128)S(1)} %get-tuple-element.49), channel_id=1, source_target_pairs={{0,1},{1,2},{2,3},{3,4},{4,5},{5,6},{6,7},{7,8},{8,9},{9,10},{10,1... | collective-permute-start | bytes 294920 | tf_op jit(solution)/shard_map/ppermute | solution.py:701
  54.3 4.1 %collective-permute-start.11 = (f32[24,8,128]{2,1,0:T(8,128)S(1)}, f32[24,8,128]{2,1,0:T(8,128)S(1)}, u32[]{:S(2)}, u32[]{:S(2)}) collective-permute-start(f32[24,8,128]{2,1,0:T(8,128)S(1)} %get-tuple-element.50), channel_id=1, source_target_pairs={{1,0},{2,1},{3,2},{4,3},{5,4},{6,5},{7,6},{8,7},{9,8},{10,9},{11,1... | collective-permute-start | bytes 294920 | tf_op jit(solution)/shard_map/ppermute | solution.py:701

commit v4 on v3

--- a/solution.py
+++ b/solution.py
@@ -25,7 +25,7 @@
 VMEM = pl.BlockSpec(memory_space=pltpu.VMEM)
 
 
-HBM = pl.BlockSpec(memory_space=pltpu.HBM)
+ANY = pl.BlockSpec(memory_space=pl.ANY)
 
 
 def call(body, outs, ins, scratch=(), limit=8, where=VMEM, us=1):
@@ -33,7 +33,7 @@
         body,
         out_shape=[jax.ShapeDtypeStruct(s, jnp.float32) for s in outs],
         in_specs=[where] * len(ins),
-        out_specs=[VMEM] * len(outs),
+        out_specs=[where] * len(outs),
         scratch_shapes=[pltpu.VMEM(s, jnp.float32) if isinstance(s, tuple) else s for s in scratch],
         compiler_params=pltpu.CompilerParams(vmem_limit_bytes=limit * MIB),
         cost_estimate=pl.CostEstimate(
@@ -59,13 +59,14 @@
 UP_W = [(0, 5), (0, 6), (0, 7), (1, 6), (1, 7), (2, 6), (2, 7)]
 DN_W = [(0, 0), (0, 1), (1, 0), (1, 1), (2, 0), (2, 1)]
 NV = H * LY
-NXU = NV + 2 * len(UP_W) + 2 * CX
-NXD = NV + 2 * len(DN_W) + 2 * CX
+NXU = K * H + len(UP_W)
+NXD = K * H + len(DN_W)
+NXB = NV + 2 * len(UP_W)
 NYB = H * LX + LX + CX
 CELLS = [(1, 1), (1, 2), (2, 1)]
 WP = [-2, -1, LX, LX + 1]
 CWP = [-3, -2, -1, CX, CX + 1, CX + 2]
-NCB = 2 * len(CELLS) + len(WP) + len(CWP)
+NCB = 2 * len(CELLS) + len(WP)
 
 
 def put_rows(up, down, n, lows, highs):
@@ -89,15 +90,25 @@
     return msg[n, r : r + 4, z : z + 128]
 
 
-def prepare(v_, wx_, wy_, wz_, vt, wm, cw, xu, xd, yu, yd, v, wx, wy, wz, Q, sem):
-    copies = [
-        pltpu.make_async_copy(a, b, sem.at[n])
-        for n, (a, b) in enumerate(((v_, v), (wx_, wx), (wy_, wy), (wz_, wz)))
-    ]
+def x_send(v, wx, wy, wz, xu, xd, sem):
+    pairs = []
+    for k in range(K):
+        pairs.append((v.at[k, LX - H : LX], xu.at[H * k : H * k + H]))
+        pairs.append((v.at[k, 0:H], xd.at[H * k : H * k + H]))
+    for msg, side in ((xu, UP_W), (xd, DN_W)):
+        at = K * H
+        for w, ref in enumerate((wx, wy, wz)):
+            p = [x for q, x in side if q == w]
+            pairs.append((ref.at[p[0] : p[-1] + 1], msg.at[at : at + len(p)]))
+            at += len(p)
+    copies = [pltpu.make_async_copy(a, b, sem.at[n]) for n, (a, b) in enumerate(pairs)]
     for c in copies:
         c.start()
-    for c in copies[1:]:
+    for c in copies:
         c.wait()
+
+
+def local(v, wx, wy, wz, vt, wm, cw, yu, yd, Q):
     last_x = lax.axis_index("gx") == lax.axis_size("gx") - 1
     last_y = lax.axis_index("gy") == lax.axis_size("gy") - 1
     keep_x = jnp.where(last_x, 0.0, 1.0)
@@ -137,16 +148,6 @@
         for x in range(CX):
             cw[a, x] = w[x * CY : (x + 1) * CY]
 
-    for msg, planes_ in ((xu, UP_W), (xd, DN_W)):
-        at = NV
-        for w, x in planes_:
-            msg[at] = wm[w, x, 0:8]
-            msg[at + 1] = wm[w, x, 8:16]
-            at += 2
-        for x in range(CX):
-            for a in range(4):
-                z = 128 * (a & 1)
-                msg[at + 2 * x + (a >> 1), :, z : z + 128] = cw[a, x]
     for x in range(LX):
         put_rows(
             yu,
@@ -158,13 +159,9 @@
     for x in range(CX):
         put_coarse_rows(yu, yd, H * LX + LX + x, [cw[a, x] for a in range(4)])
 
-    copies[0].wait()
     for x in range(LX):
         for t in range(0, LY, 8):
             vt[x, t : t + 8] = jnp.swapaxes(v[:, x, t : t + 8, :], 0, 1)
-    for d in range(H):
-        xu[d * LY : (d + 1) * LY] = vt[LX - H + d]
-        xd[d * LY : (d + 1) * LY] = vt[d]
     for x in range(LX):
         for d in range(1, H + 1):
             yu[x * H + d - 1] = vt[x, LY - d]
@@ -183,14 +180,29 @@
     return xr[at], xr[at + 1]
 
 
-def x_coarse(xl, xr, a, p):
-    z = 128 * (a & 1)
-    if p < 0:
-        return xl[NXU - 2 * CX + 2 * (p + CX) + (a >> 1), :, z : z + 128]
-    return xr[NXD - 2 * CX + 2 * (p - CX) + (a >> 1), :, z : z + 128]
-
-
-def corner_send(xl, xr, cu, cd):
+def x_receive(rl, rr, after, xl, xr, cu, cd):
+    first_x = lax.axis_index("gx") == 0
+    last_y = lax.axis_index("gy") == lax.axis_size("gy") - 1
+    keep_x = jnp.where(first_x, 0.0, 1.0)
+    keep_y = jnp.where(last_y, 0.0, 1.0)
+    sub = lax.broadcasted_iota(jnp.int32, (8, NZ), 0)
+    lane = lax.broadcasted_iota(jnp.int32, (8, NZ), 1)
+    for src, dst, side in ((rl, xl, UP_W), (rr, xr, DN_W)):
+        for d in range(H):
+            for t in range(0, LY, 8):
+                block = jnp.stack([src[H * k + d, t : t + 8] for k in range(K)])
+                dst[d * LY + t : d * LY + t + 8] = jnp.swapaxes(block, 0, 1)
+        for n, (w, x) in enumerate(side):
+            lo, hi = src[K * H + n, 0:8], src[K * H + n, 8:16]
+            if w == 0 and x == LX - 1:
+                lo, hi = lo * keep_x, hi * keep_x
+            if w == 1:
+                hi = jnp.where(sub == 7, hi * keep_y, hi)
+            if w == 2:
+                lo = jnp.where(lane == NZ - 1, 0.0, lo)
+                hi = jnp.where(lane == NZ - 1, 0.0, hi)
+            dst[NV + 2 * n] = lo
+            dst[NV + 2 * n + 1] = hi
     n = 0
     for side in (-1, 1):
         for dx, dy in CELLS:
@@ -202,9 +214,6 @@
         tiles = [x_weight(xl, xr, w, p) for w in range(3)]
         put_rows(cu, cd, n, [t[0] for t in tiles], [t[1] for t in tiles])
         n += 1
-    for p in CWP:
-        put_coarse_rows(cu, cd, n, [x_coarse(xl, xr, a, p) for a in range(4)])
-        n += 1
 
 
 def planes(radius, body, own, halo):
@@ -250,90 +259,162 @@
     )
 
 
-def fine_level(vt, wm, cw, xl, xr, yl, yr, V, W, NW, Y1, Y2, Y3, f, over):
-    V[H : H + LX, H : H + LY] = vt[...]
-    for d in range(H):
-        V[d, H : H + LY] = xl[d * LY : (d + 1) * LY]
-        V[H + LX + d, H : H + LY] = xr[d * LY : (d + 1) * LY]
+NH = [-2, -1, 0, 8, 9]
+Y1E = [-2, -1, 0, 7, 8, 9]
+Y2E = [-1, 0, 1, 6, 7, 8]
+Y3E = [0, 1, 2, 5, 6, 7]
+
+
+def pick(near, edge, planes_):
+    first = next(p for p in range(LX) if p not in planes_)
+
+    def cell(p, y):
+        if p in planes_:
+            return edge[planes_.index(p), y + H]
+        return near[p - first, y + H]
+
+    return cell
+
+
+def v_cell(vt, xl, xr, yl, yr):
+    def cell(p, y):
+        if not isinstance(p, int) or 0 <= p < LX:
+            if y < 0:
+                return yl[p * H - y - 1]
+            if y >= LY:
+                return yr[p * H + y - LY]
+            return vt[p, y]
+        return x_cell(xl, xr, p, y)
+
+    return cell
+
+
+def w_row(NW, NE, a, p, y):
+    if p in NH:
+        return row(NE, a, NH.index(p), y)
+    return row(NW, a, p - 1, y + JW)
+
+
+def normalise(dst, i, wx, lx, wy, ly, wz):
+    lz = down_z(wz)
+    deg = wx + lx + wy + ly + wz + lz
+    inv = 1.0 / deg
+    for a, w in enumerate((wx, lx, wy, ly, wz, lz)):
+        dst[a, i] = w * inv
+    dst[6, i] = deg
+
+
+def fine_inner(vt, wm, cw, yl, yr, W, NW, Y1, Y2, Y3):
+    for w in range(3):
+        W[w, :, JW : JW + LY] = wm[w]
     for x in range(LX):
-        for d in range(1, H + 1):
-            V[x + H, H - d] = yl[x * H + d - 1]
-            V[x + H, H + LY - 1 + d] = yr[x * H + d - 1]
-    for w in range(3):
-        W[w, H : H + LX, JW : JW + LY] = wm[w]
-        for p in list(range(-H if w == 0 else -2, 0)) + [LX, LX + 1]:
-            lo, hi = x_weight(xl, xr, w, p)
-            W[w, p + H, JW : JW + 8] = lo
-            W[w, p + H, JW + 8 : JW + 16] = hi
-    for x in range(LX):
-        n, i = H * LX + x, x + H
-        W[0, i, JW - 2 : JW] = yl[n, 0:2]
-        W[1, i, JW - 3 : JW] = yl[n, 2:5]
-        W[2, i, JW - 2 : JW] = yl[n, 6:8]
-        W[0, i, JW + LY : JW + LY + 2] = yr[n, 0:2]
-        W[1, i, JW + LY : JW + LY + 2] = yr[n, 2:4]
-        W[2, i, JW + LY : JW + LY + 2] = yr[n, 4:6]
-
-    def norm(i, _):
-        wx, lx = W[0, i], W[0, i - 1]
-        wy = W[1, i]
+        n = H * LX + x
+        W[0, x, JW - 2 : JW] = yl[n, 0:2]
+        W[1, x, JW - 3 : JW] = yl[n, 2:5]
+        W[2, x, JW - 2 : JW] = yl[n, 6:8]
+        W[0, x, JW + LY : JW + LY + 2] = yr[n, 0:2]
+        W[1, x, JW + LY : JW + LY + 2] = yr[n, 2:4]
+        W[2, x, JW + LY : JW + LY + 2] = yr[n, 4:6]
+
+    def norm(x, _):
+        wy = W[1, x]
+        normalise(NW, x - 1, W[0, x], W[0, x - 1], wy, pltpu.roll(wy, 1, 0), W[2, x])
+        return 0
+
+    lax.fori_loop(1, LX, norm, 0)
+    v = v_cell(vt, None, None, yl, yr)
+
+    def power(at, dst, first, count, low, high):
+        def body(n, _):
+            p = first + n
+            for y in range(low, high + 1):
+                dst[n, y + H] = stencil(
+                    lambda a: row(NW, a, p - 1, y + JW), lambda dx, dy: at(p + dx, y + dy)
+                )
+            return 0
+
+        lax.fori_loop(0, count, body, 0)
+
+    power(v, Y1, 1, 6, -2, 17)
+    power(lambda p, y: Y1[p - 1, y + H], Y2, 2, 4, -1, 16)
+    power(lambda p, y: Y2[p - 2, y + H], Y3, 3, 2, 0, 15)
+
+
+def fine_outer(vt, wm, cw, xl, xr, yl, yr, W, NW, Y1, Y2, Y3, NE, Y1X, Y2X, Y3X, f, over):
+    def own(w, p):
+        if 0 <= p < LX:
+            return wm[w, p]
+        return jnp.concatenate(x_weight(xl, xr, w, p), 0)
+
+    top = lax.broadcasted_iota(jnp.int32, (LY, NZ), 0) == 0
+    for n, p in enumerate(NH):
+        wy = own(1, p)
         ly = pltpu.roll(wy, 1, 0)
-        wz = W[2, i]
-        lz = down_z(wz)
-        deg = wx + lx + wy + ly + wz + lz
-        inv = 1.0 / deg
-        for a, w in enumerate((wx, lx, wy, ly, wz, lz)):
-            NW[a, i] = w * inv
-        NW[6, i] = deg
-        return 0
-
-    lax.fori_loop(1, LX + 5, norm, 0)
-
-    def apply(src, dst, *parts):
-        for first, step, count, low, high in parts:
-
-            def body(n, _):
-                i = H + first + step * n
-                for y in range(low, high + 1):
-                    r, j = y + JW, y + H
-                    dst[i, j] = stencil(
-                        lambda a: row(NW, a, i, r), lambda dx, dy: src[i + dx, j + dy]
-                    )
-                return 0
-
-            lax.fori_loop(0, count, body, 0)
-
-    apply(V, Y1, (1, 1, 6, -2, 17), (0, 7, 2, 0, 15), (-2, 1, 2, 1, 14), (8, 1, 2, 1, 14))
-    apply(Y1, Y2, (2, 1, 4, -1, 16), (1, 5, 2, 0, 15), (0, 7, 2, 1, 14), (-1, 9, 2, 2, 13))
-    apply(Y2, Y3, (2, 1, 4, 0, 15), (1, 5, 2, 1, 14), (0, 7, 2, 2, 13))
+        if p == 0:
+            ly = jnp.where(top, jnp.broadcast_to(W[1, 0, JW - 1 : JW], (LY, NZ)), ly)
+        normalise(NE, n, own(0, p), own(0, p - 1), wy, ly, own(2, p))
+
+    def power(at, dst, planes_, rows_):
+        for n, p in enumerate(planes_):
+            low, high = rows_[n if n < 3 else 5 - n]
+            for y in range(low, high + 1):
+                dst[n, y + H] = stencil(
+                    lambda a: w_row(NW, NE, a, p, y), lambda dx, dy: at(p + dx, y + dy)
+                )
+
+    v = v_cell(vt, xl, xr, yl, yr)
+    y1, y2, y3 = pick(Y1, Y1X, Y1E), pick(Y2, Y2X, Y2E), pick(Y3, Y3X, Y3E)
+    power(v, Y1X, Y1E, ((1, 14), (1, 14), (0, 15)))
+    power(y1, Y2X, Y2E, ((2, 13), (1, 14), (0, 15)))
+    power(y2, Y3X, Y3E, ((2, 13), (1, 14), (0, 15)))
 
     first_row = lax.broadcasted_iota(jnp.int32, (CY, CZ), 0) == 0
     for x in range(CX):
         cx, cy, cz = cw[0, x], cw[1, x], cw[2, x]
-        lcx = cw[0, x - 1] if x else x_coarse(xl, xr, 0, -1)
+        if x:
+            lcx = cw[0, x - 1]
+        else:
+            both = pair_rows()
+            flat = jnp.concatenate(
+                [compress(t) for t in x_weight(xl, xr, 0, -1)], 0
+            )
+            lcx = jnp.dot(
+                both, flat, precision=lax.Precision.HIGHEST, preferred_element_type=jnp.float32
+            )
         edge = coarse_rows(yl, H * LX + LX + x, 1)[3:4]
         lcy = jnp.where(first_row, jnp.broadcast_to(edge, (CY, CZ)), pltpu.roll(cy, 1, 0))
         over[x] = 1.0 / (
             DIAG * (cx + lcx + cy + lcy + cz + down_z(cz)) + SHIFT * cw[3, x]
         )
 
-    def block(x, _):
+    for x in range(CX):
         for y in range(CY):
+            if x in (0, CX - 1) and y in (0, CY - 1):
+                continue
             ra, rb = 0.0, 0.0
             for dx in range(2):
                 for dy in range(2):
-                    i = H + 2 * x + dx
-                    j = H + 2 * y + dy
-                    ga, gb = rest(V[i, j], Y1[i, j], Y2[i, j], Y3[i, j])
-                    deg = row(NW, 6, i, j - H + JW)
+                    p, q = 2 * x + dx, 2 * y + dy
+                    ga, gb = rest(v(p, q), y1(p, q), y2(p, q), y3(p, q))
+                    deg = w_row(NW, NE, 6, p, q)
                     ra = ra + deg * ga
                     rb = rb + deg * gb
             inv = row(over, x, y)
-            f[x, y, 0] = compress(ra) * inv
-            f[x, y, 1] = compress(rb) * inv
-        return 0
-
-    lax.fori_loop(0, CX, block, 0)
+            at = 2 * (x * CY + y)
+            f[at] = compress(ra) * inv
+            f[at + 1] = compress(rb) * inv
+    for a in range(4):
+        for x in range(CX):
+            f[NF + 4 * a + x] = cw[a, x]
+
+
+NF = 2 * CX * CY
+
+
+def pair_rows():
+    ri = lax.broadcasted_iota(jnp.int32, (CY, LY), 0)
+    ci = lax.broadcasted_iota(jnp.int32, (CY, LY), 1)
+    return jnp.where((ci >> 1) == ri, 1.0, 0.0)
 
 
 def rest(v, y1, y2, y3):
@@ -346,8 +427,16 @@
     return v - (b - (B0 * y1 + B1 * y2 + B2 * y3)), b
 
 
-def fine_corners(V, W, NW, Y1, Y2, Y3, f_, over, cl, cr, f, fix):
+def fine_corners(
+    vt, xl, xr, yl, yr, W, NW, Y1, Y2, Y3, NE, Y1X, Y2X, Y3X, f_, over, cl, cr, f, fu, fd, fix
+):
     f[...] = f_[...]
+    old = (
+        v_cell(vt, xl, xr, yl, yr),
+        pick(Y1, Y1X, Y1E),
+        pick(Y2, Y2X, Y2E),
+        pick(Y3, Y3X, Y3E),
+    )
     for side in range(2):
         for top in range(2):
             msg = cr if top else cl
@@ -372,7 +461,10 @@
                     else:
                         r = (2, 5, 8)[w] + y
                     return msg[n, r : r + 1]
-                return W[w, x + H, y + JW : y + JW + 1]
+                if out_x:
+                    tile = x_weight(xl, xr, w, x)[y >> 3]
+                    return tile[y & 7 : (y & 7) + 1]
+                return W[w, x, y + JW : y + JW + 1]
 
             weights = {}
 
@@ -386,9 +478,9 @@
                     weights[x, y] = [jnp.broadcast_to(w * inv, (8, NZ)) for w in ws]
                 return weights[x, y]
 
-            def look(known, ref):
+            def look(known, cell):
                 def at(x, y):
-                    return known[x, y] if (x, y) in known else ref[x + H, y + H]
+                    return known[x, y] if (x, y) in known else cell(x, y)
 
                 return at
 
@@ -399,7 +491,7 @@
                     if fresh(dx, dy):
                         ws = weight(x, y)
                     else:
-                        ws = [row(NW, a, x + H, y + JW) for a in range(6)]
+                        ws = [w_row(NW, NE, a, x, y) for a in range(6)]
                     out[x, y] = stencil(
                         lambda a: ws[a], lambda ex, ey: at(x + ex, y + ey)
                     )
@@ -408,16 +500,16 @@
             def fresh(dx, dy):
                 return (dx > 0 and dy >= 0) or (dy > 0 and dx >= 0)
 
-            v = look(got, V)
-            y1 = look(run(v, [(1, 0), (2, 0), (1, 1), (0, 1), (0, 2)], fresh), Y1)
-            y2 = look(run(y1, [(0, 0), (1, 0), (1, -1), (0, 1), (-1, 1)], fresh), Y2)
-            y3 = look(run(y2, [(0, 0), (-1, 0), (0, -1)], fresh), Y3)
+            v = look(got, old[0])
+            y1 = look(run(v, [(1, 0), (2, 0), (1, 1), (0, 1), (0, 2)], fresh), old[1])
+            y2 = look(run(y1, [(0, 0), (1, 0), (1, -1), (0, 1), (-1, 1)], fresh), old[2])
+            y3 = look(run(y2, [(0, 0), (-1, 0), (0, -1)], fresh), old[3])
             ra, rb = 0.0, 0.0
             for n, (dx, dy) in enumerate(((0, 0), (-1, 0), (0, -1), (-1, -1))):
                 x, y = px(dx), py(dy)
                 four = (v(x, y), y1(x, y), y2(x, y), y3(x, y))
                 ga, gb = rest(*four)
-                deg = row(NW, 6, x + H, y + JW)
+                deg = w_row(NW, NE, 6, x, y)
                 ra = ra + deg * ga
                 rb = rb + deg * gb
                 p, b = smooth(*four)
@@ -425,45 +517,106 @@
                 fix[2 * side + top, n, 8:16] = b
             x, y = (CX - 1) * side, (CY - 1) * top
             inv = row(over, x, y)
-            f[x, y, 0] = compress(ra) * inv
-            f[x, y, 1] = compress(rb) * inv
-
-
-def meanwhile(vt, NW, Y1, Y2, Y3, fix, cw, xl, xr, yl, yr, cl, cr, pb, nd, CW, R):
-    def step(x, sums):
-        num, den = sums
-        for y in range(LY):
-            v, y1 = vt[x, y], Y1[x + H, y + H]
-            p, b = smooth(v, y1, Y2[x + H, y + H], Y3[x + H, y + H])
-            pb[x, y, 0:8] = p
-            pb[x, y, 8:16] = b
-            dv = row(NW, 6, x + H, y + JW) * v
-            num = num + dv * (v - y1)
-            den = den + dv * v
-        return num, den
-
-    zero = jnp.zeros((8, NZ), jnp.float32)
-    num, den = lax.fori_loop(0, LX, step, (zero, zero))
-    nd[0] = num
-    nd[1] = den
+            at = 2 * (x * CY + y)
+            f[at] = compress(ra) * inv
+            f[at + 1] = compress(rb) * inv
+    for x in range(CX):
+        at = 2 * x * CY
+        fd[8 * x : 8 * x + 8] = f[at : at + 8]
+        fu[8 * x : 8 * x + 8] = f[at + 8 : at + 16]
+
+
+def meanwhile(vt, NW, NE, Y1, Y2, Y3, Y1X, Y2X, Y3X, fix, pb, nd):
+    y1, y2, y3 = pick(Y1, Y1X, Y1E), pick(Y2, Y2X, Y2E), pick(Y3, Y3X, Y3E)
+    num = den = jnp.zeros((8, NZ), jnp.float32)
+    corner = {}
     for side in range(2):
         for top in range(2):
             for n, (dx, dy) in enumerate(((0, 0), (-1, 0), (0, -1), (-1, -1))):
                 x = LX - 1 + dx if side else -dx
                 y = LY - 1 + dy if top else -dy
-                pb[x, y] = fix[2 * side + top, n]
+                corner[x, y] = 2 * side + top, n
+    for x in range(LX):
+        for y in range(LY):
+            v, nv = vt[x, y], y1(x, y)
+            if (x, y) in corner:
+                pb[x, y] = fix[corner[x, y]]
+            else:
+                p, b = smooth(v, nv, y2(x, y), y3(x, y))
+                pb[x, y, 0:8] = p
+                pb[x, y, 8:16] = b
+            dv = w_row(NW, NE, 6, x, y) * v
+            num = num + dv * (v - nv)
+            den = den + dv * v
+    nd[0] = num
+    nd[1] = den
+
+
+JC = 8
+CCELLS = [(dx, dy) for dx in (1, 2, 3) for dy in range(1, CH + 1 - dx)]
+
+
+NCC = 4 * len(CCELLS) + 2 * len(CWP)
+
+
+def coarse_corner_send(left, right, after, yl, yr, cu, cd):
+    n = 0
+    for side in range(2):
+        for dx, dy in CCELLS:
+            x = dx - 1 if side else CX - dx
+            src = right if side else left
+            for half in range(2):
+                cu[n] = src[2 * (x * CY + CY - dy) + half]
+                cd[n] = src[2 * (x * CY + dy - 1) + half]
+                n += 1
+    for p in CWP:
+        src, x = (left, p + CX) if p < 0 else (right, p - CX)
+        for a in range(4):
+            w = src[NF + 4 * a + x]
+            m, r = n + (a >> 1), 4 * (a & 1)
+            cu[m, r : r + 4] = w[4:8]
+            cd[m, r : r + 4] = w[0:4]
+        n += 2
+
+
+def coarse_level(
+    own, left, right, yl, yr, cl, cr, gl, gr, pb, NW, NE, nd, po, bo, mine, other, F, EA, EB, EX, CW, R
+):
+    def put(i, j, half, f):
+        f = OMEGA * f
+        F[i, j, half] = f
+        EA[i, j, half] = f
+
+    for x in range(CX):
+        for half in range(2):
+            for y in range(CY):
+                at = 2 * (x * CY + y) + half
+                put(x, y + CH, half, left[at])
+                put(x + CH, y + CH, half, own[at])
+                put(x + CH + CX, y + CH, half, right[at])
+            for y in range(CH):
+                put(x + CH, y, half, yl[2 * (x * CH + y) + half])
+                put(x + CH, y + CH + CY, half, yr[2 * (x * CH + y) + half])
+    n = 0
+    for side in range(2):
+        for dx, dy in CCELLS:
+            i = CH + CX - 1 + dx if side else CH - dx
+            for half in range(2):
+                put(i, CH - dy, half, cl[n])
+                put(i, CH + CY - 1 + dy, half, cr[n])
+                n += 1
 
     for a in range(4):
         for i in range(CX + 2 * CH):
             p = i - CH
-            mid = cw[a, p] if 0 <= p < CX else x_coarse(xl, xr, a, p)
-            R[a, i, JC : JC + CY] = mid
+            src, x = (left, p + CX) if p < 0 else (own, p) if p < CX else (right, p - CX)
+            R[a, i, JC : JC + CY] = src[NF + 4 * a + x]
             if 0 <= p < CX:
-                lo = coarse_rows(yl, H * LX + LX + p, a)
-                hi = coarse_rows(yr, H * LX + LX + p, a)
+                lo = coarse_rows(gl, H * LX + LX + p, a)
+                hi = coarse_rows(gr, H * LX + LX + p, a)
             elif p in CWP:
-                n = 2 * len(CELLS) + len(WP) + CWP.index(p)
-                lo, hi = coarse_rows(cl, n, a), coarse_rows(cr, n, a)
+                m, r = n + 2 * CWP.index(p) + (a >> 1), 4 * (a & 1)
+                lo, hi = cl[m, r : r + 4], cr[m, r : r + 4]
             else:
                 continue
             R[a, i, JC - 4 : JC] = lo
@@ -475,47 +628,6 @@
         inv = OMEGA / (DIAG * total + SHIFT * R[3, i])
         for a in range(6):
             CW[a, i] = ws[a] * inv
-
-
-JC = 8
-CCELLS = [(dx, dy) for dx in (1, 2, 3) for dy in range(1, CH + 1 - dx)]
-
-
-def coarse_corner_send(left, right, cu, cd):
-    n = 0
-    for side in range(2):
-        for dx, dy in CCELLS:
-            x = dx - 1 if side else CX - dx
-            src = right if side else left
-            for half in range(2):
-                cu[n] = src[x, CY - dy, half]
-                cd[n] = src[x, dy - 1, half]
-                n += 1
-
-
-def coarse_level(own, left, right, yl, yr, cl, cr, CW, pb, NW, nd, po, bo, sums, F, EA, EB, EX):
-    def put(i, j, half, f):
-        f = OMEGA * f
-        F[i, j, half] = f
-        EA[i, j, half] = f
-
-    for x in range(CX):
-        for half in range(2):
-            for y in range(CY):
-                put(x, y + CH, half, left[x, y, half])
-                put(x + CH, y + CH, half, own[x, y, half])
-                put(x + CH + CX, y + CH, half, right[x, y, half])
-            for y in range(CH):
-                put(x + CH, y, half, yl[x, y, half])
-                put(x + CH, y + CH + CY, half, yr[x, y, half])
-    n = 0
-    for side in range(2):
-        for dx, dy in CCELLS:
-            i = CH + CX - 1 + dx if side else CH - dx
-            for half in range(2):
-                put(i, CH - dy, half, cl[n])
-                put(i, CH + CY - 1 + dy, half, cr[n])
-                n += 1
 
     def sweep(src, dst):
         def body(i, reach):
@@ -548,7 +660,7 @@
 
     planes(1, spread, CX, CH)
 
-    def block(x, _):
+    for x in range(CX):
         for y in range(CY):
             for half in range(2):
                 e = EX[x + CH, y + CH, half]
@@ -560,7 +672,7 @@
                     for dy in range(2):
                         ey = C * EX[x + CH, y + CH + 2 * dy - 1, half]
                         xx, yy = 2 * x + dx, 2 * y + dy
-                        nw = [row(NW, a, xx + H, yy + JW) for a in range(6)]
+                        nw = [w_row(NW, NE, a, xx, yy) for a in range(6)]
                         s = (
                             ke
                             + (nw[dx] + nw[2 + dy]) * ce
@@ -572,16 +684,11 @@
                             po[xx, yy] = pb[xx, yy, 0:8] - s
                         else:
                             bo[xx, yy] = pb[xx, yy, 8:16] + s
-        return 0
-
-    lax.fori_loop(0, CX, block, 0)
-
-    def gram(n, acc):
-        x = n >> 2
+
+    def gram(x, edge, acc):
         acc = list(acc)
-        for q in range(4):
-            yy = (n & 3) * 4 + q
-            deg = row(NW, 6, x + H, yy + JW)
+        for yy in range(LY):
+            deg = row(NE, 6, NH.index(0), yy) if edge else row(NW, 6, x - 1, yy + JW)
             for h in range(0, NZ, 128):
                 z = slice(h, h + 128)
                 p = po[x, yy, :, z]
@@ -598,7 +705,8 @@
         return tuple(acc)
 
     zero = jnp.zeros((8, 128), jnp.float32)
-    acc = list(lax.fori_loop(0, 4 * LX, gram, (zero,) * 18))
+    acc = gram(0, True, (zero,) * 18)
+    acc = list(lax.fori_loop(1, LX, lambda x, acc: gram(x, False, acc), acc))
     for q in range(2):
         acc.append(nd[q, :, :128] + nd[q, :, 128:])
     ones = jnp.ones((8, 128), jnp.float32)
@@ -614,17 +722,22 @@
 
     t0 = over_lanes(jnp.concatenate(acc[:16], 0))
     t1 = over_lanes(jnp.concatenate(acc[16:] + [zero] * 12, 0))
-    both = jnp.concatenate([t0[0:1], t1[0:1]], 0)
-    sums[...] = jnp.broadcast_to(both[None], sums.shape)
+    even = lax.axis_index("gy") % 2 == 0
+    mine[...] = jnp.where(even, t0[0:1], t1[0:1])
+    other[...] = jnp.where(even, t1[0:1], t0[0:1])
+
+
+def spread_sums(a, b, out):
+    out[...] = jnp.broadcast_to((a[...] + b[...])[None], out.shape)
 
 
 def finish(parts, po, bo, out, eig, SP):
     t = parts[...]
     n = t.shape[0]
-    while n > 1:
+    while n > 2:
         n //= 2
         t = t[:n] + t[n:]
-    t = t[0]
+    t = t[:, 0]
     eye = lax.broadcasted_iota(jnp.int32, (128, 128), 0) == lax.broadcasted_iota(
         jnp.int32, (128, 128), 1
     )
@@ -702,74 +815,91 @@
 
 
 def per_device(vectors, weight_x, weight_y, weight_z):
-    vt, wm, cw, xu, xd, yu, yd = call(
-        prepare,
+    args = (vectors, weight_x, weight_y, weight_z)
+    xu, xd = call(
+        x_send,
+        [(NXU, LY, NZ), (NXD, LY, NZ)],
+        args,
+        [pltpu.SemaphoreType.DMA((2 * K + 6,))],
+        limit=56,
+        where=ANY,
+    )
+    rl, rr = both_ways(xu, xd, "gx")
+    vt, wm, cw, yu, yd = call(
+        local,
         [
             (LX, LY, K, NZ),
             (3, LX, LY, NZ),
             (4, CX, CY, CZ),
-            (NXU, 8, NZ),
-            (NXD, 8, NZ),
             (NYB, 8, NZ),
             (NYB, 8, NZ),
         ],
-        (vectors, weight_x, weight_y, weight_z),
+        args,
+        [(5, CX * LY, CZ)],
+    )
+    yl, yr = both_ways(yu, yd, "gy")
+    tall = LY + 2 * H
+    W, NW, Y1, Y2, Y3 = call(
+        fine_inner,
         [
-            (K, LX, LY, NZ),
-            (LX, LY, NZ),
-            (LX, LY, NZ),
-            (LX, LY, NZ),
-            (5, CX * LY, CZ),
-            pltpu.SemaphoreType.DMA((4,)),
+            (3, LX, 32, NZ),
+            (7, LX - 1, 32, NZ),
+            (6, tall, K, NZ),
+            (4, tall, K, NZ),
+            (2, tall, K, NZ),
         ],
-        where=HBM,
-        limit=56,
-    )
-    xl, xr = both_ways(xu, xd, "gx")
-    yl, yr = both_ways(yu, yd, "gy")
-    cu, cd = call(corner_send, [(NCB, 8, NZ)] * 2, (xl, xr))
+        (vt, wm, cw, yl, yr),
+        us=3,
+    )
+    xl, xr, cu, cd = call(
+        x_receive, [(NXB, 8, NZ), (NXB, 8, NZ), (NCB, 8, NZ), (NCB, 8, NZ)], (rl, rr, Y3)
+    )
     cl, cr = both_ways(cu, cd, "gy")
-    ext = (LX + 2 * H, LY + 2 * H, K, NZ)
-    V, W, NW, Y1, Y2, Y3, f, over = call(
-        fine_level,
+    NE, Y1X, Y2X, Y3X, f, over = call(
+        fine_outer,
         [
-            ext,
-            (3, LX + 2 * H, 32, NZ),
-            (7, LX + 2 * H, 32, NZ),
-            ext,
-            ext,
-            ext,
-            (CX, CY, 2, 8, CZ),
+            (7, len(NH), LY, NZ),
+            (6, tall, K, NZ),
+            (6, tall, K, NZ),
+            (6, tall, K, NZ),
+            (NF + 4 * CX, 8, CZ),
             (CX, CY, CZ),
         ],
-        (vt, wm, cw, xl, xr, yl, yr),
-        us=6,
-    )
-    f, fix = call(
+        (vt, wm, cw, xl, xr, yl, yr, W, NW, Y1, Y2, Y3),
+        us=4,
+    )
+    f, fu, fd, fix = call(
         fine_corners,
-        [(CX, CY, 2, 8, CZ), (4, 4, 16, NZ)],
-        (V, W, NW, Y1, Y2, Y3, f, over, cl, cr),
+        [(NF + 4 * CX, 8, CZ), (NF // 2, 8, CZ), (NF // 2, 8, CZ), (4, 4, 16, NZ)],
+        (vt, xl, xr, yl, yr, W, NW, Y1, Y2, Y3, NE, Y1X, Y2X, Y3X, f, over, cl, cr),
     )
     left, right = both_ways(f, f, "gx")
-    fl, fr = both_ways(f[:, CY - CH :], f[:, :CH], "gy")
-    pb, nd, CW = call(
+    fl, fr = both_ways(fu, fd, "gy")
+    pb, nd = call(
         meanwhile,
-        [(LX, LY, 16, NZ), (2, 8, NZ), (6, CX + 2 * CH, 24, CZ)],
-        (vt, NW, Y1, Y2, Y3, fix, cw, xl, xr, yl, yr, cl, cr),
-        [(4, CX + 2 * CH, 24, CZ)],
-        us=2,
-    )
-    cu, cd = call(coarse_corner_send, [(4 * len(CCELLS), 8, CZ)] * 2, (left, right))
+        [(LX, LY, 16, NZ), (2, 8, NZ)],
+        (vt, NW, NE, Y1, Y2, Y3, Y1X, Y2X, Y3X, fix),
+    )
+    cu, cd = call(coarse_corner_send, [(NCC, 8, CZ)] * 2, (left, right, nd, fl, fr))
     cl, cr = both_ways(cu, cd, "gy")
-    n = lax.axis_size("gx") * lax.axis_size("gy")
     cext = (CX + 2 * CH, CY + 2 * CH, 2, 8, CZ)
-    po, bo, sums = call(
+    po, bo, mine, other = call(
         coarse_level,
-        [(LX, LY, K, NZ), (LX, LY, K, NZ), (n, 2, 128)],
-        (f, left, right, fl, fr, cl, cr, CW, pb, NW, nd),
-        [cext, cext, cext, (CX + 2 * CH, CY + 2 * CH, 2, 8, NZ)],
+        [(LX, LY, K, NZ), (LX, LY, K, NZ), (1, 128), (1, 128)],
+        (f, left, right, fl, fr, cl, cr, yl, yr, pb, NW, NE, nd),
+        [
+            cext,
+            cext,
+            cext,
+            (CX + 2 * CH, CY + 2 * CH, 2, 8, NZ),
+            (6, CX + 2 * CH, 24, CZ),
+            (4, CX + 2 * CH, 24, CZ),
+        ],
         limit=12,
     )
+    n = lax.axis_size("gy")
+    theirs = lax.ppermute(other, "gy", [(i, i ^ 1) for i in range(n)])
+    (sums,) = call(spread_sums, [(n * lax.axis_size("gx"), 1, 128)], (mine, theirs))
     parts = lax.all_to_all(sums, ("gx", "gy"), 0, 0)
     refined, eig = call(
         finish,

time: 91.2 us -> 113 us (1.24)
  Pallas kernels: 20.1 us -> 49.4 us
  blocking collectives: 24 us -> 20.9 us
  local copies, waits for them, and re-layouts: 3.08 us -> 0.02 us
  starting transfers between devices: 26.2 us -> 24.1 us
    pallas_call x8 -> x11, Pallas kernels: 20.1 us -> 49.4 us  [call(): pl.pallas_call(body, out_shape=[jax.ShapeDtypeStruct(s, jnp.float32) for...]
    all_to_all x1, blocking collectives: 24 us -> 20.9 us  [per_device(): parts = lax.all_to_all(sums, ('gx', 'gy'), 0, 0)]
    unnamed x8, local copies, waits for them, and re-layouts: 3.06 us -> 0.02 us
    ppermute x12, starting transfers between devices: 26.2 us -> 24.1 us  [both_ways(): return (lax.ppermute(up, axis, fwd), lax.ppermute(down, axis, back))]
    ppermute x0 -> x1, waiting for transfers between devices: none -> 1.14 us  [per_device(): theirs = lax.ppermute(other, 'gy', [(i, i ^ 1) for i in range(n)])]
  transfers between devices with their start and end apart: 12 -> 13, of which waited for: 6 -> 8; matrix products, arithmetic and copies ran while one was open for 0% -> 0% of each run, Pallas kernels for 8% -> 8%
where the time goes in v4:
time: 113 us
  Pallas kernels  49.4 us (44%)
  starting transfers between devices  24.1 us (21%)
  blocking collectives  20.9 us (18%)
  waiting for transfers between devices  17.4 us (15%)
    pallas_call x11, Pallas kernels, call(): pl.pallas_call(body, out_shape=[jax.ShapeDtypeStruct(s, jnp.float32) for...  49.4 us
    ppermute x12, starting transfers between devices, both_ways(): return (lax.ppermute(up, axis, fwd), lax.ppermute(down, axis, back))  24.1 us
    all_to_all x1, blocking collectives, per_device(): parts = lax.all_to_all(sums, ('gx', 'gy'), 0, 0)  20.9 us
    ppermute x12, waiting for transfers between devices, both_ways(): return (lax.ppermute(up, axis, fwd), lax.ppermute(down, axis, back))  16.2 us
  transfers between devices with their start and end apart: 13, of which 8 were waited for; matrix products, arithmetic and copies ran while one was open for 0% of the time, Pallas kernels for 8%

profile of v4, /device:TPU:1, one launch (start us, length us, event | category | flops | bytes accessed | tf_op | source)
XLA Modules:
  0.0 112.6 jit_solution(6889652456794828750)
XLA Ops:
  0.6 0.0 copy-start.3
  0.6 0.0 copy-start.2
  0.7 0.0 copy-start.1
  0.7 0.0 copy-start
  0.7 31.6 %shard_map.60 = (f32[31,16,256]{2,1,0:T(8,128)}, f32[30,16,256]{2,1,0:T(8,128)}) custom-call(f32[8,8,16,256]{3,2,1,0:T(8,128)} %v.3, f32[8,16,256]{2,1,0:T(8,128)} %wx.3, f32[8,16,256]{2,1,0:T(8,128)} %wy.3, f32[8,16,256]{2,1,0:T(8,128)} %wz.3), custom_call_target="tpu_custom_call" | custom-call | bytes 3000000 | tf_op jit(solution)/shard_map/pallas_call | solution.py:32
  32.3 2.1 %collective-permute-start = (f32[31,16,256]{2,1,0:T(8,128)}, f32[31,16,256]{2,1,0:T(8,128)S(1)}, u32[]{:S(2)}, u32[]{:S(2)}) collective-permute-start(f32[31,16,256]{2,1,0:T(8,128)} %get-tuple-element.39), channel_id=1, source_target_pairs={{0,16},{16,32},{32,48},{48,64},{64,80},{80,96},{96,112},{112,128},... | collective-permute-start | bytes 1523720 | tf_op jit(solution)/shard_map/ppermute | solution.py:814
  34.4 3.8 %collective-permute-start.1 = (f32[30,16,256]{2,1,0:T(8,128)}, f32[30,16,256]{2,1,0:T(8,128)S(1)}, u32[]{:S(2)}, u32[]{:S(2)}) collective-permute-start(f32[30,16,256]{2,1,0:T(8,128)} %get-tuple-element.40), channel_id=1, source_target_pairs={{16,0},{32,16},{48,32},{64,48},{80,64},{96,80},{112,96},{128,112},... | collective-permute-start | bytes 1474568 | tf_op jit(solution)/shard_map/ppermute | solution.py:814
  38.2 0.0 copy-done.3
  38.2 0.0 copy-done.2
  38.2 0.0 copy-done.1
  38.2 0.0 copy-done
  38.2 0.7 shard_map.59
  38.9 2.5 %collective-permute-start.2 = (f32[36,8,256]{2,1,0:T(8,128)S(1)}, f32[36,8,256]{2,1,0:T(8,128)S(1)}, u32[]{:S(2)}, u32[]{:S(2)}) collective-permute-start(f32[36,8,256]{2,1,0:T(8,128)S(1)} %get-tuple-element.43), channel_id=1, source_target_pairs={{0,1},{1,2},{2,3},{3,4},{4,5},{5,6},{6,7},{7,8},{8,9},{9,10},{10,1... | collective-permute-start | bytes 884744 | tf_op jit(solution)/shard_map/ppermute | solution.py:814
  41.4 0.2 collective-permute-start.3
  41.7 3.4 %collective-permute-done.2.yl.gl = f32[36,8,256]{2,1,0:T(8,128)S(1)} collective-permute-done((f32[36,8,256]{2,1,0:T(8,128)S(1)}, f32[36,8,256]{2,1,0:T(8,128)S(1)}, u32[]{:S(2)}, u32[]{:S(2)}) %collective-permute-start.2) | collective-permute-done | bytes 294944 | tf_op jit(solution)/shard_map/ppermute | solution.py:814
  45.1 2.8 %collective-permute-done.3.yr.gr = f32[36,8,256]{2,1,0:T(8,128)S(1)} collective-permute-done((f32[36,8,256]{2,1,0:T(8,128)S(1)}, f32[36,8,256]{2,1,0:T(8,128)S(1)}, u32[]{:S(2)}, u32[]{:S(2)}) %collective-permute-start.3) | collective-permute-done | bytes 294944 | tf_op jit(solution)/shard_map/ppermute | solution.py:814
  47.9 2.6 %shard_map.61 = (f32[3,8,32,256]{3,2,1,0:T(8,128)S(1)}, f32[7,7,32,256]{3,2,1,0:T(8,128)S(1)}, f32[6,22,8,256]{3,2,1,0:T(8,128)S(1)}, f32[4,22,8,256]{3,2,1,0:T(8,128)S(1)}, f32[2,22,8,256]{3,2,1,0:T(8,128)S(1)}) custom-call(f32[8,16,8,256]{3,2,1,0:T(8,128)S(1)} %get-tuple-element.38.vt, f32[3,8,16,256]{3,2,1,0:T(8,128)S(1)} %get-tuple-element.41.wm, ...), custom_call_target="tpu_custom_call" | custom-call | bytes 9000000 | tf_op jit(solution)/shard_map/pallas_call | solution.py:32
  50.4 0.0 collective-permute-done.1.rr
  50.5 0.0 collective-permute-done.rl
  50.5 0.2 shard_map.62
  50.6 1.9 %collective-permute-start.4 = (f32[10,8,256]{2,1,0:T(8,128)S(1)}, f32[10,8,256]{2,1,0:T(8,128)S(1)}, u32[]{:S(2)}, u32[]{:S(2)}) collective-permute-start(f32[10,8,256]{2,1,0:T(8,128)S(1)} %get-tuple-element.58), channel_id=1, source_target_pairs={{0,1},{1,2},{2,3},{3,4},{4,5},{5,6},{6,7},{7,8},{8,9},{9,10},{10,1... | collective-permute-start | bytes 245768 | tf_op jit(solution)/shard_map/ppermute | solution.py:814
  52.5 0.0 collective-permute-start.5
  52.5 4.8 %shard_map.63 = (f32[7,5,16,256]{3,2,1,0:T(8,128)S(1)}, f32[6,22,8,256]{3,2,1,0:T(8,128)S(1)}, f32[6,22,8,256]{3,2,1,0:T(8,128)S(1)}, f32[6,22,8,256]{3,2,1,0:T(...) custom-call(f32[8,16,8,256]{3,2,1,0:T(8,128)S(1)} %get-tuple-element.38.vt, ...), custom_call_target="tpu_custom_call" | custom-call | bytes 12000000 | tf_op jit(solution)/shard_map/pallas_call | solution.py:32
  57.3 0.0 collective-permute-done.4.cl
  57.4 0.0 collective-permute-done.5.cr
  57.4 0.7 shard_map.64
  58.1 4.6 %collective-permute-start.7 = (f32[80,8,128]{2,1,0:T(8,128)S(1)}, f32[80,8,128]{2,1,0:T(8,128)S(1)}, u32[]{:S(2)}, u32[]{:S(2)}) collective-permute-start(f32[80,8,128]{2,1,0:T(8,128)S(1)} %get-tuple-element.60.own), channel_id=1, source_target_pairs={{16,0},{32,16},{48,32},{64,48},{80,64},{96,80},{112,96},{128,112},... | collective-permute-start | bytes 983048 | tf_op jit(solution)/shard_map/ppermute | solution.py:814
  62.7 0.0 collective-permute-start.6
  62.7 2.0 %collective-permute-start.8 = (f32[32,8,128]{2,1,0:T(8,128)S(1)}, f32[32,8,128]{2,1,0:T(8,128)S(1)}, u32[]{:S(2)}, u32[]{:S(2)}) collective-permute-start(f32[32,8,128]{2,1,0:T(8,128)S(1)} %get-tuple-element.61), channel_id=1, source_target_pairs={{0,1},{1,2},{2,3},{3,4},{4,5},{5,6},{6,7},{7,8},{8,9},{9,10},{10,1... | collective-permute-start | bytes 393224 | tf_op jit(solution)/shard_map/ppermute | solution.py:814
  64.7 1.1 %collective-permute-start.9 = (f32[32,8,128]{2,1,0:T(8,128)S(1)}, f32[32,8,128]{2,1,0:T(8,128)S(1)}, u32[]{:S(2)}, u32[]{:S(2)}) collective-permute-start(f32[32,8,128]{2,1,0:T(8,128)S(1)} %get-tuple-element.62), channel_id=1, source_target_pairs={{1,0},{2,1},{3,2},{4,3},{5,4},{6,5},{7,6},{8,7},{9,8},{10,9},{11,1... | collective-permute-start | bytes 393224 | tf_op jit(solution)/shard_map/ppermute | solution.py:814
  65.8 0.6 shard_map.65
  66.4 0.2 collective-permute-done.8.yl
  66.7 2.4 %collective-permute-done.9.yr = f32[32,8,128]{2,1,0:T(8,128)S(1)} collective-permute-done((f32[32,8,128]{2,1,0:T(8,128)S(1)}, f32[32,8,128]{2,1,0:T(8,128)S(1)}, u32[]{:S(2)}, u32[]{:S(2)}) %collective-permute-start.9) | collective-permute-done | bytes 131104 | tf_op jit(solution)/shard_map/ppermute | solution.py:814
  69.1 0.0 collective-permute-done.7.right
  69.1 2.8 %collective-permute-done.6.left = f32[80,8,128]{2,1,0:T(8,128)S(1)} collective-permute-done((f32[80,8,128]{2,1,0:T(8,128)S(1)}, f32[80,8,128]{2,1,0:T(8,128)S(1)}, u32[]{:S(2)}, u32[]{:S(2)}) %collective-permute-start.6) | collective-permute-done | bytes 327712 | tf_op jit(solution)/shard_map/ppermute | solution.py:814
  71.9 5.7 %collective-permute-start.10 = (f32[36,8,128]{2,1,0:T(8,128)S(1)}, f32[36,8,128]{2,1,0:T(8,128)S(1)}, u32[]{:S(2)}, u32[]{:S(2)}) collective-permute-start(f32[36,8,128]{2,1,0:T(8,128)S(1)} %get-tuple-element.65), channel_id=1, source_target_pairs={{0,1},{1,2},{2,3},{3,4},{4,5},{5,6},{6,7},{7,8},{8,9},{9,10},{10,1... | collective-permute-start | bytes 442376 | tf_op jit(solution)/shard_map/ppermute | solution.py:814
  77.7 0.0 collective-permute-start.11
  77.7 2.1 %collective-permute-done.10.cl = f32[36,8,128]{2,1,0:T(8,128)S(1)} collective-permute-done((f32[36,8,128]{2,1,0:T(8,128)S(1)}, f32[36,8,128]{2,1,0:T(8,128)S(1)}, u32[]{:S(2)}, u32[]{:S(2)}) %collective-permute-start.10) | collective-permute-done | bytes 147488 | tf_op jit(solution)/shard_map/ppermute | solution.py:814
  79.8 2.5 %collective-permute-done.11.cr = f32[36,8,128]{2,1,0:T(8,128)S(1)} collective-permute-done((f32[36,8,128]{2,1,0:T(8,128)S(1)}, f32[36,8,128]{2,1,0:T(8,128)S(1)}, u32[]{:S(2)}, u32[]{:S(2)}) %collective-permute-start.11) | collective-permute-done | bytes 147488 | tf_op jit(solution)/shard_map/ppermute | solution.py:814
  82.2 6.0 %shard_map.67 = (f32[8,16,8,256]{3,2,1,0:T(8,128)S(1)}, f32[8,16,8,256]{3,2,1,0:T(8,128)S(1)}, f32[1,128]{1,0:T(1,128)S(1)}, f32[1,128]{1,0:T(1,128)S(1)}) custom-call(f32[80,8,128]{2,1,0:T(8,128)S(1)} %get-tuple-element.60.own, f32[80,8,128]{2,1,0:T(8,128)S(1)} %collective-permute-done.6.left, f32[80,8,128]{2,1,0:T(8,128)S(1)} %collective-permute-done.7.right, ...), custom_call_target="tpu_custom_call" | custom-call | bytes 3000000 | tf_op jit(solution)/shard_map/pallas_call | solution.py:32
  88.2 0.1 collective-permute-start.12
  88.3 1.1 %collective-permute-done.12.b = f32[1,128]{1,0:T(1,128)S(1)} collective-permute-done((f32[1,128]{1,0:T(1,128)S(1)}, f32[1,128]{1,0:T(1,128)S(1)}, u32[]{:S(2)}, u32[]{:S(2)}) %collective-permute-start.12) | collective-permute-done | bytes 544 | tf_op jit(solution)/shard_map/ppermute | solution.py:901
  89.4 0.1 shard_map.68
  89.5 20.9 %all_to_all.5.parts = f32[256,1,128]{2,1,0:T(1,128)S(1)} all-to-all(f32[256,1,128]{2,1,0:T(1,128)S(1)} %shard_map.68), channel_id=1, replica_groups=mesh['gx'=16,'gy'=16] {'gx','gy'}, dimensions={0} | all-to-all | bytes 262144 | tf_op jit(solution)/shard_map/all_to_all | solution.py:903
  110.4 2.2 %shard_map.69 = (f32[8,8,16,256]{3,2,1,0:T(8,128)}, f32[1,8]{1,0:T(1,128)}) custom-call(f32[256,1,128]{2,1,0:T(1,128)S(1)} %all_to_all.5.parts, f32[8,16,8,256]{3,2,1,0:T(8,128)S(1)} %get-tuple-element.70.po, f32[8,16,8,256]{3,2,1,0:T(8,128)S(1)} %get-tuple-element.71.bo), custom_call_target="tpu_custom_call" | custom-call | bytes 3000000 | tf_op jit(solution)/shard_map/pallas_call | solution.py:32
  (1 shorter events, 0.0 us)
Async XLA Ops:
  0.6 37.6 %copy-start.3 = (f32[8,16,256]{2,1,0:T(8,128)S(1)}, f32[8,16,256]{2,1,0:T(8,128)}, u32[]{:S(2)}) copy-start(f32[8,16,256]{2,1,0:T(8,128)} %wz.3) | copy-start | bytes 393220
  0.6 37.5 %copy-start.2 = (f32[8,16,256]{2,1,0:T(8,128)S(1)}, f32[8,16,256]{2,1,0:T(8,128)}, u32[]{:S(2)}) copy-start(f32[8,16,256]{2,1,0:T(8,128)} %wy.3) | copy-start | bytes 393220
  0.7 37.5 %copy-start.1 = (f32[8,16,256]{2,1,0:T(8,128)S(1)}, f32[8,16,256]{2,1,0:T(8,128)}, u32[]{:S(2)}) copy-start(f32[8,16,256]{2,1,0:T(8,128)} %wx.3) | copy-start | bytes 393220
  0.7 37.5 %copy-start = (f32[8,8,16,256]{3,2,1,0:T(8,128)S(1)}, f32[8,8,16,256]{3,2,1,0:T(8,128)}, u32[]{:S(2)}) copy-start(f32[8,8,16,256]{3,2,1,0:T(8,128)} %v.3) | copy-start | bytes 3145732
  32.3 18.2 %collective-permute-start = (f32[31,16,256]{2,1,0:T(8,128)}, f32[31,16,256]{2,1,0:T(8,128)S(1)}, u32[]{:S(2)}, u32[]{:S(2)}) collective-permute-start(f32[31,16,256]{2,1,0:T(8,128)} %get-tuple-element.39), channel_id=1, source_target_pairs={{0,16},{16,32},{32,48},{48,64},{64,80},{80,96},{96,112},{112,128},... | collective-permute-start | bytes 1523720 | tf_op jit(solution)/shard_map/ppermute | solution.py:814
  34.4 16.1 %collective-permute-start.1 = (f32[30,16,256]{2,1,0:T(8,128)}, f32[30,16,256]{2,1,0:T(8,128)S(1)}, u32[]{:S(2)}, u32[]{:S(2)}) collective-permute-start(f32[30,16,256]{2,1,0:T(8,128)} %get-tuple-element.40), channel_id=1, source_target_pairs={{16,0},{32,16},{48,32},{64,48},{80,64},{96,80},{112,96},{128,112},... | collective-permute-start | bytes 1474568 | tf_op jit(solution)/shard_map/ppermute | solution.py:814
  38.9 6.2 %collective-permute-start.2 = (f32[36,8,256]{2,1,0:T(8,128)S(1)}, f32[36,8,256]{2,1,0:T(8,128)S(1)}, u32[]{:S(2)}, u32[]{:S(2)}) collective-permute-start(f32[36,8,256]{2,1,0:T(8,128)S(1)} %get-tuple-element.43), channel_id=1, source_target_pairs={{0,1},{1,2},{2,3},{3,4},{4,5},{5,6},{6,7},{7,8},{8,9},{9,10},{10,1... | collective-permute-start | bytes 884744 | tf_op jit(solution)/shard_map/ppermute | solution.py:814
  41.4 6.4 %collective-permute-start.3 = (f32[36,8,256]{2,1,0:T(8,128)S(1)}, f32[36,8,256]{2,1,0:T(8,128)S(1)}, u32[]{:S(2)}, u32[]{:S(2)}) collective-permute-start(f32[36,8,256]{2,1,0:T(8,128)S(1)} %get-tuple-element.44), channel_id=1, source_target_pairs={{1,0},{2,1},{3,2},{4,3},{5,4},{6,5},{7,6},{8,7},{9,8},{10,9},{11,1... | collective-permute-start | bytes 884744 | tf_op jit(solution)/shard_map/ppermute | solution.py:814
  50.6 6.7 %collective-permute-start.4 = (f32[10,8,256]{2,1,0:T(8,128)S(1)}, f32[10,8,256]{2,1,0:T(8,128)S(1)}, u32[]{:S(2)}, u32[]{:S(2)}) collective-permute-start(f32[10,8,256]{2,1,0:T(8,128)S(1)} %get-tuple-element.58), channel_id=1, source_target_pairs={{0,1},{1,2},{2,3},{3,4},{4,5},{5,6},{6,7},{7,8},{8,9},{9,10},{10,1... | collective-permute-start | bytes 245768 | tf_op jit(solution)/shard_map/ppermute | solution.py:814
  52.5 4.8 %collective-permute-start.5 = (f32[10,8,256]{2,1,0:T(8,128)S(1)}, f32[10,8,256]{2,1,0:T(8,128)S(1)}, u32[]{:S(2)}, u32[]{:S(2)}) collective-permute-start(f32[10,8,256]{2,1,0:T(8,128)S(1)} %get-tuple-element.59), channel_id=1, source_target_pairs={{1,0},{2,1},{3,2},{4,3},{5,4},{6,5},{7,6},{8,7},{9,8},{10,9},{11,1... | collective-permute-start | bytes 245768 | tf_op jit(solution)/shard_map/ppermute | solution.py:814
  58.1 11.0 %collective-permute-start.7 = (f32[80,8,128]{2,1,0:T(8,128)S(1)}, f32[80,8,128]{2,1,0:T(8,128)S(1)}, u32[]{:S(2)}, u32[]{:S(2)}) collective-permute-start(f32[80,8,128]{2,1,0:T(8,128)S(1)} %get-tuple-element.60.own), channel_id=1, source_target_pairs={{16,0},{32,16},{48,32},{64,48},{80,64},{96,80},{112,96},{128,112},... | collective-permute-start | bytes 983048 | tf_op jit(solution)/shard_map/ppermute | solution.py:814
  62.7 9.2 %collective-permute-start.6 = (f32[80,8,128]{2,1,0:T(8,128)S(1)}, f32[80,8,128]{2,1,0:T(8,128)S(1)}, u32[]{:S(2)}, u32[]{:S(2)}) collective-permute-start(f32[80,8,128]{2,1,0:T(8,128)S(1)} %get-tuple-element.60.own), channel_id=1, source_target_pairs={{0,16},{16,32},{32,48},{48,64},{64,80},{80,96},{96,112},{112,128},... | collective-permute-start | bytes 983048 | tf_op jit(solution)/shard_map/ppermute | solution.py:814
  62.7 4.0 %collective-permute-start.8 = (f32[32,8,128]{2,1,0:T(8,128)S(1)}, f32[32,8,128]{2,1,0:T(8,128)S(1)}, u32[]{:S(2)}, u32[]{:S(2)}) collective-permute-start(f32[32,8,128]{2,1,0:T(8,128)S(1)} %get-tuple-element.61), channel_id=1, source_target_pairs={{0,1},{1,2},{2,3},{3,4},{4,5},{5,6},{6,7},{7,8},{8,9},{9,10},{10,1... | collective-permute-start | bytes 393224 | tf_op jit(solution)/shard_map/ppermute | solution.py:814
  64.7 4.4 %collective-permute-start.9 = (f32[32,8,128]{2,1,0:T(8,128)S(1)}, f32[32,8,128]{2,1,0:T(8,128)S(1)}, u32[]{:S(2)}, u32[]{:S(2)}) collective-permute-start(f32[32,8,128]{2,1,0:T(8,128)S(1)} %get-tuple-element.62), channel_id=1, source_target_pairs={{1,0},{2,1},{3,2},{4,3},{5,4},{6,5},{7,6},{8,7},{9,8},{10,9},{11,1... | collective-permute-start | bytes 393224 | tf_op jit(solution)/shard_map/ppermute | solution.py:814
  71.9 7.8 %collective-permute-start.10 = (f32[36,8,128]{2,1,0:T(8,128)S(1)}, f32[36,8,128]{2,1,0:T(8,128)S(1)}, u32[]{:S(2)}, u32[]{:S(2)}) collective-permute-start(f32[36,8,128]{2,1,0:T(8,128)S(1)} %get-tuple-element.65), channel_id=1, source_target_pairs={{0,1},{1,2},{2,3},{3,4},{4,5},{5,6},{6,7},{7,8},{8,9},{9,10},{10,1... | collective-permute-start | bytes 442376 | tf_op jit(solution)/shard_map/ppermute | solution.py:814
  77.7 4.6 %collective-permute-start.11 = (f32[36,8,128]{2,1,0:T(8,128)S(1)}, f32[36,8,128]{2,1,0:T(8,128)S(1)}, u32[]{:S(2)}, u32[]{:S(2)}) collective-permute-start(f32[36,8,128]{2,1,0:T(8,128)S(1)} %get-tuple-element.66), channel_id=1, source_target_pairs={{1,0},{2,1},{3,2},{4,3},{5,4},{6,5},{7,6},{8,7},{9,8},{10,9},{11,1... | collective-permute-start | bytes 442376 | tf_op jit(solution)/shard_map/ppermute | solution.py:814
  88.2 1.2 %collective-permute-start.12 = (f32[1,128]{1,0:T(1,128)S(1)}, f32[1,128]{1,0:T(1,128)S(1)}, u32[]{:S(2)}, u32[]{:S(2)}) collective-permute-start(f32[1,128]{1,0:T(1,128)S(1)} %get-tuple-element.69), channel_id=1, source_target_pairs={{0,1},{1,0},{2,3},{3,2},{4,5},{5,4},{6,7},{7,6},{8,9},{9,8},{10,11... | collective-permute-start | bytes 1544 | tf_op jit(solution)/shard_map/ppermute | solution.py:901

commit v5 on v4

--- a/solution.py
+++ b/solution.py
@@ -28,12 +28,12 @@
 ANY = pl.BlockSpec(memory_space=pl.ANY)
 
 
-def call(body, outs, ins, scratch=(), limit=8, where=VMEM, us=1):
+def call(body, outs, ins, scratch=(), limit=8, where=VMEM, us=1, out_where=None):
     return pl.pallas_call(
         body,
         out_shape=[jax.ShapeDtypeStruct(s, jnp.float32) for s in outs],
         in_specs=[where] * len(ins),
-        out_specs=[where] * len(outs),
+        out_specs=out_where or [where] * len(outs),
         scratch_shapes=[pltpu.VMEM(s, jnp.float32) if isinstance(s, tuple) else s for s in scratch],
         compiler_params=pltpu.CompilerParams(vmem_limit_bytes=limit * MIB),
         cost_estimate=pl.CostEstimate(
@@ -90,22 +90,28 @@
     return msg[n, r : r + 4, z : z + 128]
 
 
-def x_send(v, wx, wy, wz, xu, xd, sem):
+def x_send(v, wx, wy, wz, xu, xd, bu, bd, sem):
     pairs = []
     for k in range(K):
-        pairs.append((v.at[k, LX - H : LX], xu.at[H * k : H * k + H]))
-        pairs.append((v.at[k, 0:H], xd.at[H * k : H * k + H]))
-    for msg, side in ((xu, UP_W), (xd, DN_W)):
+        pairs.append((v.at[k, LX - H : LX], bu.at[H * k : H * k + H], xu.at[H * k : H * k + H]))
+        pairs.append((v.at[k, 0:H], bd.at[H * k : H * k + H], xd.at[H * k : H * k + H]))
+    for buf, msg, side in ((bu, xu, UP_W), (bd, xd, DN_W)):
         at = K * H
         for w, ref in enumerate((wx, wy, wz)):
             p = [x for q, x in side if q == w]
-            pairs.append((ref.at[p[0] : p[-1] + 1], msg.at[at : at + len(p)]))
+            here = slice(at, at + len(p))
+            pairs.append((ref.at[p[0] : p[-1] + 1], buf.at[here], msg.at[here]))
             at += len(p)
-    copies = [pltpu.make_async_copy(a, b, sem.at[n]) for n, (a, b) in enumerate(pairs)]
-    for c in copies:
+    n = len(pairs)
+    ins = [pltpu.make_async_copy(a, b, sem.at[i]) for i, (a, b, _) in enumerate(pairs)]
+    outs = [pltpu.make_async_copy(b, c, sem.at[n + i]) for i, (_, b, c) in enumerate(pairs)]
+    for c in ins:
         c.start()
-    for c in copies:
-        c.wait()
+    for i, o in zip(ins, outs):
+        i.wait()
+        o.start()
+    for o in outs:
+        o.wait()
 
 
 def local(v, wx, wy, wz, vt, wm, cw, yu, yd, Q):
@@ -731,7 +737,7 @@
     out[...] = jnp.broadcast_to((a[...] + b[...])[None], out.shape)
 
 
-def finish(parts, po, bo, out, eig, SP):
+def finish(parts, po, bo, out, eig, SP, buf, sem):
     t = parts[...]
     n = t.shape[0]
     while n > 2:
@@ -801,10 +807,17 @@
                         u = u - SP[at[k, j] : at[k, j] + 8] * done[j]
                     u = u * SP[64 + 8 * k : 72 + 8 * k]
                     done.append(u)
-                    out[k, x, t : t + 8, z] = u
+                    buf[k, x, t : t + 8, z] = u
+        copy(x).start()
         return 0
 
+    def copy(x):
+        here = pl.ds(x, 1)
+        return pltpu.make_async_copy(buf.at[:, here], out.at[:, here], sem.at[x])
+
     lax.fori_loop(0, LX, body, 0)
+    for x in range(LX):
+        copy(x).wait()
 
 
 def both_ways(up, down, axis):
@@ -820,7 +833,7 @@
         x_send,
         [(NXU, LY, NZ), (NXD, LY, NZ)],
         args,
-        [pltpu.SemaphoreType.DMA((2 * K + 6,))],
+        [(NXU, LY, NZ), (NXD, LY, NZ), pltpu.SemaphoreType.DMA((4 * K + 12,))],
         limit=56,
         where=ANY,
     )
@@ -905,7 +918,8 @@
         finish,
         [(K, LX, LY, NZ), (1, K)],
         (parts, po, bo),
-        [(384, 128)],
+        [(384, 128), (K, LX, LY, NZ), pltpu.SemaphoreType.DMA((LX,))],
+        out_where=[ANY, VMEM],
     )
     return refined, eig.reshape(K)
 

time: 113 us -> 83.7 us (0.74)
  Pallas kernels: 49.4 us -> 20.3 us
    pallas_call x11, Pallas kernels: 49.4 us -> 20.3 us  [call(): pl.pallas_call(body, out_shape=[jax.ShapeDtypeStruct(s, jnp.float32) for...]
  transfers between devices with their start and end apart: 13 -> 13, of which waited for: 8 -> 8; matrix products, arithmetic and copies ran while one was open for 0% -> 0% of each run, Pallas kernels for 8% -> 10%
where the time goes in v5:
time: 83.7 us; the launch traced here: 83.6 us
  starting transfers between devices  24.1 us (29%)
  blocking collectives  20.9 us (25%)
  Pallas kernels  20.3 us (24%)
  waiting for transfers between devices  17.4 us (21%)
    ppermute x12, starting transfers between devices, both_ways(): return (lax.ppermute(up, axis, fwd), lax.ppermute(down, axis, back))  24.1 us
    all_to_all x1, blocking collectives, per_device(): parts = lax.all_to_all(sums, ('gx', 'gy'), 0, 0)  20.9 us
    pallas_call x11, Pallas kernels, call(): pl.pallas_call(body, out_shape=[jax.ShapeDtypeStruct(s, jnp.float32) for...  20.3 us
    ppermute x12, waiting for transfers between devices, both_ways(): return (lax.ppermute(up, axis, fwd), lax.ppermute(down, axis, back))  16.2 us
  transfers between devices with their start and end apart: 13, of which 8 were waited for; matrix products, arithmetic and copies ran while one was open for 0% of the time, Pallas kernels for 10%

profile of v5, /device:TPU:1, one launch (start us, length us, event | category | flops | bytes accessed | tf_op | source)
XLA Modules:
  0.0 83.6 jit_solution(14491420661599827537)
XLA Ops:
  0.6 0.0 copy-start.3
  0.6 0.0 copy-start.2
  0.7 0.0 copy-start.1
  0.7 0.0 copy-start
  0.7 2.3 %shard_map.60 = (f32[31,16,256]{2,1,0:T(8,128)}, f32[30,16,256]{2,1,0:T(8,128)}) custom-call(f32[8,8,16,256]{3,2,1,0:T(8,128)} %v.3, f32[8,16,256]{2,1,0:T(8,128)} %wx.3, f32[8,16,256]{2,1,0:T(8,128)} %wy.3, f32[8,16,256]{2,1,0:T(8,128)} %wz.3), custom_call_target="tpu_custom_call" | custom-call | bytes 3000000 | tf_op jit(solution)/shard_map/pallas_call | solution.py:32
  3.0 2.1 %collective-permute-start = (f32[31,16,256]{2,1,0:T(8,128)}, f32[31,16,256]{2,1,0:T(8,128)S(1)}, u32[]{:S(2)}, u32[]{:S(2)}) collective-permute-start(f32[31,16,256]{2,1,0:T(8,128)} %get-tuple-element.39), channel_id=1, source_target_pairs={{0,16},{16,32},{32,48},{48,64},{64,80},{80,96},{96,112},{112,128},... | collective-permute-start | bytes 1523720 | tf_op jit(solution)/shard_map/ppermute | solution.py:827
  5.1 3.8 %collective-permute-start.1 = (f32[30,16,256]{2,1,0:T(8,128)}, f32[30,16,256]{2,1,0:T(8,128)S(1)}, u32[]{:S(2)}, u32[]{:S(2)}) collective-permute-start(f32[30,16,256]{2,1,0:T(8,128)} %get-tuple-element.40), channel_id=1, source_target_pairs={{16,0},{32,16},{48,32},{64,48},{80,64},{96,80},{112,96},{128,112},... | collective-permute-start | bytes 1474568 | tf_op jit(solution)/shard_map/ppermute | solution.py:827
  8.9 0.0 copy-done.3
  8.9 0.0 copy-done.2
  8.9 0.0 copy-done.1
  8.9 0.0 copy-done
  8.9 0.7 shard_map.59
  9.6 2.5 %collective-permute-start.2 = (f32[36,8,256]{2,1,0:T(8,128)S(1)}, f32[36,8,256]{2,1,0:T(8,128)S(1)}, u32[]{:S(2)}, u32[]{:S(2)}) collective-permute-start(f32[36,8,256]{2,1,0:T(8,128)S(1)} %get-tuple-element.43), channel_id=1, source_target_pairs={{0,1},{1,2},{2,3},{3,4},{4,5},{5,6},{6,7},{7,8},{8,9},{9,10},{10,1... | collective-permute-start | bytes 884744 | tf_op jit(solution)/shard_map/ppermute | solution.py:827
  12.2 0.2 collective-permute-start.3
  12.4 3.4 %collective-permute-done.2.yl.gl = f32[36,8,256]{2,1,0:T(8,128)S(1)} collective-permute-done((f32[36,8,256]{2,1,0:T(8,128)S(1)}, f32[36,8,256]{2,1,0:T(8,128)S(1)}, u32[]{:S(2)}, u32[]{:S(2)}) %collective-permute-start.2) | collective-permute-done | bytes 294944 | tf_op jit(solution)/shard_map/ppermute | solution.py:827
  15.8 2.8 %collective-permute-done.3.yr.gr = f32[36,8,256]{2,1,0:T(8,128)S(1)} collective-permute-done((f32[36,8,256]{2,1,0:T(8,128)S(1)}, f32[36,8,256]{2,1,0:T(8,128)S(1)}, u32[]{:S(2)}, u32[]{:S(2)}) %collective-permute-start.3) | collective-permute-done | bytes 294944 | tf_op jit(solution)/shard_map/ppermute | solution.py:827
  18.6 2.6 %shard_map.61 = (f32[3,8,32,256]{3,2,1,0:T(8,128)S(1)}, f32[7,7,32,256]{3,2,1,0:T(8,128)S(1)}, f32[6,22,8,256]{3,2,1,0:T(8,128)S(1)}, f32[4,22,8,256]{3,2,1,0:T(8,128)S(1)}, f32[2,22,8,256]{3,2,1,0:T(8,128)S(1)}) custom-call(f32[8,16,8,256]{3,2,1,0:T(8,128)S(1)} %get-tuple-element.38.vt, f32[3,8,16,256]{3,2,1,0:T(8,128)S(1)} %get-tuple-element.41.wm, ...), custom_call_target="tpu_custom_call" | custom-call | bytes 9000000 | tf_op jit(solution)/shard_map/pallas_call | solution.py:32
  21.2 0.0 collective-permute-done.1.rr
  21.2 0.0 collective-permute-done.rl
  21.2 0.2 shard_map.62
  21.4 1.9 %collective-permute-start.4 = (f32[10,8,256]{2,1,0:T(8,128)S(1)}, f32[10,8,256]{2,1,0:T(8,128)S(1)}, u32[]{:S(2)}, u32[]{:S(2)}) collective-permute-start(f32[10,8,256]{2,1,0:T(8,128)S(1)} %get-tuple-element.58), channel_id=1, source_target_pairs={{0,1},{1,2},{2,3},{3,4},{4,5},{5,6},{6,7},{7,8},{8,9},{9,10},{10,1... | collective-permute-start | bytes 245768 | tf_op jit(solution)/shard_map/ppermute | solution.py:827
  23.3 0.0 collective-permute-start.5
  23.3 4.8 %shard_map.63 = (f32[7,5,16,256]{3,2,1,0:T(8,128)S(1)}, f32[6,22,8,256]{3,2,1,0:T(8,128)S(1)}, f32[6,22,8,256]{3,2,1,0:T(8,128)S(1)}, f32[6,22,8,256]{3,2,1,0:T(...) custom-call(f32[8,16,8,256]{3,2,1,0:T(8,128)S(1)} %get-tuple-element.38.vt, ...), custom_call_target="tpu_custom_call" | custom-call | bytes 12000000 | tf_op jit(solution)/shard_map/pallas_call | solution.py:32
  28.1 0.0 collective-permute-done.4.cl
  28.1 0.0 collective-permute-done.5.cr
  28.1 0.7 shard_map.64
  28.8 4.6 %collective-permute-start.7 = (f32[80,8,128]{2,1,0:T(8,128)S(1)}, f32[80,8,128]{2,1,0:T(8,128)S(1)}, u32[]{:S(2)}, u32[]{:S(2)}) collective-permute-start(f32[80,8,128]{2,1,0:T(8,128)S(1)} %get-tuple-element.60.own), channel_id=1, source_target_pairs={{16,0},{32,16},{48,32},{64,48},{80,64},{96,80},{112,96},{128,112},... | collective-permute-start | bytes 983048 | tf_op jit(solution)/shard_map/ppermute | solution.py:827
  33.4 0.0 collective-permute-start.6
  33.4 2.0 %collective-permute-start.8 = (f32[32,8,128]{2,1,0:T(8,128)S(1)}, f32[32,8,128]{2,1,0:T(8,128)S(1)}, u32[]{:S(2)}, u32[]{:S(2)}) collective-permute-start(f32[32,8,128]{2,1,0:T(8,128)S(1)} %get-tuple-element.61), channel_id=1, source_target_pairs={{0,1},{1,2},{2,3},{3,4},{4,5},{5,6},{6,7},{7,8},{8,9},{9,10},{10,1... | collective-permute-start | bytes 393224 | tf_op jit(solution)/shard_map/ppermute | solution.py:827
  35.4 1.1 %collective-permute-start.9 = (f32[32,8,128]{2,1,0:T(8,128)S(1)}, f32[32,8,128]{2,1,0:T(8,128)S(1)}, u32[]{:S(2)}, u32[]{:S(2)}) collective-permute-start(f32[32,8,128]{2,1,0:T(8,128)S(1)} %get-tuple-element.62), channel_id=1, source_target_pairs={{1,0},{2,1},{3,2},{4,3},{5,4},{6,5},{7,6},{8,7},{9,8},{10,9},{11,1... | collective-permute-start | bytes 393224 | tf_op jit(solution)/shard_map/ppermute | solution.py:827
  36.5 0.6 shard_map.65
  37.2 0.2 collective-permute-done.8.yl
  37.4 2.4 %collective-permute-done.9.yr = f32[32,8,128]{2,1,0:T(8,128)S(1)} collective-permute-done((f32[32,8,128]{2,1,0:T(8,128)S(1)}, f32[32,8,128]{2,1,0:T(8,128)S(1)}, u32[]{:S(2)}, u32[]{:S(2)}) %collective-permute-start.9) | collective-permute-done | bytes 131104 | tf_op jit(solution)/shard_map/ppermute | solution.py:827
  39.8 0.0 collective-permute-done.7.right
  39.8 2.8 %collective-permute-done.6.left = f32[80,8,128]{2,1,0:T(8,128)S(1)} collective-permute-done((f32[80,8,128]{2,1,0:T(8,128)S(1)}, f32[80,8,128]{2,1,0:T(8,128)S(1)}, u32[]{:S(2)}, u32[]{:S(2)}) %collective-permute-start.6) | collective-permute-done | bytes 327712 | tf_op jit(solution)/shard_map/ppermute | solution.py:827
  42.7 5.7 %collective-permute-start.10 = (f32[36,8,128]{2,1,0:T(8,128)S(1)}, f32[36,8,128]{2,1,0:T(8,128)S(1)}, u32[]{:S(2)}, u32[]{:S(2)}) collective-permute-start(f32[36,8,128]{2,1,0:T(8,128)S(1)} %get-tuple-element.65), channel_id=1, source_target_pairs={{0,1},{1,2},{2,3},{3,4},{4,5},{5,6},{6,7},{7,8},{8,9},{9,10},{10,1... | collective-permute-start | bytes 442376 | tf_op jit(solution)/shard_map/ppermute | solution.py:827
  48.4 0.0 collective-permute-start.11
  48.4 2.1 %collective-permute-done.10.cl = f32[36,8,128]{2,1,0:T(8,128)S(1)} collective-permute-done((f32[36,8,128]{2,1,0:T(8,128)S(1)}, f32[36,8,128]{2,1,0:T(8,128)S(1)}, u32[]{:S(2)}, u32[]{:S(2)}) %collective-permute-start.10) | collective-permute-done | bytes 147488 | tf_op jit(solution)/shard_map/ppermute | solution.py:827
  50.5 2.5 %collective-permute-done.11.cr = f32[36,8,128]{2,1,0:T(8,128)S(1)} collective-permute-done((f32[36,8,128]{2,1,0:T(8,128)S(1)}, f32[36,8,128]{2,1,0:T(8,128)S(1)}, u32[]{:S(2)}, u32[]{:S(2)}) %collective-permute-start.11) | collective-permute-done | bytes 147488 | tf_op jit(solution)/shard_map/ppermute | solution.py:827
  53.0 6.0 %shard_map.67 = (f32[8,16,8,256]{3,2,1,0:T(8,128)S(1)}, f32[8,16,8,256]{3,2,1,0:T(8,128)S(1)}, f32[1,128]{1,0:T(1,128)S(1)}, f32[1,128]{1,0:T(1,128)S(1)}) custom-call(f32[80,8,128]{2,1,0:T(8,128)S(1)} %get-tuple-element.60.own, f32[80,8,128]{2,1,0:T(8,128)S(1)} %collective-permute-done.6.left, f32[80,8,128]{2,1,0:T(8,128)S(1)} %collective-permute-done.7.right, ...), custom_call_target="tpu_custom_call" | custom-call | bytes 3000000 | tf_op jit(solution)/shard_map/pallas_call | solution.py:32
  58.9 0.1 collective-permute-start.12
  59.0 1.1 %collective-permute-done.12.b = f32[1,128]{1,0:T(1,128)S(1)} collective-permute-done((f32[1,128]{1,0:T(1,128)S(1)}, f32[1,128]{1,0:T(1,128)S(1)}, u32[]{:S(2)}, u32[]{:S(2)}) %collective-permute-start.12) | collective-permute-done | bytes 544 | tf_op jit(solution)/shard_map/ppermute | solution.py:914
  60.1 0.1 shard_map.68
  60.2 20.9 %all_to_all.5.parts = f32[256,1,128]{2,1,0:T(1,128)S(1)} all-to-all(f32[256,1,128]{2,1,0:T(1,128)S(1)} %shard_map.68), channel_id=1, replica_groups=mesh['gx'=16,'gy'=16] {'gx','gy'}, dimensions={0} | all-to-all | bytes 262144 | tf_op jit(solution)/shard_map/all_to_all | solution.py:916
  81.1 2.5 %shard_map.69 = (f32[8,8,16,256]{3,2,1,0:T(8,128)}, f32[1,8]{1,0:T(1,128)}) custom-call(f32[256,1,128]{2,1,0:T(1,128)S(1)} %all_to_all.5.parts, f32[8,16,8,256]{3,2,1,0:T(8,128)S(1)} %get-tuple-element.70.po, f32[8,16,8,256]{3,2,1,0:T(8,128)S(1)} %get-tuple-element.71.bo), custom_call_target="tpu_custom_call" | custom-call | bytes 3000000 | tf_op jit(solution)/shard_map/pallas_call | solution.py:32
  (1 shorter events, 0.0 us)
Async XLA Ops:
  0.6 8.3 %copy-start.3 = (f32[8,16,256]{2,1,0:T(8,128)S(1)}, f32[8,16,256]{2,1,0:T(8,128)}, u32[]{:S(2)}) copy-start(f32[8,16,256]{2,1,0:T(8,128)} %wz.3) | copy-start | bytes 393220
  0.6 8.3 %copy-start.2 = (f32[8,16,256]{2,1,0:T(8,128)S(1)}, f32[8,16,256]{2,1,0:T(8,128)}, u32[]{:S(2)}) copy-start(f32[8,16,256]{2,1,0:T(8,128)} %wy.3) | copy-start | bytes 393220
  0.7 8.3 %copy-start.1 = (f32[8,16,256]{2,1,0:T(8,128)S(1)}, f32[8,16,256]{2,1,0:T(8,128)}, u32[]{:S(2)}) copy-start(f32[8,16,256]{2,1,0:T(8,128)} %wx.3) | copy-start | bytes 393220
  0.7 8.3 %copy-start = (f32[8,8,16,256]{3,2,1,0:T(8,128)S(1)}, f32[8,8,16,256]{3,2,1,0:T(8,128)}, u32[]{:S(2)}) copy-start(f32[8,8,16,256]{3,2,1,0:T(8,128)} %v.3) | copy-start | bytes 3145732
  3.0 18.2 %collective-permute-start = (f32[31,16,256]{2,1,0:T(8,128)}, f32[31,16,256]{2,1,0:T(8,128)S(1)}, u32[]{:S(2)}, u32[]{:S(2)}) collective-permute-start(f32[31,16,256]{2,1,0:T(8,128)} %get-tuple-element.39), channel_id=1, source_target_pairs={{0,16},{16,32},{32,48},{48,64},{64,80},{80,96},{96,112},{112,128},... | collective-permute-start | bytes 1523720 | tf_op jit(solution)/shard_map/ppermute | solution.py:827
  5.1 16.1 %collective-permute-start.1 = (f32[30,16,256]{2,1,0:T(8,128)}, f32[30,16,256]{2,1,0:T(8,128)S(1)}, u32[]{:S(2)}, u32[]{:S(2)}) collective-permute-start(f32[30,16,256]{2,1,0:T(8,128)} %get-tuple-element.40), channel_id=1, source_target_pairs={{16,0},{32,16},{48,32},{64,48},{80,64},{96,80},{112,96},{128,112},... | collective-permute-start | bytes 1474568 | tf_op jit(solution)/shard_map/ppermute | solution.py:827
  9.6 6.2 %collective-permute-start.2 = (f32[36,8,256]{2,1,0:T(8,128)S(1)}, f32[36,8,256]{2,1,0:T(8,128)S(1)}, u32[]{:S(2)}, u32[]{:S(2)}) collective-permute-start(f32[36,8,256]{2,1,0:T(8,128)S(1)} %get-tuple-element.43), channel_id=1, source_target_pairs={{0,1},{1,2},{2,3},{3,4},{4,5},{5,6},{6,7},{7,8},{8,9},{9,10},{10,1... | collective-permute-start | bytes 884744 | tf_op jit(solution)/shard_map/ppermute | solution.py:827
  12.2 6.4 %collective-permute-start.3 = (f32[36,8,256]{2,1,0:T(8,128)S(1)}, f32[36,8,256]{2,1,0:T(8,128)S(1)}, u32[]{:S(2)}, u32[]{:S(2)}) collective-permute-start(f32[36,8,256]{2,1,0:T(8,128)S(1)} %get-tuple-element.44), channel_id=1, source_target_pairs={{1,0},{2,1},{3,2},{4,3},{5,4},{6,5},{7,6},{8,7},{9,8},{10,9},{11,1... | collective-permute-start | bytes 884744 | tf_op jit(solution)/shard_map/ppermute | solution.py:827
  21.4 6.7 %collective-permute-start.4 = (f32[10,8,256]{2,1,0:T(8,128)S(1)}, f32[10,8,256]{2,1,0:T(8,128)S(1)}, u32[]{:S(2)}, u32[]{:S(2)}) collective-permute-start(f32[10,8,256]{2,1,0:T(8,128)S(1)} %get-tuple-element.58), channel_id=1, source_target_pairs={{0,1},{1,2},{2,3},{3,4},{4,5},{5,6},{6,7},{7,8},{8,9},{9,10},{10,1... | collective-permute-start | bytes 245768 | tf_op jit(solution)/shard_map/ppermute | solution.py:827
  23.3 4.8 %collective-permute-start.5 = (f32[10,8,256]{2,1,0:T(8,128)S(1)}, f32[10,8,256]{2,1,0:T(8,128)S(1)}, u32[]{:S(2)}, u32[]{:S(2)}) collective-permute-start(f32[10,8,256]{2,1,0:T(8,128)S(1)} %get-tuple-element.59), channel_id=1, source_target_pairs={{1,0},{2,1},{3,2},{4,3},{5,4},{6,5},{7,6},{8,7},{9,8},{10,9},{11,1... | collective-permute-start | bytes 245768 | tf_op jit(solution)/shard_map/ppermute | solution.py:827
  28.8 11.0 %collective-permute-start.7 = (f32[80,8,128]{2,1,0:T(8,128)S(1)}, f32[80,8,128]{2,1,0:T(8,128)S(1)}, u32[]{:S(2)}, u32[]{:S(2)}) collective-permute-start(f32[80,8,128]{2,1,0:T(8,128)S(1)} %get-tuple-element.60.own), channel_id=1, source_target_pairs={{16,0},{32,16},{48,32},{64,48},{80,64},{96,80},{112,96},{128,112},... | collective-permute-start | bytes 983048 | tf_op jit(solution)/shard_map/ppermute | solution.py:827
  33.4 9.2 %collective-permute-start.6 = (f32[80,8,128]{2,1,0:T(8,128)S(1)}, f32[80,8,128]{2,1,0:T(8,128)S(1)}, u32[]{:S(2)}, u32[]{:S(2)}) collective-permute-start(f32[80,8,128]{2,1,0:T(8,128)S(1)} %get-tuple-element.60.own), channel_id=1, source_target_pairs={{0,16},{16,32},{32,48},{48,64},{64,80},{80,96},{96,112},{112,128},... | collective-permute-start | bytes 983048 | tf_op jit(solution)/shard_map/ppermute | solution.py:827
  33.4 4.0 %collective-permute-start.8 = (f32[32,8,128]{2,1,0:T(8,128)S(1)}, f32[32,8,128]{2,1,0:T(8,128)S(1)}, u32[]{:S(2)}, u32[]{:S(2)}) collective-permute-start(f32[32,8,128]{2,1,0:T(8,128)S(1)} %get-tuple-element.61), channel_id=1, source_target_pairs={{0,1},{1,2},{2,3},{3,4},{4,5},{5,6},{6,7},{7,8},{8,9},{9,10},{10,1... | collective-permute-start | bytes 393224 | tf_op jit(solution)/shard_map/ppermute | solution.py:827
  35.4 4.4 %collective-permute-start.9 = (f32[32,8,128]{2,1,0:T(8,128)S(1)}, f32[32,8,128]{2,1,0:T(8,128)S(1)}, u32[]{:S(2)}, u32[]{:S(2)}) collective-permute-start(f32[32,8,128]{2,1,0:T(8,128)S(1)} %get-tuple-element.62), channel_id=1, source_target_pairs={{1,0},{2,1},{3,2},{4,3},{5,4},{6,5},{7,6},{8,7},{9,8},{10,9},{11,1... | collective-permute-start | bytes 393224 | tf_op jit(solution)/shard_map/ppermute | solution.py:827
  42.7 7.8 %collective-permute-start.10 = (f32[36,8,128]{2,1,0:T(8,128)S(1)}, f32[36,8,128]{2,1,0:T(8,128)S(1)}, u32[]{:S(2)}, u32[]{:S(2)}) collective-permute-start(f32[36,8,128]{2,1,0:T(8,128)S(1)} %get-tuple-element.65), channel_id=1, source_target_pairs={{0,1},{1,2},{2,3},{3,4},{4,5},{5,6},{6,7},{7,8},{8,9},{9,10},{10,1... | collective-permute-start | bytes 442376 | tf_op jit(solution)/shard_map/ppermute | solution.py:827
  48.4 4.6 %collective-permute-start.11 = (f32[36,8,128]{2,1,0:T(8,128)S(1)}, f32[36,8,128]{2,1,0:T(8,128)S(1)}, u32[]{:S(2)}, u32[]{:S(2)}) collective-permute-start(f32[36,8,128]{2,1,0:T(8,128)S(1)} %get-tuple-element.66), channel_id=1, source_target_pairs={{1,0},{2,1},{3,2},{4,3},{5,4},{6,5},{7,6},{8,7},{9,8},{10,9},{11,1... | collective-permute-start | bytes 442376 | tf_op jit(solution)/shard_map/ppermute | solution.py:827
  58.9 1.2 %collective-permute-start.12 = (f32[1,128]{1,0:T(1,128)S(1)}, f32[1,128]{1,0:T(1,128)S(1)}, u32[]{:S(2)}, u32[]{:S(2)}) collective-permute-start(f32[1,128]{1,0:T(1,128)S(1)} %get-tuple-element.69), channel_id=1, source_target_pairs={{0,1},{1,0},{2,3},{3,2},{4,5},{5,4},{6,7},{7,6},{8,9},{9,8},{10,11... | collective-permute-start | bytes 1544 | tf_op jit(solution)/shard_map/ppermute | solution.py:914

commit v6 on v5

--- a/solution.py
+++ b/solution.py
@@ -591,7 +591,6 @@
     def put(i, j, half, f):
         f = OMEGA * f
         F[i, j, half] = f
-        EA[i, j, half] = f
 
     for x in range(CX):
         for half in range(2):
@@ -655,7 +654,7 @@
 
         return body
 
-    planes(3, sweep(EA, EB), CX, CH)
+    planes(3, sweep(F, EB), CX, CH)
     planes(2, sweep(EB, EA), CX, CH)
     planes(1, sweep(EA, EB), CX, CH)
 
@@ -691,6 +690,9 @@
                         else:
                             bo[xx, yy] = pb[xx, yy, 8:16] + s
 
+    def row8(ref, x, y, m, z):
+        return jnp.broadcast_to(ref[x, y, m : m + 1, z], (8, 128))
+
     def gram(x, edge, acc):
         acc = list(acc)
         for yy in range(LY):
@@ -701,36 +703,33 @@
                 b = bo[x, yy, :, z]
                 dp = deg[:, z] * p
                 db = deg[:, z] * b
-                for s in range(8):
-                    rb = pltpu.roll(db, s, 0) if s else db
-                    if s < 5:
-                        rp = pltpu.roll(dp, s, 0) if s else dp
-                        acc[s] = acc[s] + p * rp
-                        acc[5 + s] = acc[5 + s] + b * rb
-                    acc[10 + s] = acc[10 + s] + p * rb
+                for m in range(8):
+                    acc[m] = acc[m] + dp * row8(po, x, yy, m, z)
+                    acc[13 + m] = acc[13 + m] + dp * row8(bo, x, yy, m, z)
+                for s in range(5):
+                    acc[8 + s] = acc[8 + s] + b * (pltpu.roll(db, s, 0) if s else db)
         return tuple(acc)
 
     zero = jnp.zeros((8, 128), jnp.float32)
-    acc = gram(0, True, (zero,) * 18)
+    acc = gram(0, True, (zero,) * 21)
     acc = list(lax.fori_loop(1, LX, lambda x, acc: gram(x, False, acc), acc))
     for q in range(2):
         acc.append(nd[q, :, :128] + nd[q, :, 128:])
-    ones = jnp.ones((8, 128), jnp.float32)
-
-    def over_lanes(m):
-        return lax.dot_general(
-            ones,
-            m,
-            (((1,), (1,)), ((), ())),
-            precision=lax.Precision.HIGHEST,
-            preferred_element_type=jnp.float32,
-        )
-
-    t0 = over_lanes(jnp.concatenate(acc[:16], 0))
-    t1 = over_lanes(jnp.concatenate(acc[16:] + [zero] * 12, 0))
+    lane = lax.broadcasted_iota(jnp.int32, (8, 128), 1)
+    sub = lax.broadcasted_iota(jnp.int32, (8, 128), 0)
+
+    def collect(blocks):
+        x = zero
+        for n, a in enumerate(blocks):
+            total = jnp.broadcast_to(jnp.sum(a, axis=1, keepdims=True), (8, 128))
+            x = x + jnp.where(lane == 8 * n + sub, total, 0.0)
+        return jnp.sum(x, axis=0, keepdims=True)
+
+    t0 = collect(acc[:16])
+    t1 = collect(acc[16:])
     even = lax.axis_index("gy") % 2 == 0
-    mine[...] = jnp.where(even, t0[0:1], t1[0:1])
-    other[...] = jnp.where(even, t1[0:1], t0[0:1])
+    mine[...] = jnp.where(even, t0, t1)
+    other[...] = jnp.where(even, t1, t0)
 
 
 def spread_sums(a, b, out):
@@ -744,35 +743,28 @@
         n //= 2
         t = t[:n] + t[n:]
     t = t[:, 0]
-    eye = lax.broadcasted_iota(jnp.int32, (128, 128), 0) == lax.broadcasted_iota(
-        jnp.int32, (128, 128), 1
-    )
-    ones = jnp.ones((128, 128), jnp.float32)
-    for q in range(2):
-        m = jnp.where(eye, jnp.broadcast_to(t[q : q + 1], (128, 128)), 0.0)
-        SP[128 * q : 128 * (q + 1)] = jnp.dot(
-            m, ones, precision=lax.Precision.HIGHEST, preferred_element_type=jnp.float32
-        )
     lams = t[1:2] / pltpu.roll(t[1:2], 120, 1)
-    eig[...] = pltpu.roll(lams, 112, 1)[:, :K]
+    eig[...] = pltpu.roll(lams, 88, 1)[:, :K]
+    half = [jnp.broadcast_to(t[q : q + 1], (8, 128)) for q in range(2)]
 
     def entry(block, k):
-        return row(SP, 8 * block + k)
-
-    def sym(base, a, b):
+        at = 8 * (block % 16) + k
+        return jnp.broadcast_to(half[block // 16][:, at : at + 1], (8, 128))
+
+    def sym(a, b):
         s = (a - b) % 8
-        return entry(base + s, a) if s < 5 else entry(base + 8 - s, b)
+        return entry(8 + s, a) if s < 5 else entry(16 - s, b)
 
     def cross(a, b):
-        return entry(10 + (a - b) % 8, a)
-
-    lam = [entry(18, k) / entry(19, k) for k in range(K)]
+        return entry(13 + b, a)
+
+    lam = [entry(21, k) / entry(22, k) for k in range(K)]
     voxels = LX * LY * NZ * lax.axis_size("gx") * lax.axis_size("gy")
     g = {}
     for a in range(K):
         for b in range(a + 1):
             g[a, b] = (
-                sym(0, a, b) + lam[b] * cross(a, b) + lam[a] * (cross(b, a) + lam[b] * sym(5, a, b))
+                entry(b, a) + lam[b] * cross(a, b) + lam[a] * (cross(b, a) + lam[b] * sym(a, b))
             ) * (1.0 / voxels)
     low, inv = {}, []
     for j in range(K):

time: 83.7 us -> 83.6 us (level)
  no operation moved by 1% of the time
where the time goes in v6:
time: 83.6 us; the launch traced here: 83.4 us
  starting transfers between devices  24.2 us (29%)
  blocking collectives  20.9 us (25%)
  Pallas kernels  20.2 us (24%)
  waiting for transfers between devices  17.4 us (21%)
    ppermute x12, starting transfers between devices, both_ways(): return (lax.ppermute(up, axis, fwd), lax.ppermute(down, axis, back))  24.1 us
    all_to_all x1, blocking collectives, per_device(): parts = lax.all_to_all(sums, ('gx', 'gy'), 0, 0)  20.9 us
    pallas_call x11, Pallas kernels, call(): pl.pallas_call(body, out_shape=[jax.ShapeDtypeStruct(s, jnp.float32) for...  20.2 us
    ppermute x12, waiting for transfers between devices, both_ways(): return (lax.ppermute(up, axis, fwd), lax.ppermute(down, axis, back))  16.2 us
  transfers between devices with their start and end apart: 13, of which 8 were waited for; matrix products, arithmetic and copies ran while one was open for 0% of the time, Pallas kernels for 10%

profile of v6, /device:TPU:1, one launch (start us, length us, event | category | flops | bytes accessed | tf_op | source)
XLA Modules:
  0.0 83.4 jit_solution(8019967713006512999)
XLA Ops:
  0.6 0.0 copy-start.3
  0.6 0.0 copy-start.2
  0.7 0.0 copy-start.1
  0.7 0.0 copy-start
  0.7 2.3 %shard_map.60 = (f32[31,16,256]{2,1,0:T(8,128)}, f32[30,16,256]{2,1,0:T(8,128)}) custom-call(f32[8,8,16,256]{3,2,1,0:T(8,128)} %v.3, f32[8,16,256]{2,1,0:T(8,128)} %wx.3, f32[8,16,256]{2,1,0:T(8,128)} %wy.3, f32[8,16,256]{2,1,0:T(8,128)} %wz.3), custom_call_target="tpu_custom_call" | custom-call | bytes 3000000 | tf_op jit(solution)/shard_map/pallas_call | solution.py:32
  3.0 2.1 %collective-permute-start = (f32[31,16,256]{2,1,0:T(8,128)}, f32[31,16,256]{2,1,0:T(8,128)S(1)}, u32[]{:S(2)}, u32[]{:S(2)}) collective-permute-start(f32[31,16,256]{2,1,0:T(8,128)} %get-tuple-element.39), channel_id=1, source_target_pairs={{0,16},{16,32},{32,48},{48,64},{64,80},{80,96},{96,112},{112,128},... | collective-permute-start | bytes 1523720 | tf_op jit(solution)/shard_map/ppermute | solution.py:819
  5.1 3.8 %collective-permute-start.1 = (f32[30,16,256]{2,1,0:T(8,128)}, f32[30,16,256]{2,1,0:T(8,128)S(1)}, u32[]{:S(2)}, u32[]{:S(2)}) collective-permute-start(f32[30,16,256]{2,1,0:T(8,128)} %get-tuple-element.40), channel_id=1, source_target_pairs={{16,0},{32,16},{48,32},{64,48},{80,64},{96,80},{112,96},{128,112},... | collective-permute-start | bytes 1474568 | tf_op jit(solution)/shard_map/ppermute | solution.py:819
  8.9 0.0 copy-done.3
  8.9 0.0 copy-done.2
  8.9 0.0 copy-done.1
  8.9 0.0 copy-done
  8.9 0.7 shard_map.59
  9.6 2.5 %collective-permute-start.2 = (f32[36,8,256]{2,1,0:T(8,128)S(1)}, f32[36,8,256]{2,1,0:T(8,128)S(1)}, u32[]{:S(2)}, u32[]{:S(2)}) collective-permute-start(f32[36,8,256]{2,1,0:T(8,128)S(1)} %get-tuple-element.43), channel_id=1, source_target_pairs={{0,1},{1,2},{2,3},{3,4},{4,5},{5,6},{6,7},{7,8},{8,9},{9,10},{10,1... | collective-permute-start | bytes 884744 | tf_op jit(solution)/shard_map/ppermute | solution.py:819
  12.2 0.2 collective-permute-start.3
  12.4 3.4 %collective-permute-done.2.yl.gl = f32[36,8,256]{2,1,0:T(8,128)S(1)} collective-permute-done((f32[36,8,256]{2,1,0:T(8,128)S(1)}, f32[36,8,256]{2,1,0:T(8,128)S(1)}, u32[]{:S(2)}, u32[]{:S(2)}) %collective-permute-start.2) | collective-permute-done | bytes 294944 | tf_op jit(solution)/shard_map/ppermute | solution.py:819
  15.8 2.8 %collective-permute-done.3.yr.gr = f32[36,8,256]{2,1,0:T(8,128)S(1)} collective-permute-done((f32[36,8,256]{2,1,0:T(8,128)S(1)}, f32[36,8,256]{2,1,0:T(8,128)S(1)}, u32[]{:S(2)}, u32[]{:S(2)}) %collective-permute-start.3) | collective-permute-done | bytes 294944 | tf_op jit(solution)/shard_map/ppermute | solution.py:819
  18.6 2.6 %shard_map.61 = (f32[3,8,32,256]{3,2,1,0:T(8,128)S(1)}, f32[7,7,32,256]{3,2,1,0:T(8,128)S(1)}, f32[6,22,8,256]{3,2,1,0:T(8,128)S(1)}, f32[4,22,8,256]{3,2,1,0:T(8,128)S(1)}, f32[2,22,8,256]{3,2,1,0:T(8,128)S(1)}) custom-call(f32[8,16,8,256]{3,2,1,0:T(8,128)S(1)} %get-tuple-element.38.vt, f32[3,8,16,256]{3,2,1,0:T(8,128)S(1)} %get-tuple-element.41.wm, ...), custom_call_target="tpu_custom_call" | custom-call | bytes 9000000 | tf_op jit(solution)/shard_map/pallas_call | solution.py:32
  21.2 0.0 collective-permute-done.1.rr
  21.2 0.0 collective-permute-done.rl
  21.2 0.2 shard_map.62
  21.4 1.9 %collective-permute-start.4 = (f32[10,8,256]{2,1,0:T(8,128)S(1)}, f32[10,8,256]{2,1,0:T(8,128)S(1)}, u32[]{:S(2)}, u32[]{:S(2)}) collective-permute-start(f32[10,8,256]{2,1,0:T(8,128)S(1)} %get-tuple-element.58), channel_id=1, source_target_pairs={{0,1},{1,2},{2,3},{3,4},{4,5},{5,6},{6,7},{7,8},{8,9},{9,10},{10,1... | collective-permute-start | bytes 245768 | tf_op jit(solution)/shard_map/ppermute | solution.py:819
  23.3 0.0 collective-permute-start.5
  23.3 4.8 %shard_map.63 = (f32[7,5,16,256]{3,2,1,0:T(8,128)S(1)}, f32[6,22,8,256]{3,2,1,0:T(8,128)S(1)}, f32[6,22,8,256]{3,2,1,0:T(8,128)S(1)}, f32[6,22,8,256]{3,2,1,0:T(...) custom-call(f32[8,16,8,256]{3,2,1,0:T(8,128)S(1)} %get-tuple-element.38.vt, ...), custom_call_target="tpu_custom_call" | custom-call | bytes 12000000 | tf_op jit(solution)/shard_map/pallas_call | solution.py:32
  28.1 0.0 collective-permute-done.4.cl
  28.1 0.0 collective-permute-done.5.cr
  28.1 0.7 shard_map.64
  28.8 4.6 %collective-permute-start.7 = (f32[80,8,128]{2,1,0:T(8,128)S(1)}, f32[80,8,128]{2,1,0:T(8,128)S(1)}, u32[]{:S(2)}, u32[]{:S(2)}) collective-permute-start(f32[80,8,128]{2,1,0:T(8,128)S(1)} %get-tuple-element.60.own), channel_id=1, source_target_pairs={{16,0},{32,16},{48,32},{64,48},{80,64},{96,80},{112,96},{128,112},... | collective-permute-start | bytes 983048 | tf_op jit(solution)/shard_map/ppermute | solution.py:819
  33.4 0.0 collective-permute-start.6
  33.4 2.0 %collective-permute-start.8 = (f32[32,8,128]{2,1,0:T(8,128)S(1)}, f32[32,8,128]{2,1,0:T(8,128)S(1)}, u32[]{:S(2)}, u32[]{:S(2)}) collective-permute-start(f32[32,8,128]{2,1,0:T(8,128)S(1)} %get-tuple-element.61), channel_id=1, source_target_pairs={{0,1},{1,2},{2,3},{3,4},{4,5},{5,6},{6,7},{7,8},{8,9},{9,10},{10,1... | collective-permute-start | bytes 393224 | tf_op jit(solution)/shard_map/ppermute | solution.py:819
  35.4 1.1 %collective-permute-start.9 = (f32[32,8,128]{2,1,0:T(8,128)S(1)}, f32[32,8,128]{2,1,0:T(8,128)S(1)}, u32[]{:S(2)}, u32[]{:S(2)}) collective-permute-start(f32[32,8,128]{2,1,0:T(8,128)S(1)} %get-tuple-element.62), channel_id=1, source_target_pairs={{1,0},{2,1},{3,2},{4,3},{5,4},{6,5},{7,6},{8,7},{9,8},{10,9},{11,1... | collective-permute-start | bytes 393224 | tf_op jit(solution)/shard_map/ppermute | solution.py:819
  36.5 0.6 shard_map.65
  37.2 0.2 collective-permute-done.8.yl
  37.4 2.4 %collective-permute-done.9.yr = f32[32,8,128]{2,1,0:T(8,128)S(1)} collective-permute-done((f32[32,8,128]{2,1,0:T(8,128)S(1)}, f32[32,8,128]{2,1,0:T(8,128)S(1)}, u32[]{:S(2)}, u32[]{:S(2)}) %collective-permute-start.9) | collective-permute-done | bytes 131104 | tf_op jit(solution)/shard_map/ppermute | solution.py:819
  39.8 0.0 collective-permute-done.7.right
  39.8 2.8 %collective-permute-done.6.left = f32[80,8,128]{2,1,0:T(8,128)S(1)} collective-permute-done((f32[80,8,128]{2,1,0:T(8,128)S(1)}, f32[80,8,128]{2,1,0:T(8,128)S(1)}, u32[]{:S(2)}, u32[]{:S(2)}) %collective-permute-start.6) | collective-permute-done | bytes 327712 | tf_op jit(solution)/shard_map/ppermute | solution.py:819
  42.7 5.7 %collective-permute-start.10 = (f32[36,8,128]{2,1,0:T(8,128)S(1)}, f32[36,8,128]{2,1,0:T(8,128)S(1)}, u32[]{:S(2)}, u32[]{:S(2)}) collective-permute-start(f32[36,8,128]{2,1,0:T(8,128)S(1)} %get-tuple-element.65), channel_id=1, source_target_pairs={{0,1},{1,2},{2,3},{3,4},{4,5},{5,6},{6,7},{7,8},{8,9},{9,10},{10,1... | collective-permute-start | bytes 442376 | tf_op jit(solution)/shard_map/ppermute | solution.py:819
  48.4 0.0 collective-permute-start.11
  48.4 2.1 %collective-permute-done.10.cl = f32[36,8,128]{2,1,0:T(8,128)S(1)} collective-permute-done((f32[36,8,128]{2,1,0:T(8,128)S(1)}, f32[36,8,128]{2,1,0:T(8,128)S(1)}, u32[]{:S(2)}, u32[]{:S(2)}) %collective-permute-start.10) | collective-permute-done | bytes 147488 | tf_op jit(solution)/shard_map/ppermute | solution.py:819
  50.5 2.5 %collective-permute-done.11.cr = f32[36,8,128]{2,1,0:T(8,128)S(1)} collective-permute-done((f32[36,8,128]{2,1,0:T(8,128)S(1)}, f32[36,8,128]{2,1,0:T(8,128)S(1)}, u32[]{:S(2)}, u32[]{:S(2)}) %collective-permute-start.11) | collective-permute-done | bytes 147488 | tf_op jit(solution)/shard_map/ppermute | solution.py:819
  53.0 5.8 %shard_map.67 = (f32[8,16,8,256]{3,2,1,0:T(8,128)S(1)}, f32[8,16,8,256]{3,2,1,0:T(8,128)S(1)}, f32[1,128]{1,0:T(1,128)S(1)}, f32[1,128]{1,0:T(1,128)S(1)}) custom-call(f32[80,8,128]{2,1,0:T(8,128)S(1)} %get-tuple-element.60.own, f32[80,8,128]{2,1,0:T(8,128)S(1)} %collective-permute-done.6.left, f32[80,8,128]{2,1,0:T(8,128)S(1)} %collective-permute-done.7.right, ...), custom_call_target="tpu_custom_call" | custom-call | bytes 3000000 | tf_op jit(solution)/shard_map/pallas_call | solution.py:32
  58.8 0.1 collective-permute-start.12
  58.9 1.1 %collective-permute-done.12.b = f32[1,128]{1,0:T(1,128)S(1)} collective-permute-done((f32[1,128]{1,0:T(1,128)S(1)}, f32[1,128]{1,0:T(1,128)S(1)}, u32[]{:S(2)}, u32[]{:S(2)}) %collective-permute-start.12) | collective-permute-done | bytes 544 | tf_op jit(solution)/shard_map/ppermute | solution.py:906
  60.0 0.1 shard_map.68
  60.1 20.9 %all_to_all.5.parts = f32[256,1,128]{2,1,0:T(1,128)S(1)} all-to-all(f32[256,1,128]{2,1,0:T(1,128)S(1)} %shard_map.68), channel_id=1, replica_groups=mesh['gx'=16,'gy'=16] {'gx','gy'}, dimensions={0} | all-to-all | bytes 262144 | tf_op jit(solution)/shard_map/all_to_all | solution.py:908
  81.0 2.4 %shard_map.69 = (f32[8,8,16,256]{3,2,1,0:T(8,128)}, f32[1,8]{1,0:T(1,128)}) custom-call(f32[256,1,128]{2,1,0:T(1,128)S(1)} %all_to_all.5.parts, f32[8,16,8,256]{3,2,1,0:T(8,128)S(1)} %get-tuple-element.70.po, f32[8,16,8,256]{3,2,1,0:T(8,128)S(1)} %get-tuple-element.71.bo), custom_call_target="tpu_custom_call" | custom-call | bytes 3000000 | tf_op jit(solution)/shard_map/pallas_call | solution.py:32
  (1 shorter events, 0.0 us)
Async XLA Ops:
  0.6 8.3 %copy-start.3 = (f32[8,16,256]{2,1,0:T(8,128)S(1)}, f32[8,16,256]{2,1,0:T(8,128)}, u32[]{:S(2)}) copy-start(f32[8,16,256]{2,1,0:T(8,128)} %wz.3) | copy-start | bytes 393220
  0.6 8.3 %copy-start.2 = (f32[8,16,256]{2,1,0:T(8,128)S(1)}, f32[8,16,256]{2,1,0:T(8,128)}, u32[]{:S(2)}) copy-start(f32[8,16,256]{2,1,0:T(8,128)} %wy.3) | copy-start | bytes 393220
  0.7 8.3 %copy-start.1 = (f32[8,16,256]{2,1,0:T(8,128)S(1)}, f32[8,16,256]{2,1,0:T(8,128)}, u32[]{:S(2)}) copy-start(f32[8,16,256]{2,1,0:T(8,128)} %wx.3) | copy-start | bytes 393220
  0.7 8.3 %copy-start = (f32[8,8,16,256]{3,2,1,0:T(8,128)S(1)}, f32[8,8,16,256]{3,2,1,0:T(8,128)}, u32[]{:S(2)}) copy-start(f32[8,8,16,256]{3,2,1,0:T(8,128)} %v.3) | copy-start | bytes 3145732
  3.0 18.2 %collective-permute-start = (f32[31,16,256]{2,1,0:T(8,128)}, f32[31,16,256]{2,1,0:T(8,128)S(1)}, u32[]{:S(2)}, u32[]{:S(2)}) collective-permute-start(f32[31,16,256]{2,1,0:T(8,128)} %get-tuple-element.39), channel_id=1, source_target_pairs={{0,16},{16,32},{32,48},{48,64},{64,80},{80,96},{96,112},{112,128},... | collective-permute-start | bytes 1523720 | tf_op jit(solution)/shard_map/ppermute | solution.py:819
  5.1 16.1 %collective-permute-start.1 = (f32[30,16,256]{2,1,0:T(8,128)}, f32[30,16,256]{2,1,0:T(8,128)S(1)}, u32[]{:S(2)}, u32[]{:S(2)}) collective-permute-start(f32[30,16,256]{2,1,0:T(8,128)} %get-tuple-element.40), channel_id=1, source_target_pairs={{16,0},{32,16},{48,32},{64,48},{80,64},{96,80},{112,96},{128,112},... | collective-permute-start | bytes 1474568 | tf_op jit(solution)/shard_map/ppermute | solution.py:819
  9.6 6.2 %collective-permute-start.2 = (f32[36,8,256]{2,1,0:T(8,128)S(1)}, f32[36,8,256]{2,1,0:T(8,128)S(1)}, u32[]{:S(2)}, u32[]{:S(2)}) collective-permute-start(f32[36,8,256]{2,1,0:T(8,128)S(1)} %get-tuple-element.43), channel_id=1, source_target_pairs={{0,1},{1,2},{2,3},{3,4},{4,5},{5,6},{6,7},{7,8},{8,9},{9,10},{10,1... | collective-permute-start | bytes 884744 | tf_op jit(solution)/shard_map/ppermute | solution.py:819
  12.2 6.4 %collective-permute-start.3 = (f32[36,8,256]{2,1,0:T(8,128)S(1)}, f32[36,8,256]{2,1,0:T(8,128)S(1)}, u32[]{:S(2)}, u32[]{:S(2)}) collective-permute-start(f32[36,8,256]{2,1,0:T(8,128)S(1)} %get-tuple-element.44), channel_id=1, source_target_pairs={{1,0},{2,1},{3,2},{4,3},{5,4},{6,5},{7,6},{8,7},{9,8},{10,9},{11,1... | collective-permute-start | bytes 884744 | tf_op jit(solution)/shard_map/ppermute | solution.py:819
  21.4 6.7 %collective-permute-start.4 = (f32[10,8,256]{2,1,0:T(8,128)S(1)}, f32[10,8,256]{2,1,0:T(8,128)S(1)}, u32[]{:S(2)}, u32[]{:S(2)}) collective-permute-start(f32[10,8,256]{2,1,0:T(8,128)S(1)} %get-tuple-element.58), channel_id=1, source_target_pairs={{0,1},{1,2},{2,3},{3,4},{4,5},{5,6},{6,7},{7,8},{8,9},{9,10},{10,1... | collective-permute-start | bytes 245768 | tf_op jit(solution)/shard_map/ppermute | solution.py:819
  23.3 4.8 %collective-permute-start.5 = (f32[10,8,256]{2,1,0:T(8,128)S(1)}, f32[10,8,256]{2,1,0:T(8,128)S(1)}, u32[]{:S(2)}, u32[]{:S(2)}) collective-permute-start(f32[10,8,256]{2,1,0:T(8,128)S(1)} %get-tuple-element.59), channel_id=1, source_target_pairs={{1,0},{2,1},{3,2},{4,3},{5,4},{6,5},{7,6},{8,7},{9,8},{10,9},{11,1... | collective-permute-start | bytes 245768 | tf_op jit(solution)/shard_map/ppermute | solution.py:819
  28.8 11.0 %collective-permute-start.7 = (f32[80,8,128]{2,1,0:T(8,128)S(1)}, f32[80,8,128]{2,1,0:T(8,128)S(1)}, u32[]{:S(2)}, u32[]{:S(2)}) collective-permute-start(f32[80,8,128]{2,1,0:T(8,128)S(1)} %get-tuple-element.60.own), channel_id=1, source_target_pairs={{16,0},{32,16},{48,32},{64,48},{80,64},{96,80},{112,96},{128,112},... | collective-permute-start | bytes 983048 | tf_op jit(solution)/shard_map/ppermute | solution.py:819
  33.4 9.2 %collective-permute-start.6 = (f32[80,8,128]{2,1,0:T(8,128)S(1)}, f32[80,8,128]{2,1,0:T(8,128)S(1)}, u32[]{:S(2)}, u32[]{:S(2)}) collective-permute-start(f32[80,8,128]{2,1,0:T(8,128)S(1)} %get-tuple-element.60.own), channel_id=1, source_target_pairs={{0,16},{16,32},{32,48},{48,64},{64,80},{80,96},{96,112},{112,128},... | collective-permute-start | bytes 983048 | tf_op jit(solution)/shard_map/ppermute | solution.py:819
  33.4 4.0 %collective-permute-start.8 = (f32[32,8,128]{2,1,0:T(8,128)S(1)}, f32[32,8,128]{2,1,0:T(8,128)S(1)}, u32[]{:S(2)}, u32[]{:S(2)}) collective-permute-start(f32[32,8,128]{2,1,0:T(8,128)S(1)} %get-tuple-element.61), channel_id=1, source_target_pairs={{0,1},{1,2},{2,3},{3,4},{4,5},{5,6},{6,7},{7,8},{8,9},{9,10},{10,1... | collective-permute-start | bytes 393224 | tf_op jit(solution)/shard_map/ppermute | solution.py:819
  35.4 4.4 %collective-permute-start.9 = (f32[32,8,128]{2,1,0:T(8,128)S(1)}, f32[32,8,128]{2,1,0:T(8,128)S(1)}, u32[]{:S(2)}, u32[]{:S(2)}) collective-permute-start(f32[32,8,128]{2,1,0:T(8,128)S(1)} %get-tuple-element.62), channel_id=1, source_target_pairs={{1,0},{2,1},{3,2},{4,3},{5,4},{6,5},{7,6},{8,7},{9,8},{10,9},{11,1... | collective-permute-start | bytes 393224 | tf_op jit(solution)/shard_map/ppermute | solution.py:819
  42.7 7.8 %collective-permute-start.10 = (f32[36,8,128]{2,1,0:T(8,128)S(1)}, f32[36,8,128]{2,1,0:T(8,128)S(1)}, u32[]{:S(2)}, u32[]{:S(2)}) collective-permute-start(f32[36,8,128]{2,1,0:T(8,128)S(1)} %get-tuple-element.65), channel_id=1, source_target_pairs={{0,1},{1,2},{2,3},{3,4},{4,5},{5,6},{6,7},{7,8},{8,9},{9,10},{10,1... | collective-permute-start | bytes 442376 | tf_op jit(solution)/shard_map/ppermute | solution.py:819
  48.4 4.6 %collective-permute-start.11 = (f32[36,8,128]{2,1,0:T(8,128)S(1)}, f32[36,8,128]{2,1,0:T(8,128)S(1)}, u32[]{:S(2)}, u32[]{:S(2)}) collective-permute-start(f32[36,8,128]{2,1,0:T(8,128)S(1)} %get-tuple-element.66), channel_id=1, source_target_pairs={{1,0},{2,1},{3,2},{4,3},{5,4},{6,5},{7,6},{8,7},{9,8},{10,9},{11,1... | collective-permute-start | bytes 442376 | tf_op jit(solution)/shard_map/ppermute | solution.py:819
  58.8 1.2 %collective-permute-start.12 = (f32[1,128]{1,0:T(1,128)S(1)}, f32[1,128]{1,0:T(1,128)S(1)}, u32[]{:S(2)}, u32[]{:S(2)}) collective-permute-start(f32[1,128]{1,0:T(1,128)S(1)} %get-tuple-element.69), channel_id=1, source_target_pairs={{0,1},{1,0},{2,3},{3,2},{4,5},{5,4},{6,7},{7,6},{8,9},{9,8},{10,11... | collective-permute-start | bytes 1544 | tf_op jit(solution)/shard_map/ppermute | solution.py:906

commit v7 on v6

--- a/solution.py
+++ b/solution.py
@@ -222,17 +222,6 @@
         n += 1
 
 
-def planes(radius, body, own, halo):
-    def step(n, _):
-        body(n + halo, radius)
-        return 0
-
-    lax.fori_loop(0, own, step, 0)
-    for d in range(1, radius + 1):
-        body(halo - d, radius - d)
-        body(halo + own - 1 + d, radius - d)
-
-
 SUM, EVEN, ODD = 0, 1, 2
 
 
@@ -585,32 +574,33 @@
         n += 2
 
 
-def coarse_level(
-    own, left, right, yl, yr, cl, cr, gl, gr, pb, NW, NE, nd, po, bo, mine, other, F, EA, EB, EX, CW, R
-):
-    def put(i, j, half, f):
-        f = OMEGA * f
-        F[i, j, half] = f
-
-    for x in range(CX):
-        for half in range(2):
-            for y in range(CY):
-                at = 2 * (x * CY + y) + half
-                put(x, y + CH, half, left[at])
-                put(x + CH, y + CH, half, own[at])
-                put(x + CH + CX, y + CH, half, right[at])
-            for y in range(CH):
-                put(x + CH, y, half, yl[2 * (x * CH + y) + half])
-                put(x + CH, y + CH + CY, half, yr[2 * (x * CH + y) + half])
-    n = 0
-    for side in range(2):
-        for dx, dy in CCELLS:
-            i = CH + CX - 1 + dx if side else CH - dx
-            for half in range(2):
-                put(i, CH - dy, half, cl[n])
-                put(i, CH + CY - 1 + dy, half, cr[n])
-                n += 1
-
+def beyond(i, j):
+    return max(CH - i, i - CH - CX + 1, 0), max(CH - j, j - CH - CY + 1, 0)
+
+
+def cells_within(radius):
+    every = [(i, j) for i in range(CX + 2 * CH) for j in range(CY + 2 * CH)]
+    return [c for c in every if sum(beyond(*c)) <= radius]
+
+
+def early(before, radius):
+    out = set()
+    for i, j in cells_within(radius):
+        dx, dy = beyond(i, j)
+        if dx and not CH < j < CH + CY - 1 or dy and not CH < i < CH + CX - 1:
+            continue
+        if {(i, j), (i + 1, j), (i - 1, j), (i, j + 1), (i, j - 1)} <= before:
+            out.add((i, j))
+    return out
+
+
+EARLY0 = {c for c in cells_within(CH) if 0 in beyond(*c)}
+EARLY1 = early(EARLY0, 3)
+EARLY2 = early(EARLY1, 2)
+EARLY3 = early(EARLY2, 1)
+
+
+def coarse_weights(own, left, right, gl, gr, corner, CW, R):
     for a in range(4):
         for i in range(CX + 2 * CH):
             p = i - CH
@@ -619,9 +609,9 @@
             if 0 <= p < CX:
                 lo = coarse_rows(gl, H * LX + LX + p, a)
                 hi = coarse_rows(gr, H * LX + LX + p, a)
-            elif p in CWP:
-                m, r = n + 2 * CWP.index(p) + (a >> 1), 4 * (a & 1)
-                lo, hi = cl[m, r : r + 4], cr[m, r : r + 4]
+            elif corner and p in CWP:
+                m, r = 4 * len(CCELLS) + 2 * CWP.index(p) + (a >> 1), 4 * (a & 1)
+                lo, hi = corner[0][m, r : r + 4], corner[1][m, r : r + 4]
             else:
                 continue
             R[a, i, JC - 4 : JC] = lo
@@ -634,36 +624,99 @@
         for a in range(6):
             CW[a, i] = ws[a] * inv
 
-    def sweep(src, dst):
-        def body(i, reach):
-            for j in range(CH - reach, CH + CY + reach):
-                r = j - CH + JC
-                ws = [row(CW, a, i, r) for a in range(6)]
-                for half in range(2):
-                    c = src[i, j, half]
-                    dst[i, j, half] = (
-                        (1.0 - OMEGA) * c
-                        + F[i, j, half]
-                        + ws[0] * src[i + 1, j, half]
-                        + ws[1] * src[i - 1, j, half]
-                        + ws[2] * src[i, j + 1, half]
-                        + ws[3] * src[i, j - 1, half]
-                        + ws[4] * up_z(c)
-                        + ws[5] * down_z(c)
-                    )
-
-        return body
-
-    planes(3, sweep(F, EB), CX, CH)
-    planes(2, sweep(EB, EA), CX, CH)
-    planes(1, sweep(EA, EB), CX, CH)
-
-    def spread(i, reach):
-        for j in range(CH - reach, CH + CY + reach):
+
+def sweep(cells, at, f, CW, dst):
+    for i, j in cells:
+        ws = [row(CW, a, i, j - CH + JC) for a in range(6)]
+        for half in range(2):
+            c = at(i, j, half)
+            dst[i, j, half] = (
+                (1.0 - OMEGA) * c
+                + f(i, j, half)
+                + ws[0] * at(i + 1, j, half)
+                + ws[1] * at(i - 1, j, half)
+                + ws[2] * at(i, j + 1, half)
+                + ws[3] * at(i, j - 1, half)
+                + ws[4] * up_z(c)
+                + ws[5] * down_z(c)
+            )
+
+
+def coarse_early(own, left, right, yl, yr, gl, gr, F, E1, E2, E3, CW, R):
+    for x in range(CX):
+        for half in range(2):
+            for y in range(CY):
+                at = 2 * (x * CY + y) + half
+                F[x, y + CH, half] = OMEGA * left[at]
+                F[x + CH, y + CH, half] = OMEGA * own[at]
+                F[x + CH + CX, y + CH, half] = OMEGA * right[at]
+            for y in range(CH):
+                F[x + CH, y, half] = OMEGA * yl[2 * (x * CH + y) + half]
+                F[x + CH, y + CH + CY, half] = OMEGA * yr[2 * (x * CH + y) + half]
+    coarse_weights(own, left, right, gl, gr, None, CW, R)
+
+    def of(ref):
+        return lambda i, j, half: ref[i, j, half]
+
+    sweep(sorted(EARLY1), of(F), of(F), CW, E1)
+    sweep(sorted(EARLY2), of(E1), of(F), CW, E2)
+    sweep(sorted(EARLY3), of(E2), of(F), CW, E3)
+
+
+def coarse_level(
+    own,
+    left,
+    right,
+    cl,
+    cr,
+    gl,
+    gr,
+    F,
+    E1,
+    E2,
+    E3,
+    pb,
+    NW,
+    NE,
+    nd,
+    po,
+    bo,
+    mine,
+    other,
+    X1,
+    X2,
+    X3,
+    EX,
+    CW,
+    R,
+):
+    coarse_weights(own, left, right, gl, gr, (cl, cr), CW, R)
+    corner = {}
+    n = 0
+    for side in range(2):
+        for dx, dy in CCELLS:
+            i = CH + CX - 1 + dx if side else CH - dx
             for half in range(2):
-                EX[i, j, half] = expand(EB[i, j, half])
-
-    planes(1, spread, CX, CH)
+                corner[i, CH - dy, half] = cl, n
+                corner[i, CH + CY - 1 + dy, half] = cr, n
+                n += 1
+
+    def f(i, j, half):
+        if (i, j, half) in corner:
+            msg, n = corner[i, j, half]
+            return OMEGA * msg[n]
+        return F[i, j, half]
+
+    def both(first, cells, then):
+        return lambda i, j, half: (first if (i, j) in cells else then)[i, j, half]
+
+    e1, e2, e3 = both(E1, EARLY1, X1), both(E2, EARLY2, X2), both(E3, EARLY3, X3)
+    sweep([c for c in cells_within(3) if c not in EARLY1], f, f, CW, X1)
+    sweep([c for c in cells_within(2) if c not in EARLY2], e1, f, CW, X2)
+    sweep([c for c in cells_within(1) if c not in EARLY3], e2, f, CW, X3)
+    for i, j in cells_within(1):
+        for half in range(2):
+            EX[i, j, half] = expand(e3(i, j, half))
 
     for x in range(CX):
         for y in range(CY):
@@ -778,8 +831,10 @@
             for b in range(j + 1, a + 1):
                 g[a, b] = g[a, b] - low[a, j] * low[b, j]
 
+    sub = lax.broadcasted_iota(jnp.int32, (8, 128), 0)
+    lam_rows = jnp.zeros((8, 128), jnp.float32)
     for k in range(K):
-        SP[8 * k : 8 * k + 8] = lam[k]
+        lam_rows = jnp.where(sub == k, lam[k], lam_rows)
         SP[64 + 8 * k : 72 + 8 * k] = inv[k]
     at = {}
     for n, (a, b) in enumerate(sorted(low)):
@@ -790,11 +845,11 @@
         for t in range(0, LY, 8):
             for h in range(0, NZ, 128):
                 z = slice(h, h + 128)
-                p = jnp.swapaxes(po[x, t : t + 8, :, z], 0, 1)
-                b = jnp.swapaxes(bo[x, t : t + 8, :, z], 0, 1)
+                upd = po[x, t : t + 8, :, z] + lam_rows[None] * bo[x, t : t + 8, :, z]
+                upd = jnp.swapaxes(upd, 0, 1)
                 done = []
                 for k in range(K):
-                    u = p[k] + SP[8 * k : 8 * k + 8] * b[k]
+                    u = upd[k]
                     for j in range(k):
                         u = u - SP[at[k, j] : at[k, j] + 8] * done[j]
                     u = u * SP[64 + 8 * k : 72 + 8 * k]
@@ -888,18 +943,15 @@
     cu, cd = call(coarse_corner_send, [(NCC, 8, CZ)] * 2, (left, right, nd, fl, fr))
     cl, cr = both_ways(cu, cd, "gy")
     cext = (CX + 2 * CH, CY + 2 * CH, 2, 8, CZ)
+    weights = [(6, CX + 2 * CH, 24, CZ), (4, CX + 2 * CH, 24, CZ)]
+    early_ = call(
+        coarse_early, [cext] * 4, (f, left, right, fl, fr, yl, yr), weights, us=2
+    )
     po, bo, mine, other = call(
         coarse_level,
         [(LX, LY, K, NZ), (LX, LY, K, NZ), (1, 128), (1, 128)],
-        (f, left, right, fl, fr, cl, cr, yl, yr, pb, NW, NE, nd),
-        [
-            cext,
-            cext,
-            cext,
-            (CX + 2 * CH, CY + 2 * CH, 2, 8, NZ),
-            (6, CX + 2 * CH, 24, CZ),
-            (4, CX + 2 * CH, 24, CZ),
-        ],
+        (f, left, right, cl, cr, yl, yr, *early_, pb, NW, NE, nd),
+        [cext, cext, cext, (CX + 2 * CH, CY + 2 * CH, 2, 8, NZ)] + weights,
         limit=12,
     )
     n = lax.axis_size("gy")

time: 83.6 us -> 81.8 us (0.978)
  starting transfers between devices: 24.2 us -> 21.4 us
  local copies, waits for them, and re-layouts: 0.02 us -> 2.72 us
  Pallas kernels: 20.2 us -> 19.3 us
  waiting for transfers between devices: 17.4 us -> 16.5 us
    ppermute x12, starting transfers between devices: 24.1 us -> 21.3 us  [both_ways(): return (lax.ppermute(up, axis, fwd), lax.ppermute(down, axis, back))]
    unnamed x8, local copies, waits for them, and re-layouts: 0.02 us -> 2.72 us
    ppermute x12, waiting for transfers between devices: 16.2 us -> 15.4 us  [both_ways(): return (lax.ppermute(up, axis, fwd), lax.ppermute(down, axis, back))]
    pallas_call x11 -> x12, Pallas kernels: 20.2 us -> 19.3 us  [call(): pl.pallas_call(body, out_shape=[jax.ShapeDtypeStruct(s, jnp.float32) for...]
  transfers between devices with their start and end apart: 13 -> 13, of which waited for: 8 -> 8; matrix products, arithmetic and copies ran while one was open for 0% -> 0% of each run, Pallas kernels for 10% -> 12%
where the time goes in v7:
time: 81.8 us; the launch traced here: 81.6 us
  starting transfers between devices  21.4 us (26%)
  blocking collectives  20.9 us (26%)
  Pallas kernels  19.3 us (24%)
  waiting for transfers between devices  16.5 us (20%)
  local copies, waits for them, and re-layouts  2.72 us (3%)
    ppermute x12, starting transfers between devices, both_ways(): return (lax.ppermute(up, axis, fwd), lax.ppermute(down, axis, back))  21.3 us
    all_to_all x1, blocking collectives, per_device(): parts = lax.all_to_all(sums, ('gx', 'gy'), 0, 0)  20.9 us
    pallas_call x12, Pallas kernels, call(): pl.pallas_call(body, out_shape=[jax.ShapeDtypeStruct(s, jnp.float32) for...  19.3 us
    ppermute x12, waiting for transfers between devices, both_ways(): return (lax.ppermute(up, axis, fwd), lax.ppermute(down, axis, back))  15.4 us
    unnamed x8, local copies, waits for them, and re-layouts  2.72 us
  transfers between devices with their start and end apart: 13, of which 8 were waited for; matrix products, arithmetic and copies ran while one was open for 0% of the time, Pallas kernels for 12%

profile of v7, /device:TPU:1, one launch (start us, length us, event | category | flops | bytes accessed | tf_op | source)
XLA Modules:
  0.0 81.6 jit_solution(8746117444281498242)
XLA Ops:
  0.6 0.0 copy-start
  0.6 2.3 %shard_map.60 = (f32[31,16,256]{2,1,0:T(8,128)}, f32[30,16,256]{2,1,0:T(8,128)}) custom-call(f32[8,8,16,256]{3,2,1,0:T(8,128)} %v.3, f32[8,16,256]{2,1,0:T(8,128)} %wx.3, f32[8,16,256]{2,1,0:T(8,128)} %wy.3, f32[8,16,256]{2,1,0:T(8,128)} %wz.3), custom_call_target="tpu_custom_call" | custom-call | bytes 3000000 | tf_op jit(solution)/shard_map/pallas_call | solution.py:32
  2.9 2.1 %collective-permute-start = (f32[31,16,256]{2,1,0:T(8,128)}, f32[31,16,256]{2,1,0:T(8,128)S(1)}, u32[]{:S(2)}, u32[]{:S(2)}) collective-permute-start(f32[31,16,256]{2,1,0:T(8,128)} %get-tuple-element.43), channel_id=1, source_target_pairs={{0,16},{16,32},{32,48},{48,64},{64,80},{80,96},{96,112},{112,128},... | collective-permute-start | bytes 1523720 | tf_op jit(solution)/shard_map/ppermute | solution.py:874
  5.0 3.8 %collective-permute-start.1 = (f32[30,16,256]{2,1,0:T(8,128)}, f32[30,16,256]{2,1,0:T(8,128)S(1)}, u32[]{:S(2)}, u32[]{:S(2)}) collective-permute-start(f32[30,16,256]{2,1,0:T(8,128)} %get-tuple-element.44), channel_id=1, source_target_pairs={{16,0},{32,16},{48,32},{64,48},{80,64},{96,80},{112,96},{128,112},... | collective-permute-start | bytes 1474568 | tf_op jit(solution)/shard_map/ppermute | solution.py:874
  8.8 0.0 copy-done
  8.8 0.0 copy-start.1
  8.9 0.9 %copy-done.1 = f32[8,16,256]{2,1,0:T(8,128)S(1)} copy-done((f32[8,16,256]{2,1,0:T(8,128)S(1)}, f32[8,16,256]{2,1,0:T(8,128)}, u32[]{:S(2)}) %copy-start.1) | copy-done | bytes 131096
  9.8 0.0 copy-start.2
  9.8 0.9 %copy-done.2 = f32[8,16,256]{2,1,0:T(8,128)S(1)} copy-done((f32[8,16,256]{2,1,0:T(8,128)S(1)}, f32[8,16,256]{2,1,0:T(8,128)}, u32[]{:S(2)}) %copy-start.2) | copy-done | bytes 131096
  10.7 0.0 copy-start.3
  10.7 0.9 %copy-done.3 = f32[8,16,256]{2,1,0:T(8,128)S(1)} copy-done((f32[8,16,256]{2,1,0:T(8,128)S(1)}, f32[8,16,256]{2,1,0:T(8,128)}, u32[]{:S(2)}) %copy-start.3) | copy-done | bytes 131096
  11.6 0.7 shard_map.59
  12.3 2.5 %collective-permute-start.2 = (f32[36,8,256]{2,1,0:T(8,128)S(1)}, f32[36,8,256]{2,1,0:T(8,128)S(1)}, u32[]{:S(2)}, u32[]{:S(2)}) collective-permute-start(f32[36,8,256]{2,1,0:T(8,128)S(1)} %get-tuple-element.47), channel_id=1, source_target_pairs={{0,1},{1,2},{2,3},{3,4},{4,5},{5,6},{6,7},{7,8},{8,9},{9,10},{10,1... | collective-permute-start | bytes 884744 | tf_op jit(solution)/shard_map/ppermute | solution.py:874
  14.8 0.2 collective-permute-start.3
  15.0 3.4 %collective-permute-done.2.yl.gl = f32[36,8,256]{2,1,0:T(8,128)S(1)} collective-permute-done((f32[36,8,256]{2,1,0:T(8,128)S(1)}, f32[36,8,256]{2,1,0:T(8,128)S(1)}, u32[]{:S(2)}, u32[]{:S(2)}) %collective-permute-start.2) | collective-permute-done | bytes 294944 | tf_op jit(solution)/shard_map/ppermute | solution.py:874
  18.5 2.8 %collective-permute-done.3.yr.gr = f32[36,8,256]{2,1,0:T(8,128)S(1)} collective-permute-done((f32[36,8,256]{2,1,0:T(8,128)S(1)}, f32[36,8,256]{2,1,0:T(8,128)S(1)}, u32[]{:S(2)}, u32[]{:S(2)}) %collective-permute-start.3) | collective-permute-done | bytes 294944 | tf_op jit(solution)/shard_map/ppermute | solution.py:874
  21.2 2.7 %shard_map.61 = (f32[3,8,32,256]{3,2,1,0:T(8,128)S(1)}, f32[7,7,32,256]{3,2,1,0:T(8,128)S(1)}, f32[6,22,8,256]{3,2,1,0:T(8,128)S(1)}, f32[4,22,8,256]{3,2,1,0:T(8,128)S(1)}, f32[2,22,8,256]{3,2,1,0:T(8,128)S(1)}) custom-call(f32[8,16,8,256]{3,2,1,0:T(8,128)S(1)} %get-tuple-element.42.vt, f32[3,8,16,256]{3,2,1,0:T(8,128)S(1)} %get-tuple-element.45.wm, ...), custom_call_target="tpu_custom_call" | custom-call | bytes 9000000 | tf_op jit(solution)/shard_map/pallas_call | solution.py:32
  24.0 0.0 collective-permute-done.1.rr
  24.0 0.0 collective-permute-done.rl
  24.0 0.2 shard_map.62
  24.2 0.0 collective-permute-start.4
  24.2 1.4 %collective-permute-start.5 = (f32[10,8,256]{2,1,0:T(8,128)S(1)}, f32[10,8,256]{2,1,0:T(8,128)S(1)}, u32[]{:S(2)}, u32[]{:S(2)}) collective-permute-start(f32[10,8,256]{2,1,0:T(8,128)S(1)} %get-tuple-element.63), channel_id=1, source_target_pairs={{1,0},{2,1},{3,2},{4,3},{5,4},{6,5},{7,6},{8,7},{9,8},{10,9},{11,1... | collective-permute-start | bytes 245768 | tf_op jit(solution)/shard_map/ppermute | solution.py:874
  25.6 4.9 %shard_map.63 = (f32[7,5,16,256]{3,2,1,0:T(8,128)S(1)}, f32[6,22,8,256]{3,2,1,0:T(8,128)S(1)}, f32[6,22,8,256]{3,2,1,0:T(8,128)S(1)}, f32[6,22,8,256]{3,2,1,0:T(...) custom-call(f32[8,16,8,256]{3,2,1,0:T(8,128)S(1)} %get-tuple-element.42.vt, ...), custom_call_target="tpu_custom_call" | custom-call | bytes 12000000 | tf_op jit(solution)/shard_map/pallas_call | solution.py:32
  30.5 0.0 collective-permute-done.4.cl
  30.5 0.0 collective-permute-done.5.cr
  30.5 0.7 shard_map.64
  31.2 2.2 %collective-permute-start.7 = (f32[80,8,128]{2,1,0:T(8,128)S(1)}, f32[80,8,128]{2,1,0:T(8,128)S(1)}, u32[]{:S(2)}, u32[]{:S(2)}) collective-permute-start(f32[80,8,128]{2,1,0:T(8,128)S(1)} %get-tuple-element.64.own), channel_id=1, source_target_pairs={{16,0},{32,16},{48,32},{64,48},{80,64},{96,80},{112,96},{128,112},... | collective-permute-start | bytes 983048 | tf_op jit(solution)/shard_map/ppermute | solution.py:874
  33.4 0.0 collective-permute-start.6
  33.4 2.0 %collective-permute-start.8 = (f32[32,8,128]{2,1,0:T(8,128)S(1)}, f32[32,8,128]{2,1,0:T(8,128)S(1)}, u32[]{:S(2)}, u32[]{:S(2)}) collective-permute-start(f32[32,8,128]{2,1,0:T(8,128)S(1)} %get-tuple-element.67), channel_id=1, source_target_pairs={{0,1},{1,2},{2,3},{3,4},{4,5},{5,6},{6,7},{7,8},{8,9},{9,10},{10,1... | collective-permute-start | bytes 393224 | tf_op jit(solution)/shard_map/ppermute | solution.py:874
  35.4 1.2 %collective-permute-start.9 = (f32[32,8,128]{2,1,0:T(8,128)S(1)}, f32[32,8,128]{2,1,0:T(8,128)S(1)}, u32[]{:S(2)}, u32[]{:S(2)}) collective-permute-start(f32[32,8,128]{2,1,0:T(8,128)S(1)} %get-tuple-element.68), channel_id=1, source_target_pairs={{1,0},{2,1},{3,2},{4,3},{5,4},{6,5},{7,6},{8,7},{9,8},{10,9},{11,1... | collective-permute-start | bytes 393224 | tf_op jit(solution)/shard_map/ppermute | solution.py:874
  36.6 0.6 shard_map.65
  37.2 0.2 collective-permute-done.8.yl
  37.4 2.7 %collective-permute-done.9.yr = f32[32,8,128]{2,1,0:T(8,128)S(1)} collective-permute-done((f32[32,8,128]{2,1,0:T(8,128)S(1)}, f32[32,8,128]{2,1,0:T(8,128)S(1)}, u32[]{:S(2)}, u32[]{:S(2)}) %collective-permute-start.9) | collective-permute-done | bytes 131104 | tf_op jit(solution)/shard_map/ppermute | solution.py:874
  40.1 0.0 collective-permute-done.7.right
  40.1 2.5 %collective-permute-done.6.left = f32[80,8,128]{2,1,0:T(8,128)S(1)} collective-permute-done((f32[80,8,128]{2,1,0:T(8,128)S(1)}, f32[80,8,128]{2,1,0:T(8,128)S(1)}, u32[]{:S(2)}, u32[]{:S(2)}) %collective-permute-start.6) | collective-permute-done | bytes 327712 | tf_op jit(solution)/shard_map/ppermute | solution.py:874
  42.7 5.7 %collective-permute-start.10 = (f32[36,8,128]{2,1,0:T(8,128)S(1)}, f32[36,8,128]{2,1,0:T(8,128)S(1)}, u32[]{:S(2)}, u32[]{:S(2)}) collective-permute-start(f32[36,8,128]{2,1,0:T(8,128)S(1)} %get-tuple-element.69), channel_id=1, source_target_pairs={{0,1},{1,2},{2,3},{3,4},{4,5},{5,6},{6,7},{7,8},{8,9},{9,10},{10,1... | collective-permute-start | bytes 442376 | tf_op jit(solution)/shard_map/ppermute | solution.py:874
  48.4 0.0 collective-permute-start.11
  48.4 0.8 shard_map.67
  49.2 1.3 %collective-permute-done.10.cl = f32[36,8,128]{2,1,0:T(8,128)S(1)} collective-permute-done((f32[36,8,128]{2,1,0:T(8,128)S(1)}, f32[36,8,128]{2,1,0:T(8,128)S(1)}, u32[]{:S(2)}, u32[]{:S(2)}) %collective-permute-start.10) | collective-permute-done | bytes 147488 | tf_op jit(solution)/shard_map/ppermute | solution.py:874
  50.5 2.5 %collective-permute-done.11.cr = f32[36,8,128]{2,1,0:T(8,128)S(1)} collective-permute-done((f32[36,8,128]{2,1,0:T(8,128)S(1)}, f32[36,8,128]{2,1,0:T(8,128)S(1)}, u32[]{:S(2)}, u32[]{:S(2)}) %collective-permute-start.11) | collective-permute-done | bytes 147488 | tf_op jit(solution)/shard_map/ppermute | solution.py:874
  53.0 4.1 %shard_map.68 = (f32[8,16,8,256]{3,2,1,0:T(8,128)S(1)}, f32[8,16,8,256]{3,2,1,0:T(8,128)S(1)}, f32[1,128]{1,0:T(1,128)S(1)}, f32[1,128]{1,0:T(1,128)S(1)}) custom-call(f32[80,8,128]{2,1,0:T(8,128)S(1)} %get-tuple-element.64.own, f32[80,8,128]{2,1,0:T(8,128)S(1)} %collective-permute-done.6.left, f32[80,8,128]{2,1,0:T(8,128)S(1)} %collective-permute-done.7.right, ...), custom_call_target="tpu_custom_call" | custom-call | bytes 3000000 | tf_op jit(solution)/shard_map/pallas_call | solution.py:32
  57.1 0.1 collective-permute-start.12
  57.2 1.1 %collective-permute-done.12.b = f32[1,128]{1,0:T(1,128)S(1)} collective-permute-done((f32[1,128]{1,0:T(1,128)S(1)}, f32[1,128]{1,0:T(1,128)S(1)}, u32[]{:S(2)}, u32[]{:S(2)}) %collective-permute-start.12) | collective-permute-done | bytes 544 | tf_op jit(solution)/shard_map/ppermute | solution.py:958
  58.3 0.1 shard_map.69
  58.4 20.9 %all_to_all.5.parts = f32[256,1,128]{2,1,0:T(1,128)S(1)} all-to-all(f32[256,1,128]{2,1,0:T(1,128)S(1)} %shard_map.69), channel_id=1, replica_groups=mesh['gx'=16,'gy'=16] {'gx','gy'}, dimensions={0} | all-to-all | bytes 262144 | tf_op jit(solution)/shard_map/all_to_all | solution.py:960
  79.3 2.3 %shard_map.70 = (f32[8,8,16,256]{3,2,1,0:T(8,128)}, f32[1,8]{1,0:T(1,128)}) custom-call(f32[256,1,128]{2,1,0:T(1,128)S(1)} %all_to_all.5.parts, f32[8,16,8,256]{3,2,1,0:T(8,128)S(1)} %get-tuple-element.78.po, f32[8,16,8,256]{3,2,1,0:T(8,128)S(1)} %get-tuple-element.79.bo), custom_call_target="tpu_custom_call" | custom-call | bytes 3000000 | tf_op jit(solution)/shard_map/pallas_call | solution.py:32
  (1 shorter events, 0.0 us)
Async XLA Ops:
  0.6 8.2 %copy-start = (f32[8,8,16,256]{3,2,1,0:T(8,128)S(1)}, f32[8,8,16,256]{3,2,1,0:T(8,128)}, u32[]{:S(2)}) copy-start(f32[8,8,16,256]{3,2,1,0:T(8,128)} %v.3) | copy-start | bytes 3145732
  2.9 21.1 %collective-permute-start = (f32[31,16,256]{2,1,0:T(8,128)}, f32[31,16,256]{2,1,0:T(8,128)S(1)}, u32[]{:S(2)}, u32[]{:S(2)}) collective-permute-start(f32[31,16,256]{2,1,0:T(8,128)} %get-tuple-element.43), channel_id=1, source_target_pairs={{0,16},{16,32},{32,48},{48,64},{64,80},{80,96},{96,112},{112,128},... | collective-permute-start | bytes 1523720 | tf_op jit(solution)/shard_map/ppermute | solution.py:874
  5.0 18.9 %collective-permute-start.1 = (f32[30,16,256]{2,1,0:T(8,128)}, f32[30,16,256]{2,1,0:T(8,128)S(1)}, u32[]{:S(2)}, u32[]{:S(2)}) collective-permute-start(f32[30,16,256]{2,1,0:T(8,128)} %get-tuple-element.44), channel_id=1, source_target_pairs={{16,0},{32,16},{48,32},{64,48},{80,64},{96,80},{112,96},{128,112},... | collective-permute-start | bytes 1474568 | tf_op jit(solution)/shard_map/ppermute | solution.py:874
  8.8 0.9 %copy-start.1 = (f32[8,16,256]{2,1,0:T(8,128)S(1)}, f32[8,16,256]{2,1,0:T(8,128)}, u32[]{:S(2)}) copy-start(f32[8,16,256]{2,1,0:T(8,128)} %wx.3) | copy-start | bytes 393220
  9.8 0.9 %copy-start.2 = (f32[8,16,256]{2,1,0:T(8,128)S(1)}, f32[8,16,256]{2,1,0:T(8,128)}, u32[]{:S(2)}) copy-start(f32[8,16,256]{2,1,0:T(8,128)} %wy.3) | copy-start | bytes 393220
  10.7 0.9 %copy-start.3 = (f32[8,16,256]{2,1,0:T(8,128)S(1)}, f32[8,16,256]{2,1,0:T(8,128)}, u32[]{:S(2)}) copy-start(f32[8,16,256]{2,1,0:T(8,128)} %wz.3) | copy-start | bytes 393220
  12.3 6.2 %collective-permute-start.2 = (f32[36,8,256]{2,1,0:T(8,128)S(1)}, f32[36,8,256]{2,1,0:T(8,128)S(1)}, u32[]{:S(2)}, u32[]{:S(2)}) collective-permute-start(f32[36,8,256]{2,1,0:T(8,128)S(1)} %get-tuple-element.47), channel_id=1, source_target_pairs={{0,1},{1,2},{2,3},{3,4},{4,5},{5,6},{6,7},{7,8},{8,9},{9,10},{10,1... | collective-permute-start | bytes 884744 | tf_op jit(solution)/shard_map/ppermute | solution.py:874
  14.8 6.4 %collective-permute-start.3 = (f32[36,8,256]{2,1,0:T(8,128)S(1)}, f32[36,8,256]{2,1,0:T(8,128)S(1)}, u32[]{:S(2)}, u32[]{:S(2)}) collective-permute-start(f32[36,8,256]{2,1,0:T(8,128)S(1)} %get-tuple-element.48), channel_id=1, source_target_pairs={{1,0},{2,1},{3,2},{4,3},{5,4},{6,5},{7,6},{8,7},{9,8},{10,9},{11,1... | collective-permute-start | bytes 884744 | tf_op jit(solution)/shard_map/ppermute | solution.py:874
  24.2 6.3 %collective-permute-start.4 = (f32[10,8,256]{2,1,0:T(8,128)S(1)}, f32[10,8,256]{2,1,0:T(8,128)S(1)}, u32[]{:S(2)}, u32[]{:S(2)}) collective-permute-start(f32[10,8,256]{2,1,0:T(8,128)S(1)} %get-tuple-element.62), channel_id=1, source_target_pairs={{0,1},{1,2},{2,3},{3,4},{4,5},{5,6},{6,7},{7,8},{8,9},{9,10},{10,1... | collective-permute-start | bytes 245768 | tf_op jit(solution)/shard_map/ppermute | solution.py:874
  24.2 6.3 %collective-permute-start.5 = (f32[10,8,256]{2,1,0:T(8,128)S(1)}, f32[10,8,256]{2,1,0:T(8,128)S(1)}, u32[]{:S(2)}, u32[]{:S(2)}) collective-permute-start(f32[10,8,256]{2,1,0:T(8,128)S(1)} %get-tuple-element.63), channel_id=1, source_target_pairs={{1,0},{2,1},{3,2},{4,3},{5,4},{6,5},{7,6},{8,7},{9,8},{10,9},{11,1... | collective-permute-start | bytes 245768 | tf_op jit(solution)/shard_map/ppermute | solution.py:874
  31.2 8.9 %collective-permute-start.7 = (f32[80,8,128]{2,1,0:T(8,128)S(1)}, f32[80,8,128]{2,1,0:T(8,128)S(1)}, u32[]{:S(2)}, u32[]{:S(2)}) collective-permute-start(f32[80,8,128]{2,1,0:T(8,128)S(1)} %get-tuple-element.64.own), channel_id=1, source_target_pairs={{16,0},{32,16},{48,32},{64,48},{80,64},{96,80},{112,96},{128,112},... | collective-permute-start | bytes 983048 | tf_op jit(solution)/shard_map/ppermute | solution.py:874
  33.4 9.2 %collective-permute-start.6 = (f32[80,8,128]{2,1,0:T(8,128)S(1)}, f32[80,8,128]{2,1,0:T(8,128)S(1)}, u32[]{:S(2)}, u32[]{:S(2)}) collective-permute-start(f32[80,8,128]{2,1,0:T(8,128)S(1)} %get-tuple-element.64.own), channel_id=1, source_target_pairs={{0,16},{16,32},{32,48},{48,64},{64,80},{80,96},{96,112},{112,128},... | collective-permute-start | bytes 983048 | tf_op jit(solution)/shard_map/ppermute | solution.py:874
  33.4 4.0 %collective-permute-start.8 = (f32[32,8,128]{2,1,0:T(8,128)S(1)}, f32[32,8,128]{2,1,0:T(8,128)S(1)}, u32[]{:S(2)}, u32[]{:S(2)}) collective-permute-start(f32[32,8,128]{2,1,0:T(8,128)S(1)} %get-tuple-element.67), channel_id=1, source_target_pairs={{0,1},{1,2},{2,3},{3,4},{4,5},{5,6},{6,7},{7,8},{8,9},{9,10},{10,1... | collective-permute-start | bytes 393224 | tf_op jit(solution)/shard_map/ppermute | solution.py:874
  35.4 4.7 %collective-permute-start.9 = (f32[32,8,128]{2,1,0:T(8,128)S(1)}, f32[32,8,128]{2,1,0:T(8,128)S(1)}, u32[]{:S(2)}, u32[]{:S(2)}) collective-permute-start(f32[32,8,128]{2,1,0:T(8,128)S(1)} %get-tuple-element.68), channel_id=1, source_target_pairs={{1,0},{2,1},{3,2},{4,3},{5,4},{6,5},{7,6},{8,7},{9,8},{10,9},{11,1... | collective-permute-start | bytes 393224 | tf_op jit(solution)/shard_map/ppermute | solution.py:874
  42.7 7.8 %collective-permute-start.10 = (f32[36,8,128]{2,1,0:T(8,128)S(1)}, f32[36,8,128]{2,1,0:T(8,128)S(1)}, u32[]{:S(2)}, u32[]{:S(2)}) collective-permute-start(f32[36,8,128]{2,1,0:T(8,128)S(1)} %get-tuple-element.69), channel_id=1, source_target_pairs={{0,1},{1,2},{2,3},{3,4},{4,5},{5,6},{6,7},{7,8},{8,9},{9,10},{10,1... | collective-permute-start | bytes 442376 | tf_op jit(solution)/shard_map/ppermute | solution.py:874
  48.4 4.6 %collective-permute-start.11 = (f32[36,8,128]{2,1,0:T(8,128)S(1)}, f32[36,8,128]{2,1,0:T(8,128)S(1)}, u32[]{:S(2)}, u32[]{:S(2)}) collective-permute-start(f32[36,8,128]{2,1,0:T(8,128)S(1)} %get-tuple-element.70), channel_id=1, source_target_pairs={{1,0},{2,1},{3,2},{4,3},{5,4},{6,5},{7,6},{8,7},{9,8},{10,9},{11,1... | collective-permute-start | bytes 442376 | tf_op jit(solution)/shard_map/ppermute | solution.py:874
  57.1 1.2 %collective-permute-start.12 = (f32[1,128]{1,0:T(1,128)S(1)}, f32[1,128]{1,0:T(1,128)S(1)}, u32[]{:S(2)}, u32[]{:S(2)}) collective-permute-start(f32[1,128]{1,0:T(1,128)S(1)} %get-tuple-element.77), channel_id=1, source_target_pairs={{0,1},{1,0},{2,3},{3,2},{4,5},{5,4},{6,7},{7,6},{8,9},{9,8},{10,11... | collective-permute-start | bytes 1544 | tf_op jit(solution)/shard_map/ppermute | solution.py:958

commit v8 on v7

--- a/solution.py
+++ b/solution.py
@@ -28,12 +28,12 @@
 ANY = pl.BlockSpec(memory_space=pl.ANY)
 
 
-def call(body, outs, ins, scratch=(), limit=8, where=VMEM, us=1, out_where=None):
+def call(body, outs, ins, scratch=(), limit=8, where=VMEM, us=1):
     return pl.pallas_call(
         body,
         out_shape=[jax.ShapeDtypeStruct(s, jnp.float32) for s in outs],
         in_specs=[where] * len(ins),
-        out_specs=out_where or [where] * len(outs),
+        out_specs=[where] * len(outs),
         scratch_shapes=[pltpu.VMEM(s, jnp.float32) if isinstance(s, tuple) else s for s in scratch],
         compiler_params=pltpu.CompilerParams(vmem_limit_bytes=limit * MIB),
         cost_estimate=pl.CostEstimate(
@@ -114,17 +114,17 @@
         o.wait()
 
 
-def local(v, wx, wy, wz, vt, wm, cw, yu, yd, Q):
+def local(v, w_, vt, wm, cw, yu, yd, Q):
     last_x = lax.axis_index("gx") == lax.axis_size("gx") - 1
     last_y = lax.axis_index("gy") == lax.axis_size("gy") - 1
     keep_x = jnp.where(last_x, 0.0, 1.0)
     keep_y = jnp.where(last_y, 0.0, 1.0)
-    wm[0] = wx[...]
-    wm[0, LX - 1] = wx[LX - 1] * keep_x
+    wm[0] = w_[0]
+    wm[0, LX - 1] = w_[0, LX - 1] * keep_x
     sub = lax.broadcasted_iota(jnp.int32, (LX, LY, NZ), 1)
-    wm[1] = jnp.where(sub == LY - 1, wy[...] * keep_y, wy[...])
+    wm[1] = jnp.where(sub == LY - 1, w_[1] * keep_y, w_[1])
     lane = lax.broadcasted_iota(jnp.int32, (LX, LY, NZ), 2)
-    wm[2] = jnp.where(lane == NZ - 1, 0.0, wz[...])
+    wm[2] = jnp.where(lane == NZ - 1, 0.0, w_[2])
 
     for x in range(CX):
         i = 2 * x
@@ -242,22 +242,20 @@
     )
 
 
-def stencil(w, at):
+def stencil(w, at, without=None):
     c = at(0, 0)
-    return (
-        w(0) * at(1, 0)
-        + w(1) * at(-1, 0)
-        + w(2) * at(0, 1)
-        + w(3) * at(0, -1)
-        + w(4) * up_z(c)
-        + w(5) * down_z(c)
-    )
+    total = w(2) * at(0, 1) + w(3) * at(0, -1) + w(4) * up_z(c) + w(5) * down_z(c)
+    for a, dx in ((0, 1), (1, -1)):
+        if a != without:
+            total = total + w(a) * at(dx, 0)
+    return total
 
 
 NH = [-2, -1, 0, 8, 9]
 Y1E = [-2, -1, 0, 7, 8, 9]
 Y2E = [-1, 0, 1, 6, 7, 8]
 Y3E = [0, 1, 2, 5, 6, 7]
+LACK = {(1, 7): 0, (2, 1): 1, (2, 6): 0, (3, 2): 1, (3, 5): 0}
 
 
 def pick(near, edge, planes_):
@@ -299,7 +297,7 @@
     dst[6, i] = deg
 
 
-def fine_inner(vt, wm, cw, yl, yr, W, NW, Y1, Y2, Y3):
+def fine_inner(vt, wm, cw, yl, yr, W, NW, Y1, Y2, Y3, PX):
     for w in range(3):
         W[w, :, JW : JW + LY] = wm[w]
     for x in range(LX):
@@ -330,12 +328,24 @@
 
         lax.fori_loop(0, count, body, 0)
 
+    def y1(p, y):
+        return Y1[p - 1, y + H]
+
+    def y2(p, y):
+        return Y2[p - 2, y + H]
+
     power(v, Y1, 1, 6, -2, 17)
-    power(lambda p, y: Y1[p - 1, y + H], Y2, 2, 4, -1, 16)
-    power(lambda p, y: Y2[p - 2, y + H], Y3, 3, 2, 0, 15)
-
-
-def fine_outer(vt, wm, cw, xl, xr, yl, yr, W, NW, Y1, Y2, Y3, NE, Y1X, Y2X, Y3X, f, over):
+    power(y1, Y2, 2, 4, -1, 16)
+    power(y2, Y3, 3, 2, 0, 15)
+    for n, ((power_, p), without) in enumerate(LACK.items()):
+        at = (v, y1, y2)[power_ - 1]
+        for y in range(LY):
+            PX[n, y] = stencil(
+                lambda a: row(NW, a, p - 1, y + JW), lambda dx, dy: at(p + dx, y + dy), without
+            )
+
+
+def fine_outer(vt, wm, cw, xl, xr, yl, yr, W, NW, Y1, Y2, Y3, PX, NE, Y1X, Y2X, Y3X, f, over):
     def own(w, p):
         if 0 <= p < LX:
             return wm[w, p]
@@ -349,19 +359,25 @@
             ly = jnp.where(top, jnp.broadcast_to(W[1, 0, JW - 1 : JW], (LY, NZ)), ly)
         normalise(NE, n, own(0, p), own(0, p - 1), wy, ly, own(2, p))
 
-    def power(at, dst, planes_, rows_):
+    def power(power_, at, dst, planes_, rows_):
         for n, p in enumerate(planes_):
             low, high = rows_[n if n < 3 else 5 - n]
+            lack = LACK.get((power_, p))
             for y in range(low, high + 1):
+                if lack is not None:
+                    m = list(LACK).index((power_, p))
+                    term = w_row(NW, NE, lack, p, y) * at(p + (-1 if lack else 1), y)
+                    dst[n, y + H] = PX[m, y] + term
+                    continue
                 dst[n, y + H] = stencil(
                     lambda a: w_row(NW, NE, a, p, y), lambda dx, dy: at(p + dx, y + dy)
                 )
 
     v = v_cell(vt, xl, xr, yl, yr)
     y1, y2, y3 = pick(Y1, Y1X, Y1E), pick(Y2, Y2X, Y2E), pick(Y3, Y3X, Y3E)
-    power(v, Y1X, Y1E, ((1, 14), (1, 14), (0, 15)))
-    power(y1, Y2X, Y2E, ((2, 13), (1, 14), (0, 15)))
-    power(y2, Y3X, Y3E, ((2, 13), (1, 14), (0, 15)))
+    power(1, v, Y1X, Y1E, ((1, 14), (1, 14), (0, 15)))
+    power(2, y1, Y2X, Y2E, ((2, 13), (1, 14), (0, 15)))
+    power(3, y2, Y3X, Y3E, ((2, 13), (1, 14), (0, 15)))
 
     first_row = lax.broadcasted_iota(jnp.int32, (CY, CZ), 0) == 0
     for x in range(CX):
@@ -789,7 +805,7 @@
     out[...] = jnp.broadcast_to((a[...] + b[...])[None], out.shape)
 
 
-def finish(parts, po, bo, out, eig, SP, buf, sem):
+def finish(parts, po, bo, out, eig, SP):
     t = parts[...]
     n = t.shape[0]
     while n > 2:
@@ -854,17 +870,10 @@
                         u = u - SP[at[k, j] : at[k, j] + 8] * done[j]
                     u = u * SP[64 + 8 * k : 72 + 8 * k]
                     done.append(u)
-                    buf[k, x, t : t + 8, z] = u
-        copy(x).start()
+                    out[k, x, t : t + 8, z] = u
         return 0
 
-    def copy(x):
-        here = pl.ds(x, 1)
-        return pltpu.make_async_copy(buf.at[:, here], out.at[:, here], sem.at[x])
-
     lax.fori_loop(0, LX, body, 0)
-    for x in range(LX):
-        copy(x).wait()
 
 
 def both_ways(up, down, axis):
@@ -894,12 +903,12 @@
             (NYB, 8, NZ),
             (NYB, 8, NZ),
         ],
-        args,
+        (vectors, jnp.stack(args[1:])),
         [(5, CX * LY, CZ)],
     )
     yl, yr = both_ways(yu, yd, "gy")
     tall = LY + 2 * H
-    W, NW, Y1, Y2, Y3 = call(
+    W, NW, Y1, Y2, Y3, PX = call(
         fine_inner,
         [
             (3, LX, 32, NZ),
@@ -907,6 +916,7 @@
             (6, tall, K, NZ),
             (4, tall, K, NZ),
             (2, tall, K, NZ),
+            (len(LACK), LY, K, NZ),
         ],
         (vt, wm, cw, yl, yr),
         us=3,
@@ -925,7 +935,7 @@
             (NF + 4 * CX, 8, CZ),
             (CX, CY, CZ),
         ],
-        (vt, wm, cw, xl, xr, yl, yr, W, NW, Y1, Y2, Y3),
+        (vt, wm, cw, xl, xr, yl, yr, W, NW, Y1, Y2, Y3, PX),
         us=4,
     )
     f, fu, fd, fix = call(
@@ -962,8 +972,7 @@
         finish,
         [(K, LX, LY, NZ), (1, K)],
         (parts, po, bo),
-        [(384, 128), (K, LX, LY, NZ), pltpu.SemaphoreType.DMA((LX,))],
-        out_where=[ANY, VMEM],
+        [(384, 128)],
     )
     return refined, eig.reshape(K)
 

time: 81.8 us -> 81.2 us (level)
  local copies, waits for them, and re-layouts: 2.72 us -> 0.01 us
  starting transfers between devices: 21.4 us -> 22.5 us
  other arithmetic: 0 us -> 1.06 us
    unnamed x8 -> x2, local copies, waits for them, and re-layouts: 2.72 us -> 0.01 us
    ppermute x12, starting transfers between devices: 21.3 us -> 22.4 us  [both_ways(): return (lax.ppermute(up, axis, fwd), lax.ppermute(down, axis, back))]
    another operation x0 -> x1, other arithmetic: none -> 1.06 us  [per_device(): jnp.stack(args[1:])]
  transfers between devices with their start and end apart: 13 -> 13, of which waited for: 8 -> 8; matrix products, arithmetic and copies ran while one was open for 0% -> 1% of each run, Pallas kernels for 12% -> 12%
where the time goes in v8:
time: 81.2 us; the launch traced here: 81 us
  starting transfers between devices  22.5 us (28%)
  blocking collectives  20.9 us (26%)
  Pallas kernels  19.2 us (24%)
  waiting for transfers between devices  16.5 us (20%)
  other arithmetic  1.06 us (1%)
    ppermute x12, starting transfers between devices, both_ways(): return (lax.ppermute(up, axis, fwd), lax.ppermute(down, axis, back))  22.4 us
    all_to_all x1, blocking collectives, per_device(): parts = lax.all_to_all(sums, ('gx', 'gy'), 0, 0)  20.9 us
    pallas_call x12, Pallas kernels, call(): pl.pallas_call(body, out_shape=[jax.ShapeDtypeStruct(s, jnp.float32) for...  19.2 us
    ppermute x12, waiting for transfers between devices, both_ways(): return (lax.ppermute(up, axis, fwd), lax.ppermute(down, axis, back))  15.4 us
  transfers between devices with their start and end apart: 13, of which 8 were waited for; matrix products, arithmetic and copies ran while one was open for 1% of the time, Pallas kernels for 12%

profile of v8, /device:TPU:1, one launch (start us, length us, event | category | flops | bytes accessed | tf_op | source)
XLA Modules:
  0.0 81.0 jit_solution(11911187427688464400)
XLA Ops:
  0.6 0.0 copy-start
  0.6 2.3 %shard_map.60 = (f32[31,16,256]{2,1,0:T(8,128)}, f32[30,16,256]{2,1,0:T(8,128)}) custom-call(f32[8,8,16,256]{3,2,1,0:T(8,128)} %v.3, f32[8,16,256]{2,1,0:T(8,128)} %wx.1, f32[8,16,256]{2,1,0:T(8,128)} %wy.1, f32[8,16,256]{2,1,0:T(8,128)} %wz.1), custom_call_target="tpu_custom_call" | custom-call | bytes 3000000 | tf_op jit(solution)/shard_map/pallas_call | solution.py:32
  2.9 2.1 %collective-permute-start = (f32[31,16,256]{2,1,0:T(8,128)}, f32[31,16,256]{2,1,0:T(8,128)S(1)}, u32[]{:S(2)}, u32[]{:S(2)}) collective-permute-start(f32[31,16,256]{2,1,0:T(8,128)} %get-tuple-element.44), channel_id=1, source_target_pairs={{0,16},{16,32},{32,48},{48,64},{64,80},{80,96},{96,112},{112,128},... | collective-permute-start | bytes 1523720 | tf_op jit(solution)/shard_map/ppermute | solution.py:883
  5.0 3.8 %collective-permute-start.1 = (f32[30,16,256]{2,1,0:T(8,128)}, f32[30,16,256]{2,1,0:T(8,128)S(1)}, u32[]{:S(2)}, u32[]{:S(2)}) collective-permute-start(f32[30,16,256]{2,1,0:T(8,128)} %get-tuple-element.45), channel_id=1, source_target_pairs={{16,0},{32,16},{48,32},{64,48},{80,64},{96,80},{112,96},{128,112},... | collective-permute-start | bytes 1474568 | tf_op jit(solution)/shard_map/ppermute | solution.py:883
  8.9 1.1 %pad_maximum_fusion.w_ = f32[3,8,16,256]{3,2,1,0:T(8,128)S(1)} fusion(f32[1,8,16,256]{3,2,1,0:T(8,128)} %bitcast.4, f32[1,8,16,256]{3,2,1,0:T(8,128)} %bitcast.5, f32[1,8,16,256]{3,2,1,0:T(8,128)} %bitcast.6), kind=kLoop, calls=%fused_computation | loop fusion | flops 196608 | bytes 786432 | tf_op jit(solution)/shard_map/stack | solution.py:906
  9.9 0.0 copy-done
  9.9 0.7 shard_map.59
  10.6 2.5 %collective-permute-start.2 = (f32[36,8,256]{2,1,0:T(8,128)S(1)}, f32[36,8,256]{2,1,0:T(8,128)S(1)}, u32[]{:S(2)}, u32[]{:S(2)}) collective-permute-start(f32[36,8,256]{2,1,0:T(8,128)S(1)} %get-tuple-element.48), channel_id=1, source_target_pairs={{0,1},{1,2},{2,3},{3,4},{4,5},{5,6},{6,7},{7,8},{8,9},{9,10},{10,1... | collective-permute-start | bytes 884744 | tf_op jit(solution)/shard_map/ppermute | solution.py:883
  13.2 0.2 collective-permute-start.3
  13.4 3.4 %collective-permute-done.2.yl.gl = f32[36,8,256]{2,1,0:T(8,128)S(1)} collective-permute-done((f32[36,8,256]{2,1,0:T(8,128)S(1)}, f32[36,8,256]{2,1,0:T(8,128)S(1)}, u32[]{:S(2)}, u32[]{:S(2)}) %collective-permute-start.2) | collective-permute-done | bytes 294944 | tf_op jit(solution)/shard_map/ppermute | solution.py:883
  16.8 2.8 %collective-permute-done.3.yr.gr = f32[36,8,256]{2,1,0:T(8,128)S(1)} collective-permute-done((f32[36,8,256]{2,1,0:T(8,128)S(1)}, f32[36,8,256]{2,1,0:T(8,128)S(1)}, u32[]{:S(2)}, u32[]{:S(2)}) %collective-permute-start.3) | collective-permute-done | bytes 294944 | tf_op jit(solution)/shard_map/ppermute | solution.py:883
  19.6 3.2 %shard_map.61 = (f32[3,8,32,256]{3,2,1,0:T(8,128)S(1)}, f32[7,7,32,256]{3,2,1,0:T(8,128)S(1)}, f32[6,22,8,256]{3,2,1,0:T(8,128)S(1)}, f32[4,22,8,256]{3,2,1,0:T(...) custom-call(f32[8,16,8,256]{3,2,1,0:T(8,128)S(1)} %get-tuple-element.43.vt, ...), custom_call_target="tpu_custom_call" | custom-call | bytes 9000000 | tf_op jit(solution)/shard_map/pallas_call | solution.py:32
  22.8 0.0 collective-permute-done.1.rr
  22.8 0.0 collective-permute-done.rl
  22.8 0.2 shard_map.62
  23.0 0.2 collective-permute-start.4
  23.2 1.2 %collective-permute-start.5 = (f32[10,8,256]{2,1,0:T(8,128)S(1)}, f32[10,8,256]{2,1,0:T(8,128)S(1)}, u32[]{:S(2)}, u32[]{:S(2)}) collective-permute-start(f32[10,8,256]{2,1,0:T(8,128)S(1)} %get-tuple-element.65), channel_id=1, source_target_pairs={{1,0},{2,1},{3,2},{4,3},{5,4},{6,5},{7,6},{8,7},{9,8},{10,9},{11,1... | collective-permute-start | bytes 245768 | tf_op jit(solution)/shard_map/ppermute | solution.py:883
  24.5 4.5 %shard_map.63 = (f32[7,5,16,256]{3,2,1,0:T(8,128)S(1)}, f32[6,22,8,256]{3,2,1,0:T(8,128)S(1)}, f32[6,22,8,256]{3,2,1,0:T(8,128)S(1)}, f32[6,22,8,256]{3,2,1,0:T(...) custom-call(f32[8,16,8,256]{3,2,1,0:T(8,128)S(1)} %get-tuple-element.43.vt, ...), custom_call_target="tpu_custom_call" | custom-call | bytes 12000000 | tf_op jit(solution)/shard_map/pallas_call | solution.py:32
  29.0 0.0 collective-permute-done.4.cl
  29.0 0.0 collective-permute-done.5.cr
  29.0 0.7 shard_map.64
  29.7 3.4 %collective-permute-start.7 = (f32[80,8,128]{2,1,0:T(8,128)S(1)}, f32[80,8,128]{2,1,0:T(8,128)S(1)}, u32[]{:S(2)}, u32[]{:S(2)}) collective-permute-start(f32[80,8,128]{2,1,0:T(8,128)S(1)} %get-tuple-element.66.own), channel_id=1, source_target_pairs={{16,0},{32,16},{48,32},{64,48},{80,64},{96,80},{112,96},{128,112},... | collective-permute-start | bytes 983048 | tf_op jit(solution)/shard_map/ppermute | solution.py:883
  33.1 0.0 collective-permute-start.6
  33.1 2.0 %collective-permute-start.8 = (f32[32,8,128]{2,1,0:T(8,128)S(1)}, f32[32,8,128]{2,1,0:T(8,128)S(1)}, u32[]{:S(2)}, u32[]{:S(2)}) collective-permute-start(f32[32,8,128]{2,1,0:T(8,128)S(1)} %get-tuple-element.69), channel_id=1, source_target_pairs={{0,1},{1,2},{2,3},{3,4},{4,5},{5,6},{6,7},{7,8},{8,9},{9,10},{10,1... | collective-permute-start | bytes 393224 | tf_op jit(solution)/shard_map/ppermute | solution.py:883
  35.1 1.1 %collective-permute-start.9 = (f32[32,8,128]{2,1,0:T(8,128)S(1)}, f32[32,8,128]{2,1,0:T(8,128)S(1)}, u32[]{:S(2)}, u32[]{:S(2)}) collective-permute-start(f32[32,8,128]{2,1,0:T(8,128)S(1)} %get-tuple-element.70), channel_id=1, source_target_pairs={{1,0},{2,1},{3,2},{4,3},{5,4},{6,5},{7,6},{8,7},{9,8},{10,9},{11,1... | collective-permute-start | bytes 393224 | tf_op jit(solution)/shard_map/ppermute | solution.py:883
  36.3 0.6 shard_map.65
  36.9 0.2 collective-permute-done.8.yl
  37.1 2.7 %collective-permute-done.9.yr = f32[32,8,128]{2,1,0:T(8,128)S(1)} collective-permute-done((f32[32,8,128]{2,1,0:T(8,128)S(1)}, f32[32,8,128]{2,1,0:T(8,128)S(1)}, u32[]{:S(2)}, u32[]{:S(2)}) %collective-permute-start.9) | collective-permute-done | bytes 131104 | tf_op jit(solution)/shard_map/ppermute | solution.py:883
  39.8 0.0 collective-permute-done.7.right
  39.8 2.6 %collective-permute-done.6.left = f32[80,8,128]{2,1,0:T(8,128)S(1)} collective-permute-done((f32[80,8,128]{2,1,0:T(8,128)S(1)}, f32[80,8,128]{2,1,0:T(8,128)S(1)}, u32[]{:S(2)}, u32[]{:S(2)}) %collective-permute-start.6) | collective-permute-done | bytes 327712 | tf_op jit(solution)/shard_map/ppermute | solution.py:883
  42.4 5.7 %collective-permute-start.10 = (f32[36,8,128]{2,1,0:T(8,128)S(1)}, f32[36,8,128]{2,1,0:T(8,128)S(1)}, u32[]{:S(2)}, u32[]{:S(2)}) collective-permute-start(f32[36,8,128]{2,1,0:T(8,128)S(1)} %get-tuple-element.71), channel_id=1, source_target_pairs={{0,1},{1,2},{2,3},{3,4},{4,5},{5,6},{6,7},{7,8},{8,9},{9,10},{10,1... | collective-permute-start | bytes 442376 | tf_op jit(solution)/shard_map/ppermute | solution.py:883
  48.1 0.0 collective-permute-start.11
  48.1 0.8 shard_map.67
  48.9 1.3 %collective-permute-done.10.cl = f32[36,8,128]{2,1,0:T(8,128)S(1)} collective-permute-done((f32[36,8,128]{2,1,0:T(8,128)S(1)}, f32[36,8,128]{2,1,0:T(8,128)S(1)}, u32[]{:S(2)}, u32[]{:S(2)}) %collective-permute-start.10) | collective-permute-done | bytes 147488 | tf_op jit(solution)/shard_map/ppermute | solution.py:883
  50.2 2.5 %collective-permute-done.11.cr = f32[36,8,128]{2,1,0:T(8,128)S(1)} collective-permute-done((f32[36,8,128]{2,1,0:T(8,128)S(1)}, f32[36,8,128]{2,1,0:T(8,128)S(1)}, u32[]{:S(2)}, u32[]{:S(2)}) %collective-permute-start.11) | collective-permute-done | bytes 147488 | tf_op jit(solution)/shard_map/ppermute | solution.py:883
  52.7 4.1 %shard_map.68 = (f32[8,16,8,256]{3,2,1,0:T(8,128)S(1)}, f32[8,16,8,256]{3,2,1,0:T(8,128)S(1)}, f32[1,128]{1,0:T(1,128)S(1)}, f32[1,128]{1,0:T(1,128)S(1)}) custom-call(f32[80,8,128]{2,1,0:T(8,128)S(1)} %get-tuple-element.66.own, f32[80,8,128]{2,1,0:T(8,128)S(1)} %collective-permute-done.6.left, f32[80,8,128]{2,1,0:T(8,128)S(1)} %collective-permute-done.7.right, ...), custom_call_target="tpu_custom_call" | custom-call | bytes 3000000 | tf_op jit(solution)/shard_map/pallas_call | solution.py:32
  56.8 0.1 collective-permute-start.12
  56.9 1.1 %collective-permute-done.12.b = f32[1,128]{1,0:T(1,128)S(1)} collective-permute-done((f32[1,128]{1,0:T(1,128)S(1)}, f32[1,128]{1,0:T(1,128)S(1)}, u32[]{:S(2)}, u32[]{:S(2)}) %collective-permute-start.12) | collective-permute-done | bytes 544 | tf_op jit(solution)/shard_map/ppermute | solution.py:968
  58.0 0.1 shard_map.69
  58.1 20.9 %all_to_all.5.parts = f32[256,1,128]{2,1,0:T(1,128)S(1)} all-to-all(f32[256,1,128]{2,1,0:T(1,128)S(1)} %shard_map.69), channel_id=1, replica_groups=mesh['gx'=16,'gy'=16] {'gx','gy'}, dimensions={0} | all-to-all | bytes 262144 | tf_op jit(solution)/shard_map/all_to_all | solution.py:970
  79.0 2.0 %shard_map.70 = (f32[8,8,16,256]{3,2,1,0:T(8,128)}, f32[1,8]{1,0:T(1,128)}) custom-call(f32[256,1,128]{2,1,0:T(1,128)S(1)} %all_to_all.5.parts, f32[8,16,8,256]{3,2,1,0:T(8,128)S(1)} %get-tuple-element.80.po, f32[8,16,8,256]{3,2,1,0:T(8,128)S(1)} %get-tuple-element.81.bo), custom_call_target="tpu_custom_call" | custom-call | bytes 3000000 | tf_op jit(solution)/shard_map/pallas_call | solution.py:32
  (1 shorter events, 0.0 us)
Async XLA Ops:
  0.6 9.3 %copy-start = (f32[8,8,16,256]{3,2,1,0:T(8,128)S(1)}, f32[8,8,16,256]{3,2,1,0:T(8,128)}, u32[]{:S(2)}) copy-start(f32[8,8,16,256]{3,2,1,0:T(8,128)} %v.3) | copy-start | bytes 3145732
  2.9 19.9 %collective-permute-start = (f32[31,16,256]{2,1,0:T(8,128)}, f32[31,16,256]{2,1,0:T(8,128)S(1)}, u32[]{:S(2)}, u32[]{:S(2)}) collective-permute-start(f32[31,16,256]{2,1,0:T(8,128)} %get-tuple-element.44), channel_id=1, source_target_pairs={{0,16},{16,32},{32,48},{48,64},{64,80},{80,96},{96,112},{112,128},... | collective-permute-start | bytes 1523720 | tf_op jit(solution)/shard_map/ppermute | solution.py:883
  5.0 17.8 %collective-permute-start.1 = (f32[30,16,256]{2,1,0:T(8,128)}, f32[30,16,256]{2,1,0:T(8,128)S(1)}, u32[]{:S(2)}, u32[]{:S(2)}) collective-permute-start(f32[30,16,256]{2,1,0:T(8,128)} %get-tuple-element.45), channel_id=1, source_target_pairs={{16,0},{32,16},{48,32},{64,48},{80,64},{96,80},{112,96},{128,112},... | collective-permute-start | bytes 1474568 | tf_op jit(solution)/shard_map/ppermute | solution.py:883
  10.6 6.2 %collective-permute-start.2 = (f32[36,8,256]{2,1,0:T(8,128)S(1)}, f32[36,8,256]{2,1,0:T(8,128)S(1)}, u32[]{:S(2)}, u32[]{:S(2)}) collective-permute-start(f32[36,8,256]{2,1,0:T(8,128)S(1)} %get-tuple-element.48), channel_id=1, source_target_pairs={{0,1},{1,2},{2,3},{3,4},{4,5},{5,6},{6,7},{7,8},{8,9},{9,10},{10,1... | collective-permute-start | bytes 884744 | tf_op jit(solution)/shard_map/ppermute | solution.py:883
  13.2 6.4 %collective-permute-start.3 = (f32[36,8,256]{2,1,0:T(8,128)S(1)}, f32[36,8,256]{2,1,0:T(8,128)S(1)}, u32[]{:S(2)}, u32[]{:S(2)}) collective-permute-start(f32[36,8,256]{2,1,0:T(8,128)S(1)} %get-tuple-element.49), channel_id=1, source_target_pairs={{1,0},{2,1},{3,2},{4,3},{5,4},{6,5},{7,6},{8,7},{9,8},{10,9},{11,1... | collective-permute-start | bytes 884744 | tf_op jit(solution)/shard_map/ppermute | solution.py:883
  23.0 6.0 %collective-permute-start.4 = (f32[10,8,256]{2,1,0:T(8,128)S(1)}, f32[10,8,256]{2,1,0:T(8,128)S(1)}, u32[]{:S(2)}, u32[]{:S(2)}) collective-permute-start(f32[10,8,256]{2,1,0:T(8,128)S(1)} %get-tuple-element.64), channel_id=1, source_target_pairs={{0,1},{1,2},{2,3},{3,4},{4,5},{5,6},{6,7},{7,8},{8,9},{9,10},{10,1... | collective-permute-start | bytes 245768 | tf_op jit(solution)/shard_map/ppermute | solution.py:883
  23.2 5.8 %collective-permute-start.5 = (f32[10,8,256]{2,1,0:T(8,128)S(1)}, f32[10,8,256]{2,1,0:T(8,128)S(1)}, u32[]{:S(2)}, u32[]{:S(2)}) collective-permute-start(f32[10,8,256]{2,1,0:T(8,128)S(1)} %get-tuple-element.65), channel_id=1, source_target_pairs={{1,0},{2,1},{3,2},{4,3},{5,4},{6,5},{7,6},{8,7},{9,8},{10,9},{11,1... | collective-permute-start | bytes 245768 | tf_op jit(solution)/shard_map/ppermute | solution.py:883
  29.7 10.0 %collective-permute-start.7 = (f32[80,8,128]{2,1,0:T(8,128)S(1)}, f32[80,8,128]{2,1,0:T(8,128)S(1)}, u32[]{:S(2)}, u32[]{:S(2)}) collective-permute-start(f32[80,8,128]{2,1,0:T(8,128)S(1)} %get-tuple-element.66.own), channel_id=1, source_target_pairs={{16,0},{32,16},{48,32},{64,48},{80,64},{96,80},{112,96},{128,112},... | collective-permute-start | bytes 983048 | tf_op jit(solution)/shard_map/ppermute | solution.py:883
  33.1 9.2 %collective-permute-start.6 = (f32[80,8,128]{2,1,0:T(8,128)S(1)}, f32[80,8,128]{2,1,0:T(8,128)S(1)}, u32[]{:S(2)}, u32[]{:S(2)}) collective-permute-start(f32[80,8,128]{2,1,0:T(8,128)S(1)} %get-tuple-element.66.own), channel_id=1, source_target_pairs={{0,16},{16,32},{32,48},{48,64},{64,80},{80,96},{96,112},{112,128},... | collective-permute-start | bytes 983048 | tf_op jit(solution)/shard_map/ppermute | solution.py:883
  33.1 4.0 %collective-permute-start.8 = (f32[32,8,128]{2,1,0:T(8,128)S(1)}, f32[32,8,128]{2,1,0:T(8,128)S(1)}, u32[]{:S(2)}, u32[]{:S(2)}) collective-permute-start(f32[32,8,128]{2,1,0:T(8,128)S(1)} %get-tuple-element.69), channel_id=1, source_target_pairs={{0,1},{1,2},{2,3},{3,4},{4,5},{5,6},{6,7},{7,8},{8,9},{9,10},{10,1... | collective-permute-start | bytes 393224 | tf_op jit(solution)/shard_map/ppermute | solution.py:883
  35.1 4.6 %collective-permute-start.9 = (f32[32,8,128]{2,1,0:T(8,128)S(1)}, f32[32,8,128]{2,1,0:T(8,128)S(1)}, u32[]{:S(2)}, u32[]{:S(2)}) collective-permute-start(f32[32,8,128]{2,1,0:T(8,128)S(1)} %get-tuple-element.70), channel_id=1, source_target_pairs={{1,0},{2,1},{3,2},{4,3},{5,4},{6,5},{7,6},{8,7},{9,8},{10,9},{11,1... | collective-permute-start | bytes 393224 | tf_op jit(solution)/shard_map/ppermute | solution.py:883
  42.4 7.8 %collective-permute-start.10 = (f32[36,8,128]{2,1,0:T(8,128)S(1)}, f32[36,8,128]{2,1,0:T(8,128)S(1)}, u32[]{:S(2)}, u32[]{:S(2)}) collective-permute-start(f32[36,8,128]{2,1,0:T(8,128)S(1)} %get-tuple-element.71), channel_id=1, source_target_pairs={{0,1},{1,2},{2,3},{3,4},{4,5},{5,6},{6,7},{7,8},{8,9},{9,10},{10,1... | collective-permute-start | bytes 442376 | tf_op jit(solution)/shard_map/ppermute | solution.py:883
  48.1 4.6 %collective-permute-start.11 = (f32[36,8,128]{2,1,0:T(8,128)S(1)}, f32[36,8,128]{2,1,0:T(8,128)S(1)}, u32[]{:S(2)}, u32[]{:S(2)}) collective-permute-start(f32[36,8,128]{2,1,0:T(8,128)S(1)} %get-tuple-element.72), channel_id=1, source_target_pairs={{1,0},{2,1},{3,2},{4,3},{5,4},{6,5},{7,6},{8,7},{9,8},{10,9},{11,1... | collective-permute-start | bytes 442376 | tf_op jit(solution)/shard_map/ppermute | solution.py:883
  56.8 1.2 %collective-permute-start.12 = (f32[1,128]{1,0:T(1,128)S(1)}, f32[1,128]{1,0:T(1,128)S(1)}, u32[]{:S(2)}, u32[]{:S(2)}) collective-permute-start(f32[1,128]{1,0:T(1,128)S(1)} %get-tuple-element.79), channel_id=1, source_target_pairs={{0,1},{1,0},{2,3},{3,2},{4,5},{5,4},{6,7},{7,6},{8,9},{9,8},{10,11... | collective-permute-start | bytes 1544 | tf_op jit(solution)/shard_map/ppermute | solution.py:968

commit v9 on v8

--- a/solution.py
+++ b/solution.py
@@ -614,6 +614,12 @@
 EARLY1 = early(EARLY0, 3)
 EARLY2 = early(EARLY1, 2)
 EARLY3 = early(EARLY2, 1)
+BLOCKS = [(x, y) for x in range(CX) for y in range(CY)]
+DONE = [
+    (x, y)
+    for x, y in BLOCKS
+    if {(x + CH + i, y + CH + j) for i, j in ((0, 0), (1, 0), (-1, 0), (0, 1), (0, -1))} <= EARLY3
+]
 
 
 def coarse_weights(own, left, right, gl, gr, corner, CW, R):
@@ -658,7 +664,57 @@
             )
 
 
-def coarse_early(own, left, right, yl, yr, gl, gr, F, E1, E2, E3, CW, R):
+def last_sweep(blocks, cell, pb, NW, NE, po, bo):
+    for x, y in blocks:
+        for half in range(2):
+            e = cell(x + CH, y + CH, half)
+            ez = (up_z(e), down_z(e))
+            ke = KEEP * e
+            ce = C * e
+            for dx in range(2):
+                ex = C * cell(x + CH + 2 * dx - 1, y + CH, half)
+                for dy in range(2):
+                    ey = C * cell(x + CH, y + CH + 2 * dy - 1, half)
+                    xx, yy = 2 * x + dx, 2 * y + dy
+                    nw = [w_row(NW, NE, a, xx, yy) for a in range(6)]
+                    s = (
+                        ke
+                        + (nw[dx] + nw[2 + dy]) * ce
+                        + nw[1 - dx] * ex
+                        + nw[3 - dy] * ey
+                        + C * (nw[4] * ez[0] + nw[5] * ez[1])
+                    )
+                    if half == 0:
+                        po[xx, yy] = pb[xx, yy, 0:8] - s
+                    else:
+                        bo[xx, yy] = pb[xx, yy, 8:16] + s
+
+
+def row8(ref, x, y, m, z):
+    return jnp.broadcast_to(ref[x, y, m : m + 1, z], (8, 128))
+
+
+def add_gram(blocks, acc, po, bo, NW, NE):
+    for x, y in blocks:
+        for n in range(4):
+            xx, yy = 2 * x + (n >> 1), 2 * y + (n & 1)
+            deg = w_row(NW, NE, 6, xx, yy)
+            for h in range(0, NZ, 128):
+                z = slice(h, h + 128)
+                p = po[xx, yy, :, z]
+                b = bo[xx, yy, :, z]
+                dp = deg[:, z] * p
+                db = deg[:, z] * b
+                for m in range(8):
+                    acc[m] = acc[m] + dp * row8(po, xx, yy, m, z)
+                    acc[13 + m] = acc[13 + m] + dp * row8(bo, xx, yy, m, z)
+                for s in range(5):
+                    acc[8 + s] = acc[8 + s] + b * (pltpu.roll(db, s, 0) if s else db)
+
+
+def coarse_early(
+    own, left, right, yl, yr, gl, gr, pb, NW, NE, F, E1, E2, EX, po, bo, g, E3, CW, R
+):
     for x in range(CX):
         for half in range(2):
             for y in range(CY):
@@ -677,6 +733,14 @@
     sweep(sorted(EARLY1), of(F), of(F), CW, E1)
     sweep(sorted(EARLY2), of(E1), of(F), CW, E2)
     sweep(sorted(EARLY3), of(E2), of(F), CW, E3)
+    for i, j in sorted(EARLY3):
+        for half in range(2):
+            EX[i, j, half] = expand(E3[i, j, half])
+    last_sweep(DONE, of(EX), pb, NW, NE, po, bo)
+    acc = [jnp.zeros((8, 128), jnp.float32)] * 21
+    add_gram(DONE, acc, po, bo, NW, NE)
+    for n in range(21):
+        g[n] = acc[n]
 
 
 def coarse_level(
@@ -690,7 +754,10 @@
     F,
     E1,
     E2,
-    E3,
+    EXE,
+    pe,
+    be,
+    ge,
     pb,
     NW,
     NE,
@@ -726,62 +793,23 @@
     def both(first, cells, then):
         return lambda i, j, half: (first if (i, j) in cells else then)[i, j, half]
 
-    e1, e2, e3 = both(E1, EARLY1, X1), both(E2, EARLY2, X2), both(E3, EARLY3, X3)
+    e1, e2 = both(E1, EARLY1, X1), both(E2, EARLY2, X2)
     sweep([c for c in cells_within(3) if c not in EARLY1], f, f, CW, X1)
     sweep([c for c in cells_within(2) if c not in EARLY2], e1, f, CW, X2)
     sweep([c for c in cells_within(1) if c not in EARLY3], e2, f, CW, X3)
     for i, j in cells_within(1):
-        for half in range(2):
-            EX[i, j, half] = expand(e3(i, j, half))
-
-    for x in range(CX):
-        for y in range(CY):
+        if (i, j) not in EARLY3:
             for half in range(2):
-                e = EX[x + CH, y + CH, half]
-                ez = (up_z(e), down_z(e))
-                ke = KEEP * e
-                ce = C * e
-                for dx in range(2):
-                    ex = C * EX[x + CH + 2 * dx - 1, y + CH, half]
-                    for dy in range(2):
-                        ey = C * EX[x + CH, y + CH + 2 * dy - 1, half]
-                        xx, yy = 2 * x + dx, 2 * y + dy
-                        nw = [w_row(NW, NE, a, xx, yy) for a in range(6)]
-                        s = (
-                            ke
-                            + (nw[dx] + nw[2 + dy]) * ce
-                            + nw[1 - dx] * ex
-                            + nw[3 - dy] * ey
-                            + C * (nw[4] * ez[0] + nw[5] * ez[1])
-                        )
-                        if half == 0:
-                            po[xx, yy] = pb[xx, yy, 0:8] - s
-                        else:
-                            bo[xx, yy] = pb[xx, yy, 8:16] + s
-
-    def row8(ref, x, y, m, z):
-        return jnp.broadcast_to(ref[x, y, m : m + 1, z], (8, 128))
-
-    def gram(x, edge, acc):
-        acc = list(acc)
-        for yy in range(LY):
-            deg = row(NE, 6, NH.index(0), yy) if edge else row(NW, 6, x - 1, yy + JW)
-            for h in range(0, NZ, 128):
-                z = slice(h, h + 128)
-                p = po[x, yy, :, z]
-                b = bo[x, yy, :, z]
-                dp = deg[:, z] * p
-                db = deg[:, z] * b
-                for m in range(8):
-                    acc[m] = acc[m] + dp * row8(po, x, yy, m, z)
-                    acc[13 + m] = acc[13 + m] + dp * row8(bo, x, yy, m, z)
-                for s in range(5):
-                    acc[8 + s] = acc[8 + s] + b * (pltpu.roll(db, s, 0) if s else db)
-        return tuple(acc)
-
+                EX[i, j, half] = expand(X3[i, j, half])
+    for x, y in DONE:
+        here = slice(2 * x, 2 * x + 2), slice(2 * y, 2 * y + 2)
+        po[here] = pe[here]
+        bo[here] = be[here]
+    left_over = [c for c in BLOCKS if c not in DONE]
+    last_sweep(left_over, both(EXE, EARLY3, EX), pb, NW, NE, po, bo)
     zero = jnp.zeros((8, 128), jnp.float32)
-    acc = gram(0, True, (zero,) * 21)
-    acc = list(lax.fori_loop(1, LX, lambda x, acc: gram(x, False, acc), acc))
+    acc = [ge[n] for n in range(21)]
+    add_gram(left_over, acc, po, bo, NW, NE)
     for q in range(2):
         acc.append(nd[q, :, :128] + nd[q, :, 128:])
     lane = lax.broadcasted_iota(jnp.int32, (8, 128), 1)
@@ -955,7 +983,12 @@
     cext = (CX + 2 * CH, CY + 2 * CH, 2, 8, CZ)
     weights = [(6, CX + 2 * CH, 24, CZ), (4, CX + 2 * CH, 24, CZ)]
     early_ = call(
-        coarse_early, [cext] * 4, (f, left, right, fl, fr, yl, yr), weights, us=2
+        coarse_early,
+        [cext] * 3
+        + [(CX + 2 * CH, CY + 2 * CH, 2, 8, NZ), (LX, LY, K, NZ), (LX, LY, K, NZ), (21, 8, 128)],
+        (f, left, right, fl, fr, yl, yr, pb, NW, NE),
+        [cext] + weights,
+        us=2,
     )
     po, bo, mine, other = call(
         coarse_level,

time: 81.2 us -> 80 us (0.985)
  waiting for transfers between devices: 16.5 us -> 15.2 us
    ppermute x12, waiting for transfers between devices: 15.4 us -> 14.1 us  [both_ways(): return (lax.ppermute(up, axis, fwd), lax.ppermute(down, axis, back))]
  transfers between devices with their start and end apart: 13 -> 13, of which waited for: 8 -> 7; matrix products, arithmetic and copies ran while one was open for 1% -> 1% of each run, Pallas kernels for 12% -> 14%
where the time goes in v9:
time: 80 us; the launch traced here: 79.9 us
  starting transfers between devices  22.5 us (28%)
  blocking collectives  20.9 us (26%)
  Pallas kernels  19.4 us (24%)
  waiting for transfers between devices  15.2 us (19%)
  other arithmetic  1.06 us (1%)
    ppermute x12, starting transfers between devices, both_ways(): return (lax.ppermute(up, axis, fwd), lax.ppermute(down, axis, back))  22.4 us
    all_to_all x1, blocking collectives, per_device(): parts = lax.all_to_all(sums, ('gx', 'gy'), 0, 0)  20.9 us
    pallas_call x12, Pallas kernels, call(): pl.pallas_call(body, out_shape=[jax.ShapeDtypeStruct(s, jnp.float32) for...  19.4 us
    ppermute x12, waiting for transfers between devices, both_ways(): return (lax.ppermute(up, axis, fwd), lax.ppermute(down, axis, back))  14.1 us
  transfers between devices with their start and end apart: 13, of which 7 were waited for; matrix products, arithmetic and copies ran while one was open for 1% of the time, Pallas kernels for 14%

profile of v9, /device:TPU:1, one launch (start us, length us, event | category | flops | bytes accessed | tf_op | source)
XLA Modules:
  0.0 79.9 jit_solution(387244487740724962)
XLA Ops:
  0.6 0.0 copy-start
  0.6 2.3 %shard_map.60 = (f32[31,16,256]{2,1,0:T(8,128)}, f32[30,16,256]{2,1,0:T(8,128)}) custom-call(f32[8,8,16,256]{3,2,1,0:T(8,128)} %v.3, f32[8,16,256]{2,1,0:T(8,128)} %wx.1, f32[8,16,256]{2,1,0:T(8,128)} %wy.1, f32[8,16,256]{2,1,0:T(8,128)} %wz.1), custom_call_target="tpu_custom_call" | custom-call | bytes 3000000 | tf_op jit(solution)/shard_map/pallas_call | solution.py:32
  2.9 2.1 %collective-permute-start = (f32[31,16,256]{2,1,0:T(8,128)}, f32[31,16,256]{2,1,0:T(8,128)S(1)}, u32[]{:S(2)}, u32[]{:S(2)}) collective-permute-start(f32[31,16,256]{2,1,0:T(8,128)} %get-tuple-element.47), channel_id=1, source_target_pairs={{0,16},{16,32},{32,48},{48,64},{64,80},{80,96},{96,112},{112,128},... | collective-permute-start | bytes 1523720 | tf_op jit(solution)/shard_map/ppermute | solution.py:911
  5.0 3.8 %collective-permute-start.1 = (f32[30,16,256]{2,1,0:T(8,128)}, f32[30,16,256]{2,1,0:T(8,128)S(1)}, u32[]{:S(2)}, u32[]{:S(2)}) collective-permute-start(f32[30,16,256]{2,1,0:T(8,128)} %get-tuple-element.48), channel_id=1, source_target_pairs={{16,0},{32,16},{48,32},{64,48},{80,64},{96,80},{112,96},{128,112},... | collective-permute-start | bytes 1474568 | tf_op jit(solution)/shard_map/ppermute | solution.py:911
  8.9 1.1 %pad_maximum_fusion.w_ = f32[3,8,16,256]{3,2,1,0:T(8,128)S(1)} fusion(f32[1,8,16,256]{3,2,1,0:T(8,128)} %bitcast.4, f32[1,8,16,256]{3,2,1,0:T(8,128)} %bitcast.5, f32[1,8,16,256]{3,2,1,0:T(8,128)} %bitcast.6), kind=kLoop, calls=%fused_computation | loop fusion | flops 196608 | bytes 786432 | tf_op jit(solution)/shard_map/stack | solution.py:934
  9.9 0.0 copy-done
  9.9 0.7 shard_map.59
  10.6 2.5 %collective-permute-start.2 = (f32[36,8,256]{2,1,0:T(8,128)S(1)}, f32[36,8,256]{2,1,0:T(8,128)S(1)}, u32[]{:S(2)}, u32[]{:S(2)}) collective-permute-start(f32[36,8,256]{2,1,0:T(8,128)S(1)} %get-tuple-element.51), channel_id=1, source_target_pairs={{0,1},{1,2},{2,3},{3,4},{4,5},{5,6},{6,7},{7,8},{8,9},{9,10},{10,1... | collective-permute-start | bytes 884744 | tf_op jit(solution)/shard_map/ppermute | solution.py:911
  13.2 0.2 collective-permute-start.3
  13.4 3.4 %collective-permute-done.2.yl.gl = f32[36,8,256]{2,1,0:T(8,128)S(1)} collective-permute-done((f32[36,8,256]{2,1,0:T(8,128)S(1)}, f32[36,8,256]{2,1,0:T(8,128)S(1)}, u32[]{:S(2)}, u32[]{:S(2)}) %collective-permute-start.2) | collective-permute-done | bytes 294944 | tf_op jit(solution)/shard_map/ppermute | solution.py:911
  16.8 2.8 %collective-permute-done.3.yr.gr = f32[36,8,256]{2,1,0:T(8,128)S(1)} collective-permute-done((f32[36,8,256]{2,1,0:T(8,128)S(1)}, f32[36,8,256]{2,1,0:T(8,128)S(1)}, u32[]{:S(2)}, u32[]{:S(2)}) %collective-permute-start.3) | collective-permute-done | bytes 294944 | tf_op jit(solution)/shard_map/ppermute | solution.py:911
  19.6 3.2 %shard_map.61 = (f32[3,8,32,256]{3,2,1,0:T(8,128)S(1)}, f32[7,7,32,256]{3,2,1,0:T(8,128)S(1)}, f32[6,22,8,256]{3,2,1,0:T(8,128)S(1)}, f32[4,22,8,256]{3,2,1,0:T(...) custom-call(f32[8,16,8,256]{3,2,1,0:T(8,128)S(1)} %get-tuple-element.46.vt, ...), custom_call_target="tpu_custom_call" | custom-call | bytes 9000000 | tf_op jit(solution)/shard_map/pallas_call | solution.py:32
  22.8 0.0 collective-permute-done.1.rr
  22.8 0.0 collective-permute-done.rl
  22.8 0.2 shard_map.62
  23.0 0.2 collective-permute-start.4
  23.2 1.2 %collective-permute-start.5 = (f32[10,8,256]{2,1,0:T(8,128)S(1)}, f32[10,8,256]{2,1,0:T(8,128)S(1)}, u32[]{:S(2)}, u32[]{:S(2)}) collective-permute-start(f32[10,8,256]{2,1,0:T(8,128)S(1)} %get-tuple-element.68), channel_id=1, source_target_pairs={{1,0},{2,1},{3,2},{4,3},{5,4},{6,5},{7,6},{8,7},{9,8},{10,9},{11,1... | collective-permute-start | bytes 245768 | tf_op jit(solution)/shard_map/ppermute | solution.py:911
  24.4 4.5 %shard_map.63 = (f32[7,5,16,256]{3,2,1,0:T(8,128)S(1)}, f32[6,22,8,256]{3,2,1,0:T(8,128)S(1)}, f32[6,22,8,256]{3,2,1,0:T(8,128)S(1)}, f32[6,22,8,256]{3,2,1,0:T(...) custom-call(f32[8,16,8,256]{3,2,1,0:T(8,128)S(1)} %get-tuple-element.46.vt, ...), custom_call_target="tpu_custom_call" | custom-call | bytes 12000000 | tf_op jit(solution)/shard_map/pallas_call | solution.py:32
  29.0 0.0 collective-permute-done.4.cl
  29.0 0.0 collective-permute-done.5.cr
  29.0 0.7 shard_map.64
  29.7 3.4 %collective-permute-start.7 = (f32[80,8,128]{2,1,0:T(8,128)S(1)}, f32[80,8,128]{2,1,0:T(8,128)S(1)}, u32[]{:S(2)}, u32[]{:S(2)}) collective-permute-start(f32[80,8,128]{2,1,0:T(8,128)S(1)} %get-tuple-element.69.own), channel_id=1, source_target_pairs={{16,0},{32,16},{48,32},{64,48},{80,64},{96,80},{112,96},{128,112},... | collective-permute-start | bytes 983048 | tf_op jit(solution)/shard_map/ppermute | solution.py:911
  33.1 0.0 collective-permute-start.6
  33.1 2.0 %collective-permute-start.8 = (f32[32,8,128]{2,1,0:T(8,128)S(1)}, f32[32,8,128]{2,1,0:T(8,128)S(1)}, u32[]{:S(2)}, u32[]{:S(2)}) collective-permute-start(f32[32,8,128]{2,1,0:T(8,128)S(1)} %get-tuple-element.72), channel_id=1, source_target_pairs={{0,1},{1,2},{2,3},{3,4},{4,5},{5,6},{6,7},{7,8},{8,9},{9,10},{10,1... | collective-permute-start | bytes 393224 | tf_op jit(solution)/shard_map/ppermute | solution.py:911
  35.1 1.1 %collective-permute-start.9 = (f32[32,8,128]{2,1,0:T(8,128)S(1)}, f32[32,8,128]{2,1,0:T(8,128)S(1)}, u32[]{:S(2)}, u32[]{:S(2)}) collective-permute-start(f32[32,8,128]{2,1,0:T(8,128)S(1)} %get-tuple-element.73), channel_id=1, source_target_pairs={{1,0},{2,1},{3,2},{4,3},{5,4},{6,5},{7,6},{8,7},{9,8},{10,9},{11,1... | collective-permute-start | bytes 393224 | tf_op jit(solution)/shard_map/ppermute | solution.py:911
  36.2 0.6 shard_map.65
  36.8 0.3 collective-permute-done.8.yl
  37.1 2.7 %collective-permute-done.9.yr = f32[32,8,128]{2,1,0:T(8,128)S(1)} collective-permute-done((f32[32,8,128]{2,1,0:T(8,128)S(1)}, f32[32,8,128]{2,1,0:T(8,128)S(1)}, u32[]{:S(2)}, u32[]{:S(2)}) %collective-permute-start.9) | collective-permute-done | bytes 131104 | tf_op jit(solution)/shard_map/ppermute | solution.py:911
  39.7 0.0 collective-permute-done.7.right
  39.7 2.6 %collective-permute-done.6.left = f32[80,8,128]{2,1,0:T(8,128)S(1)} collective-permute-done((f32[80,8,128]{2,1,0:T(8,128)S(1)}, f32[80,8,128]{2,1,0:T(8,128)S(1)}, u32[]{:S(2)}, u32[]{:S(2)}) %collective-permute-start.6) | collective-permute-done | bytes 327712 | tf_op jit(solution)/shard_map/ppermute | solution.py:911
  42.3 5.7 %collective-permute-start.10 = (f32[36,8,128]{2,1,0:T(8,128)S(1)}, f32[36,8,128]{2,1,0:T(8,128)S(1)}, u32[]{:S(2)}, u32[]{:S(2)}) collective-permute-start(f32[36,8,128]{2,1,0:T(8,128)S(1)} %get-tuple-element.74), channel_id=1, source_target_pairs={{0,1},{1,2},{2,3},{3,4},{4,5},{5,6},{6,7},{7,8},{8,9},{9,10},{10,1... | collective-permute-start | bytes 442376 | tf_op jit(solution)/shard_map/ppermute | solution.py:911
  48.1 0.0 collective-permute-start.11
  48.1 2.2 %shard_map.67 = (f32[12,16,2,8,128]{4,3,2,1,0:T(8,128)S(1)}, f32[12,16,2,8,128]{4,3,2,1,0:T(8,128)S(1)}, f32[12,16,2,8,128]{4,3,2,1,0:T(8,128)S(1)}, f32[12,16,2...) custom-call(f32[80,8,128]{2,1,0:T(8,128)S(1)} %get-tuple-element.69., ...), custom_call_target="tpu_custom_call" | custom-call | bytes 6000000 | tf_op jit(solution)/shard_map/pallas_call | solution.py:32
  50.2 0.0 collective-permute-done.10.cl
  50.3 2.4 %collective-permute-done.11.cr = f32[36,8,128]{2,1,0:T(8,128)S(1)} collective-permute-done((f32[36,8,128]{2,1,0:T(8,128)S(1)}, f32[36,8,128]{2,1,0:T(8,128)S(1)}, u32[]{:S(2)}, u32[]{:S(2)}) %collective-permute-start.11) | collective-permute-done | bytes 147488 | tf_op jit(solution)/shard_map/ppermute | solution.py:911
  52.6 3.0 %shard_map.68 = (f32[8,16,8,256]{3,2,1,0:T(8,128)S(1)}, f32[8,16,8,256]{3,2,1,0:T(8,128)S(1)}, f32[1,128]{1,0:T(1,128)S(1)}, f32[1,128]{1,0:T(1,128)S(1)}) custom-call(f32[80,8,128]{2,1,0:T(8,128)S(1)} %get-tuple-element.69.own, f32[80,8,128]{2,1,0:T(8,128)S(1)} %collective-permute-done.6.left, f32[80,8,128]{2,1,0:T(8,128)S(1)} %collective-permute-done.7.right, ...), custom_call_target="tpu_custom_call" | custom-call | bytes 3000000 | tf_op jit(solution)/shard_map/pallas_call | solution.py:32
  55.6 0.1 collective-permute-start.12
  55.7 1.1 %collective-permute-done.12.b = f32[1,128]{1,0:T(1,128)S(1)} collective-permute-done((f32[1,128]{1,0:T(1,128)S(1)}, f32[1,128]{1,0:T(1,128)S(1)}, u32[]{:S(2)}, u32[]{:S(2)}) %collective-permute-start.12) | collective-permute-done | bytes 544 | tf_op jit(solution)/shard_map/ppermute | solution.py:1001
  56.8 0.1 shard_map.69
  56.9 20.9 %all_to_all.5.parts = f32[256,1,128]{2,1,0:T(1,128)S(1)} all-to-all(f32[256,1,128]{2,1,0:T(1,128)S(1)} %shard_map.69), channel_id=1, replica_groups=mesh['gx'=16,'gy'=16] {'gx','gy'}, dimensions={0} | all-to-all | bytes 262144 | tf_op jit(solution)/shard_map/all_to_all | solution.py:1003
  77.8 2.1 %shard_map.70 = (f32[8,8,16,256]{3,2,1,0:T(8,128)}, f32[1,8]{1,0:T(1,128)}) custom-call(f32[256,1,128]{2,1,0:T(1,128)S(1)} %all_to_all.5.parts, f32[8,16,8,256]{3,2,1,0:T(8,128)S(1)} %get-tuple-element.86.po, f32[8,16,8,256]{3,2,1,0:T(8,128)S(1)} %get-tuple-element.87.bo), custom_call_target="tpu_custom_call" | custom-call | bytes 3000000 | tf_op jit(solution)/shard_map/pallas_call | solution.py:32
  (1 shorter events, 0.0 us)
Async XLA Ops:
  0.6 9.3 %copy-start = (f32[8,8,16,256]{3,2,1,0:T(8,128)S(1)}, f32[8,8,16,256]{3,2,1,0:T(8,128)}, u32[]{:S(2)}) copy-start(f32[8,8,16,256]{3,2,1,0:T(8,128)} %v.3) | copy-start | bytes 3145732
  2.9 19.9 %collective-permute-start = (f32[31,16,256]{2,1,0:T(8,128)}, f32[31,16,256]{2,1,0:T(8,128)S(1)}, u32[]{:S(2)}, u32[]{:S(2)}) collective-permute-start(f32[31,16,256]{2,1,0:T(8,128)} %get-tuple-element.47), channel_id=1, source_target_pairs={{0,16},{16,32},{32,48},{48,64},{64,80},{80,96},{96,112},{112,128},... | collective-permute-start | bytes 1523720 | tf_op jit(solution)/shard_map/ppermute | solution.py:911
  5.0 17.7 %collective-permute-start.1 = (f32[30,16,256]{2,1,0:T(8,128)}, f32[30,16,256]{2,1,0:T(8,128)S(1)}, u32[]{:S(2)}, u32[]{:S(2)}) collective-permute-start(f32[30,16,256]{2,1,0:T(8,128)} %get-tuple-element.48), channel_id=1, source_target_pairs={{16,0},{32,16},{48,32},{64,48},{80,64},{96,80},{112,96},{128,112},... | collective-permute-start | bytes 1474568 | tf_op jit(solution)/shard_map/ppermute | solution.py:911
  10.6 6.2 %collective-permute-start.2 = (f32[36,8,256]{2,1,0:T(8,128)S(1)}, f32[36,8,256]{2,1,0:T(8,128)S(1)}, u32[]{:S(2)}, u32[]{:S(2)}) collective-permute-start(f32[36,8,256]{2,1,0:T(8,128)S(1)} %get-tuple-element.51), channel_id=1, source_target_pairs={{0,1},{1,2},{2,3},{3,4},{4,5},{5,6},{6,7},{7,8},{8,9},{9,10},{10,1... | collective-permute-start | bytes 884744 | tf_op jit(solution)/shard_map/ppermute | solution.py:911
  13.2 6.4 %collective-permute-start.3 = (f32[36,8,256]{2,1,0:T(8,128)S(1)}, f32[36,8,256]{2,1,0:T(8,128)S(1)}, u32[]{:S(2)}, u32[]{:S(2)}) collective-permute-start(f32[36,8,256]{2,1,0:T(8,128)S(1)} %get-tuple-element.52), channel_id=1, source_target_pairs={{1,0},{2,1},{3,2},{4,3},{5,4},{6,5},{7,6},{8,7},{9,8},{10,9},{11,1... | collective-permute-start | bytes 884744 | tf_op jit(solution)/shard_map/ppermute | solution.py:911
  23.0 6.0 %collective-permute-start.4 = (f32[10,8,256]{2,1,0:T(8,128)S(1)}, f32[10,8,256]{2,1,0:T(8,128)S(1)}, u32[]{:S(2)}, u32[]{:S(2)}) collective-permute-start(f32[10,8,256]{2,1,0:T(8,128)S(1)} %get-tuple-element.67), channel_id=1, source_target_pairs={{0,1},{1,2},{2,3},{3,4},{4,5},{5,6},{6,7},{7,8},{8,9},{9,10},{10,1... | collective-permute-start | bytes 245768 | tf_op jit(solution)/shard_map/ppermute | solution.py:911
  23.2 5.8 %collective-permute-start.5 = (f32[10,8,256]{2,1,0:T(8,128)S(1)}, f32[10,8,256]{2,1,0:T(8,128)S(1)}, u32[]{:S(2)}, u32[]{:S(2)}) collective-permute-start(f32[10,8,256]{2,1,0:T(8,128)S(1)} %get-tuple-element.68), channel_id=1, source_target_pairs={{1,0},{2,1},{3,2},{4,3},{5,4},{6,5},{7,6},{8,7},{9,8},{10,9},{11,1... | collective-permute-start | bytes 245768 | tf_op jit(solution)/shard_map/ppermute | solution.py:911
  29.7 10.0 %collective-permute-start.7 = (f32[80,8,128]{2,1,0:T(8,128)S(1)}, f32[80,8,128]{2,1,0:T(8,128)S(1)}, u32[]{:S(2)}, u32[]{:S(2)}) collective-permute-start(f32[80,8,128]{2,1,0:T(8,128)S(1)} %get-tuple-element.69.own), channel_id=1, source_target_pairs={{16,0},{32,16},{48,32},{64,48},{80,64},{96,80},{112,96},{128,112},... | collective-permute-start | bytes 983048 | tf_op jit(solution)/shard_map/ppermute | solution.py:911
  33.1 9.2 %collective-permute-start.6 = (f32[80,8,128]{2,1,0:T(8,128)S(1)}, f32[80,8,128]{2,1,0:T(8,128)S(1)}, u32[]{:S(2)}, u32[]{:S(2)}) collective-permute-start(f32[80,8,128]{2,1,0:T(8,128)S(1)} %get-tuple-element.69.own), channel_id=1, source_target_pairs={{0,16},{16,32},{32,48},{48,64},{64,80},{80,96},{96,112},{112,128},... | collective-permute-start | bytes 983048 | tf_op jit(solution)/shard_map/ppermute | solution.py:911
  33.1 4.0 %collective-permute-start.8 = (f32[32,8,128]{2,1,0:T(8,128)S(1)}, f32[32,8,128]{2,1,0:T(8,128)S(1)}, u32[]{:S(2)}, u32[]{:S(2)}) collective-permute-start(f32[32,8,128]{2,1,0:T(8,128)S(1)} %get-tuple-element.72), channel_id=1, source_target_pairs={{0,1},{1,2},{2,3},{3,4},{4,5},{5,6},{6,7},{7,8},{8,9},{9,10},{10,1... | collective-permute-start | bytes 393224 | tf_op jit(solution)/shard_map/ppermute | solution.py:911
  35.1 4.6 %collective-permute-start.9 = (f32[32,8,128]{2,1,0:T(8,128)S(1)}, f32[32,8,128]{2,1,0:T(8,128)S(1)}, u32[]{:S(2)}, u32[]{:S(2)}) collective-permute-start(f32[32,8,128]{2,1,0:T(8,128)S(1)} %get-tuple-element.73), channel_id=1, source_target_pairs={{1,0},{2,1},{3,2},{4,3},{5,4},{6,5},{7,6},{8,7},{9,8},{10,9},{11,1... | collective-permute-start | bytes 393224 | tf_op jit(solution)/shard_map/ppermute | solution.py:911
  42.3 7.9 %collective-permute-start.10 = (f32[36,8,128]{2,1,0:T(8,128)S(1)}, f32[36,8,128]{2,1,0:T(8,128)S(1)}, u32[]{:S(2)}, u32[]{:S(2)}) collective-permute-start(f32[36,8,128]{2,1,0:T(8,128)S(1)} %get-tuple-element.74), channel_id=1, source_target_pairs={{0,1},{1,2},{2,3},{3,4},{4,5},{5,6},{6,7},{7,8},{8,9},{9,10},{10,1... | collective-permute-start | bytes 442376 | tf_op jit(solution)/shard_map/ppermute | solution.py:911
  48.1 4.6 %collective-permute-start.11 = (f32[36,8,128]{2,1,0:T(8,128)S(1)}, f32[36,8,128]{2,1,0:T(8,128)S(1)}, u32[]{:S(2)}, u32[]{:S(2)}) collective-permute-start(f32[36,8,128]{2,1,0:T(8,128)S(1)} %get-tuple-element.75), channel_id=1, source_target_pairs={{1,0},{2,1},{3,2},{4,3},{5,4},{6,5},{7,6},{8,7},{9,8},{10,9},{11,1... | collective-permute-start | bytes 442376 | tf_op jit(solution)/shard_map/ppermute | solution.py:911
  55.6 1.2 %collective-permute-start.12 = (f32[1,128]{1,0:T(1,128)S(1)}, f32[1,128]{1,0:T(1,128)S(1)}, u32[]{:S(2)}, u32[]{:S(2)}) collective-permute-start(f32[1,128]{1,0:T(1,128)S(1)} %get-tuple-element.85), channel_id=1, source_target_pairs={{0,1},{1,0},{2,3},{3,2},{4,5},{5,4},{6,7},{7,6},{8,9},{9,8},{10,11... | collective-permute-start | bytes 1544 | tf_op jit(solution)/shard_map/ppermute | solution.py:1001

commit v10 on v9

--- a/solution.py
+++ b/solution.py
@@ -901,7 +901,7 @@
                     out[k, x, t : t + 8, z] = u
         return 0
 
-    lax.fori_loop(0, LX, body, 0)
+    lax.fori_loop(0, LX, body, 0, unroll=2)
 
 
 def both_ways(up, down, axis):

time: 80 us -> 80 us (level)
  no operation moved by 1% of the time
where the time goes in v10:
time: 80 us; the launch traced here: 79.8 us
  starting transfers between devices  22.5 us (28%)
  blocking collectives  20.9 us (26%)
  Pallas kernels  19.3 us (24%)
  waiting for transfers between devices  15.2 us (19%)
  other arithmetic  1.06 us (1%)
    ppermute x12, starting transfers between devices, both_ways(): return (lax.ppermute(up, axis, fwd), lax.ppermute(down, axis, back))  22.4 us
    all_to_all x1, blocking collectives, per_device(): parts = lax.all_to_all(sums, ('gx', 'gy'), 0, 0)  20.9 us
    pallas_call x12, Pallas kernels, call(): pl.pallas_call(body, out_shape=[jax.ShapeDtypeStruct(s, jnp.float32) for...  19.3 us
    ppermute x12, waiting for transfers between devices, both_ways(): return (lax.ppermute(up, axis, fwd), lax.ppermute(down, axis, back))  14.1 us
  transfers between devices with their start and end apart: 13, of which 7 were waited for; matrix products, arithmetic and copies ran while one was open for 1% of the time, Pallas kernels for 14%

profile of v10, /device:TPU:1, one launch (start us, length us, event | category | flops | bytes accessed | tf_op | source)
XLA Modules:
  0.0 79.8 jit_solution(13451673176954033526)
XLA Ops:
  0.6 0.0 copy-start
  0.6 2.3 %shard_map.60 = (f32[31,16,256]{2,1,0:T(8,128)}, f32[30,16,256]{2,1,0:T(8,128)}) custom-call(f32[8,8,16,256]{3,2,1,0:T(8,128)} %v.3, f32[8,16,256]{2,1,0:T(8,128)} %wx.1, f32[8,16,256]{2,1,0:T(8,128)} %wy.1, f32[8,16,256]{2,1,0:T(8,128)} %wz.1), custom_call_target="tpu_custom_call" | custom-call | bytes 3000000 | tf_op jit(solution)/shard_map/pallas_call | solution.py:32
  2.9 2.1 %collective-permute-start = (f32[31,16,256]{2,1,0:T(8,128)}, f32[31,16,256]{2,1,0:T(8,128)S(1)}, u32[]{:S(2)}, u32[]{:S(2)}) collective-permute-start(f32[31,16,256]{2,1,0:T(8,128)} %get-tuple-element.47), channel_id=1, source_target_pairs={{0,16},{16,32},{32,48},{48,64},{64,80},{80,96},{96,112},{112,128},... | collective-permute-start | bytes 1523720 | tf_op jit(solution)/shard_map/ppermute | solution.py:911
  5.0 3.8 %collective-permute-start.1 = (f32[30,16,256]{2,1,0:T(8,128)}, f32[30,16,256]{2,1,0:T(8,128)S(1)}, u32[]{:S(2)}, u32[]{:S(2)}) collective-permute-start(f32[30,16,256]{2,1,0:T(8,128)} %get-tuple-element.48), channel_id=1, source_target_pairs={{16,0},{32,16},{48,32},{64,48},{80,64},{96,80},{112,96},{128,112},... | collective-permute-start | bytes 1474568 | tf_op jit(solution)/shard_map/ppermute | solution.py:911
  8.9 1.1 %pad_maximum_fusion.w_ = f32[3,8,16,256]{3,2,1,0:T(8,128)S(1)} fusion(f32[1,8,16,256]{3,2,1,0:T(8,128)} %bitcast.4, f32[1,8,16,256]{3,2,1,0:T(8,128)} %bitcast.5, f32[1,8,16,256]{3,2,1,0:T(8,128)} %bitcast.6), kind=kLoop, calls=%fused_computation | loop fusion | flops 196608 | bytes 786432 | tf_op jit(solution)/shard_map/stack | solution.py:934
  9.9 0.0 copy-done
  9.9 0.7 shard_map.59
  10.6 2.5 %collective-permute-start.2 = (f32[36,8,256]{2,1,0:T(8,128)S(1)}, f32[36,8,256]{2,1,0:T(8,128)S(1)}, u32[]{:S(2)}, u32[]{:S(2)}) collective-permute-start(f32[36,8,256]{2,1,0:T(8,128)S(1)} %get-tuple-element.51), channel_id=1, source_target_pairs={{0,1},{1,2},{2,3},{3,4},{4,5},{5,6},{6,7},{7,8},{8,9},{9,10},{10,1... | collective-permute-start | bytes 884744 | tf_op jit(solution)/shard_map/ppermute | solution.py:911
  13.2 0.2 collective-permute-start.3
  13.4 3.4 %collective-permute-done.2.yl.gl = f32[36,8,256]{2,1,0:T(8,128)S(1)} collective-permute-done((f32[36,8,256]{2,1,0:T(8,128)S(1)}, f32[36,8,256]{2,1,0:T(8,128)S(1)}, u32[]{:S(2)}, u32[]{:S(2)}) %collective-permute-start.2) | collective-permute-done | bytes 294944 | tf_op jit(solution)/shard_map/ppermute | solution.py:911
  16.8 2.8 %collective-permute-done.3.yr.gr = f32[36,8,256]{2,1,0:T(8,128)S(1)} collective-permute-done((f32[36,8,256]{2,1,0:T(8,128)S(1)}, f32[36,8,256]{2,1,0:T(8,128)S(1)}, u32[]{:S(2)}, u32[]{:S(2)}) %collective-permute-start.3) | collective-permute-done | bytes 294944 | tf_op jit(solution)/shard_map/ppermute | solution.py:911
  19.6 3.2 %shard_map.61 = (f32[3,8,32,256]{3,2,1,0:T(8,128)S(1)}, f32[7,7,32,256]{3,2,1,0:T(8,128)S(1)}, f32[6,22,8,256]{3,2,1,0:T(8,128)S(1)}, f32[4,22,8,256]{3,2,1,0:T(...) custom-call(f32[8,16,8,256]{3,2,1,0:T(8,128)S(1)} %get-tuple-element.46.vt, ...), custom_call_target="tpu_custom_call" | custom-call | bytes 9000000 | tf_op jit(solution)/shard_map/pallas_call | solution.py:32
  22.8 0.0 collective-permute-done.1.rr
  22.8 0.0 collective-permute-done.rl
  22.8 0.2 shard_map.62
  23.0 0.2 collective-permute-start.4
  23.2 1.2 %collective-permute-start.5 = (f32[10,8,256]{2,1,0:T(8,128)S(1)}, f32[10,8,256]{2,1,0:T(8,128)S(1)}, u32[]{:S(2)}, u32[]{:S(2)}) collective-permute-start(f32[10,8,256]{2,1,0:T(8,128)S(1)} %get-tuple-element.68), channel_id=1, source_target_pairs={{1,0},{2,1},{3,2},{4,3},{5,4},{6,5},{7,6},{8,7},{9,8},{10,9},{11,1... | collective-permute-start | bytes 245768 | tf_op jit(solution)/shard_map/ppermute | solution.py:911
  24.4 4.5 %shard_map.63 = (f32[7,5,16,256]{3,2,1,0:T(8,128)S(1)}, f32[6,22,8,256]{3,2,1,0:T(8,128)S(1)}, f32[6,22,8,256]{3,2,1,0:T(8,128)S(1)}, f32[6,22,8,256]{3,2,1,0:T(...) custom-call(f32[8,16,8,256]{3,2,1,0:T(8,128)S(1)} %get-tuple-element.46.vt, ...), custom_call_target="tpu_custom_call" | custom-call | bytes 12000000 | tf_op jit(solution)/shard_map/pallas_call | solution.py:32
  29.0 0.0 collective-permute-done.4.cl
  29.0 0.0 collective-permute-done.5.cr
  29.0 0.7 shard_map.64
  29.7 3.4 %collective-permute-start.7 = (f32[80,8,128]{2,1,0:T(8,128)S(1)}, f32[80,8,128]{2,1,0:T(8,128)S(1)}, u32[]{:S(2)}, u32[]{:S(2)}) collective-permute-start(f32[80,8,128]{2,1,0:T(8,128)S(1)} %get-tuple-element.69.own), channel_id=1, source_target_pairs={{16,0},{32,16},{48,32},{64,48},{80,64},{96,80},{112,96},{128,112},... | collective-permute-start | bytes 983048 | tf_op jit(solution)/shard_map/ppermute | solution.py:911
  33.1 0.0 collective-permute-start.6
  33.1 2.0 %collective-permute-start.8 = (f32[32,8,128]{2,1,0:T(8,128)S(1)}, f32[32,8,128]{2,1,0:T(8,128)S(1)}, u32[]{:S(2)}, u32[]{:S(2)}) collective-permute-start(f32[32,8,128]{2,1,0:T(8,128)S(1)} %get-tuple-element.72), channel_id=1, source_target_pairs={{0,1},{1,2},{2,3},{3,4},{4,5},{5,6},{6,7},{7,8},{8,9},{9,10},{10,1... | collective-permute-start | bytes 393224 | tf_op jit(solution)/shard_map/ppermute | solution.py:911
  35.1 1.1 %collective-permute-start.9 = (f32[32,8,128]{2,1,0:T(8,128)S(1)}, f32[32,8,128]{2,1,0:T(8,128)S(1)}, u32[]{:S(2)}, u32[]{:S(2)}) collective-permute-start(f32[32,8,128]{2,1,0:T(8,128)S(1)} %get-tuple-element.73), channel_id=1, source_target_pairs={{1,0},{2,1},{3,2},{4,3},{5,4},{6,5},{7,6},{8,7},{9,8},{10,9},{11,1... | collective-permute-start | bytes 393224 | tf_op jit(solution)/shard_map/ppermute | solution.py:911
  36.2 0.6 shard_map.65
  36.8 0.3 collective-permute-done.8.yl
  37.1 2.7 %collective-permute-done.9.yr = f32[32,8,128]{2,1,0:T(8,128)S(1)} collective-permute-done((f32[32,8,128]{2,1,0:T(8,128)S(1)}, f32[32,8,128]{2,1,0:T(8,128)S(1)}, u32[]{:S(2)}, u32[]{:S(2)}) %collective-permute-start.9) | collective-permute-done | bytes 131104 | tf_op jit(solution)/shard_map/ppermute | solution.py:911
  39.7 0.0 collective-permute-done.7.right
  39.7 2.6 %collective-permute-done.6.left = f32[80,8,128]{2,1,0:T(8,128)S(1)} collective-permute-done((f32[80,8,128]{2,1,0:T(8,128)S(1)}, f32[80,8,128]{2,1,0:T(8,128)S(1)}, u32[]{:S(2)}, u32[]{:S(2)}) %collective-permute-start.6) | collective-permute-done | bytes 327712 | tf_op jit(solution)/shard_map/ppermute | solution.py:911
  42.3 5.7 %collective-permute-start.10 = (f32[36,8,128]{2,1,0:T(8,128)S(1)}, f32[36,8,128]{2,1,0:T(8,128)S(1)}, u32[]{:S(2)}, u32[]{:S(2)}) collective-permute-start(f32[36,8,128]{2,1,0:T(8,128)S(1)} %get-tuple-element.74), channel_id=1, source_target_pairs={{0,1},{1,2},{2,3},{3,4},{4,5},{5,6},{6,7},{7,8},{8,9},{9,10},{10,1... | collective-permute-start | bytes 442376 | tf_op jit(solution)/shard_map/ppermute | solution.py:911
  48.1 0.0 collective-permute-start.11
  48.1 2.2 %shard_map.67 = (f32[12,16,2,8,128]{4,3,2,1,0:T(8,128)S(1)}, f32[12,16,2,8,128]{4,3,2,1,0:T(8,128)S(1)}, f32[12,16,2,8,128]{4,3,2,1,0:T(8,128)S(1)}, f32[12,16,2...) custom-call(f32[80,8,128]{2,1,0:T(8,128)S(1)} %get-tuple-element.69., ...), custom_call_target="tpu_custom_call" | custom-call | bytes 6000000 | tf_op jit(solution)/shard_map/pallas_call | solution.py:32
  50.2 0.0 collective-permute-done.10.cl
  50.3 2.4 %collective-permute-done.11.cr = f32[36,8,128]{2,1,0:T(8,128)S(1)} collective-permute-done((f32[36,8,128]{2,1,0:T(8,128)S(1)}, f32[36,8,128]{2,1,0:T(8,128)S(1)}, u32[]{:S(2)}, u32[]{:S(2)}) %collective-permute-start.11) | collective-permute-done | bytes 147488 | tf_op jit(solution)/shard_map/ppermute | solution.py:911
  52.6 3.0 %shard_map.68 = (f32[8,16,8,256]{3,2,1,0:T(8,128)S(1)}, f32[8,16,8,256]{3,2,1,0:T(8,128)S(1)}, f32[1,128]{1,0:T(1,128)S(1)}, f32[1,128]{1,0:T(1,128)S(1)}) custom-call(f32[80,8,128]{2,1,0:T(8,128)S(1)} %get-tuple-element.69.own, f32[80,8,128]{2,1,0:T(8,128)S(1)} %collective-permute-done.6.left, f32[80,8,128]{2,1,0:T(8,128)S(1)} %collective-permute-done.7.right, ...), custom_call_target="tpu_custom_call" | custom-call | bytes 3000000 | tf_op jit(solution)/shard_map/pallas_call | solution.py:32
  55.6 0.1 collective-permute-start.12
  55.7 1.1 %collective-permute-done.12.b = f32[1,128]{1,0:T(1,128)S(1)} collective-permute-done((f32[1,128]{1,0:T(1,128)S(1)}, f32[1,128]{1,0:T(1,128)S(1)}, u32[]{:S(2)}, u32[]{:S(2)}) %collective-permute-start.12) | collective-permute-done | bytes 544 | tf_op jit(solution)/shard_map/ppermute | solution.py:1001
  56.8 0.1 shard_map.69
  56.9 20.9 %all_to_all.5.parts = f32[256,1,128]{2,1,0:T(1,128)S(1)} all-to-all(f32[256,1,128]{2,1,0:T(1,128)S(1)} %shard_map.69), channel_id=1, replica_groups=mesh['gx'=16,'gy'=16] {'gx','gy'}, dimensions={0} | all-to-all | bytes 262144 | tf_op jit(solution)/shard_map/all_to_all | solution.py:1003
  77.8 2.0 %shard_map.70 = (f32[8,8,16,256]{3,2,1,0:T(8,128)}, f32[1,8]{1,0:T(1,128)}) custom-call(f32[256,1,128]{2,1,0:T(1,128)S(1)} %all_to_all.5.parts, f32[8,16,8,256]{3,2,1,0:T(8,128)S(1)} %get-tuple-element.86.po, f32[8,16,8,256]{3,2,1,0:T(8,128)S(1)} %get-tuple-element.87.bo), custom_call_target="tpu_custom_call" | custom-call | bytes 3000000 | tf_op jit(solution)/shard_map/pallas_call | solution.py:32
  (1 shorter events, 0.0 us)
Async XLA Ops:
  0.6 9.3 %copy-start = (f32[8,8,16,256]{3,2,1,0:T(8,128)S(1)}, f32[8,8,16,256]{3,2,1,0:T(8,128)}, u32[]{:S(2)}) copy-start(f32[8,8,16,256]{3,2,1,0:T(8,128)} %v.3) | copy-start | bytes 3145732
  2.9 19.9 %collective-permute-start = (f32[31,16,256]{2,1,0:T(8,128)}, f32[31,16,256]{2,1,0:T(8,128)S(1)}, u32[]{:S(2)}, u32[]{:S(2)}) collective-permute-start(f32[31,16,256]{2,1,0:T(8,128)} %get-tuple-element.47), channel_id=1, source_target_pairs={{0,16},{16,32},{32,48},{48,64},{64,80},{80,96},{96,112},{112,128},... | collective-permute-start | bytes 1523720 | tf_op jit(solution)/shard_map/ppermute | solution.py:911
  5.0 17.7 %collective-permute-start.1 = (f32[30,16,256]{2,1,0:T(8,128)}, f32[30,16,256]{2,1,0:T(8,128)S(1)}, u32[]{:S(2)}, u32[]{:S(2)}) collective-permute-start(f32[30,16,256]{2,1,0:T(8,128)} %get-tuple-element.48), channel_id=1, source_target_pairs={{16,0},{32,16},{48,32},{64,48},{80,64},{96,80},{112,96},{128,112},... | collective-permute-start | bytes 1474568 | tf_op jit(solution)/shard_map/ppermute | solution.py:911
  10.6 6.2 %collective-permute-start.2 = (f32[36,8,256]{2,1,0:T(8,128)S(1)}, f32[36,8,256]{2,1,0:T(8,128)S(1)}, u32[]{:S(2)}, u32[]{:S(2)}) collective-permute-start(f32[36,8,256]{2,1,0:T(8,128)S(1)} %get-tuple-element.51), channel_id=1, source_target_pairs={{0,1},{1,2},{2,3},{3,4},{4,5},{5,6},{6,7},{7,8},{8,9},{9,10},{10,1... | collective-permute-start | bytes 884744 | tf_op jit(solution)/shard_map/ppermute | solution.py:911
  13.2 6.4 %collective-permute-start.3 = (f32[36,8,256]{2,1,0:T(8,128)S(1)}, f32[36,8,256]{2,1,0:T(8,128)S(1)}, u32[]{:S(2)}, u32[]{:S(2)}) collective-permute-start(f32[36,8,256]{2,1,0:T(8,128)S(1)} %get-tuple-element.52), channel_id=1, source_target_pairs={{1,0},{2,1},{3,2},{4,3},{5,4},{6,5},{7,6},{8,7},{9,8},{10,9},{11,1... | collective-permute-start | bytes 884744 | tf_op jit(solution)/shard_map/ppermute | solution.py:911
  23.0 6.0 %collective-permute-start.4 = (f32[10,8,256]{2,1,0:T(8,128)S(1)}, f32[10,8,256]{2,1,0:T(8,128)S(1)}, u32[]{:S(2)}, u32[]{:S(2)}) collective-permute-start(f32[10,8,256]{2,1,0:T(8,128)S(1)} %get-tuple-element.67), channel_id=1, source_target_pairs={{0,1},{1,2},{2,3},{3,4},{4,5},{5,6},{6,7},{7,8},{8,9},{9,10},{10,1... | collective-permute-start | bytes 245768 | tf_op jit(solution)/shard_map/ppermute | solution.py:911
  23.2 5.8 %collective-permute-start.5 = (f32[10,8,256]{2,1,0:T(8,128)S(1)}, f32[10,8,256]{2,1,0:T(8,128)S(1)}, u32[]{:S(2)}, u32[]{:S(2)}) collective-permute-start(f32[10,8,256]{2,1,0:T(8,128)S(1)} %get-tuple-element.68), channel_id=1, source_target_pairs={{1,0},{2,1},{3,2},{4,3},{5,4},{6,5},{7,6},{8,7},{9,8},{10,9},{11,1... | collective-permute-start | bytes 245768 | tf_op jit(solution)/shard_map/ppermute | solution.py:911
  29.7 10.0 %collective-permute-start.7 = (f32[80,8,128]{2,1,0:T(8,128)S(1)}, f32[80,8,128]{2,1,0:T(8,128)S(1)}, u32[]{:S(2)}, u32[]{:S(2)}) collective-permute-start(f32[80,8,128]{2,1,0:T(8,128)S(1)} %get-tuple-element.69.own), channel_id=1, source_target_pairs={{16,0},{32,16},{48,32},{64,48},{80,64},{96,80},{112,96},{128,112},... | collective-permute-start | bytes 983048 | tf_op jit(solution)/shard_map/ppermute | solution.py:911
  33.1 9.2 %collective-permute-start.6 = (f32[80,8,128]{2,1,0:T(8,128)S(1)}, f32[80,8,128]{2,1,0:T(8,128)S(1)}, u32[]{:S(2)}, u32[]{:S(2)}) collective-permute-start(f32[80,8,128]{2,1,0:T(8,128)S(1)} %get-tuple-element.69.own), channel_id=1, source_target_pairs={{0,16},{16,32},{32,48},{48,64},{64,80},{80,96},{96,112},{112,128},... | collective-permute-start | bytes 983048 | tf_op jit(solution)/shard_map/ppermute | solution.py:911
  33.1 4.0 %collective-permute-start.8 = (f32[32,8,128]{2,1,0:T(8,128)S(1)}, f32[32,8,128]{2,1,0:T(8,128)S(1)}, u32[]{:S(2)}, u32[]{:S(2)}) collective-permute-start(f32[32,8,128]{2,1,0:T(8,128)S(1)} %get-tuple-element.72), channel_id=1, source_target_pairs={{0,1},{1,2},{2,3},{3,4},{4,5},{5,6},{6,7},{7,8},{8,9},{9,10},{10,1... | collective-permute-start | bytes 393224 | tf_op jit(solution)/shard_map/ppermute | solution.py:911
  35.1 4.6 %collective-permute-start.9 = (f32[32,8,128]{2,1,0:T(8,128)S(1)}, f32[32,8,128]{2,1,0:T(8,128)S(1)}, u32[]{:S(2)}, u32[]{:S(2)}) collective-permute-start(f32[32,8,128]{2,1,0:T(8,128)S(1)} %get-tuple-element.73), channel_id=1, source_target_pairs={{1,0},{2,1},{3,2},{4,3},{5,4},{6,5},{7,6},{8,7},{9,8},{10,9},{11,1... | collective-permute-start | bytes 393224 | tf_op jit(solution)/shard_map/ppermute | solution.py:911
  42.3 7.9 %collective-permute-start.10 = (f32[36,8,128]{2,1,0:T(8,128)S(1)}, f32[36,8,128]{2,1,0:T(8,128)S(1)}, u32[]{:S(2)}, u32[]{:S(2)}) collective-permute-start(f32[36,8,128]{2,1,0:T(8,128)S(1)} %get-tuple-element.74), channel_id=1, source_target_pairs={{0,1},{1,2},{2,3},{3,4},{4,5},{5,6},{6,7},{7,8},{8,9},{9,10},{10,1... | collective-permute-start | bytes 442376 | tf_op jit(solution)/shard_map/ppermute | solution.py:911
  48.1 4.6 %collective-permute-start.11 = (f32[36,8,128]{2,1,0:T(8,128)S(1)}, f32[36,8,128]{2,1,0:T(8,128)S(1)}, u32[]{:S(2)}, u32[]{:S(2)}) collective-permute-start(f32[36,8,128]{2,1,0:T(8,128)S(1)} %get-tuple-element.75), channel_id=1, source_target_pairs={{1,0},{2,1},{3,2},{4,3},{5,4},{6,5},{7,6},{8,7},{9,8},{10,9},{11,1... | collective-permute-start | bytes 442376 | tf_op jit(solution)/shard_map/ppermute | solution.py:911
  55.6 1.2 %collective-permute-start.12 = (f32[1,128]{1,0:T(1,128)S(1)}, f32[1,128]{1,0:T(1,128)S(1)}, u32[]{:S(2)}, u32[]{:S(2)}) collective-permute-start(f32[1,128]{1,0:T(1,128)S(1)} %get-tuple-element.85), channel_id=1, source_target_pairs={{0,1},{1,0},{2,3},{3,2},{4,5},{5,4},{6,7},{7,6},{8,9},{9,8},{10,11... | collective-permute-start | bytes 1544 | tf_op jit(solution)/shard_map/ppermute | solution.py:1001
